TPU v7x, 256 devices: a whole 4x4x8 slice. The times are simulated.
256 devices in a mesh: dp: 4 (over z_hi, core), seq: 64 (over x, z_lo, y).
Axes of the slice: x: 4, y: 4, z: 8 (z_hi: 2, z_lo: 4; z = z_hi * 4 + z_lo), core: 2. Of those that a mesh axis runs over, the one named last changes fastest.
Arguments:
- inputs: bfloat16 [4, 8192, 1536], P('dp', 'seq'), may hold values from -16 to 16
- out_grad: bfloat16 [4, 8192, 1536], P('dp', 'seq'), may hold values from -16 to 16
- conv_weight: bfloat16 [3, 1536, 768], P(None, 'dp'), may hold values from -0.09375 to 0.09375
- point_weight: bfloat16 [768, 1536], P('dp'), may hold values from -0.21875 to 0.21875
Outputs:
- in_grad: bfloat16 [4, 8192, 1536], P('dp', 'seq')
- conv_grad: float32 [3, 1536, 768], P(None, ('dp', 'seq'))
- point_grad: float32 [768, 1536], P(('dp', 'seq'))
All inputs are finite; a program needn't handle non-finite values.
Results may differ from a plain program's by a relative error of at most 0.0065.
Values may be sent and summed in bfloat16 or wider, within the bound.
No kernel may reach another device: no remote copies, remote signals or barrier semaphores. Data moves between devices by JAX's collectives and lax.ppermute only.
A program may use at most 64 MiB of HBM per device.

v0:
```python
import jax
import jax.numpy as jnp
from jax import lax
from jax.experimental import pallas as pl
from jax.experimental.pallas import tpu as pltpu
from jax.sharding import PartitionSpec as P

DILATION_STEP = 1024
BF16 = jnp.bfloat16
F32 = jnp.float32


def coords(index):
    dp, seq = divmod(index, 64)
    return seq // 16, seq % 4, (dp // 2) * 4 + (seq // 4) % 4, dp % 2


def index_of(x, y, z, core):
    return ((z % 8) // 4 * 2 + core % 2) * 64 + (x % 4) * 16 + (z % 4) * 4 + y % 4


def send(value, target, sources=range(256)):
    pairs = [(device, index_of(*target(*coords(device)))) for device in sources]
    return lax.ppermute(value, ("dp", "seq"), pairs)


def send_a(value, steps):
    return send(value, lambda x, y, z, c: (x + steps * (1 - c), y + steps * c, z, c))


def send_b(value, steps):
    return send(value, lambda x, y, z, c: (x + steps * c, y + steps * (1 - c), z, c))


def shifted(value, steps):
    first, last = (max(0, -steps), min(64, 64 - steps))
    return lax.ppermute(value, "seq", [(source, source + steps) for source in range(first, last)])


def dot(left, right, dims):
    return lax.dot_general(left, right, ((dims[:1], dims[1:]), ((), ())), preferred_element_type=F32)


def pick(value, axis, index):
    return lax.dynamic_index_in_dim(value, index, axis, keepdims=False)


def run(kernel, scalars, arrays, outs, scratch=(), flops=0):
    vmem = pl.BlockSpec(memory_space=pltpu.VMEM)
    held = sum(v.size * v.dtype.itemsize for v in arrays)
    made = sum(o.size * o.dtype.itemsize for o in outs)
    return pl.pallas_call(
        kernel,
        out_shape=outs,
        in_specs=[pl.BlockSpec(memory_space=pltpu.SMEM)] + [vmem] * len(arrays),
        out_specs=[vmem] * len(outs),
        scratch_shapes=scratch,
        compiler_params=pltpu.CompilerParams(vmem_limit_bytes=48 * 1024 * 1024),
        cost_estimate=pl.CostEstimate(flops=flops, bytes_accessed=held + made, transcendentals=0),
    )(scalars, *arrays)


def shape(dims, dtype):
    return jax.ShapeDtypeStruct(tuple(dims), dtype)


def lanes(start, size):
    return pl.ds(pl.multiple_of(start * size, size), size)


def forward_kernel(meta, x0, x0o, x1, x1o, x2, x2o, og, ogo, mine, got, pw, far0, far1, far2, far3, order,
                   hg, hidden_t, taps, ogs, wfar, pws):
    core, zh, a, b = (meta[i] for i in range(4))
    rows = x0.shape[0]
    for k, (own, other) in enumerate(((x0, x0o), (x1, x1o), (x2, x2o))):
        taps[k, :rows] = own[...]
        taps[k, rows:] = other[...]
    ogs[:rows] = og[...]
    ogs[rows:] = ogo[...]
    piece, width = far0.shape[2:]
    for y in range(4):
        pws[y, zh] = pw[:, y * width:(y + 1) * width].reshape(4, piece, width)
    for j, far in enumerate((far0, far1, far2, far3)):
        for k in range(4):
            ak, bj = lax.rem(a + k, 4), lax.rem(b + j, 4)
            x, y = jnp.where(core == 0, ak, bj), jnp.where(core == 0, bj, ak)
            for t in range(3):
                wfar[t, x * 4 + y] = far[k, t]
            pws[y, 1 - zh, x] = far[k, 3]
    quarter = mine.shape[1]
    d = zh * 2 + core
    pre = jnp.zeros((2 * rows, width), F32)
    for t in range(3):
        pre += dot(taps[t, :, lanes(d, quarter)], mine[t], (1, 0))
        pre += dot(taps[t, :, lanes(zh * 2 + 1 - core, quarter)], got[t], (1, 0))
        pre += dot(taps[t, :, lanes(1 - zh, 2 * quarter)], wfar[t].reshape(2 * quarter, width), (1, 0))
    arriving = jnp.zeros((2 * rows, width), F32)
    for y in range(4):
        arriving += dot(ogs[:, y * width:(y + 1) * width], pws[y].reshape(width, width), (1, 1))
    scale, cubic = 0.7978845608028654, 0.044715
    square = pre * pre
    tanh = jnp.tanh(scale * (pre + cubic * (square * pre)))
    half = 0.5 * (1.0 + tanh)
    slope = half + 0.5 * pre * (1.0 - tanh * tanh) * (scale * (1.0 + 3.0 * cubic * square))
    hg[...] = (arriving * slope).astype(BF16)
    hidden_t[...] = dot(order[...], (pre * half).astype(BF16), (1, 1)).astype(BF16)


def gradient_kernel(meta, taps, ogs, hg, hidden_t, order, own, send1, send2, send3):
    core, zh = meta[0], meta[1]
    outs = (own, send1, send2, send3)
    both, width = hg.shape
    quarter = order.shape[0]
    unit, piece = quarter // 4, quarter // 16
    grads = hg[...]
    for u in range(2):
        moved = []
        for v in range(2):
            d = lax.rem(zh + u, 2) * 2 + lax.rem(core + v, 2)
            block = taps[:, :, lanes(d, quarter)].reshape(3 * both, quarter)
            moved.append(dot(order[...], block, (1, 1)).astype(BF16))
        for t in range(3):
            parts = [dot(m[:, t * both:(t + 1) * both], grads, (1, 0)) for m in moved]
            for r in range(4):
                for q in range(4):
                    at = r * unit + q * piece
                    pair = jnp.concatenate([p[at:at + piece] for p in parts], 0)
                    first = (t * 2 + u) * 2 * piece
                    outs[r][q, first:first + 2 * piece] = pair.astype(outs[r].dtype)
    unit = hidden_t.shape[0] // 4
    small = unit // 4
    base = 12 * piece
    for h in range(ogs.shape[1] // (2 * width)):
        parts = [dot(hidden_t[...], ogs[:, (2 * h + p) * width:(2 * h + p + 1) * width], (1, 0)) for p in range(2)]
        for r in range(4):
            for q in range(4):
                at = r * unit + q * small
                pair = jnp.concatenate([p[at:at + small] for p in parts], 0)
                first = base + h * 2 * small
                outs[r][q, first:first + 2 * small] = pair.astype(outs[r].dtype)


def reduce_kernel(meta, own, got1, got2, got3, kept, send1, send2, send3):
    for q, out in enumerate((kept, send1, send2, send3)):
        total = own[q] + got1[q].astype(F32) + got2[q].astype(F32) + got3[q].astype(F32)
        out[...] = total.astype(out.dtype)


def input_kernel(meta, hg, later, earlier, mine, got, wfar, kept, other):
    core, zh = meta[0], meta[1]
    quarter = mine.shape[1]
    rows = kept.shape[0]
    grads = (later[...], hg[...], earlier[...])
    for weights, at, size in ((mine, zh * 2 + core, quarter), (got, zh * 2 + 1 - core, quarter), (wfar, 1 - zh, 2 * quarter)):
        total = sum(dot(grads[t], weights[t], (1, 1)) for t in range(3))
        kept[:, lanes(at, size)] = total[:rows]
        other[:, lanes(at, size)] = total[rows:]


def local(inputs, out_grad, conv_weight, point_weight):
    x, og = inputs[0], out_grad[0]
    rows, C = x.shape
    H = conv_weight.shape[2]
    Cq, Hq, Hh = C // 4, H // 4, H // 2
    piece = C // 32
    hops = DILATION_STEP // rows
    dp, seq = lax.axis_index("dp"), lax.axis_index("seq")
    zh, core = dp // 2, dp % 2
    xi, zl, yi = seq // 16, seq // 4 % 4, seq % 4
    a, b = jnp.where(core == 0, xi, yi), jnp.where(core == 0, yi, xi)
    meta = jnp.stack([core, zh, a, b]).astype(jnp.int32)

    def columns(value, c):
        return jnp.concatenate(
            [lax.dynamic_slice_in_dim(value, half * 2 * Hq + c * Hq, Hq, 2) for half in (0, 1)], axis=2
        )

    at = xi * 4 + yi
    conv_piece = lax.dynamic_slice_in_dim(conv_weight, at % 8 * piece, piece, 1)
    point_piece = lax.dynamic_slice(point_weight, (xi * (Hq // 4), yi * Hh), (Hq // 4, Hh))
    holders = [d for d in range(256) if coords(d)[3] == coords(d)[0] // 2]

    def mirror(x, y, z, c):
        return x, y, 7 - z, c

    def partner(x, y, z, c):
        return x, y, z, 1 - c

    conv_piece = send(conv_piece, mirror, holders)
    point_piece = send(point_piece, mirror)
    prev, following = shifted(x, hops), shifted(x, -hops)
    conv_piece, point_piece, conv_weight, x_swap, og_swap = lax.optimization_barrier(
        (conv_piece, point_piece, conv_weight, x, og)
    )
    handed = send(columns(conv_piece, 1 - core), partner, holders)
    conv_piece = jnp.where(core == xi // 2, columns(conv_piece, core), handed)
    far = jnp.concatenate([conv_piece, point_piece[None]])
    far = jnp.stack([far] + [send_a(far, -k) for k in (1, 2, 3)])
    fars = [far] + [send_b(far, -k) for k in (1, 2, 3)]

    mine = columns(conv_weight, core)
    got = send(columns(conv_weight, 1 - core), partner)
    x_other, og_other = send(x_swap, partner), send(og_swap, partner)
    prev, following, fars[1] = lax.optimization_barrier((prev, following, fars[1]))
    prev_other, following_other = send(prev, partner), send(following, partner)

    def order(width, unit, count):
        new = jnp.arange(width)
        inner = new % (4 * unit)
        u = new // (4 * unit) % count
        r, q = new // (16 * unit * count), new // (4 * unit * count) % 4
        an, bn = (a + r) % 4, (b + q) % 4
        xn, yn = jnp.where(core == 0, an, bn), jnp.where(core == 0, bn, an)
        half = (zh + u) % 2 if count == 2 else 0
        old = half * (64 * unit) + xn * (16 * unit) + (zl + inner // unit) % 4 * (4 * unit) + yn * unit + inner % unit
        return (old[:, None] == jnp.arange(width)[None, :]).astype(BF16)

    hg, hidden_t, taps, ogs, wfar = run(
        forward_kernel,
        meta,
        [prev, prev_other, x, x_other, following, following_other, og, og_other, mine, got, point_weight, *fars,
         order(Hh, Hq // 64, 2)],
        [shape((2 * rows, Hh), BF16), shape((Hh, 2 * rows), BF16), shape((3, 2 * rows, C), BF16),
         shape((2 * rows, C), BF16), shape((3, 16, piece, Hh), BF16)],
        [pltpu.VMEM((4, 2, 4, Hq // 4, Hh), BF16)],
        flops=4 * 2 * 2 * rows * C * Hh,
    )
    later, earlier = shifted(hg, -hops), shifted(hg, hops)
    big = (4, 16 * piece // 2, Hh)
    own, *sends = run(
        gradient_kernel, meta, [taps, ogs, hg, hidden_t, order(Cq, Cq // 64, 1)],
        [shape(big, F32)] + [shape(big, BF16)] * 3,
        flops=4 * 2 * 2 * rows * C * Hh,
    )
    got_a = [send_a(part, k + 1) for k, part in enumerate(sends)]

    kept, other = run(
        input_kernel, meta, [hg, later, earlier, mine, got, wfar.reshape(3, 2 * Cq, Hh)],
        [shape((rows, C), F32)] * 2,
        flops=3 * 2 * 2 * rows * C * Hh,
    )
    in_grad = (og.astype(F32) + kept + send(other, partner)).astype(BF16)
    in_grad, *got_a = lax.optimization_barrier((in_grad, *got_a))

    own, *sends = run(reduce_kernel, meta, [own, *got_a], [shape(big[1:], F32)] + [shape(big[1:], BF16)] * 3)
    total = own
    for k, part in enumerate(sends):
        total = total + send_b(part, k + 1).astype(F32)
    n = 12 * (Cq // 16)
    conv = total[:n].reshape(3, 2, 2, 4, Cq // 64, Hh).transpose(3, 1, 0, 2, 4, 5).reshape(4, 2, -1, Hh)
    point = total[n:].reshape(C // Hh, 2, 4, Hq // 64, Hh).transpose(2, 1, 0, 3, 4).reshape(4, 2, -1, Hh)
    by_z = jnp.concatenate([conv, point], 2)
    last = by_z[0]
    for t in (1, 2, 3):
        got_z = send(by_z[t].astype(BF16), lambda x, y, z, c: (x, y, z // 4 * 4 + (z + t) % 4, c))
        last = last + got_z.astype(F32)
    last = last[0] + send(last[1].astype(BF16), lambda x, y, z, c: (x, y, z + 4, c)).astype(F32)
    n = conv.shape[2]
    conv = last[:n].reshape(3, 2, Cq // 64, Hh)
    point_mine = last[n:].reshape(C // Hh, Hq // 64, Hh).transpose(1, 0, 2).reshape(Hq // 64, C)
    kept, swapped = conv[:, 0], send(conv[:, 1], partner)
    kept, swapped = (part.reshape(3, Cq // 64, 2, 1, Hq) for part in (kept, swapped))
    conv_mine = jnp.where(
        core == 0, jnp.concatenate([kept, swapped], 3), jnp.concatenate([swapped, kept], 3)
    ).reshape(3, Cq // 64, H)
    return in_grad[None], conv_mine, point_mine


def solution(mesh):
    placed = (P("dp", "seq", None), P("dp", "seq", None), P(None, "dp", None), P("dp", None))
    return jax.shard_map(
        local,
        mesh=mesh,
        in_specs=placed,
        out_specs=(P("dp", "seq", None), P(None, ("dp", "seq"), None), P(("dp", "seq"), None)),
        check_vma=False,
    )
```

profile of v0, /device:TPU:1, one launch (start us, length us, event | category | flops | bytes accessed | tf_op | source)
XLA Modules:
  0.0 187.0 jit_solution(18213460122890361088)
XLA Ops:
  3.2 6.4 %collective-permute-start.3 = (bf16[48,384]{1,0:T(8,128)(2,1)S(1)}, bf16[48,384]{1,0:T(8,128)(2,1)S(1)}, u32[]{:S(2)}, u32[]{:S(2)}) collective-permute-start(bf16[48,384]{1,0:T(8,128)(2,1)S(1)} %dynamic_slice.31), channel_id=1, source_target_pairs={{0,140},{1,141},{2,142},{3,143},{4,136},{5,137},{6,138},{7,139},{8... | collective-permute-start | bytes 110600 | tf_op jit(solution)/shard_map/ppermute | solution.py:24
  12.5 7.6 %collective-permute-done.4 = bf16[3,48,384]{2,1,0:T(8,128)(2,1)S(1)} collective-permute-done((bf16[3,48,384]{2,1,0:T(8,128)(2,1)S(1)}, bf16[3,48,384]{2,1,0:T(8,128)(2,1)S(1)}, u32[]{:S(2)}, u32[]{:S(2)}) %collective-permute-start.4) | collective-permute-done | bytes 110624 | tf_op jit(solution)/shard_map/ppermute | solution.py:24
  21.6 2.6 %collective-permute-start.6 = (bf16[4,48,384]{2,1,0:T(8,128)(2,1)S(1)}, bf16[4,48,384]{2,1,0:T(8,128)(2,1)S(1)}, u32[]{:S(2)}, u32[]{:S(2)}) collective-permute-start(bf16[4,48,384]{2,1,0:T(8,128)(2,1)S(1)} %get-tuple-element.69), channel_id=1, source_target_pairs={{0,32},{1,33},{2,34},{3,35},{4,36},{5,37},{6,38},{7,39},{8,40},{9,... | collective-permute-start | bytes 442376 | tf_op jit(solution)/shard_map/ppermute | solution.py:24
  25.3 5.0 %collective-permute-start = (bf16[128,1536]{1,0:T(8,128)(2,1)S(1)}, bf16[128,1536]{1,0:T(8,128)(2,1)S(1)}, u32[]{:S(2)}, u32[]{:S(2)}) collective-permute-start(bf16[128,1536]{1,0:T(8,128)(2,1)S(1)} %bitcast.45), channel_id=1, source_target_pairs={{0,8},{1,9},{2,10},{3,11},{4,12},{5,13},{6,14},{7,15},{8,16},{9,17... | collective-permute-start | bytes 1179656 | tf_op jit(solution)/shard_map/ppermute | solution.py:37
  31.7 3.0 %collective-permute-start.8 = (bf16[4,4,48,384]{3,2,1,0:T(8,128)(2,1)S(1)}, bf16[4,4,48,384]{3,2,1,0:T(8,128)(2,1)S(1)}, u32[]{:S(2)}, u32[]{:S(2)}) collective-permute-start(bf16[4,4,48,384]{3,2,1,0:T(8,128)(2,1)S(1)} %pad_maximum_fusion.3.far0), channel_id=1, source_target_pairs={{0,3},{1,0},{2,1},{3,2},{4,7},{5,4},{6,5},{7,6},{8,11},{9,8},{10,9... | collective-permute-start | bytes 1769480 | tf_op jit(solution)/shard_map/ppermute | solution.py:24
  34.8 4.0 %constant_dynamic-slice_fusion.1 = (bf16[3,384,192]{2,1,0:T(8,128)(2,1)S(1)}, bf16[3,384,192]{2,1,0:T(8,128)(2,1)S(1)}, bf16[3,384,192]{2,1,0:T(8,128)(2,1)}, bf16[3,384,192]{2,1,0:T(8,128)(2,1)}) fusion(bf16[3,384,768]{2,1,0:T(8,128)(2,1)} %param.6, s32[]{:T(128)S(6)} %select_n.281, s32[]{:T(128)S(6)} %select_n.282, s32[]{:T(128)S(6)} %select_n.280, ...), kind=kLoop, calls=%fused_computation.71 | loop fusion | bytes 3538960 | tf_op jit(solution)/shard_map/dynamic_slice | solution.py:175
  41.3 23.9 %collective-permute-done.1.x2 = bf16[128,1536]{1,0:T(8,128)(2,1)} collective-permute-done((bf16[128,1536]{1,0:T(8,128)(2,1)S(1)}, bf16[128,1536]{1,0:T(8,128)(2,1)}, u32[]{:S(2)}, u32[]{:S(2)}) %collective-permute-start.1) | collective-permute-done | bytes 393248 | tf_op jit(solution)/shard_map/ppermute | solution.py:37
  67.7 2.5 %pad_maximum_fusion.mine = bf16[3,384,384]{2,1,0:T(8,128)(2,1)} fusion(bf16[3,384,192]{2,1,0:T(8,128)(2,1)} %get-tuple-element.59, bf16[3,384,192]{2,1,0:T(8,128)(2,1)} %get-tuple-element.60), kind=kLoop, calls=%fused_computation | loop fusion | flops 1769472 | bytes 1769472 | tf_op jit(solution)/shard_map/concatenate | solution.py:174
  70.2 5.6 %collective-permute-done.14.far2 = bf16[4,4,48,384]{3,2,1,0:T(8,128)(2,1)S(1)} collective-permute-done((bf16[4,4,48,384]{3,2,1,0:T(8,128)(2,1)S(1)}, bf16[4,4,48,384]{3,2,1,0:T(8,128)(2,1)S(1)}, u32[]{:S(2)}, u32[]{:S(2)}) %collective-permute-start.14) | collective-permute-done | bytes 589856 | tf_op jit(solution)/shard_map/ppermute | solution.py:24
  75.8 6.3 %collective-permute-done.15.far3 = bf16[4,4,48,384]{3,2,1,0:T(8,128)(2,1)S(1)} collective-permute-done((bf16[4,4,48,384]{3,2,1,0:T(8,128)(2,1)S(1)}, bf16[4,4,48,384]{3,2,1,0:T(8,128)(2,1)S(1)}, u32[]{:S(2)}, u32[]{:S(2)}) %collective-permute-start.15) | collective-permute-done | bytes 589856 | tf_op jit(solution)/shard_map/ppermute | solution.py:24
  83.2 6.2 %shard_map.67 = (bf16[256,384]{1,0:T(8,128)(2,1)S(1)}, bf16[384,256]{1,0:T(8,128)(2,1)S(1)}, bf16[3,256,1536]{2,1,0:T(8,128)(2,1)}, bf16[256,1536]{1,0:T(8,128)(2,1)}, bf16[3,16,48,384]{3,2,1,0:T(8,128)(2,1)}) custom-call(s32[4]{0:T(128)S(1)} %pad_add_fusion.meta, bf16[128,1536]{1,0:T(8,128)(2,1)S(1)} %copy-done.8, ...), custom_call_target="tpu_custom_call" | custom-call | flops 1207959552 | bytes 13467648 | tf_op jit(solution)/shard_map/pallas_call | solution.py:52
  90.8 4.9 %collective-permute-start.17 = (bf16[256,384]{1,0:T(8,128)(2,1)S(1)}, bf16[256,384]{1,0:T(8,128)(2,1)S(1)}, u32[]{:S(2)}, u32[]{:S(2)}) collective-permute-start(bf16[256,384]{1,0:T(8,128)(2,1)S(1)} %get-tuple-element.38.hg), channel_id=1, source_target_pairs={{0,8},{1,9},{2,10},{3,11},{4,12},{5,13},{6,14},{7,15},{8,16},{9,17... | collective-permute-start | bytes 589832 | tf_op jit(solution)/shard_map/ppermute | solution.py:37
  95.7 11.3 %collective-permute-done.16.later = bf16[256,384]{1,0:T(8,128)(2,1)S(1)} collective-permute-done((bf16[256,384]{1,0:T(8,128)(2,1)S(1)}, bf16[256,384]{1,0:T(8,128)(2,1)S(1)}, u32[]{:S(2)}, u32[]{:S(2)}) %collective-permute-start.16) | collective-permute-done | bytes 196640 | tf_op jit(solution)/shard_map/ppermute | solution.py:37
  112.6 6.1 %shard_map.69 = (f32[4,384,384]{2,1,0:T(8,128)}, bf16[4,384,384]{2,1,0:T(8,128)(2,1)S(1)}, bf16[4,384,384]{2,1,0:T(8,128)(2,1)S(1)}, bf16[4,384,384]{2,1,0:T(8,128)(2,1)S(1)}) custom-call(s32[4]{0:T(128)S(1)} %pad_add_fusion.meta, bf16[3,256,1536]{2,1,0:T(8,128)(2,1)} %get-tuple-element.42.taps, bf16[256,1536]{1,0:T(8,128)(2,1)S(1)} %copy-done.9, ...), custom_call_target="tpu_custom_call" | custom-call | flops 1207959552 | bytes 9732096 | tf_op jit(solution)/shard_map/pallas_call | solution.py:52
  122.5 25.3 %collective-permute-done.19.got1 = bf16[4,384,384]{2,1,0:T(8,128)(2,1)S(1)} collective-permute-done((bf16[4,384,384]{2,1,0:T(8,128)(2,1)S(1)}, bf16[4,384,384]{2,1,0:T(8,128)(2,1)S(1)}, u32[]{:S(2)}, u32[]{:S(2)}) %collective-permute-start.19) | collective-permute-done | bytes 1179680 | tf_op jit(solution)/shard_map/ppermute | solution.py:24
  148.5 2.2 %shard_map.70 = (f32[384,384]{1,0:T(8,128)S(1)}, bf16[384,384]{1,0:T(8,128)(2,1)S(1)}, bf16[384,384]{1,0:T(8,128)(2,1)S(1)}, bf16[384,384]{1,0:T(8,128)(2,1)S(1)}) custom-call(s32[4]{0:T(128)S(1)} %pad_add_fusion.meta, f32[4,384,384]{2,1,0:T(8,128)} %get-tuple-element.49.own, bf16[4,384,384]{2,1,0:T(8,128)(2,1)S(1)} %collective-permute-done.19.got1, ...), custom_call_target="tpu_custom_call" | custom-call | bytes 7372800 | tf_op jit(solution)/shard_map/pallas_call | solution.py:52
  150.7 5.3 %collective-permute-start.24 = (bf16[384,384]{1,0:T(8,128)(2,1)S(1)}, bf16[384,384]{1,0:T(8,128)(2,1)S(1)}, u32[]{:S(2)}, u32[]{:S(2)}) collective-permute-start(bf16[384,384]{1,0:T(8,128)(2,1)S(1)} %get-tuple-element.56), channel_id=1, source_target_pairs={{0,3},{1,0},{2,1},{3,2},{4,7},{5,4},{6,5},{7,6},{8,11},{9,8},{10,9... | collective-permute-start | bytes 884744 | tf_op jit(solution)/shard_map/ppermute | solution.py:24
  157.9 2.6 %collective-permute-done.24 = bf16[384,384]{1,0:T(8,128)(2,1)S(1)} collective-permute-done((bf16[384,384]{1,0:T(8,128)(2,1)S(1)}, bf16[384,384]{1,0:T(8,128)(2,1)S(1)}, u32[]{:S(2)}, u32[]{:S(2)}) %collective-permute-start.24) | collective-permute-done | bytes 294944 | tf_op jit(solution)/shard_map/ppermute | solution.py:24
  160.5 2.7 %collective-permute-done.23 = bf16[384,384]{1,0:T(8,128)(2,1)S(1)} collective-permute-done((bf16[384,384]{1,0:T(8,128)(2,1)S(1)}, bf16[384,384]{1,0:T(8,128)(2,1)S(1)}, u32[]{:S(2)}, u32[]{:S(2)}) %collective-permute-start.23) | collective-permute-done | bytes 294944 | tf_op jit(solution)/shard_map/ppermute | solution.py:24
  163.2 3.1 %collective-permute-done.22 = bf16[384,384]{1,0:T(8,128)(2,1)S(1)} collective-permute-done((bf16[384,384]{1,0:T(8,128)(2,1)S(1)}, bf16[384,384]{1,0:T(8,128)(2,1)S(1)}, u32[]{:S(2)}, u32[]{:S(2)}) %collective-permute-start.22) | collective-permute-done | bytes 294944 | tf_op jit(solution)/shard_map/ppermute | solution.py:24
  169.1 2.4 %collective-permute-done.27 = bf16[2,48,384]{2,0,1:T(2,128)(2,1)S(1)} collective-permute-done((bf16[2,48,384]{2,0,1:T(2,128)(2,1)S(1)}, bf16[2,48,384]{2,0,1:T(2,128)(2,1)S(1)}, u32[]{:S(2)}, u32[]{:S(2)}) %collective-permute-start.27) | collective-permute-done | bytes 73760 | tf_op jit(solution)/shard_map/ppermute | solution.py:24
  171.5 4.2 %collective-permute-done.26 = bf16[2,48,384]{2,0,1:T(2,128)(2,1)S(1)} collective-permute-done((bf16[2,48,384]{2,0,1:T(2,128)(2,1)S(1)}, bf16[2,48,384]{2,0,1:T(2,128)(2,1)S(1)}, u32[]{:S(2)}, u32[]{:S(2)}) %collective-permute-start.26) | collective-permute-done | bytes 73760 | tf_op jit(solution)/shard_map/ppermute | solution.py:24
  176.0 4.5 %collective-permute-start.28 = (bf16[48,384]{1,0:T(8,128)(2,1)S(1)}, bf16[48,384]{1,0:T(8,128)(2,1)S(1)}, u32[]{:S(2)}, u32[]{:S(2)}) collective-permute-start(bf16[48,384]{1,0:T(8,128)(2,1)S(1)} %bitcast.61), channel_id=1, source_target_pairs={{0,128},{1,129},{2,130},{3,131},{4,132},{5,133},{6,134},{7,135},{8... | collective-permute-start | bytes 110600 | tf_op jit(solution)/shard_map/ppermute | solution.py:24
  180.5 2.4 %collective-permute-done.28 = bf16[48,384]{1,0:T(8,128)(2,1)S(1)} collective-permute-done((bf16[48,384]{1,0:T(8,128)(2,1)S(1)}, bf16[48,384]{1,0:T(8,128)(2,1)S(1)}, u32[]{:S(2)}, u32[]{:S(2)}) %collective-permute-start.28) | collective-permute-done | bytes 36896 | tf_op jit(solution)/shard_map/ppermute | solution.py:24
  (102 shorter events, 35.7 us)
Async XLA Ops:
  1.7 9.2 %collective-permute-start.2 = (bf16[3,48,768]{2,1,0:T(8,128)(2,1)S(1)}, bf16[3,48,768]{2,1,0:T(8,128)(2,1)S(1)}, u32[]{:S(2)}, u32[]{:S(2)}) collective-permute-start(bf16[3,48,768]{2,1,0:T(8,128)(2,1)S(1)} %constant_dynamic-slice_fusion.8), channel_id=1, source_target_pairs={{0,140},{1,141},{2,142},{3,143},{4,136},{5,137},{6,138},{7,139},{8... | collective-permute-start | bytes 663560 | tf_op jit(solution)/shard_map/ppermute | solution.py:24
  3.2 7.8 %collective-permute-start.3 = (bf16[48,384]{1,0:T(8,128)(2,1)S(1)}, bf16[48,384]{1,0:T(8,128)(2,1)S(1)}, u32[]{:S(2)}, u32[]{:S(2)}) collective-permute-start(bf16[48,384]{1,0:T(8,128)(2,1)S(1)} %dynamic_slice.31), channel_id=1, source_target_pairs={{0,140},{1,141},{2,142},{3,143},{4,136},{5,137},{6,138},{7,139},{8... | collective-permute-start | bytes 110600 | tf_op jit(solution)/shard_map/ppermute | solution.py:24
  11.2 8.9 %collective-permute-start.4 = (bf16[3,48,384]{2,1,0:T(8,128)(2,1)S(1)}, bf16[3,48,384]{2,1,0:T(8,128)(2,1)S(1)}, u32[]{:S(2)}, u32[]{:S(2)}) collective-permute-start(bf16[3,48,384]{2,1,0:T(8,128)(2,1)S(1)} %pad_maximum_fusion.5), channel_id=1, source_target_pairs={{0,64},{1,65},{2,66},{3,67},{4,68},{5,69},{6,70},{7,71},{8,72},{9,... | collective-permute-start | bytes 331784 | tf_op jit(solution)/shard_map/ppermute | solution.py:24
  20.2 11.4 %collective-permute-start.7 = (bf16[4,48,384]{2,1,0:T(8,128)(2,1)S(1)}, bf16[4,48,384]{2,1,0:T(8,128)(2,1)S(1)}, u32[]{:S(2)}, u32[]{:S(2)}) collective-permute-start(bf16[4,48,384]{2,1,0:T(8,128)(2,1)S(1)} %get-tuple-element.69), channel_id=1, source_target_pairs={{0,16},{1,17},{2,18},{3,19},{4,20},{5,21},{6,22},{7,23},{8,24},{9,... | collective-permute-start | bytes 442376 | tf_op jit(solution)/shard_map/ppermute | solution.py:24
  21.6 10.0 %collective-permute-start.6 = (bf16[4,48,384]{2,1,0:T(8,128)(2,1)S(1)}, bf16[4,48,384]{2,1,0:T(8,128)(2,1)S(1)}, u32[]{:S(2)}, u32[]{:S(2)}) collective-permute-start(bf16[4,48,384]{2,1,0:T(8,128)(2,1)S(1)} %get-tuple-element.69), channel_id=1, source_target_pairs={{0,32},{1,33},{2,34},{3,35},{4,36},{5,37},{6,38},{7,39},{8,40},{9,... | collective-permute-start | bytes 442376 | tf_op jit(solution)/shard_map/ppermute | solution.py:24
  25.3 15.3 %collective-permute-start = (bf16[128,1536]{1,0:T(8,128)(2,1)S(1)}, bf16[128,1536]{1,0:T(8,128)(2,1)S(1)}, u32[]{:S(2)}, u32[]{:S(2)}) collective-permute-start(bf16[128,1536]{1,0:T(8,128)(2,1)S(1)} %bitcast.45), channel_id=1, source_target_pairs={{0,8},{1,9},{2,10},{3,11},{4,12},{5,13},{6,14},{7,15},{8,16},{9,17... | collective-permute-start | bytes 1179656 | tf_op jit(solution)/shard_map/ppermute | solution.py:37
  30.3 35.0 %collective-permute-start.1 = (bf16[128,1536]{1,0:T(8,128)(2,1)S(1)}, bf16[128,1536]{1,0:T(8,128)(2,1)}, u32[]{:S(2)}, u32[]{:S(2)}) collective-permute-start(bf16[128,1536]{1,0:T(8,128)(2,1)S(1)} %bitcast.46), channel_id=1, source_target_pairs={{8,0},{9,1},{10,2},{11,3},{12,4},{13,5},{14,6},{15,7},{16,8},{17,9... | collective-permute-start | bytes 1179656 | tf_op jit(solution)/shard_map/ppermute | solution.py:37
  31.7 34.5 %collective-permute-start.8 = (bf16[4,4,48,384]{3,2,1,0:T(8,128)(2,1)S(1)}, bf16[4,4,48,384]{3,2,1,0:T(8,128)(2,1)S(1)}, u32[]{:S(2)}, u32[]{:S(2)}) collective-permute-start(bf16[4,4,48,384]{3,2,1,0:T(8,128)(2,1)S(1)} %pad_maximum_fusion.3.far0), channel_id=1, source_target_pairs={{0,3},{1,0},{2,1},{3,2},{4,7},{5,4},{6,5},{7,6},{8,11},{9,8},{10,9... | collective-permute-start | bytes 1769480 | tf_op jit(solution)/shard_map/ppermute | solution.py:24
  40.1 42.1 %collective-permute-start.13 = (bf16[3,384,384]{2,1,0:T(8,128)(2,1)}, bf16[3,384,384]{2,1,0:T(8,128)(2,1)S(1)}, u32[]{:S(2)}, u32[]{:S(2)}) collective-permute-start(bf16[3,384,384]{2,1,0:T(8,128)(2,1)} %pad_maximum_fusion.1), channel_id=1, source_target_pairs={{0,64},{1,65},{2,66},{3,67},{4,68},{5,69},{6,70},{7,71},{8,72},{9,... | collective-permute-start | bytes 2654216 | tf_op jit(solution)/shard_map/ppermute | solution.py:24
  40.1 26.2 %collective-permute-start.10 = (bf16[128,1536]{1,0:T(8,128)(2,1)S(1)}, bf16[128,1536]{1,0:T(8,128)(2,1)}, u32[]{:S(2)}, u32[]{:S(2)}) collective-permute-start(bf16[128,1536]{1,0:T(8,128)(2,1)S(1)} %bitcast.47), channel_id=1, source_target_pairs={{0,64},{1,65},{2,66},{3,67},{4,68},{5,69},{6,70},{7,71},{8,72},{9,... | collective-permute-start | bytes 1179656 | tf_op jit(solution)/shard_map/ppermute | solution.py:24
  41.3 25.9 %collective-permute-start.12 = (bf16[128,1536]{1,0:T(8,128)(2,1)S(1)}, bf16[128,1536]{1,0:T(8,128)(2,1)}, u32[]{:S(2)}, u32[]{:S(2)}) collective-permute-start(bf16[128,1536]{1,0:T(8,128)(2,1)S(1)} %bitcast.43), channel_id=1, source_target_pairs={{0,64},{1,65},{2,66},{3,67},{4,68},{5,69},{6,70},{7,71},{8,72},{9,... | collective-permute-start | bytes 1179656 | tf_op jit(solution)/shard_map/ppermute | solution.py:24
  65.3 10.6 %collective-permute-start.14 = (bf16[4,4,48,384]{3,2,1,0:T(8,128)(2,1)S(1)}, bf16[4,4,48,384]{3,2,1,0:T(8,128)(2,1)S(1)}, u32[]{:S(2)}, u32[]{:S(2)}) collective-permute-start(bf16[4,4,48,384]{3,2,1,0:T(8,128)(2,1)S(1)} %pad_maximum_fusion.3.far0), channel_id=1, source_target_pairs={{0,2},{1,3},{2,0},{3,1},{4,6},{5,7},{6,4},{7,5},{8,10},{9,11},{10,... | collective-permute-start | bytes 1769480 | tf_op jit(solution)/shard_map/ppermute | solution.py:24
  66.2 15.9 %collective-permute-start.15 = (bf16[4,4,48,384]{3,2,1,0:T(8,128)(2,1)S(1)}, bf16[4,4,48,384]{3,2,1,0:T(8,128)(2,1)S(1)}, u32[]{:S(2)}, u32[]{:S(2)}) collective-permute-start(bf16[4,4,48,384]{3,2,1,0:T(8,128)(2,1)S(1)} %pad_maximum_fusion.3.far0), channel_id=1, source_target_pairs={{0,1},{1,2},{2,3},{3,0},{4,5},{5,6},{6,7},{7,4},{8,9},{9,10},{10,1... | collective-permute-start | bytes 1769480 | tf_op jit(solution)/shard_map/ppermute | solution.py:24
  66.3 15.8 %collective-permute-start.9 = (bf16[128,1536]{1,0:T(8,128)(2,1)}, bf16[128,1536]{1,0:T(8,128)(2,1)S(1)}, u32[]{:S(2)}, u32[]{:S(2)}) collective-permute-start(bf16[128,1536]{1,0:T(8,128)(2,1)} %copy-done.7), channel_id=1, source_target_pairs={{0,64},{1,65},{2,66},{3,67},{4,68},{5,69},{6,70},{7,71},{8,72},{9,... | collective-permute-start | bytes 1179656 | tf_op jit(solution)/shard_map/ppermute | solution.py:24
  67.2 14.9 %collective-permute-start.11 = (bf16[128,1536]{1,0:T(8,128)(2,1)}, bf16[128,1536]{1,0:T(8,128)(2,1)S(1)}, u32[]{:S(2)}, u32[]{:S(2)}) collective-permute-start(bf16[128,1536]{1,0:T(8,128)(2,1)} %collective-permute-done.1.x2), channel_id=1, source_target_pairs={{0,64},{1,65},{2,66},{3,67},{4,68},{5,69},{6,70},{7,71},{8,72},{9,... | collective-permute-start | bytes 1179656 | tf_op jit(solution)/shard_map/ppermute | solution.py:24
  89.5 17.5 %collective-permute-start.16 = (bf16[256,384]{1,0:T(8,128)(2,1)S(1)}, bf16[256,384]{1,0:T(8,128)(2,1)S(1)}, u32[]{:S(2)}, u32[]{:S(2)}) collective-permute-start(bf16[256,384]{1,0:T(8,128)(2,1)S(1)} %get-tuple-element.38.hg), channel_id=1, source_target_pairs={{8,0},{9,1},{10,2},{11,3},{12,4},{13,5},{14,6},{15,7},{16,8},{17,9... | collective-permute-start | bytes 589832 | tf_op jit(solution)/shard_map/ppermute | solution.py:37
  90.8 16.2 %collective-permute-start.17 = (bf16[256,384]{1,0:T(8,128)(2,1)S(1)}, bf16[256,384]{1,0:T(8,128)(2,1)S(1)}, u32[]{:S(2)}, u32[]{:S(2)}) collective-permute-start(bf16[256,384]{1,0:T(8,128)(2,1)S(1)} %get-tuple-element.38.hg), channel_id=1, source_target_pairs={{0,8},{1,9},{2,10},{3,11},{4,12},{5,13},{6,14},{7,15},{8,16},{9,17... | collective-permute-start | bytes 589832 | tf_op jit(solution)/shard_map/ppermute | solution.py:37
  111.7 9.9 %collective-permute-start.18 = (f32[128,1536]{1,0:T(8,128)S(1)}, f32[128,1536]{1,0:T(8,128)S(1)}, u32[]{:S(2)}, u32[]{:S(2)}) collective-permute-start(f32[128,1536]{1,0:T(8,128)S(1)} %get-tuple-element.41), channel_id=1, source_target_pairs={{0,64},{1,65},{2,66},{3,67},{4,68},{5,69},{6,70},{7,71},{8,72},{9,... | collective-permute-start | bytes 2359304 | tf_op jit(solution)/shard_map/ppermute | solution.py:24
  118.7 29.2 %collective-permute-start.19 = (bf16[4,384,384]{2,1,0:T(8,128)(2,1)S(1)}, bf16[4,384,384]{2,1,0:T(8,128)(2,1)S(1)}, u32[]{:S(2)}, u32[]{:S(2)}) collective-permute-start(bf16[4,384,384]{2,1,0:T(8,128)(2,1)S(1)} %get-tuple-element.45), channel_id=1, source_target_pairs={{0,16},{1,17},{2,18},{3,19},{4,20},{5,21},{6,22},{7,23},{8,24},{9,... | collective-permute-start | bytes 3538952 | tf_op jit(solution)/shard_map/ppermute | solution.py:24
  119.3 28.6 %collective-permute-start.20 = (bf16[4,384,384]{2,1,0:T(8,128)(2,1)S(1)}, bf16[4,384,384]{2,1,0:T(8,128)(2,1)S(1)}, u32[]{:S(2)}, u32[]{:S(2)}) collective-permute-start(bf16[4,384,384]{2,1,0:T(8,128)(2,1)S(1)} %get-tuple-element.46), channel_id=1, source_target_pairs={{0,32},{1,33},{2,34},{3,35},{4,36},{5,37},{6,38},{7,39},{8,40},{9,... | collective-permute-start | bytes 3538952 | tf_op jit(solution)/shard_map/ppermute | solution.py:24
  119.5 29.0 %collective-permute-start.21 = (bf16[4,384,384]{2,1,0:T(8,128)(2,1)S(1)}, bf16[4,384,384]{2,1,0:T(8,128)(2,1)S(1)}, u32[]{:S(2)}, u32[]{:S(2)}) collective-permute-start(bf16[4,384,384]{2,1,0:T(8,128)(2,1)S(1)} %get-tuple-element.47), channel_id=1, source_target_pairs={{0,48},{1,49},{2,50},{3,51},{4,52},{5,53},{6,54},{7,55},{8,56},{9,... | collective-permute-start | bytes 3538952 | tf_op jit(solution)/shard_map/ppermute | solution.py:24
  150.7 9.8 %collective-permute-start.24 = (bf16[384,384]{1,0:T(8,128)(2,1)S(1)}, bf16[384,384]{1,0:T(8,128)(2,1)S(1)}, u32[]{:S(2)}, u32[]{:S(2)}) collective-permute-start(bf16[384,384]{1,0:T(8,128)(2,1)S(1)} %get-tuple-element.56), channel_id=1, source_target_pairs={{0,3},{1,0},{2,1},{3,2},{4,7},{5,4},{6,5},{7,6},{8,11},{9,8},{10,9... | collective-permute-start | bytes 884744 | tf_op jit(solution)/shard_map/ppermute | solution.py:24
  157.9 8.4 %collective-permute-start.22 = (bf16[384,384]{1,0:T(8,128)(2,1)S(1)}, bf16[384,384]{1,0:T(8,128)(2,1)S(1)}, u32[]{:S(2)}, u32[]{:S(2)}) collective-permute-start(bf16[384,384]{1,0:T(8,128)(2,1)S(1)} %get-tuple-element.54), channel_id=1, source_target_pairs={{0,1},{1,2},{2,3},{3,0},{4,5},{5,6},{6,7},{7,4},{8,9},{9,10},{10,1... | collective-permute-start | bytes 884744 | tf_op jit(solution)/shard_map/ppermute | solution.py:24
  168.1 7.6 %collective-permute-start.26 = (bf16[2,48,384]{2,0,1:T(2,128)(2,1)S(1)}, bf16[2,48,384]{2,0,1:T(2,128)(2,1)S(1)}, u32[]{:S(2)}, u32[]{:S(2)}) collective-permute-start(bf16[2,48,384]{2,0,1:T(2,128)(2,1)S(1)} %get-tuple-element.63), channel_id=1, source_target_pairs={{0,8},{1,9},{2,10},{3,11},{4,12},{5,13},{6,14},{7,15},{8,0},{9,1},... | collective-permute-start | bytes 221192 | tf_op jit(solution)/shard_map/ppermute | solution.py:24
  (17 other events, 194.7 us)
where the time goes:
time: 187 us
  waiting for transfers between devices  99.5 us (53%)
  starting transfers between devices  50.7 us (27%)
  Pallas kernels  16.7 us (9%)
  local copies, waits for them, and re-layouts  13 us (7%)
  other arithmetic  6.05 us (3%)
    ppermute x26, waiting for transfers between devices, send(): return lax.ppermute(value, ('dp', 'seq'), pairs)  64.3 us
    ppermute x26, starting transfers between devices, send(): return lax.ppermute(value, ('dp', 'seq'), pairs)  38.2 us
    ppermute x4, waiting for transfers between devices, shifted(): lax.ppermute(value, 'seq', [(source, source + steps) for source in range(...  35.2 us
    pallas_call x4, Pallas kernels, run(): pl.pallas_call(kernel, out_shape=outs, in_specs=[pl.BlockSpec(memory_spac...  16.7 us
    ppermute x4, starting transfers between devices, shifted(): lax.ppermute(value, 'seq', [(source, source + steps) for source in range(...  12.4 us
    unnamed x23, local copies, waits for them, and re-layouts  4.51 us
    dynamic_slice x2, local copies, waits for them, and re-layouts, columns(): lax.dynamic_slice_in_dim(value, half * 2 * Hq + c * Hq, Hq, 2)  4.2 us
    concatenate x3, other arithmetic, columns(): jnp.concatenate([lax.dynamic_slice_in_dim(value, half * 2 * Hq + c * Hq,...  3.9 us
  transfers between devices with their start and end apart: 30, of which 15 were waited for; matrix products, arithmetic and copies ran while one was open for 6% of the time, Pallas kernels for 3%

commit v1 on v0

v1 whole, which is shorter than its diff:
```python
import jax
import jax.numpy as jnp
from jax import lax
from jax.experimental import pallas as pl
from jax.experimental.pallas import tpu as pltpu
from jax.sharding import PartitionSpec as P

DILATION_STEP = 1024
BF16 = jnp.bfloat16
F32 = jnp.float32


def coords(index):
    dp, seq = divmod(index, 64)
    return seq // 16, seq % 4, (dp // 2) * 4 + (seq // 4) % 4, dp % 2


def index_of(x, y, z, core):
    return ((z % 8) // 4 * 2 + core % 2) * 64 + (x % 4) * 16 + (z % 4) * 4 + y % 4


def send(value, target, sources=range(256)):
    pairs = [(device, index_of(*target(*coords(device)))) for device in sources]
    return lax.ppermute(value, ("dp", "seq"), pairs)


def send_a(value, steps):
    return send(value, lambda x, y, z, c: (x + steps * (1 - c), y + steps * c, z, c))


def send_b(value, steps):
    return send(value, lambda x, y, z, c: (x + steps * c, y + steps * (1 - c), z, c))


def shifted(value, steps):
    first, last = (max(0, -steps), min(64, 64 - steps))
    return lax.ppermute(value, "seq", [(source, source + steps) for source in range(first, last)])


def dot(left, right, dims):
    return lax.dot_general(left, right, ((dims[:1], dims[1:]), ((), ())), preferred_element_type=F32)


def pick(value, axis, index):
    return lax.dynamic_index_in_dim(value, index, axis, keepdims=False)


def run(kernel, scalars, arrays, outs, scratch=()):
    vmem = pl.BlockSpec(memory_space=pltpu.VMEM)
    return pl.pallas_call(
        kernel,
        out_shape=outs,
        in_specs=[pl.BlockSpec(memory_space=pltpu.SMEM)] + [vmem] * len(arrays),
        out_specs=[vmem] * len(outs),
        scratch_shapes=scratch,
        compiler_params=pltpu.CompilerParams(vmem_limit_bytes=48 * 1024 * 1024),
        cost_estimate=pl.CostEstimate(flops=1, bytes_accessed=1, transcendentals=0),
    )(scalars, *arrays)


def shape(dims, dtype):
    return jax.ShapeDtypeStruct(tuple(dims), dtype)


def lanes(start, size):
    return pl.ds(pl.multiple_of(start * size, size), size)


def near_kernel(meta, x0, x0o, x1, x1o, og, ogo, mine, got, taps, ogs, pre):
    core, zh = meta[0], meta[1]
    rows, quarter = x0.shape[0], mine.shape[1]
    ogs[:rows] = og[...]
    ogs[rows:] = ogo[...]
    total = jnp.zeros(pre.shape, F32)
    for k, (own, other) in enumerate(((x0, x0o), (x1, x1o))):
        taps[k, :rows] = own[...]
        taps[k, rows:] = other[...]
        total += dot(taps[k, :, lanes(zh * 2 + core, quarter)], mine[k], (1, 0))
        total += dot(taps[k, :, lanes(zh * 2 + 1 - core, quarter)], got[k], (1, 0))
    pre[...] = total


def spread_block(meta, block, order, outs, first):
    core, zh = meta[0], meta[1]
    quarter = order.shape[0]
    unit = quarter // 4
    for u in range(2):
        for v in range(2):
            columns = lanes(lax.rem(zh + u, 2) * 2 + lax.rem(core + v, 2), quarter)
            moved = dot(order[...], block[:, columns], (1, 1)).astype(BF16)
            at = first + (u * 2 + v) * unit
            for r, out in enumerate(outs):
                out[at:at + unit] = moved[r * unit:(r + 1) * unit]


def centre_kernel(meta, x, xo, order, own, send1, send2, send3, both):
    rows = x.shape[0]
    both[:rows] = x[...]
    both[rows:] = xo[...]
    spread_block(meta, both, order, (own, send1, send2, send3), 0)


def spread_kernel(meta, taps, x2, x2o, order, tap2, own, send1, send2, send3):
    rows = x2.shape[0]
    tap2[:rows] = x2[...]
    tap2[rows:] = x2o[...]
    outs = (own, send1, send2, send3)
    spread_block(meta, taps.at[0], order, outs, 0)
    spread_block(meta, tap2, order, outs, own.shape[0] // 2)


def forward_kernel(meta, taps, tap2, ogs, near, mine, got, pw, far0, far1, far2, far3, order,
                   x0, x1, x2, x3, hg, hidden_t, wfar, m0, m1, m2, m3, pws):
    core, zh, a, b = (meta[i] for i in range(4))
    piece, width = far0.shape[2:]
    quarter = mine.shape[1]
    for y in range(4):
        pws[y, zh] = pw[:, y * width:(y + 1) * width].reshape(4, piece, width)
    for j, far in enumerate((far0, far1, far2, far3)):
        for k in range(4):
            ak, bj = lax.rem(a + k, 4), lax.rem(b + j, 4)
            x, y = jnp.where(core == 0, ak, bj), jnp.where(core == 0, bj, ak)
            for t in range(3):
                wfar[t, x * 4 + y] = far[k, t]
            pws[y, 1 - zh, x] = far[k, 3]
    pre = near[...]
    pre += dot(tap2[:, lanes(zh * 2 + core, quarter)], mine[2], (1, 0))
    pre += dot(tap2[:, lanes(zh * 2 + 1 - core, quarter)], got[2], (1, 0))
    for t in range(3):
        columns = lanes(1 - zh, 2 * quarter)
        block = tap2[:, columns] if t == 2 else taps[t, :, columns]
        pre += dot(block, wfar[t].reshape(2 * quarter, width), (1, 0))
    arriving = jnp.zeros(pre.shape, F32)
    for y in range(4):
        arriving += dot(ogs[:, y * width:(y + 1) * width], pws[y].reshape(width, width), (1, 1))
    scale, cubic = 0.7978845608028654, 0.044715
    square = pre * pre
    tanh = jnp.tanh(scale * (pre + cubic * (square * pre)))
    half = 0.5 * (1.0 + tanh)
    slope = half + 0.5 * pre * (1.0 - tanh * tanh) * (scale * (1.0 + 3.0 * cubic * square))
    grads = (arriving * slope).astype(BF16)
    hg[...] = grads
    count = x0.shape[0]
    place = [lax.broadcasted_iota(jnp.int32, (width, width), axis) for axis in (0, 1)]
    turned = dot((place[0] == place[1]).astype(BF16), grads, (1, 1)).astype(BF16)
    for x, message in ((x0, m0), (x1, m1), (x2, m2), (x3, m3)):
        message[:count] = x[...]
        message[count:] = turned
    hidden_t[...] = dot(order[...], (pre * half).astype(BF16), (1, 1)).astype(BF16)


def point_kernel(meta, ogs, hidden_t, own, send1, send2, send3):
    width = own.shape[2]
    unit = hidden_t.shape[0] // 4
    small = unit // 4
    for h in range(ogs.shape[1] // (2 * width)):
        parts = [dot(hidden_t[...], ogs[:, (2 * h + p) * width:(2 * h + p + 1) * width], (1, 0)) for p in range(2)]
        for r, out in enumerate((own, send1, send2, send3)):
            for q in range(4):
                at = r * unit + q * small
                pair = jnp.concatenate([p[at:at + small] for p in parts], 0)
                out[q, h * 2 * small:(h + 1) * 2 * small] = pair.astype(out.dtype)


def gradient_kernel(meta, x0, x1, x2, x3, m0, m1, m2, m3, conv):
    tap = x0.shape[0]
    total = [jnp.zeros((size, conv.shape[1]), F32) for size in (tap, 2 * tap)]
    for x, m in ((x0, m0), (x1, m1), (x2, m2), (x3, m3)):
        turned = m[2 * tap:]
        total[0] += dot(x[...], turned, (1, 1))
        total[1] += dot(m[:2 * tap], turned, (1, 1))
    conv[:tap] = total[1][:tap]
    conv[tap:2 * tap] = total[0]
    conv[2 * tap:] = total[1][tap:]


def pack_kernel(meta, conv, p0, p1, p2, p3, own, send1, send2, send3):
    unit = conv.shape[0] // 12
    piece = unit // 4
    for q, out in enumerate((own, send1, send2, send3)):
        for g in range(6):
            at = 2 * g * unit + q * piece
            pair = jnp.concatenate([conv[at:at + piece], conv[at + unit:at + unit + piece]], 0)
            out[g * 2 * piece:(g + 1) * 2 * piece] = pair.astype(out.dtype)
        point = p0[q] + p1[q].astype(F32) + p2[q].astype(F32) + p3[q].astype(F32)
        out[12 * piece:] = point.astype(out.dtype)


def input_kernel(meta, hg, later, earlier, mine, got, wfar, kept, other):
    core, zh = meta[0], meta[1]
    quarter = mine.shape[1]
    rows = kept.shape[0]
    grads = (later[...], hg[...], earlier[...])
    for weights, at, size in ((mine, zh * 2 + core, quarter), (got, zh * 2 + 1 - core, quarter), (wfar, 1 - zh, 2 * quarter)):
        total = sum(dot(grads[t], weights[t], (1, 1)) for t in range(3))
        kept[:, lanes(at, size)] = total[:rows]
        other[:, lanes(at, size)] = total[rows:]


def local(inputs, out_grad, conv_weight, point_weight):
    x, og = inputs[0], out_grad[0]
    rows, C = x.shape
    H = conv_weight.shape[2]
    Cq, Hq, Hh = C // 4, H // 4, H // 2
    piece = C // 32
    hops = DILATION_STEP // rows
    dp, seq = lax.axis_index("dp"), lax.axis_index("seq")
    zh, core = dp // 2, dp % 2
    xi, zl, yi = seq // 16, seq // 4 % 4, seq % 4
    a, b = jnp.where(core == 0, xi, yi), jnp.where(core == 0, yi, xi)
    meta = jnp.stack([core, zh, a, b]).astype(jnp.int32)

    def columns(value, c):
        return jnp.concatenate(
            [lax.dynamic_slice_in_dim(value, half * 2 * Hq + c * Hq, Hq, 2) for half in (0, 1)], axis=2
        )

    def order(width, unit, count):
        new = jnp.arange(width)
        inner = new % (4 * unit)
        u = new // (4 * unit) % count
        r, q = new // (16 * unit * count), new // (4 * unit * count) % 4
        an, bn = (a + r) % 4, (b + q) % 4
        xn, yn = jnp.where(core == 0, an, bn), jnp.where(core == 0, bn, an)
        half = (zh + u) % 2 if count == 2 else 0
        old = half * (64 * unit) + xn * (16 * unit) + (zl + inner // unit) % 4 * (4 * unit) + yn * unit + inner % unit
        return (old[:, None] == jnp.arange(width)[None, :]).astype(BF16)

    def mirror(x, y, z, c):
        return x, y, 7 - z, c

    def partner(x, y, z, c):
        return x, y, z, 1 - c

    def beside(first, second, axis):
        return jnp.where(core == 0, jnp.concatenate([first, second], axis), jnp.concatenate([second, first], axis))

    conv_piece = lax.dynamic_slice_in_dim(conv_weight, (xi * 4 + yi) % 8 * piece, piece, 1)
    point_piece = lax.dynamic_slice(point_weight, (xi * (Hq // 4), yi * Hh), (Hq // 4, Hh))
    holders = [d for d in range(256) if coords(d)[3] == coords(d)[0] // 2]
    point_piece = beside(point_piece, send(point_piece, partner), 1)
    far = send(jnp.concatenate([conv_piece, point_piece[None]]), mirror, holders)
    prev = shifted(x, hops)
    x_other = send(x, partner)
    spread = (Cq, 2 * rows)
    centre, *sends = run(
        centre_kernel, meta, [x, x_other, order(Cq, Cq // 64, 1)], [shape(spread, BF16)] * 4,
        [pltpu.VMEM((2 * rows, C), BF16)],
    )
    centres = [centre] + [send_a(part, k + 1) for k, part in enumerate(sends)]
    far, prev, conv_weight, x_late, og_late, *centres = lax.optimization_barrier(
        (far, prev, conv_weight, x, og, *centres)
    )

    def halves(c):
        return jnp.concatenate([columns(far[:3], c), lax.dynamic_slice_in_dim(far[3:], c * Hh, Hh, 2)])

    far = jnp.where(core == xi // 2, halves(core), send(halves(1 - core), partner, holders))
    mine = columns(conv_weight, core)
    got = send(columns(conv_weight, 1 - core), partner)
    prev_other, og_other = send(prev, partner), send(og_late, partner)
    following = shifted(x_late, -hops)
    fars = [send_a(far, -k) for k in (1, 2, 3)]
    far, prev_other, og_other, got, *fars = lax.optimization_barrier((far, prev_other, og_other, got, *fars))
    far = jnp.stack([far, *fars])
    fars = [far] + [send_b(far, -k) for k in (1, 2, 3)]
    taps, ogs, near = run(
        near_kernel, meta, [prev, prev_other, x, x_other, og, og_other, mine, got],
        [shape((2, 2 * rows, C), BF16), shape((2 * rows, C), BF16), shape((2 * rows, Hh), F32)],
    )
    taps, following, fars[1] = lax.optimization_barrier((taps, following, fars[1]))
    following_other = send(following, partner)
    spread = (2 * Cq, 2 * rows)
    tap2, *x_parts = run(
        spread_kernel, meta, [taps, following, following_other, order(Cq, Cq // 64, 1)],
        [shape((2 * rows, C), BF16)] + [shape(spread, BF16)] * 4,
    )
    hg, hidden_t, wfar, message, *sends = run(
        forward_kernel, meta,
        [taps, tap2, ogs, near, mine, got, point_weight, *fars, order(Hh, Hq // 64, 2), *x_parts],
        [shape((2 * rows, Hh), BF16), shape((Hh, 2 * rows), BF16), shape((3, 16, piece, Hh), BF16)]
        + [shape((2 * Cq + Hh, 2 * rows), BF16)] * 4,
        [pltpu.VMEM((4, 2, 4, Hq // 4, Hh), BF16)],
    )
    messages = [message] + [send_a(part, k + 1) for k, part in enumerate(sends)]
    block = (4, Hh // 4, Hh)
    p_own, *sends = run(point_kernel, meta, [ogs, hidden_t], [shape(block, F32)] + [shape(block, BF16)] * 3)
    p_all = [p_own] + [send_a(part, k + 1) for k, part in enumerate(sends)]
    later, earlier = shifted(hg, -hops), shifted(hg, hops)
    later, earlier, *messages = lax.optimization_barrier((later, earlier, *messages))
    conv, = run(gradient_kernel, meta, [*centres, *messages], [shape((3 * Cq, Hh), F32)])
    n = 12 * (Cq // 16)
    big = (n + Hh // 4, Hh)
    total, *sends = run(pack_kernel, meta, [conv, *p_all], [shape(big, F32)] + [shape(big, BF16)] * 3)
    hg_late, _ = lax.optimization_barrier((hg, total))

    kept, other = run(
        input_kernel, meta, [hg_late, later, earlier, mine, got, wfar.reshape(3, 2 * Cq, Hh)],
        [shape((rows, C), F32)] * 2,
    )
    in_grad = (og.astype(F32) + kept + send(other, partner)).astype(BF16)

    for k, part in enumerate(sends):
        total = total + send_b(part, k + 1).astype(F32)
    conv = total[:n].reshape(3, 2, 2, 4, Cq // 64, Hh).transpose(3, 1, 0, 2, 4, 5).reshape(4, 2, -1, Hh)
    point = total[n:].reshape(C // Hh, 2, 4, Hq // 64, Hh).transpose(2, 1, 0, 3, 4).reshape(4, 2, -1, Hh)
    by_z = jnp.concatenate([conv, point], 2)
    last = by_z[0]
    for t in (1, 2, 3):
        got_z = send(by_z[t].astype(BF16), lambda x, y, z, c: (x, y, z // 4 * 4 + (z + t) % 4, c))
        last = last + got_z.astype(F32)
    last = last[0] + send(last[1].astype(BF16), lambda x, y, z, c: (x, y, z + 4, c)).astype(F32)
    n = conv.shape[2]
    conv = last[:n].reshape(3, 2, Cq // 64, Hh)
    point_mine = last[n:].reshape(C // Hh, Hq // 64, Hh).transpose(1, 0, 2).reshape(Hq // 64, C)
    kept, swapped = conv[:, 0], send(conv[:, 1], partner)
    kept, swapped = (part.reshape(3, Cq // 64, 2, 1, Hq) for part in (kept, swapped))
    conv_mine = jnp.where(
        core == 0, jnp.concatenate([kept, swapped], 3), jnp.concatenate([swapped, kept], 3)
    ).reshape(3, Cq // 64, H)
    return in_grad[None], conv_mine, point_mine


def solution(mesh):
    placed = (P("dp", "seq", None), P("dp", "seq", None), P(None, "dp", None), P("dp", None))
    return jax.shard_map(
        local,
        mesh=mesh,
        in_specs=placed,
        out_specs=(P("dp", "seq", None), P(None, ("dp", "seq"), None), P(("dp", "seq"), None)),
        check_vma=False,
    )
```

time: 187 us -> 162 us (0.87)
  waiting for transfers between devices: 99.5 us -> 47.8 us
  starting transfers between devices: 50.7 us -> 66.3 us
  local copies, waits for them, and re-layouts: 13 us -> 21.6 us
    ppermute x26 -> x32, waiting for transfers between devices: 64.3 us -> 22.4 us  [send(): return lax.ppermute(value, ('dp', 'seq'), pairs)]
    ppermute x26 -> x32, starting transfers between devices: 38.2 us -> 59.3 us  [send(): return lax.ppermute(value, ('dp', 'seq'), pairs)]
    ppermute x4, waiting for transfers between devices: 35.2 us -> 25.4 us  [shifted(): lax.ppermute(value, 'seq', [(source, source + steps) for source in range(...]
    ppermute x4, starting transfers between devices: 12.4 us -> 7.05 us  [shifted(): lax.ppermute(value, 'seq', [(source, source + steps) for source in range(...]
    unnamed x23 -> x71, local copies, waits for them, and re-layouts: 4.51 us -> 7.11 us
    reshape x1, local copies, waits for them, and re-layouts: 0.06 us -> 2.01 us  [local(): total[:n].reshape(3, 2, 2, 4, Cq // 64, Hh).transpose(3, 1, 0, 2, 4, 5)]
    concatenate x3 -> x2, other arithmetic: 3.9 us -> 2.84 us  [columns(): jnp.concatenate([lax.dynamic_slice_in_dim(value, half * 2 * Hq + c * Hq,...]
    pallas_call x4 -> x8, Pallas kernels: 16.7 us -> 17.7 us  [run(): pl.pallas_call(kernel, out_shape=outs, in_specs=[pl.BlockSpec(memory_spac...]
  transfers between devices with their start and end apart: 30 -> 36, of which waited for: 15 -> 16; matrix products, arithmetic and copies ran while one was open for 6% -> 4% of each run, Pallas kernels for 3% -> 7%
where the time goes in v1:
time: 162 us; the launch traced here: 161 us
  starting transfers between devices  66.3 us (41%)
  waiting for transfers between devices  47.8 us (30%)
  local copies, waits for them, and re-layouts  21.6 us (13%)
  Pallas kernels  17.7 us (11%)
  other arithmetic  5.99 us (4%)
    ppermute x32, starting transfers between devices, send(): return lax.ppermute(value, ('dp', 'seq'), pairs)  59.3 us
    ppermute x4, waiting for transfers between devices, shifted(): lax.ppermute(value, 'seq', [(source, source + steps) for source in range(...  25.4 us
    ppermute x32, waiting for transfers between devices, send(): return lax.ppermute(value, ('dp', 'seq'), pairs)  22.4 us
    pallas_call x8, Pallas kernels, run(): pl.pallas_call(kernel, out_shape=outs, in_specs=[pl.BlockSpec(memory_spac...  17.7 us
    unnamed x71, local copies, waits for them, and re-layouts  7.11 us
    ppermute x4, starting transfers between devices, shifted(): lax.ppermute(value, 'seq', [(source, source + steps) for source in range(...  7.05 us
    dynamic_slice x2, local copies, waits for them, and re-layouts, columns(): lax.dynamic_slice_in_dim(value, half * 2 * Hq + c * Hq, Hq, 2)  4.99 us
  transfers between devices with their start and end apart: 36, of which 16 were waited for; matrix products, arithmetic and copies ran while one was open for 4% of the time, Pallas kernels for 7%

profile of v1, /device:TPU:1, one launch (start us, length us, event | category | flops | bytes accessed | tf_op | source)
XLA Modules:
  0.0 160.7 jit_solution(2575297509168240336)
XLA Ops:
  0.6 3.3 %collective-permute-start.3 = (bf16[128,1536]{1,0:T(8,128)(2,1)}, bf16[128,1536]{1,0:T(8,128)(2,1)S(1)}, u32[]{:S(2)}, u32[]{:S(2)}) collective-permute-start(bf16[128,1536]{1,0:T(8,128)(2,1)} %bitcast.47), channel_id=1, source_target_pairs={{0,64},{1,65},{2,66},{3,67},{4,68},{5,69},{6,70},{7,71},{8,72},{9,... | collective-permute-start | bytes 1179656 | tf_op jit(solution)/shard_map/ppermute | solution.py:24
  4.0 3.2 %collective-permute-start.2 = (bf16[128,1536]{1,0:T(8,128)(2,1)}, bf16[128,1536]{1,0:T(8,128)(2,1)S(1)}, u32[]{:S(2)}, u32[]{:S(2)}) collective-permute-start(bf16[128,1536]{1,0:T(8,128)(2,1)} %bitcast.48), channel_id=1, source_target_pairs={{0,8},{1,9},{2,10},{3,11},{4,12},{5,13},{6,14},{7,15},{8,16},{9,17... | collective-permute-start | bytes 1179656 | tf_op jit(solution)/shard_map/ppermute | solution.py:37
  13.6 2.6 %collective-permute-start.5 = (bf16[384,256]{1,0:T(8,128)(2,1)S(1)}, bf16[384,256]{1,0:T(8,128)(2,1)S(1)}, u32[]{:S(2)}, u32[]{:S(2)}) collective-permute-start(bf16[384,256]{1,0:T(8,128)(2,1)S(1)} %get-tuple-element.60), channel_id=1, source_target_pairs={{0,32},{1,33},{2,34},{3,35},{4,36},{5,37},{6,38},{7,39},{8,40},{9,... | collective-permute-start | bytes 589832 | tf_op jit(solution)/shard_map/ppermute | solution.py:24
  18.1 3.3 %collective-permute-done.5.x2 = bf16[384,256]{1,0:T(8,128)(2,1)S(1)} collective-permute-done((bf16[384,256]{1,0:T(8,128)(2,1)S(1)}, bf16[384,256]{1,0:T(8,128)(2,1)S(1)}, u32[]{:S(2)}, u32[]{:S(2)}) %collective-permute-start.5) | collective-permute-done | bytes 196640 | tf_op jit(solution)/shard_map/ppermute | solution.py:24
  22.2 4.2 %constant_dynamic-slice_fusion.1 = (bf16[3,384,192]{2,1,0:T(8,128)(2,1)}, bf16[3,384,192]{2,1,0:T(8,128)(2,1)}, bf16[3,384,192]{2,1,0:T(8,128)(2,1)S(1)}, bf16[3,384,192]{2,1,0:T(8,128)(2,1)S(1)}) fusion(bf16[3,384,768]{2,1,0:T(8,128)(2,1)} %param.6, s32[]{:T(128)S(6)} %select_n.335, s32[]{:T(128)S(6)} %select_n.336, s32[]{:T(128)S(6)} %select_n.339, ...), kind=kLoop, calls=%fused_computation.72 | loop fusion | bytes 3538960 | tf_op jit(solution)/shard_map/dynamic_slice | solution.py:215
  27.7 9.1 %collective-permute-start.10 = (bf16[3,384,384]{2,1,0:T(8,128)(2,1)}, bf16[3,384,384]{2,1,0:T(8,128)(2,1)S(1)}, u32[]{:S(2)}, u32[]{:S(2)}) collective-permute-start(bf16[3,384,384]{2,1,0:T(8,128)(2,1)} %pad_maximum_fusion), channel_id=1, source_target_pairs={{0,64},{1,65},{2,66},{3,67},{4,68},{5,69},{6,70},{7,71},{8,72},{9,... | collective-permute-start | bytes 2654216 | tf_op jit(solution)/shard_map/ppermute | solution.py:24
  41.7 2.6 %collective-permute-start.12 = (bf16[4,48,384]{2,1,0:T(8,128)(2,1)S(1)}, bf16[4,48,384]{2,1,0:T(8,128)(2,1)S(1)}, u32[]{:S(2)}, u32[]{:S(2)}) collective-permute-start(bf16[4,48,384]{2,1,0:T(8,128)(2,1)S(1)} %maximum_select_fusion), channel_id=1, source_target_pairs={{0,32},{1,33},{2,34},{3,35},{4,36},{5,37},{6,38},{7,39},{8,40},{9,... | collective-permute-start | bytes 442376 | tf_op jit(solution)/shard_map/ppermute | solution.py:24
  51.4 4.8 %collective-permute-start.18 = (bf16[4,4,48,384]{3,2,1,0:T(8,128)(2,1)S(1)}, bf16[4,4,48,384]{3,2,1,0:T(8,128)(2,1)S(1)}, u32[]{:S(2)}, u32[]{:S(2)}) collective-permute-start(bf16[4,4,48,384]{3,2,1,0:T(8,128)(2,1)S(1)} %pad_maximum_fusion.3.far0), channel_id=1, source_target_pairs={{0,1},{1,2},{2,3},{3,0},{4,5},{5,6},{6,7},{7,4},{8,9},{9,10},{10,1... | collective-permute-start | bytes 1769480 | tf_op jit(solution)/shard_map/ppermute | solution.py:24
  58.6 2.0 %shard_map.68 = (bf16[2,256,1536]{2,1,0:T(8,128)(2,1)}, bf16[256,1536]{1,0:T(8,128)(2,1)S(1)}, f32[256,384]{1,0:T(8,128)S(1)}) custom-call(s32[4]{0:T(128)S(1)} %pad_add_fusion.meta, bf16[128,1536]{1,0:T(8,128)(2,1)S(1)} %copy-done.16, bf16[128,1536]{1,0:T(8,128)(2,1)S(1)} %collective-permute-done.8.x0o, bf16[128,1536]{1,0:T(8,128)(2,1)S(1)} %bitcast.51, ...), custom_call_target="tpu_custom_call" | custom-call | flops 1 | bytes 1 | tf_op jit(solution)/shard_map/pallas_call | solution.py:50
  61.5 10.8 %collective-permute-done.14.x2 = bf16[128,1536]{1,0:T(8,128)(2,1)S(1)} collective-permute-done((bf16[128,1536]{1,0:T(8,128)(2,1)S(1)}, bf16[128,1536]{1,0:T(8,128)(2,1)S(1)}, u32[]{:S(2)}, u32[]{:S(2)}) %collective-permute-start.14) | collective-permute-done | bytes 393248 | tf_op jit(solution)/shard_map/ppermute | solution.py:37
  79.8 6.1 %shard_map.70 = (bf16[256,384]{1,0:T(8,128)(2,1)S(1)}, bf16[384,256]{1,0:T(8,128)(2,1)S(1)}, bf16[3,16,48,384]{3,2,1,0:T(8,128)(2,1)}, bf16[1152,256]{1,0:T(8,12...) custom-call(s32[4]{0:T(128)S(1)} %pad_add_fusion.meta, ...), custom_call_target="tpu_custom_call" | custom-call | flops 1 | bytes 1 | tf_op jit(solution)/shard_map/pallas_call | solution.py:50
  86.0 3.7 %collective-permute-start.22 = (bf16[1152,256]{1,0:T(8,128)(2,1)S(1)}, bf16[1152,256]{1,0:T(8,128)(2,1)S(1)}, u32[]{:S(2)}, u32[]{:S(2)}) collective-permute-start(bf16[1152,256]{1,0:T(8,128)(2,1)S(1)} %get-tuple-element.92), channel_id=1, source_target_pairs={{0,32},{1,33},{2,34},{3,35},{4,36},{5,37},{6,38},{7,39},{8,40},{9,... | collective-permute-start | bytes 1769480 | tf_op jit(solution)/shard_map/ppermute | solution.py:24
  94.4 2.8 %collective-permute-start.24 = (bf16[4,96,384]{2,1,0:T(8,128)(2,1)S(1)}, bf16[4,96,384]{2,1,0:T(8,128)(2,1)S(1)}, u32[]{:S(2)}, u32[]{:S(2)}) collective-permute-start(bf16[4,96,384]{2,1,0:T(8,128)(2,1)S(1)} %get-tuple-element.100), channel_id=1, source_target_pairs={{0,16},{1,17},{2,18},{3,19},{4,20},{5,21},{6,22},{7,23},{8,24},{9,... | collective-permute-start | bytes 884744 | tf_op jit(solution)/shard_map/ppermute | solution.py:24
  97.2 13.7 %collective-permute-done.19.later = bf16[256,384]{1,0:T(8,128)(2,1)S(1)} collective-permute-done((bf16[256,384]{1,0:T(8,128)(2,1)S(1)}, bf16[256,384]{1,0:T(8,128)(2,1)S(1)}, u32[]{:S(2)}, u32[]{:S(2)}) %collective-permute-start.19) | collective-permute-done | bytes 196640 | tf_op jit(solution)/shard_map/ppermute | solution.py:37
  112.2 2.1 %collective-permute-start.26 = (bf16[4,96,384]{2,1,0:T(8,128)(2,1)S(1)}, bf16[4,96,384]{2,1,0:T(8,128)(2,1)S(1)}, u32[]{:S(2)}, u32[]{:S(2)}) collective-permute-start(bf16[4,96,384]{2,1,0:T(8,128)(2,1)S(1)} %get-tuple-element.102), channel_id=1, source_target_pairs={{0,48},{1,49},{2,50},{3,51},{4,52},{5,53},{6,54},{7,55},{8,56},{9,... | collective-permute-start | bytes 884744 | tf_op jit(solution)/shard_map/ppermute | solution.py:24
  114.4 1.9 %shard_map.71.conv = f32[1152,384]{1,0:T(8,128)S(1)} custom-call(s32[4]{0:T(128)S(1)} %pad_add_fusion.meta, bf16[384,256]{1,0:T(8,128)(2,1)S(1)} %get-tuple-element.86.x0, bf16[384,256]{1,0:T(8,128)(2,1)S(1)} %copy-done.18, bf16[384,256]{1,0:T(8,128)(2,1)S(1)} %copy-done.20, bf16[384,256]{1,0:T(8,128)(2,1)S(1)} %copy-done.22, ...), custom_call_target="tpu_custom_call" | custom-call | flops 1 | bytes 1 | tf_op jit(solution)/shard_map/pallas_call | solution.py:50
  116.4 1.9 %collective-permute-done.25.p2 = bf16[4,96,384]{2,1,0:T(8,128)(2,1)S(1)} collective-permute-done((bf16[4,96,384]{2,1,0:T(8,128)(2,1)S(1)}, bf16[4,96,384]{2,1,0:T(8,128)(2,1)S(1)}, u32[]{:S(2)}, u32[]{:S(2)}) %collective-permute-start.25) | collective-permute-done | bytes 294944 | tf_op jit(solution)/shard_map/ppermute | solution.py:24
  121.8 2.4 %collective-permute-start.30 = (bf16[384,384]{1,0:T(8,128)(2,1)S(1)}, bf16[384,384]{1,0:T(8,128)(2,1)S(1)}, u32[]{:S(2)}, u32[]{:S(2)}) collective-permute-start(bf16[384,384]{1,0:T(8,128)(2,1)S(1)} %get-tuple-element.112), channel_id=1, source_target_pairs={{0,3},{1,0},{2,1},{3,2},{4,7},{5,4},{6,5},{7,6},{8,11},{9,8},{10,9... | collective-permute-start | bytes 884744 | tf_op jit(solution)/shard_map/ppermute | solution.py:24
  124.2 6.4 %collective-permute-done.28 = bf16[384,384]{1,0:T(8,128)(2,1)S(1)} collective-permute-done((bf16[384,384]{1,0:T(8,128)(2,1)S(1)}, bf16[384,384]{1,0:T(8,128)(2,1)S(1)}, u32[]{:S(2)}, u32[]{:S(2)}) %collective-permute-start.28) | collective-permute-done | bytes 294944 | tf_op jit(solution)/shard_map/ppermute | solution.py:24
  133.0 2.0 %reshape.261 = f32[3,2,2,4,6,384]{5,4,3,2,1,0:T(8,128)} reshape(f32[288,384]{1,0:T(8,128)} %slice.62) | data formatting | bytes 884736 | tf_op jit(solution)/shard_map/reshape | solution.py:305
  137.9 3.3 %collective-permute-start.33 = (bf16[2,48,384]{2,0,1:T(2,128)(2,1)S(1)}, bf16[2,48,384]{2,0,1:T(2,128)(2,1)S(1)}, u32[]{:S(2)}, u32[]{:S(2)}) collective-permute-start(bf16[2,48,384]{2,0,1:T(2,128)(2,1)S(1)} %get-tuple-element.118), channel_id=1, source_target_pairs={{0,12},{1,13},{2,14},{3,15},{4,0},{5,1},{6,2},{7,3},{8,4},{9,5},{1... | collective-permute-start | bytes 221192 | tf_op jit(solution)/shard_map/ppermute | solution.py:24
  143.1 3.0 %shard_map.74 = (f32[128,1536]{1,0:T(8,128)S(1)}, f32[128,1536]{1,0:T(8,128)}) custom-call(s32[4]{0:T(128)S(1)} %pad_add_fusion.meta, bf16[256,384]{1,0:T(8,128)(2,1)S(1)} %copy-done.24, bf16[256,384]{1,0:T(8,128)(2,1)S(1)} %copy-done.28, bf16[256,384]{1,0:T(8,128)(2,1)S(1)} %copy-done.26, bf16[3,384,384]{2,1,0:T(8,128)(2,1)S(1)} %copy-done.1, ...), custom_call_target="tpu_custom_call" | custom-call | flops 1 | bytes 1 | tf_op jit(solution)/shard_map/pallas_call | solution.py:50
  147.0 2.3 %collective-permute-start.27 = (f32[128,1536]{1,0:T(8,128)}, f32[128,1536]{1,0:T(8,128)S(1)}, u32[]{:S(2)}, u32[]{:S(2)}) collective-permute-start(f32[128,1536]{1,0:T(8,128)} %get-tuple-element.109), channel_id=1, source_target_pairs={{0,64},{1,65},{2,66},{3,67},{4,68},{5,69},{6,70},{7,71},{8,72},{9,... | collective-permute-start | bytes 2359304 | tf_op jit(solution)/shard_map/ppermute | solution.py:24
  149.6 5.7 %collective-permute-start.34 = (bf16[48,384]{1,0:T(8,128)(2,1)S(1)}, bf16[48,384]{1,0:T(8,128)(2,1)S(1)}, u32[]{:S(2)}, u32[]{:S(2)}) collective-permute-start(bf16[48,384]{1,0:T(8,128)(2,1)S(1)} %bitcast.63), channel_id=1, source_target_pairs={{0,128},{1,129},{2,130},{3,131},{4,132},{5,133},{6,134},{7,135},{8... | collective-permute-start | bytes 110600 | tf_op jit(solution)/shard_map/ppermute | solution.py:24
  (172 shorter events, 56.1 us)
Async XLA Ops:
  0.6 10.4 %collective-permute-start.3 = (bf16[128,1536]{1,0:T(8,128)(2,1)}, bf16[128,1536]{1,0:T(8,128)(2,1)S(1)}, u32[]{:S(2)}, u32[]{:S(2)}) collective-permute-start(bf16[128,1536]{1,0:T(8,128)(2,1)} %bitcast.47), channel_id=1, source_target_pairs={{0,64},{1,65},{2,66},{3,67},{4,68},{5,69},{6,70},{7,71},{8,72},{9,... | collective-permute-start | bytes 1179656 | tf_op jit(solution)/shard_map/ppermute | solution.py:24
  4.0 13.3 %collective-permute-start.2 = (bf16[128,1536]{1,0:T(8,128)(2,1)}, bf16[128,1536]{1,0:T(8,128)(2,1)S(1)}, u32[]{:S(2)}, u32[]{:S(2)}) collective-permute-start(bf16[128,1536]{1,0:T(8,128)(2,1)} %bitcast.48), channel_id=1, source_target_pairs={{0,8},{1,9},{2,10},{3,11},{4,12},{5,13},{6,14},{7,15},{8,16},{9,17... | collective-permute-start | bytes 1179656 | tf_op jit(solution)/shard_map/ppermute | solution.py:37
  13.6 7.8 %collective-permute-start.5 = (bf16[384,256]{1,0:T(8,128)(2,1)S(1)}, bf16[384,256]{1,0:T(8,128)(2,1)S(1)}, u32[]{:S(2)}, u32[]{:S(2)}) collective-permute-start(bf16[384,256]{1,0:T(8,128)(2,1)S(1)} %get-tuple-element.60), channel_id=1, source_target_pairs={{0,32},{1,33},{2,34},{3,35},{4,36},{5,37},{6,38},{7,39},{8,40},{9,... | collective-permute-start | bytes 589832 | tf_op jit(solution)/shard_map/ppermute | solution.py:24
  27.7 22.2 %collective-permute-start.10 = (bf16[3,384,384]{2,1,0:T(8,128)(2,1)}, bf16[3,384,384]{2,1,0:T(8,128)(2,1)S(1)}, u32[]{:S(2)}, u32[]{:S(2)}) collective-permute-start(bf16[3,384,384]{2,1,0:T(8,128)(2,1)} %pad_maximum_fusion), channel_id=1, source_target_pairs={{0,64},{1,65},{2,66},{3,67},{4,68},{5,69},{6,70},{7,71},{8,72},{9,... | collective-permute-start | bytes 2654216 | tf_op jit(solution)/shard_map/ppermute | solution.py:24
  38.3 11.7 %collective-permute-start.9 = (bf16[128,1536]{1,0:T(8,128)(2,1)S(1)}, bf16[128,1536]{1,0:T(8,128)(2,1)S(1)}, u32[]{:S(2)}, u32[]{:S(2)}) collective-permute-start(bf16[128,1536]{1,0:T(8,128)(2,1)S(1)} %bitcast.45), channel_id=1, source_target_pairs={{0,64},{1,65},{2,66},{3,67},{4,68},{5,69},{6,70},{7,71},{8,72},{9,... | collective-permute-start | bytes 1179656 | tf_op jit(solution)/shard_map/ppermute | solution.py:24
  39.5 10.4 %collective-permute-start.8 = (bf16[128,1536]{1,0:T(8,128)(2,1)S(1)}, bf16[128,1536]{1,0:T(8,128)(2,1)S(1)}, u32[]{:S(2)}, u32[]{:S(2)}) collective-permute-start(bf16[128,1536]{1,0:T(8,128)(2,1)S(1)} %collective-permute-done.2.x0), channel_id=1, source_target_pairs={{0,64},{1,65},{2,66},{3,67},{4,68},{5,69},{6,70},{7,71},{8,72},{9,... | collective-permute-start | bytes 1179656 | tf_op jit(solution)/shard_map/ppermute | solution.py:24
  50.0 22.3 %collective-permute-start.15 = (bf16[4,4,48,384]{3,2,1,0:T(8,128)(2,1)S(1)}, bf16[4,4,48,384]{3,2,1,0:T(8,128)(2,1)S(1)}, u32[]{:S(2)}, u32[]{:S(2)}) collective-permute-start(bf16[4,4,48,384]{3,2,1,0:T(8,128)(2,1)S(1)} %pad_maximum_fusion.3.far0), channel_id=1, source_target_pairs={{0,3},{1,0},{2,1},{3,2},{4,7},{5,4},{6,5},{7,6},{8,11},{9,8},{10,9... | collective-permute-start | bytes 1769480 | tf_op jit(solution)/shard_map/ppermute | solution.py:24
  50.1 22.2 %collective-permute-start.14 = (bf16[128,1536]{1,0:T(8,128)(2,1)S(1)}, bf16[128,1536]{1,0:T(8,128)(2,1)S(1)}, u32[]{:S(2)}, u32[]{:S(2)}) collective-permute-start(bf16[128,1536]{1,0:T(8,128)(2,1)S(1)} %bitcast.50), channel_id=1, source_target_pairs={{8,0},{9,1},{10,2},{11,3},{12,4},{13,5},{14,6},{15,7},{16,8},{17,9... | collective-permute-start | bytes 1179656 | tf_op jit(solution)/shard_map/ppermute | solution.py:37
  51.4 27.2 %collective-permute-start.18 = (bf16[4,4,48,384]{3,2,1,0:T(8,128)(2,1)S(1)}, bf16[4,4,48,384]{3,2,1,0:T(8,128)(2,1)S(1)}, u32[]{:S(2)}, u32[]{:S(2)}) collective-permute-start(bf16[4,4,48,384]{3,2,1,0:T(8,128)(2,1)S(1)} %pad_maximum_fusion.3.far0), channel_id=1, source_target_pairs={{0,1},{1,2},{2,3},{3,0},{4,5},{5,6},{6,7},{7,4},{8,9},{9,10},{10,1... | collective-permute-start | bytes 1769480 | tf_op jit(solution)/shard_map/ppermute | solution.py:24
  56.2 22.5 %collective-permute-start.17 = (bf16[4,4,48,384]{3,2,1,0:T(8,128)(2,1)S(1)}, bf16[4,4,48,384]{3,2,1,0:T(8,128)(2,1)S(1)}, u32[]{:S(2)}, u32[]{:S(2)}) collective-permute-start(bf16[4,4,48,384]{3,2,1,0:T(8,128)(2,1)S(1)} %pad_maximum_fusion.3.far0), channel_id=1, source_target_pairs={{0,2},{1,3},{2,0},{3,1},{4,6},{5,7},{6,4},{7,5},{8,10},{9,11},{10,... | collective-permute-start | bytes 1769480 | tf_op jit(solution)/shard_map/ppermute | solution.py:24
  85.9 26.3 %collective-permute-start.21 = (bf16[1152,256]{1,0:T(8,128)(2,1)S(1)}, bf16[1152,256]{1,0:T(8,128)(2,1)S(1)}, u32[]{:S(2)}, u32[]{:S(2)}) collective-permute-start(bf16[1152,256]{1,0:T(8,128)(2,1)S(1)} %get-tuple-element.91), channel_id=1, source_target_pairs={{0,16},{1,17},{2,18},{3,19},{4,20},{5,21},{6,22},{7,23},{8,24},{9,... | collective-permute-start | bytes 1769480 | tf_op jit(solution)/shard_map/ppermute | solution.py:24
  86.0 28.3 %collective-permute-start.22 = (bf16[1152,256]{1,0:T(8,128)(2,1)S(1)}, bf16[1152,256]{1,0:T(8,128)(2,1)S(1)}, u32[]{:S(2)}, u32[]{:S(2)}) collective-permute-start(bf16[1152,256]{1,0:T(8,128)(2,1)S(1)} %get-tuple-element.92), channel_id=1, source_target_pairs={{0,32},{1,33},{2,34},{3,35},{4,36},{5,37},{6,38},{7,39},{8,40},{9,... | collective-permute-start | bytes 1769480 | tf_op jit(solution)/shard_map/ppermute | solution.py:24
  89.8 24.6 %collective-permute-start.23 = (bf16[1152,256]{1,0:T(8,128)(2,1)S(1)}, bf16[1152,256]{1,0:T(8,128)(2,1)S(1)}, u32[]{:S(2)}, u32[]{:S(2)}) collective-permute-start(bf16[1152,256]{1,0:T(8,128)(2,1)S(1)} %get-tuple-element.93), channel_id=1, source_target_pairs={{0,48},{1,49},{2,50},{3,51},{4,52},{5,53},{6,54},{7,55},{8,56},{9,... | collective-permute-start | bytes 1769480 | tf_op jit(solution)/shard_map/ppermute | solution.py:24
  91.1 19.8 %collective-permute-start.19 = (bf16[256,384]{1,0:T(8,128)(2,1)S(1)}, bf16[256,384]{1,0:T(8,128)(2,1)S(1)}, u32[]{:S(2)}, u32[]{:S(2)}) collective-permute-start(bf16[256,384]{1,0:T(8,128)(2,1)S(1)} %get-tuple-element.104.hg), channel_id=1, source_target_pairs={{8,0},{9,1},{10,2},{11,3},{12,4},{13,5},{14,6},{15,7},{16,8},{17,9... | collective-permute-start | bytes 589832 | tf_op jit(solution)/shard_map/ppermute | solution.py:37
  94.4 21.9 %collective-permute-start.24 = (bf16[4,96,384]{2,1,0:T(8,128)(2,1)S(1)}, bf16[4,96,384]{2,1,0:T(8,128)(2,1)S(1)}, u32[]{:S(2)}, u32[]{:S(2)}) collective-permute-start(bf16[4,96,384]{2,1,0:T(8,128)(2,1)S(1)} %get-tuple-element.100), channel_id=1, source_target_pairs={{0,16},{1,17},{2,18},{3,19},{4,20},{5,21},{6,22},{7,23},{8,24},{9,... | collective-permute-start | bytes 884744 | tf_op jit(solution)/shard_map/ppermute | solution.py:24
  110.9 7.4 %collective-permute-start.25 = (bf16[4,96,384]{2,1,0:T(8,128)(2,1)S(1)}, bf16[4,96,384]{2,1,0:T(8,128)(2,1)S(1)}, u32[]{:S(2)}, u32[]{:S(2)}) collective-permute-start(bf16[4,96,384]{2,1,0:T(8,128)(2,1)S(1)} %get-tuple-element.101), channel_id=1, source_target_pairs={{0,32},{1,33},{2,34},{3,35},{4,36},{5,37},{6,38},{7,39},{8,40},{9,... | collective-permute-start | bytes 884744 | tf_op jit(solution)/shard_map/ppermute | solution.py:24
  120.3 10.3 %collective-permute-start.28 = (bf16[384,384]{1,0:T(8,128)(2,1)S(1)}, bf16[384,384]{1,0:T(8,128)(2,1)S(1)}, u32[]{:S(2)}, u32[]{:S(2)}) collective-permute-start(bf16[384,384]{1,0:T(8,128)(2,1)S(1)} %get-tuple-element.110), channel_id=1, source_target_pairs={{0,1},{1,2},{2,3},{3,0},{4,5},{5,6},{6,7},{7,4},{8,9},{9,10},{10,1... | collective-permute-start | bytes 884744 | tf_op jit(solution)/shard_map/ppermute | solution.py:24
  121.7 8.9 %collective-permute-start.29 = (bf16[384,384]{1,0:T(8,128)(2,1)S(1)}, bf16[384,384]{1,0:T(8,128)(2,1)S(1)}, u32[]{:S(2)}, u32[]{:S(2)}) collective-permute-start(bf16[384,384]{1,0:T(8,128)(2,1)S(1)} %get-tuple-element.111), channel_id=1, source_target_pairs={{0,2},{1,3},{2,0},{3,1},{4,6},{5,7},{6,4},{7,5},{8,10},{9,11},{10,... | collective-permute-start | bytes 884744 | tf_op jit(solution)/shard_map/ppermute | solution.py:24
  121.8 9.4 %collective-permute-start.30 = (bf16[384,384]{1,0:T(8,128)(2,1)S(1)}, bf16[384,384]{1,0:T(8,128)(2,1)S(1)}, u32[]{:S(2)}, u32[]{:S(2)}) collective-permute-start(bf16[384,384]{1,0:T(8,128)(2,1)S(1)} %get-tuple-element.112), channel_id=1, source_target_pairs={{0,3},{1,0},{2,1},{3,2},{4,7},{5,4},{6,5},{7,6},{8,11},{9,8},{10,9... | collective-permute-start | bytes 884744 | tf_op jit(solution)/shard_map/ppermute | solution.py:24
  137.8 11.5 %collective-permute-start.31 = (bf16[2,48,384]{2,0,1:T(2,128)(2,1)S(1)}, bf16[2,48,384]{2,0,1:T(2,128)(2,1)S(1)}, u32[]{:S(2)}, u32[]{:S(2)}) collective-permute-start(bf16[2,48,384]{2,0,1:T(2,128)(2,1)S(1)} %get-tuple-element.117), channel_id=1, source_target_pairs={{0,4},{1,5},{2,6},{3,7},{4,8},{5,9},{6,10},{7,11},{8,12},{9,13},{1... | collective-permute-start | bytes 221192 | tf_op jit(solution)/shard_map/ppermute | solution.py:24
  137.9 11.4 %collective-permute-start.33 = (bf16[2,48,384]{2,0,1:T(2,128)(2,1)S(1)}, bf16[2,48,384]{2,0,1:T(2,128)(2,1)S(1)}, u32[]{:S(2)}, u32[]{:S(2)}) collective-permute-start(bf16[2,48,384]{2,0,1:T(2,128)(2,1)S(1)} %get-tuple-element.118), channel_id=1, source_target_pairs={{0,12},{1,13},{2,14},{3,15},{4,0},{5,1},{6,2},{7,3},{8,4},{9,5},{1... | collective-permute-start | bytes 221192 | tf_op jit(solution)/shard_map/ppermute | solution.py:24
  141.2 8.1 %collective-permute-start.32 = (bf16[2,48,384]{2,0,1:T(2,128)(2,1)S(1)}, bf16[2,48,384]{2,0,1:T(2,128)(2,1)S(1)}, u32[]{:S(2)}, u32[]{:S(2)}) collective-permute-start(bf16[2,48,384]{2,0,1:T(2,128)(2,1)S(1)} %get-tuple-element.119), channel_id=1, source_target_pairs={{0,8},{1,9},{2,10},{3,11},{4,12},{5,13},{6,14},{7,15},{8,0},{9,1},... | collective-permute-start | bytes 221192 | tf_op jit(solution)/shard_map/ppermute | solution.py:24
  147.0 12.9 %collective-permute-start.27 = (f32[128,1536]{1,0:T(8,128)}, f32[128,1536]{1,0:T(8,128)S(1)}, u32[]{:S(2)}, u32[]{:S(2)}) collective-permute-start(f32[128,1536]{1,0:T(8,128)} %get-tuple-element.109), channel_id=1, source_target_pairs={{0,64},{1,65},{2,66},{3,67},{4,68},{5,69},{6,70},{7,71},{8,72},{9,... | collective-permute-start | bytes 2359304 | tf_op jit(solution)/shard_map/ppermute | solution.py:24
  149.6 7.6 %collective-permute-start.34 = (bf16[48,384]{1,0:T(8,128)(2,1)S(1)}, bf16[48,384]{1,0:T(8,128)(2,1)S(1)}, u32[]{:S(2)}, u32[]{:S(2)}) collective-permute-start(bf16[48,384]{1,0:T(8,128)(2,1)S(1)} %bitcast.63), channel_id=1, source_target_pairs={{0,128},{1,129},{2,130},{3,131},{4,132},{5,133},{6,134},{7,135},{8... | collective-permute-start | bytes 110600 | tf_op jit(solution)/shard_map/ppermute | solution.py:24
  (48 other events, 437.5 us)

commit v2 on v1

v2 whole, which is shorter than its diff:
```python
import jax
import jax.numpy as jnp
from jax import lax
from jax.experimental import pallas as pl
from jax.experimental.pallas import tpu as pltpu
from jax.sharding import PartitionSpec as P

DILATION_STEP = 1024
BF16 = jnp.bfloat16
F32 = jnp.float32


def coords(index):
    dp, seq = divmod(index, 64)
    return seq // 16, seq % 4, (dp // 2) * 4 + (seq // 4) % 4, dp % 2


def index_of(x, y, z, core):
    return ((z % 8) // 4 * 2 + core % 2) * 64 + (x % 4) * 16 + (z % 4) * 4 + y % 4


def send(value, target, sources=range(256)):
    pairs = [(device, index_of(*target(*coords(device)))) for device in sources]
    return lax.ppermute(value, ("dp", "seq"), pairs)


def send_a(value, steps):
    return send(value, lambda x, y, z, c: (x + steps * (1 - c), y + steps * c, z, c))


def send_b(value, steps):
    return send(value, lambda x, y, z, c: (x + steps * c, y + steps * (1 - c), z, c))


def shifted(value, steps):
    first, last = (max(0, -steps), min(64, 64 - steps))
    return lax.ppermute(value, "seq", [(source, source + steps) for source in range(first, last)])


def dot(left, right, dims):
    return lax.dot_general(left, right, ((dims[:1], dims[1:]), ((), ())), preferred_element_type=F32)


def pick(value, axis, index):
    return lax.dynamic_index_in_dim(value, index, axis, keepdims=False)


def run(kernel, scalars, arrays, outs, scratch=()):
    vmem = pl.BlockSpec(memory_space=pltpu.VMEM)
    return pl.pallas_call(
        kernel,
        out_shape=outs,
        in_specs=[pl.BlockSpec(memory_space=pltpu.SMEM)] + [vmem] * len(arrays),
        out_specs=[vmem] * len(outs),
        scratch_shapes=scratch,
        compiler_params=pltpu.CompilerParams(vmem_limit_bytes=48 * 1024 * 1024),
        cost_estimate=pl.CostEstimate(flops=1, bytes_accessed=1, transcendentals=0),
    )(scalars, *arrays)


def shape(dims, dtype):
    return jax.ShapeDtypeStruct(tuple(dims), dtype)


def lanes(start, size):
    return pl.ds(pl.multiple_of(start * size, size), size)


def split_kernel(meta, weight, mine, theirs):
    size = weight.shape[2] // 4
    for t in range(3):
        value = weight[t]
        parts = [value[:, k * size:(k + 1) * size] for k in range(4)]
        even, odd = jnp.concatenate(parts[::2], 1), jnp.concatenate(parts[1::2], 1)
        first = meta[0] == 0
        mine[t] = jnp.where(first, even, odd)
        theirs[t] = jnp.where(first, odd, even)


def spread_block(meta, block, order, outs, first):
    core, zh = meta[0], meta[1]
    quarter = order.shape[0]
    unit = quarter // 4
    for u in range(2):
        for v in range(2):
            columns = lanes(lax.rem(zh + u, 2) * 2 + lax.rem(core + v, 2), quarter)
            moved = dot(order[...], block[:, columns], (1, 1)).astype(BF16)
            at = first + (u * 2 + v) * unit
            for r, out in enumerate(outs):
                out[at:at + unit] = moved[r * unit:(r + 1) * unit]


def near_kernel(meta, x0, x0o, x1, x1o, og, ogo, mine, got, pw, order, taps, ogs, pre, arriving,
                keep, send1, send2, send3):
    core, zh = meta[0], meta[1]
    rows, quarter = x0.shape[0], mine.shape[1]
    ogs[:rows] = og[...]
    ogs[rows:] = ogo[...]
    total = jnp.zeros(pre.shape, F32)
    for k, (own, other) in enumerate(((x0, x0o), (x1, x1o))):
        taps[k, :rows] = own[...]
        taps[k, rows:] = other[...]
        total += dot(taps[k, :, lanes(zh * 2 + core, quarter)], mine[k], (1, 0))
        total += dot(taps[k, :, lanes(zh * 2 + 1 - core, quarter)], got[k], (1, 0))
    pre[...] = total
    arriving[...] = dot(ogs[...], pw[...], (1, 1))
    outs = (keep, send1, send2, send3)
    for k in range(2):
        spread_block(meta, taps.at[k], order, outs, k * quarter)


def late_kernel(meta, x2, x2o, near, mine, got, order, tap, pre, own, send1, send2, send3):
    core, zh = meta[0], meta[1]
    rows, quarter = x2.shape[0], order.shape[0]
    tap[:rows] = x2[...]
    tap[rows:] = x2o[...]
    total = near[...] + dot(tap[:, lanes(zh * 2 + core, quarter)], mine[2], (1, 0))
    pre[...] = total + dot(tap[:, lanes(zh * 2 + 1 - core, quarter)], got[2], (1, 0))
    spread_block(meta, tap, order, (own, send1, send2, send3), 0)


def forward_kernel(meta, taps, tap2, ogs, near, arriving, far0, far1, far2, far3, order,
                   x0, x1, x2, x3, hg, hidden_t, wfar, m0, m1, m2, m3, pws):
    core, zh, a, b = (meta[i] for i in range(4))
    piece, width = far0.shape[2:]
    half = 16 * piece
    for j, far in enumerate((far0, far1, far2, far3)):
        for k in range(4):
            ak, bj = lax.rem(a + k, 4), lax.rem(b + j, 4)
            x, y = jnp.where(core == 0, ak, bj), jnp.where(core == 0, bj, ak)
            for t in range(3):
                wfar[t, x * 4 + y] = far[k, t]
            pws[y, x] = far[k, 3]
    pre = near[...]
    for t in range(3):
        columns = lanes(1 - zh, half)
        block = tap2[:, columns] if t == 2 else taps[t, :, columns]
        pre += dot(block, wfar[t].reshape(half, width), (1, 0))
    other = jnp.zeros(arriving.shape, F32)
    for y in range(4):
        other += dot(ogs[:, y * width:(y + 1) * width], pws[y].reshape(4 * piece, width), (1, 1))
    pair = (arriving[...], other)
    grads = jnp.where(zh == 0, jnp.concatenate(pair, 1), jnp.concatenate(pair[::-1], 1))
    scale, cubic = 0.7978845608028654, 0.044715
    square = pre * pre
    tanh = jnp.tanh(scale * (pre + cubic * (square * pre)))
    gate = 0.5 * (1.0 + tanh)
    slope = gate + 0.5 * pre * (1.0 - tanh * tanh) * (scale * (1.0 + 3.0 * cubic * square))
    grads = (grads * slope).astype(BF16)
    hg[...] = grads
    count = x0.shape[0]
    place = [lax.broadcasted_iota(jnp.int32, (width, width), axis) for axis in (0, 1)]
    turned = dot((place[0] == place[1]).astype(BF16), grads, (1, 1)).astype(BF16)
    for x, message in ((x0, m0), (x1, m1), (x2, m2), (x3, m3)):
        message[:count] = x[...]
        message[count:] = turned
    hidden_t[...] = dot(order[...], (pre * gate).astype(BF16), (1, 1)).astype(BF16)


def point_kernel(meta, ogs, hidden_t, own, send1, send2, send3):
    width = own.shape[2]
    unit = hidden_t.shape[0] // 4
    small = unit // 4
    for h in range(ogs.shape[1] // (2 * width)):
        parts = [dot(hidden_t[...], ogs[:, (2 * h + p) * width:(2 * h + p + 1) * width], (1, 0)) for p in range(2)]
        for r, out in enumerate((own, send1, send2, send3)):
            for q in range(4):
                at = r * unit + q * small
                pair = jnp.concatenate([p[at:at + small] for p in parts], 0)
                out[q, h * 2 * small:(h + 1) * 2 * small] = pair.astype(out.dtype)


def gradient_kernel(meta, x0, x1, x2, x3, m0, m1, m2, m3, conv):
    early, width = x0.shape[0], conv.shape[1]
    last = conv.shape[0] - early
    total = [jnp.zeros((size, width), F32) for size in (early, last)]
    for x, m in ((x0, m0), (x1, m1), (x2, m2), (x3, m3)):
        turned = m[last:]
        total[0] += dot(x[...], turned, (1, 1))
        total[1] += dot(m[:last], turned, (1, 1))
    conv[:early] = total[0]
    conv[early:] = total[1]


def pack_kernel(meta, conv, p0, p1, p2, p3, own, send1, send2, send3):
    unit = conv.shape[0] // 12
    piece = unit // 4
    for q, out in enumerate((own, send1, send2, send3)):
        for g in range(6):
            at = 2 * g * unit + q * piece
            pair = jnp.concatenate([conv[at:at + piece], conv[at + unit:at + unit + piece]], 0)
            out[g * 2 * piece:(g + 1) * 2 * piece] = pair.astype(out.dtype)
        point = p0[q] + p1[q].astype(F32) + p2[q].astype(F32) + p3[q].astype(F32)
        out[12 * piece:] = point.astype(out.dtype)


def slice_kernel(meta, own, got1, got2, got3, kept, send1, send2, send3):
    total = own[...] + got1[...].astype(F32) + got2[...].astype(F32) + got3[...].astype(F32)
    piece = total.shape[0] // 16
    row, thin = piece // 4, piece // 8
    for t, out in enumerate((kept, send1, send2, send3)):
        parts = []
        for u in range(2):
            for g in range(3):
                at = (2 * g + u) * 2 * piece + t * row
                parts += [total[at:at + row], total[at + piece:at + piece + row]]
            for p in range(4):
                at = (12 + p) * piece + u * piece // 2 + t * thin
                parts.append(total[at:at + thin])
        out[...] = jnp.concatenate(parts, 0).astype(out.dtype)


def input_kernel(meta, hg, later, earlier, mine, got, wfar, kept, other):
    core, zh = meta[0], meta[1]
    quarter = mine.shape[1]
    rows = kept.shape[0]
    grads = (later[...], hg[...], earlier[...])
    for weights, at, size in ((mine, zh * 2 + core, quarter), (got, zh * 2 + 1 - core, quarter), (wfar, 1 - zh, 2 * quarter)):
        total = sum(dot(grads[t], weights[t], (1, 1)) for t in range(3))
        kept[:, lanes(at, size)] = total[:rows]
        other[:, lanes(at, size)] = total[rows:]


def local(inputs, out_grad, conv_weight, point_weight):
    x, og = inputs[0], out_grad[0]
    rows, C = x.shape
    H = conv_weight.shape[2]
    Cq, Hq, Hh = C // 4, H // 4, H // 2
    piece = C // 32
    hops = DILATION_STEP // rows
    dp, seq = lax.axis_index("dp"), lax.axis_index("seq")
    zh, core = dp // 2, dp % 2
    xi, zl, yi = seq // 16, seq // 4 % 4, seq % 4
    a, b = jnp.where(core == 0, xi, yi), jnp.where(core == 0, yi, xi)
    meta = jnp.stack([core, zh, a, b]).astype(jnp.int32)

    def columns(value, c):
        return jnp.concatenate(
            [lax.dynamic_slice_in_dim(value, half * 2 * Hq + c * Hq, Hq, 2) for half in (0, 1)], axis=2
        )

    def mirror(x, y, z, c):
        return x, y, 7 - z, c

    def partner(x, y, z, c):
        return x, y, z, 1 - c

    def order(width, unit, count):
        new = jnp.arange(width)
        inner = new % (4 * unit)
        u = new // (4 * unit) % count
        r, q = new // (16 * unit * count), new // (4 * unit * count) % 4
        an, bn = (a + r) % 4, (b + q) % 4
        xn, yn = jnp.where(core == 0, an, bn), jnp.where(core == 0, bn, an)
        half = (zh + u) % 2 if count == 2 else 0
        old = half * (64 * unit) + xn * (16 * unit) + (zl + inner // unit) % 4 * (4 * unit) + yn * unit + inner % unit
        return (old[:, None] == jnp.arange(width)[None, :]).astype(BF16)

    def mirror(x, y, z, c):
        return x, y, 7 - z, c

    def partner(x, y, z, c):
        return x, y, z, 1 - c

    def beside(first, second, axis):
        return jnp.where(core == 0, jnp.concatenate([first, second], axis), jnp.concatenate([second, first], axis))

    conv_piece = lax.dynamic_slice_in_dim(conv_weight, (xi * 4 + yi) % 8 * piece, piece, 1)
    point_piece = lax.dynamic_slice(point_weight, (xi * (Hq // 4), yi * Hh), (Hq // 4, Hh))
    holders = [d for d in range(256) if coords(d)[3] == coords(d)[0] // 2]
    conv_piece = send(conv_piece, mirror, holders)
    point_piece = send(point_piece, mirror)
    prev = shifted(x[:rows // 2], hops)
    x_other = send(x, partner)
    og_other = send(og, partner)
    conv_weight, _ = lax.optimization_barrier((conv_weight, x_other))
    mine, theirs = run(split_kernel, meta, [conv_weight], [shape((3, Cq, Hh), BF16)] * 2)
    conv_piece, point_piece, x_late, x_other, og_other, theirs, prev, mine = lax.optimization_barrier(
        (conv_piece, point_piece, x, x_other, og_other, theirs, prev, mine)
    )
    got = send(theirs, partner)
    handed = send(columns(conv_piece, 1 - core), partner, holders)
    conv_piece = jnp.where(core == xi // 2, columns(conv_piece, core), handed)
    far = jnp.concatenate([conv_piece, point_piece[None]])
    prev = jnp.concatenate([prev, shifted(x_late[rows // 2:], hops)])
    fars = [send_a(far, -k) for k in (1, 2, 3)]
    far, prev, x_late, got, *fars = lax.optimization_barrier((far, prev, x_late, got, *fars))
    following = shifted(x_late, -hops)
    far = jnp.stack([far, *fars])
    fars = [far] + [send_b(far, -k) for k in (1, 2, 3)]
    prev_other = send(prev, partner)
    spread = order(Cq, Cq // 64, 1)
    taps, ogs, near, arriving, *early = run(
        near_kernel, meta, [prev, prev_other, x, x_other, og, og_other, mine, got, point_weight, spread],
        [shape((2, 2 * rows, C), BF16), shape((2 * rows, C), BF16), shape((2 * rows, Hh), F32),
         shape((2 * rows, Hq), F32)] + [shape((2 * Cq, 2 * rows), BF16)] * 4,
    )
    following_other = send(following, partner)
    tap, near, *late = run(
        late_kernel, meta, [following, following_other, near, mine, got, spread],
        [shape((2 * rows, C), BF16), shape((2 * rows, Hh), F32)] + [shape((Cq, 2 * rows), BF16)] * 4,
    )
    rest = lax.optimization_barrier((*fars, *early))
    fars, early = rest[:4], rest[4:]
    early = [early[0]] + [send_a(part, k + 1) for k, part in enumerate(early[1:])]
    hg, hidden_t, wfar, *messages = run(
        forward_kernel, meta, [taps, tap, ogs, near, arriving, *fars, order(Hh, Hq // 64, 2), *late],
        [shape((2 * rows, Hh), BF16), shape((Hh, 2 * rows), BF16), shape((3, 16, piece, Hh), BF16)]
        + [shape((Cq + Hh, 2 * rows), BF16)] * 4,
        [pltpu.VMEM((4, 4, Hq // 4, Hh), BF16)],
    )
    messages = [messages[0]] + [send_a(part, k + 1) for k, part in enumerate(messages[1:])]
    block = (4, Hh // 4, Hh)
    p_own, *sends = run(point_kernel, meta, [ogs, hidden_t], [shape(block, F32)] + [shape(block, BF16)] * 3)
    p_all = [p_own] + [send_a(part, k + 1) for k, part in enumerate(sends)]
    conv, = run(gradient_kernel, meta, [*early, *messages], [shape((3 * Cq, Hh), F32)])
    hg_late, _ = lax.optimization_barrier((hg, messages[1]))
    earlier = shifted(hg_late, hops)
    earlier, conv, *p_all = lax.optimization_barrier((earlier, conv, *p_all))
    n = 12 * (Cq // 16)
    big = (n + Hh // 4, Hh)
    total, *sends = run(pack_kernel, meta, [conv, *p_all], [shape(big, F32)] + [shape(big, BF16)] * 3)
    hg_late, _ = lax.optimization_barrier((hg, total))
    later = shifted(hg_late, -hops)
    later, *got_b = lax.optimization_barrier((later, *[send_b(part, k + 1) for k, part in enumerate(sends)]))
    small = (big[0] // 4, Hh)
    last, *sends = run(
        slice_kernel, meta, [total, *got_b],
        [shape(small, F32)] + [shape(small, BF16)] * 3,
    )
    hg_late, last = lax.optimization_barrier((hg, last))
    kept, other = run(
        input_kernel, meta, [hg_late, later, earlier, mine, got, wfar.reshape(3, 2 * Cq, Hh)],
        [shape((rows, C), F32)] * 2,
    )
    in_grad = (og.astype(F32) + kept + send(other, partner)).astype(BF16)

    for t, part in enumerate(sends):
        got_z = send(part, lambda x, y, z, c: (x, y, z // 4 * 4 + (z + t + 1) % 4, c))
        last = last + got_z.astype(F32)
    last = last.reshape(2, small[0] // 2, Hh)
    last = last[0] + send(last[1].astype(BF16), lambda x, y, z, c: (x, y, z + 4, c)).astype(F32)
    n = 6 * (Cq // 64)
    conv = last[:n].reshape(3, 2, Cq // 64, Hh)
    point_mine = last[n:].reshape(C // Hh, Hq // 64, Hh).transpose(1, 0, 2).reshape(Hq // 64, C)
    kept, swapped = conv[:, 0], send(conv[:, 1], partner)
    kept, swapped = (part.reshape(3, Cq // 64, 2, 1, Hq) for part in (kept, swapped))
    conv_mine = jnp.where(
        core == 0, jnp.concatenate([kept, swapped], 3), jnp.concatenate([swapped, kept], 3)
    ).reshape(3, Cq // 64, H)
    return in_grad[None], conv_mine, point_mine


def solution(mesh):
    placed = (P("dp", "seq", None), P("dp", "seq", None), P(None, "dp", None), P("dp", None))
    return jax.shard_map(
        local,
        mesh=mesh,
        in_specs=placed,
        out_specs=(P("dp", "seq", None), P(None, ("dp", "seq"), None), P(("dp", "seq"), None)),
        check_vma=False,
    )
```

time: 162 us -> 153 us (0.944)
  local copies, waits for them, and re-layouts: 21.6 us -> 11.9 us
  starting transfers between devices: 66.3 us -> 75.9 us
  waiting for transfers between devices: 47.8 us -> 40.5 us
  other arithmetic: 5.99 us -> 2.81 us
  Pallas kernels: 17.7 us -> 19.9 us
    ppermute x4 -> x5, starting transfers between devices: 7.05 us -> 14.9 us  [shifted(): lax.ppermute(value, 'seq', [(source, source + steps) for source in range(...]
    ppermute x4 -> x5, waiting for transfers between devices: 25.4 us -> 20.2 us  [shifted(): lax.ppermute(value, 'seq', [(source, source + steps) for source in range(...]
    dynamic_slice x2 -> x1, local copies, waits for them, and re-layouts: 4.99 us -> 0.16 us  [columns(): lax.dynamic_slice_in_dim(value, half * 2 * Hq + c * Hq, Hq, 2)]
    concatenate x2 -> x1, other arithmetic: 2.84 us -> 0.09 us  [columns(): jnp.concatenate([lax.dynamic_slice_in_dim(value, half * 2 * Hq + c * Hq,...]
    pallas_call x8 -> x9, Pallas kernels: 17.7 us -> 19.9 us  [run(): pl.pallas_call(kernel, out_shape=outs, in_specs=[pl.BlockSpec(memory_spac...]
    transpose x2 -> x0, local copies, waits for them, and re-layouts: 2.18 us -> none  [the longest x1 1.45 us: local(): total[:n].reshape(3, 2, 2, 4, Cq // 64, Hh).transpose(3, 1, 0, 2, 4, 5)]
    ppermute x32, waiting for transfers between devices: 22.4 us -> 20.3 us  [send(): return lax.ppermute(value, ('dp', 'seq'), pairs)]
    reshape x2 -> x0, local copies, waits for them, and re-layouts: 2.07 us -> none  [the longest x1 2.01 us: local(): total[:n].reshape(3, 2, 2, 4, Cq // 64, Hh).transpose(3, 1, 0, 2, 4, 5)]
  transfers between devices with their start and end apart: 36 -> 37, of which waited for: 16 -> 10; matrix products, arithmetic and copies ran while one was open for 4% -> 3% of each run, Pallas kernels for 7% -> 12%
where the time goes in v2:
time: 153 us; the launch traced here: 152 us
  starting transfers between devices  75.9 us (50%)
  waiting for transfers between devices  40.5 us (26%)
  Pallas kernels  19.9 us (13%)
  local copies, waits for them, and re-layouts  11.9 us (8%)
  other arithmetic  2.81 us (2%)
    ppermute x32, starting transfers between devices, send(): return lax.ppermute(value, ('dp', 'seq'), pairs)  61 us
    ppermute x32, waiting for transfers between devices, send(): return lax.ppermute(value, ('dp', 'seq'), pairs)  20.3 us
    ppermute x5, waiting for transfers between devices, shifted(): lax.ppermute(value, 'seq', [(source, source + steps) for source in range(...  20.2 us
    pallas_call x9, Pallas kernels, run(): pl.pallas_call(kernel, out_shape=outs, in_specs=[pl.BlockSpec(memory_spac...  19.9 us
    ppermute x5, starting transfers between devices, shifted(): lax.ppermute(value, 'seq', [(source, source + steps) for source in range(...  14.9 us
    unnamed x32, local copies, waits for them, and re-layouts  7.31 us
  transfers between devices with their start and end apart: 37, of which 10 were waited for; matrix products, arithmetic and copies ran while one was open for 3% of the time, Pallas kernels for 12%

profile of v2, /device:TPU:1, one launch (start us, length us, event | category | flops | bytes accessed | tf_op | source)
XLA Modules:
  0.0 152.1 jit_solution(11858103315757509619)
XLA Ops:
  2.4 8.7 %collective-permute-start.2 = (bf16[128,1536]{1,0:T(8,128)(2,1)}, bf16[128,1536]{1,0:T(8,128)(2,1)S(1)}, u32[]{:S(2)}, u32[]{:S(2)}) collective-permute-start(bf16[128,1536]{1,0:T(8,128)(2,1)} %bitcast.26), channel_id=1, source_target_pairs={{0,64},{1,65},{2,66},{3,67},{4,68},{5,69},{6,70},{7,71},{8,72},{9,... | collective-permute-start | bytes 1179656 | tf_op jit(solution)/shard_map/ppermute | solution.py:24
  12.1 4.0 %collective-permute-start.4 = (bf16[64,1536]{1,0:T(8,128)(2,1)S(1)}, bf16[64,1536]{1,0:T(8,128)(2,1)S(1)}, u32[]{:S(2)}, u32[]{:S(2)}) collective-permute-start(bf16[64,1536]{1,0:T(8,128)(2,1)S(1)} %slice_bitcast_fusion), channel_id=1, source_target_pairs={{0,8},{1,9},{2,10},{3,11},{4,12},{5,13},{6,14},{7,15},{8,16},{9,17... | collective-permute-start | bytes 589832 | tf_op jit(solution)/shard_map/ppermute | solution.py:37
  25.3 5.8 %collective-permute-start.6 = (bf16[64,1536]{1,0:T(8,128)(2,1)S(1)}, bf16[64,1536]{1,0:T(8,128)(2,1)S(1)}, u32[]{:S(2)}, u32[]{:S(2)}) collective-permute-start(bf16[64,1536]{1,0:T(8,128)(2,1)S(1)} %slice.32), channel_id=1, source_target_pairs={{0,8},{1,9},{2,10},{3,11},{4,12},{5,13},{6,14},{7,15},{8,16},{9,17... | collective-permute-start | bytes 589832 | tf_op jit(solution)/shard_map/ppermute | solution.py:37
  32.6 2.6 %collective-permute-start.9 = (bf16[4,48,384]{2,1,0:T(8,128)(2,1)S(1)}, bf16[4,48,384]{2,1,0:T(8,128)(2,1)S(1)}, u32[]{:S(2)}, u32[]{:S(2)}) collective-permute-start(bf16[4,48,384]{2,1,0:T(8,128)(2,1)S(1)} %pad_maximum_fusion.2), channel_id=1, source_target_pairs={{0,32},{1,33},{2,34},{3,35},{4,36},{5,37},{6,38},{7,39},{8,40},{9,... | collective-permute-start | bytes 442376 | tf_op jit(solution)/shard_map/ppermute | solution.py:24
  36.6 3.1 %collective-permute-done.9 = bf16[4,48,384]{2,1,0:T(8,128)(2,1)S(1)} collective-permute-done((bf16[4,48,384]{2,1,0:T(8,128)(2,1)S(1)}, bf16[4,48,384]{2,1,0:T(8,128)(2,1)S(1)}, u32[]{:S(2)}, u32[]{:S(2)}) %collective-permute-start.9) | collective-permute-done | bytes 147488 | tf_op jit(solution)/shard_map/ppermute | solution.py:24
  41.0 5.7 %collective-permute-start.16 = (bf16[4,4,48,384]{3,2,1,0:T(8,128)(2,1)S(1)}, bf16[4,4,48,384]{3,2,1,0:T(8,128)(2,1)}, u32[]{:S(2)}, u32[]{:S(2)}) collective-permute-start(bf16[4,4,48,384]{3,2,1,0:T(8,128)(2,1)S(1)} %pad_maximum_fusion.far0), channel_id=1, source_target_pairs={{0,1},{1,2},{2,3},{3,0},{4,5},{5,6},{6,7},{7,4},{8,9},{9,10},{10,1... | collective-permute-start | bytes 1769480 | tf_op jit(solution)/shard_map/ppermute | solution.py:24
  46.8 2.4 %collective-permute-start.15 = (bf16[4,4,48,384]{3,2,1,0:T(8,128)(2,1)S(1)}, bf16[4,4,48,384]{3,2,1,0:T(8,128)(2,1)}, u32[]{:S(2)}, u32[]{:S(2)}) collective-permute-start(bf16[4,4,48,384]{3,2,1,0:T(8,128)(2,1)S(1)} %pad_maximum_fusion.far0), channel_id=1, source_target_pairs={{0,2},{1,3},{2,0},{3,1},{4,6},{5,7},{6,4},{7,5},{8,10},{9,11},{10,... | collective-permute-start | bytes 1769480 | tf_op jit(solution)/shard_map/ppermute | solution.py:24
  50.5 2.2 %collective-permute-start.11 = (bf16[128,1536]{1,0:T(8,128)(2,1)S(1)}, bf16[128,1536]{1,0:T(8,128)(2,1)S(1)}, u32[]{:S(2)}, u32[]{:S(2)}) collective-permute-start(bf16[128,1536]{1,0:T(8,128)(2,1)S(1)} %pad_maximum_fusion.1.x0), channel_id=1, source_target_pairs={{0,64},{1,65},{2,66},{3,67},{4,68},{5,69},{6,70},{7,71},{8,72},{9,... | collective-permute-start | bytes 1179656 | tf_op jit(solution)/shard_map/ppermute | solution.py:24
  52.8 10.2 %collective-permute-done.12.x2 = bf16[128,1536]{1,0:T(8,128)(2,1)} collective-permute-done((bf16[128,1536]{1,0:T(8,128)(2,1)S(1)}, bf16[128,1536]{1,0:T(8,128)(2,1)}, u32[]{:S(2)}, u32[]{:S(2)}) %collective-permute-start.12) | collective-permute-done | bytes 393248 | tf_op jit(solution)/shard_map/ppermute | solution.py:37
  66.3 3.9 %shard_map.68 = (bf16[2,256,1536]{2,1,0:T(8,128)(2,1)}, bf16[256,1536]{1,0:T(8,128)(2,1)}, f32[256,384]{1,0:T(8,128)S(1)}, f32[256,192]{1,0:T(8,128)S(1)}, bf16[...) custom-call(s32[4]{0:T(128)S(1)} %pad_add_fusion.meta, ...), custom_call_target="tpu_custom_call" | custom-call | flops 1 | bytes 1 | tf_op jit(solution)/shard_map/pallas_call | solution.py:50
  71.5 2.5 %collective-permute-start.20 = (bf16[768,256]{1,0:T(8,128)(2,1)S(1)}, bf16[768,256]{1,0:T(8,128)(2,1)S(1)}, u32[]{:S(2)}, u32[]{:S(2)}) collective-permute-start(bf16[768,256]{1,0:T(8,128)(2,1)S(1)} %get-tuple-element.119), channel_id=1, source_target_pairs={{0,32},{1,33},{2,34},{3,35},{4,36},{5,37},{6,38},{7,39},{8,40},{9,... | collective-permute-start | bytes 1179656 | tf_op jit(solution)/shard_map/ppermute | solution.py:24
  78.9 5.6 %shard_map.70 = (bf16[256,384]{1,0:T(8,128)(2,1)S(1)}, bf16[384,256]{1,0:T(8,128)(2,1)S(1)}, bf16[3,16,48,384]{3,2,1,0:T(8,128)(2,1)}, bf16[768,256]{1,0:T(8,128...) custom-call(s32[4]{0:T(128)S(1)} %pad_add_fusion.meta, ...), custom_call_target="tpu_custom_call" | custom-call | flops 1 | bytes 1 | tf_op jit(solution)/shard_map/pallas_call | solution.py:50
  90.9 6.0 %collective-permute-done.17.m1 = bf16[768,256]{1,0:T(8,128)(2,1)S(1)} collective-permute-done((bf16[768,256]{1,0:T(8,128)(2,1)S(1)}, bf16[768,256]{1,0:T(8,128)(2,1)S(1)}, u32[]{:S(2)}, u32[]{:S(2)}) %collective-permute-start.17) | collective-permute-done | bytes 393248 | tf_op jit(solution)/shard_map/ppermute | solution.py:24
  96.9 2.5 %collective-permute-start.18 = (bf16[256,384]{1,0:T(8,128)(2,1)S(1)}, bf16[256,384]{1,0:T(8,128)(2,1)S(1)}, u32[]{:S(2)}, u32[]{:S(2)}) collective-permute-start(bf16[256,384]{1,0:T(8,128)(2,1)S(1)} %get-tuple-element.143.hg), channel_id=1, source_target_pairs={{0,8},{1,9},{2,10},{3,11},{4,12},{5,13},{6,14},{7,15},{8,16},{9,17... | collective-permute-start | bytes 589832 | tf_op jit(solution)/shard_map/ppermute | solution.py:37
  99.5 1.9 %shard_map.71.conv = f32[1152,384]{1,0:T(8,128)S(1)} custom-call(s32[4]{0:T(128)S(1)} %pad_add_fusion.meta, bf16[768,256]{1,0:T(8,128)(2,1)S(1)} %get-tuple-element.117.x0, bf16[768,256]{1,0:T(8,128)(2,1)S(1)} %collective-permute-done.19.x1, bf16[768,256]{1,0:T(8,128)(2,1)S(1)} %collective-permute-done.20.x2, ...), custom_call_target="tpu_custom_call" | custom-call | flops 1 | bytes 1 | tf_op jit(solution)/shard_map/pallas_call | solution.py:50
  104.7 10.0 %collective-permute-start.28 = (bf16[384,384]{1,0:T(8,128)(2,1)S(1)}, bf16[384,384]{1,0:T(8,128)(2,1)S(1)}, u32[]{:S(2)}, u32[]{:S(2)}) collective-permute-start(bf16[384,384]{1,0:T(8,128)(2,1)S(1)} %get-tuple-element.136), channel_id=1, source_target_pairs={{0,1},{1,2},{2,3},{3,0},{4,5},{5,6},{6,7},{7,4},{8,9},{9,10},{10,1... | collective-permute-start | bytes 884744 | tf_op jit(solution)/shard_map/ppermute | solution.py:24
  116.2 1.9 %collective-permute-start.30 = (bf16[384,384]{1,0:T(8,128)(2,1)S(1)}, bf16[384,384]{1,0:T(8,128)(2,1)S(1)}, u32[]{:S(2)}, u32[]{:S(2)}) collective-permute-start(bf16[384,384]{1,0:T(8,128)(2,1)S(1)} %get-tuple-element.138), channel_id=1, source_target_pairs={{0,3},{1,0},{2,1},{3,2},{4,7},{5,4},{6,5},{7,6},{8,11},{9,8},{10,9... | collective-permute-start | bytes 884744 | tf_op jit(solution)/shard_map/ppermute | solution.py:24
  119.4 9.9 %collective-permute-done.27.later = bf16[256,384]{1,0:T(8,128)(2,1)S(1)} collective-permute-done((bf16[256,384]{1,0:T(8,128)(2,1)S(1)}, bf16[256,384]{1,0:T(8,128)(2,1)S(1)}, u32[]{:S(2)}, u32[]{:S(2)}) %collective-permute-start.27) | collective-permute-done | bytes 196640 | tf_op jit(solution)/shard_map/ppermute | solution.py:37
  130.2 3.2 %collective-permute-start.33 = (bf16[96,384]{1,0:T(8,128)(2,1)S(1)}, bf16[96,384]{1,0:T(8,128)(2,1)S(1)}, u32[]{:S(2)}, u32[]{:S(2)}) collective-permute-start(bf16[96,384]{1,0:T(8,128)(2,1)S(1)} %get-tuple-element.151), channel_id=1, source_target_pairs={{0,8},{1,9},{2,10},{3,11},{4,12},{5,13},{6,14},{7,15},{8,0},{9,1},... | collective-permute-start | bytes 221192 | tf_op jit(solution)/shard_map/ppermute | solution.py:24
  133.6 2.1 %shard_map.75 = (f32[128,1536]{1,0:T(8,128)S(1)}, f32[128,1536]{1,0:T(8,128)S(1)}) custom-call(s32[4]{0:T(128)S(1)} %pad_add_fusion.meta, bf16[256,384]{1,0:T(8,128)(2,1)S(1)} %get-tuple-element.143.hg, bf16[256,384]{1,0:T(8,128)(2,1)S(1)} %collective-permute-done.27.later, bf16[256,384]{1,0:T(8,128)(2,1)S(1)} %collective-permute-done.18.earlier, ...), custom_call_target="tpu_custom_call" | custom-call | flops 1 | bytes 1 | tf_op jit(solution)/shard_map/pallas_call | solution.py:50
  136.6 2.6 %collective-permute-done.33 = bf16[96,384]{1,0:T(8,128)(2,1)S(1)} collective-permute-done((bf16[96,384]{1,0:T(8,128)(2,1)S(1)}, bf16[96,384]{1,0:T(8,128)(2,1)S(1)}, u32[]{:S(2)}, u32[]{:S(2)}) %collective-permute-start.33) | collective-permute-done | bytes 73760 | tf_op jit(solution)/shard_map/ppermute | solution.py:24
  140.5 5.7 %collective-permute-done.35 = bf16[48,384]{1,0:T(8,128)(2,1)S(1)} collective-permute-done((bf16[48,384]{1,0:T(8,128)(2,1)S(1)}, bf16[48,384]{1,0:T(8,128)(2,1)S(1)}, u32[]{:S(2)}, u32[]{:S(2)}) %collective-permute-start.35) | collective-permute-done | bytes 36896 | tf_op jit(solution)/shard_map/ppermute | solution.py:24
  146.3 2.0 %collective-permute-start.36 = (f32[3,6,384]{2,1,0:T(8,128)S(1)}, f32[3,6,384]{2,1,0:T(8,128)S(1)}, u32[]{:S(2)}, u32[]{:S(2)}) collective-permute-start(f32[3,6,384]{2,1,0:T(8,128)S(1)} %get-tuple-element.158), channel_id=1, source_target_pairs={{0,64},{1,65},{2,66},{3,67},{4,68},{5,69},{6,70},{7,71},{8,72},{9,... | collective-permute-start | bytes 82952 | tf_op jit(solution)/shard_map/ppermute | solution.py:24
  150.1 2.0 %fusion.2 = bf16[1,128,1536]{2,1,0:T(8,128)(2,1)} fusion(f32[128,1536]{1,0:T(8,128)} %collective-permute-done.31, f32[128,1536]{1,0:T(8,128)S(1)} %get-tuple-element.147, bf16[1,128,1536]{2,1,0:T(8,128)(2,1)S(1)} %copy-done.8), kind=kLoop, calls=%fused_computation.6 | loop fusion | flops 786432 | bytes 2359296 | tf_op jit(solution)/shard_map/broadcast_in_dim | solution.py:351
  (120 shorter events, 44.3 us)
Async XLA Ops:
  1.7 19.5 %collective-permute-start = (bf16[3,48,768]{2,1,0:T(8,128)(2,1)S(1)}, bf16[3,48,768]{2,1,0:T(8,128)(2,1)S(1)}, u32[]{:S(2)}, u32[]{:S(2)}) collective-permute-start(bf16[3,48,768]{2,1,0:T(8,128)(2,1)S(1)} %constant_dynamic-slice_fusion.4), channel_id=1, source_target_pairs={{0,140},{1,141},{2,142},{3,143},{4,136},{5,137},{6,138},{7,139},{8... | collective-permute-start | bytes 663560 | tf_op jit(solution)/shard_map/ppermute | solution.py:24
  2.4 14.6 %collective-permute-start.2 = (bf16[128,1536]{1,0:T(8,128)(2,1)}, bf16[128,1536]{1,0:T(8,128)(2,1)S(1)}, u32[]{:S(2)}, u32[]{:S(2)}) collective-permute-start(bf16[128,1536]{1,0:T(8,128)(2,1)} %bitcast.26), channel_id=1, source_target_pairs={{0,64},{1,65},{2,66},{3,67},{4,68},{5,69},{6,70},{7,71},{8,72},{9,... | collective-permute-start | bytes 1179656 | tf_op jit(solution)/shard_map/ppermute | solution.py:24
  11.1 10.2 %collective-permute-start.3 = (bf16[128,1536]{1,0:T(8,128)(2,1)}, bf16[128,1536]{1,0:T(8,128)(2,1)S(1)}, u32[]{:S(2)}, u32[]{:S(2)}) collective-permute-start(bf16[128,1536]{1,0:T(8,128)(2,1)} %bitcast.24), channel_id=1, source_target_pairs={{0,64},{1,65},{2,66},{3,67},{4,68},{5,69},{6,70},{7,71},{8,72},{9,... | collective-permute-start | bytes 1179656 | tf_op jit(solution)/shard_map/ppermute | solution.py:24
  22.0 17.6 %collective-permute-start.7 = (bf16[3,384,384]{2,1,0:T(8,128)(2,1)}, bf16[3,384,384]{2,1,0:T(8,128)(2,1)S(1)}, u32[]{:S(2)}, u32[]{:S(2)}) collective-permute-start(bf16[3,384,384]{2,1,0:T(8,128)(2,1)} %get-tuple-element.85), channel_id=1, source_target_pairs={{0,64},{1,65},{2,66},{3,67},{4,68},{5,69},{6,70},{7,71},{8,72},{9,... | collective-permute-start | bytes 2654216 | tf_op jit(solution)/shard_map/ppermute | solution.py:24
  25.3 11.0 %collective-permute-start.6 = (bf16[64,1536]{1,0:T(8,128)(2,1)S(1)}, bf16[64,1536]{1,0:T(8,128)(2,1)S(1)}, u32[]{:S(2)}, u32[]{:S(2)}) collective-permute-start(bf16[64,1536]{1,0:T(8,128)(2,1)S(1)} %slice.32), channel_id=1, source_target_pairs={{0,8},{1,9},{2,10},{3,11},{4,12},{5,13},{6,14},{7,15},{8,16},{9,17... | collective-permute-start | bytes 589832 | tf_op jit(solution)/shard_map/ppermute | solution.py:37
  39.6 23.3 %collective-permute-start.12 = (bf16[128,1536]{1,0:T(8,128)(2,1)S(1)}, bf16[128,1536]{1,0:T(8,128)(2,1)}, u32[]{:S(2)}, u32[]{:S(2)}) collective-permute-start(bf16[128,1536]{1,0:T(8,128)(2,1)S(1)} %bitcast.28), channel_id=1, source_target_pairs={{8,0},{9,1},{10,2},{11,3},{12,4},{13,5},{14,6},{15,7},{16,8},{17,9... | collective-permute-start | bytes 1179656 | tf_op jit(solution)/shard_map/ppermute | solution.py:37
  41.0 29.2 %collective-permute-start.16 = (bf16[4,4,48,384]{3,2,1,0:T(8,128)(2,1)S(1)}, bf16[4,4,48,384]{3,2,1,0:T(8,128)(2,1)}, u32[]{:S(2)}, u32[]{:S(2)}) collective-permute-start(bf16[4,4,48,384]{3,2,1,0:T(8,128)(2,1)S(1)} %pad_maximum_fusion.far0), channel_id=1, source_target_pairs={{0,1},{1,2},{2,3},{3,0},{4,5},{5,6},{6,7},{7,4},{8,9},{9,10},{10,1... | collective-permute-start | bytes 1769480 | tf_op jit(solution)/shard_map/ppermute | solution.py:24
  46.8 23.4 %collective-permute-start.15 = (bf16[4,4,48,384]{3,2,1,0:T(8,128)(2,1)S(1)}, bf16[4,4,48,384]{3,2,1,0:T(8,128)(2,1)}, u32[]{:S(2)}, u32[]{:S(2)}) collective-permute-start(bf16[4,4,48,384]{3,2,1,0:T(8,128)(2,1)S(1)} %pad_maximum_fusion.far0), channel_id=1, source_target_pairs={{0,2},{1,3},{2,0},{3,1},{4,6},{5,7},{6,4},{7,5},{8,10},{9,11},{10,... | collective-permute-start | bytes 1769480 | tf_op jit(solution)/shard_map/ppermute | solution.py:24
  49.2 21.0 %collective-permute-start.14 = (bf16[4,4,48,384]{3,2,1,0:T(8,128)(2,1)S(1)}, bf16[4,4,48,384]{3,2,1,0:T(8,128)(2,1)}, u32[]{:S(2)}, u32[]{:S(2)}) collective-permute-start(bf16[4,4,48,384]{3,2,1,0:T(8,128)(2,1)S(1)} %pad_maximum_fusion.far0), channel_id=1, source_target_pairs={{0,3},{1,0},{2,1},{3,2},{4,7},{5,4},{6,5},{7,6},{8,11},{9,8},{10,9... | collective-permute-start | bytes 1769480 | tf_op jit(solution)/shard_map/ppermute | solution.py:24
  50.5 13.7 %collective-permute-start.11 = (bf16[128,1536]{1,0:T(8,128)(2,1)S(1)}, bf16[128,1536]{1,0:T(8,128)(2,1)S(1)}, u32[]{:S(2)}, u32[]{:S(2)}) collective-permute-start(bf16[128,1536]{1,0:T(8,128)(2,1)S(1)} %pad_maximum_fusion.1.x0), channel_id=1, source_target_pairs={{0,64},{1,65},{2,66},{3,67},{4,68},{5,69},{6,70},{7,71},{8,72},{9,... | collective-permute-start | bytes 1179656 | tf_op jit(solution)/shard_map/ppermute | solution.py:24
  63.0 12.0 %collective-permute-start.13 = (bf16[128,1536]{1,0:T(8,128)(2,1)}, bf16[128,1536]{1,0:T(8,128)(2,1)S(1)}, u32[]{:S(2)}, u32[]{:S(2)}) collective-permute-start(bf16[128,1536]{1,0:T(8,128)(2,1)} %collective-permute-done.12.x2), channel_id=1, source_target_pairs={{0,64},{1,65},{2,66},{3,67},{4,68},{5,69},{6,70},{7,71},{8,72},{9,... | collective-permute-start | bytes 1179656 | tf_op jit(solution)/shard_map/ppermute | solution.py:24
  70.2 15.5 %collective-permute-start.19 = (bf16[768,256]{1,0:T(8,128)(2,1)S(1)}, bf16[768,256]{1,0:T(8,128)(2,1)S(1)}, u32[]{:S(2)}, u32[]{:S(2)}) collective-permute-start(bf16[768,256]{1,0:T(8,128)(2,1)S(1)} %get-tuple-element.118), channel_id=1, source_target_pairs={{0,16},{1,17},{2,18},{3,19},{4,20},{5,21},{6,22},{7,23},{8,24},{9,... | collective-permute-start | bytes 1179656 | tf_op jit(solution)/shard_map/ppermute | solution.py:24
  71.5 17.0 %collective-permute-start.20 = (bf16[768,256]{1,0:T(8,128)(2,1)S(1)}, bf16[768,256]{1,0:T(8,128)(2,1)S(1)}, u32[]{:S(2)}, u32[]{:S(2)}) collective-permute-start(bf16[768,256]{1,0:T(8,128)(2,1)S(1)} %get-tuple-element.119), channel_id=1, source_target_pairs={{0,32},{1,33},{2,34},{3,35},{4,36},{5,37},{6,38},{7,39},{8,40},{9,... | collective-permute-start | bytes 1179656 | tf_op jit(solution)/shard_map/ppermute | solution.py:24
  74.0 15.1 %collective-permute-start.21 = (bf16[768,256]{1,0:T(8,128)(2,1)S(1)}, bf16[768,256]{1,0:T(8,128)(2,1)S(1)}, u32[]{:S(2)}, u32[]{:S(2)}) collective-permute-start(bf16[768,256]{1,0:T(8,128)(2,1)S(1)} %get-tuple-element.120), channel_id=1, source_target_pairs={{0,48},{1,49},{2,50},{3,51},{4,52},{5,53},{6,54},{7,55},{8,56},{9,... | collective-permute-start | bytes 1179656 | tf_op jit(solution)/shard_map/ppermute | solution.py:24
  84.6 12.3 %collective-permute-start.17 = (bf16[768,256]{1,0:T(8,128)(2,1)S(1)}, bf16[768,256]{1,0:T(8,128)(2,1)S(1)}, u32[]{:S(2)}, u32[]{:S(2)}) collective-permute-start(bf16[768,256]{1,0:T(8,128)(2,1)S(1)} %get-tuple-element.115), channel_id=1, source_target_pairs={{0,16},{1,17},{2,18},{3,19},{4,20},{5,21},{6,22},{7,23},{8,24},{9,... | collective-permute-start | bytes 1179656 | tf_op jit(solution)/shard_map/ppermute | solution.py:24
  85.0 11.9 %collective-permute-start.22 = (bf16[768,256]{1,0:T(8,128)(2,1)S(1)}, bf16[768,256]{1,0:T(8,128)(2,1)S(1)}, u32[]{:S(2)}, u32[]{:S(2)}) collective-permute-start(bf16[768,256]{1,0:T(8,128)(2,1)S(1)} %get-tuple-element.122), channel_id=1, source_target_pairs={{0,32},{1,33},{2,34},{3,35},{4,36},{5,37},{6,38},{7,39},{8,40},{9,... | collective-permute-start | bytes 1179656 | tf_op jit(solution)/shard_map/ppermute | solution.py:24
  85.8 13.7 %collective-permute-start.23 = (bf16[768,256]{1,0:T(8,128)(2,1)S(1)}, bf16[768,256]{1,0:T(8,128)(2,1)S(1)}, u32[]{:S(2)}, u32[]{:S(2)}) collective-permute-start(bf16[768,256]{1,0:T(8,128)(2,1)S(1)} %get-tuple-element.123), channel_id=1, source_target_pairs={{0,48},{1,49},{2,50},{3,51},{4,52},{5,53},{6,54},{7,55},{8,56},{9,... | collective-permute-start | bytes 1179656 | tf_op jit(solution)/shard_map/ppermute | solution.py:24
  88.5 14.7 %collective-permute-start.24 = (bf16[4,96,384]{2,1,0:T(8,128)(2,1)S(1)}, bf16[4,96,384]{2,1,0:T(8,128)(2,1)S(1)}, u32[]{:S(2)}, u32[]{:S(2)}) collective-permute-start(bf16[4,96,384]{2,1,0:T(8,128)(2,1)S(1)} %get-tuple-element.126), channel_id=1, source_target_pairs={{0,16},{1,17},{2,18},{3,19},{4,20},{5,21},{6,22},{7,23},{8,24},{9,... | collective-permute-start | bytes 884744 | tf_op jit(solution)/shard_map/ppermute | solution.py:24
  89.0 14.2 %collective-permute-start.25 = (bf16[4,96,384]{2,1,0:T(8,128)(2,1)S(1)}, bf16[4,96,384]{2,1,0:T(8,128)(2,1)S(1)}, u32[]{:S(2)}, u32[]{:S(2)}) collective-permute-start(bf16[4,96,384]{2,1,0:T(8,128)(2,1)S(1)} %get-tuple-element.127), channel_id=1, source_target_pairs={{0,32},{1,33},{2,34},{3,35},{4,36},{5,37},{6,38},{7,39},{8,40},{9,... | collective-permute-start | bytes 884744 | tf_op jit(solution)/shard_map/ppermute | solution.py:24
  104.7 24.7 %collective-permute-start.28 = (bf16[384,384]{1,0:T(8,128)(2,1)S(1)}, bf16[384,384]{1,0:T(8,128)(2,1)S(1)}, u32[]{:S(2)}, u32[]{:S(2)}) collective-permute-start(bf16[384,384]{1,0:T(8,128)(2,1)S(1)} %get-tuple-element.136), channel_id=1, source_target_pairs={{0,1},{1,2},{2,3},{3,0},{4,5},{5,6},{6,7},{7,4},{8,9},{9,10},{10,1... | collective-permute-start | bytes 884744 | tf_op jit(solution)/shard_map/ppermute | solution.py:24
  114.7 14.7 %collective-permute-start.29 = (bf16[384,384]{1,0:T(8,128)(2,1)S(1)}, bf16[384,384]{1,0:T(8,128)(2,1)S(1)}, u32[]{:S(2)}, u32[]{:S(2)}) collective-permute-start(bf16[384,384]{1,0:T(8,128)(2,1)S(1)} %get-tuple-element.137), channel_id=1, source_target_pairs={{0,2},{1,3},{2,0},{3,1},{4,6},{5,7},{6,4},{7,5},{8,10},{9,11},{10,... | collective-permute-start | bytes 884744 | tf_op jit(solution)/shard_map/ppermute | solution.py:24
  116.2 13.2 %collective-permute-start.30 = (bf16[384,384]{1,0:T(8,128)(2,1)S(1)}, bf16[384,384]{1,0:T(8,128)(2,1)S(1)}, u32[]{:S(2)}, u32[]{:S(2)}) collective-permute-start(bf16[384,384]{1,0:T(8,128)(2,1)S(1)} %get-tuple-element.138), channel_id=1, source_target_pairs={{0,3},{1,0},{2,1},{3,2},{4,7},{5,4},{6,5},{7,6},{8,11},{9,8},{10,9... | collective-permute-start | bytes 884744 | tf_op jit(solution)/shard_map/ppermute | solution.py:24
  118.1 11.2 %collective-permute-start.27 = (bf16[256,384]{1,0:T(8,128)(2,1)S(1)}, bf16[256,384]{1,0:T(8,128)(2,1)S(1)}, u32[]{:S(2)}, u32[]{:S(2)}) collective-permute-start(bf16[256,384]{1,0:T(8,128)(2,1)S(1)} %get-tuple-element.143.hg), channel_id=1, source_target_pairs={{8,0},{9,1},{10,2},{11,3},{12,4},{13,5},{14,6},{15,7},{16,8},{17,9... | collective-permute-start | bytes 589832 | tf_op jit(solution)/shard_map/ppermute | solution.py:37
  135.7 14.4 %collective-permute-start.31 = (f32[128,1536]{1,0:T(8,128)S(1)}, f32[128,1536]{1,0:T(8,128)}, u32[]{:S(2)}, u32[]{:S(2)}) collective-permute-start(f32[128,1536]{1,0:T(8,128)S(1)} %get-tuple-element.148), channel_id=1, source_target_pairs={{0,64},{1,65},{2,66},{3,67},{4,68},{5,69},{6,70},{7,71},{8,72},{9,... | collective-permute-start | bytes 2359304 | tf_op jit(solution)/shard_map/ppermute | solution.py:24
  (29 other events, 302.2 us)

commit v3 on v2

--- a/solution.py
+++ b/solution.py
@@ -270,7 +270,8 @@
     holders = [d for d in range(256) if coords(d)[3] == coords(d)[0] // 2]
     conv_piece = send(conv_piece, mirror, holders)
     point_piece = send(point_piece, mirror)
-    prev = shifted(x[:rows // 2], hops)
+    first = rows * 3 // 8
+    prev = shifted(x[:first], hops)
     x_other = send(x, partner)
     og_other = send(og, partner)
     conv_weight, _ = lax.optimization_barrier((conv_weight, x_other))
@@ -282,7 +283,7 @@
     handed = send(columns(conv_piece, 1 - core), partner, holders)
     conv_piece = jnp.where(core == xi // 2, columns(conv_piece, core), handed)
     far = jnp.concatenate([conv_piece, point_piece[None]])
-    prev = jnp.concatenate([prev, shifted(x_late[rows // 2:], hops)])
+    prev = jnp.concatenate([prev, shifted(x_late[first:], hops)])
     fars = [send_a(far, -k) for k in (1, 2, 3)]
     far, prev, x_late, got, *fars = lax.optimization_barrier((far, prev, x_late, got, *fars))
     following = shifted(x_late, -hops)
@@ -295,6 +296,7 @@
         [shape((2, 2 * rows, C), BF16), shape((2 * rows, C), BF16), shape((2 * rows, Hh), F32),
          shape((2 * rows, Hq), F32)] + [shape((2 * Cq, 2 * rows), BF16)] * 4,
     )
+    following, taps = lax.optimization_barrier((following, taps))
     following_other = send(following, partner)
     tap, near, *late = run(
         late_kernel, meta, [following, following_other, near, mine, got, spread],
@@ -309,20 +311,21 @@
         + [shape((Cq + Hh, 2 * rows), BF16)] * 4,
         [pltpu.VMEM((4, 4, Hq // 4, Hh), BF16)],
     )
+    hg, *rest = lax.optimization_barrier((hg, *early, *messages))
+    early, messages = rest[:4], rest[4:]
     messages = [messages[0]] + [send_a(part, k + 1) for k, part in enumerate(messages[1:])]
     block = (4, Hh // 4, Hh)
     p_own, *sends = run(point_kernel, meta, [ogs, hidden_t], [shape(block, F32)] + [shape(block, BF16)] * 3)
     p_all = [p_own] + [send_a(part, k + 1) for k, part in enumerate(sends)]
+    earlier = shifted(hg, hops)
+    earlier, hg_late, *messages = lax.optimization_barrier((earlier, hg, *messages))
+    later = shifted(hg_late, -hops)
     conv, = run(gradient_kernel, meta, [*early, *messages], [shape((3 * Cq, Hh), F32)])
-    hg_late, _ = lax.optimization_barrier((hg, messages[1]))
-    earlier = shifted(hg_late, hops)
-    earlier, conv, *p_all = lax.optimization_barrier((earlier, conv, *p_all))
+    later, conv, *p_all = lax.optimization_barrier((later, conv, *p_all))
     n = 12 * (Cq // 16)
     big = (n + Hh // 4, Hh)
     total, *sends = run(pack_kernel, meta, [conv, *p_all], [shape(big, F32)] + [shape(big, BF16)] * 3)
-    hg_late, _ = lax.optimization_barrier((hg, total))
-    later = shifted(hg_late, -hops)
-    later, *got_b = lax.optimization_barrier((later, *[send_b(part, k + 1) for k, part in enumerate(sends)]))
+    got_b = [send_b(part, k + 1) for k, part in enumerate(sends)]
     small = (big[0] // 4, Hh)
     last, *sends = run(
         slice_kernel, meta, [total, *got_b],
@@ -335,15 +338,19 @@
     )
     in_grad = (og.astype(F32) + kept + send(other, partner)).astype(BF16)
 
-    for t, part in enumerate(sends):
-        got_z = send(part, lambda x, y, z, c: (x, y, z // 4 * 4 + (z + t + 1) % 4, c))
-        last = last + got_z.astype(F32)
+    got_z = [
+        send(part, lambda x, y, z, c: (x, y, z // 4 * 4 + (z + t + 1) % 4, c)) for t, part in enumerate(sends)
+    ]
+    for part in got_z:
+        last = last + part.astype(F32)
     last = last.reshape(2, small[0] // 2, Hh)
-    last = last[0] + send(last[1].astype(BF16), lambda x, y, z, c: (x, y, z + 4, c)).astype(F32)
+    got_z = send(last[1].astype(BF16), lambda x, y, z, c: (x, y, z + 4, c))
+    last = last[0] + got_z.astype(F32)
     n = 6 * (Cq // 64)
     conv = last[:n].reshape(3, 2, Cq // 64, Hh)
     point_mine = last[n:].reshape(C // Hh, Hq // 64, Hh).transpose(1, 0, 2).reshape(Hq // 64, C)
     kept, swapped = conv[:, 0], send(conv[:, 1], partner)
+    in_grad, swapped = lax.optimization_barrier((in_grad, swapped))
     kept, swapped = (part.reshape(3, Cq // 64, 2, 1, Hq) for part in (kept, swapped))
     conv_mine = jnp.where(
         core == 0, jnp.concatenate([kept, swapped], 3), jnp.concatenate([swapped, kept], 3)

time: 153 us -> 151 us (0.987)
  starting transfers between devices: 75.9 us -> 69.9 us
  waiting for transfers between devices: 40.5 us -> 45.7 us
    ppermute x5, waiting for transfers between devices: 20.2 us -> 26.1 us  [shifted(): lax.ppermute(value, 'seq', [(source, source + steps) for source in range(...]
    ppermute x32, starting transfers between devices: 61 us -> 56.1 us  [send(): return lax.ppermute(value, ('dp', 'seq'), pairs)]
    broadcast_in_dim x1 -> x0, other arithmetic: 2 us -> none  [local(): return (in_grad[None], conv_mine, point_mine)]
  transfers between devices with their start and end apart: 37 -> 37, of which waited for: 10 -> 15; matrix products, arithmetic and copies ran while one was open for 3% -> 3% of each run, Pallas kernels for 12% -> 12%
where the time goes in v3:
time: 151 us; the launch traced here: 150 us
  starting transfers between devices  69.9 us (46%)
  waiting for transfers between devices  45.7 us (30%)
  Pallas kernels  20.2 us (13%)
  local copies, waits for them, and re-layouts  11.8 us (8%)
  other arithmetic  1.69 us (1%)
    ppermute x32, starting transfers between devices, send(): return lax.ppermute(value, ('dp', 'seq'), pairs)  56.1 us
    ppermute x5, waiting for transfers between devices, shifted(): lax.ppermute(value, 'seq', [(source, source + steps) for source in range(...  26.1 us
    pallas_call x9, Pallas kernels, run(): pl.pallas_call(kernel, out_shape=outs, in_specs=[pl.BlockSpec(memory_spac...  20.2 us
    ppermute x32, waiting for transfers between devices, send(): return lax.ppermute(value, ('dp', 'seq'), pairs)  19.7 us
    ppermute x5, starting transfers between devices, shifted(): lax.ppermute(value, 'seq', [(source, source + steps) for source in range(...  13.8 us
    unnamed x32, local copies, waits for them, and re-layouts  7.25 us
  transfers between devices with their start and end apart: 37, of which 15 were waited for; matrix products, arithmetic and copies ran while one was open for 3% of the time, Pallas kernels for 12%

profile of v3, /device:TPU:1, one launch (start us, length us, event | category | flops | bytes accessed | tf_op | source)
XLA Modules:
  0.0 150.4 jit_solution(671133450297836893)
XLA Ops:
  2.4 8.7 %collective-permute-start.2 = (bf16[128,1536]{1,0:T(8,128)(2,1)}, bf16[128,1536]{1,0:T(8,128)(2,1)S(1)}, u32[]{:S(2)}, u32[]{:S(2)}) collective-permute-start(bf16[128,1536]{1,0:T(8,128)(2,1)} %bitcast.25), channel_id=1, source_target_pairs={{0,64},{1,65},{2,66},{3,67},{4,68},{5,69},{6,70},{7,71},{8,72},{9,... | collective-permute-start | bytes 1179656 | tf_op jit(solution)/shard_map/ppermute | solution.py:24
  12.1 4.0 %collective-permute-start.4 = (bf16[48,1536]{1,0:T(8,128)(2,1)S(1)}, bf16[48,1536]{1,0:T(8,128)(2,1)S(1)}, u32[]{:S(2)}, u32[]{:S(2)}) collective-permute-start(bf16[48,1536]{1,0:T(8,128)(2,1)S(1)} %slice_bitcast_fusion), channel_id=1, source_target_pairs={{0,8},{1,9},{2,10},{3,11},{4,12},{5,13},{6,14},{7,15},{8,16},{9,17... | collective-permute-start | bytes 442376 | tf_op jit(solution)/shard_map/ppermute | solution.py:37
  25.3 6.0 %collective-permute-start.6 = (bf16[80,1536]{1,0:T(8,128)(2,1)S(1)}, bf16[80,1536]{1,0:T(8,128)(2,1)S(1)}, u32[]{:S(2)}, u32[]{:S(2)}) collective-permute-start(bf16[80,1536]{1,0:T(8,128)(2,1)S(1)} %slice.32), channel_id=1, source_target_pairs={{0,8},{1,9},{2,10},{3,11},{4,12},{5,13},{6,14},{7,15},{8,16},{9,17... | collective-permute-start | bytes 737288 | tf_op jit(solution)/shard_map/ppermute | solution.py:37
  32.8 2.6 %collective-permute-start.9 = (bf16[4,48,384]{2,1,0:T(8,128)(2,1)S(1)}, bf16[4,48,384]{2,1,0:T(8,128)(2,1)S(1)}, u32[]{:S(2)}, u32[]{:S(2)}) collective-permute-start(bf16[4,48,384]{2,1,0:T(8,128)(2,1)S(1)} %pad_maximum_fusion.2), channel_id=1, source_target_pairs={{0,32},{1,33},{2,34},{3,35},{4,36},{5,37},{6,38},{7,39},{8,40},{9,... | collective-permute-start | bytes 442376 | tf_op jit(solution)/shard_map/ppermute | solution.py:24
  36.8 2.8 %collective-permute-done.9 = bf16[4,48,384]{2,1,0:T(8,128)(2,1)S(1)} collective-permute-done((bf16[4,48,384]{2,1,0:T(8,128)(2,1)S(1)}, bf16[4,48,384]{2,1,0:T(8,128)(2,1)S(1)}, u32[]{:S(2)}, u32[]{:S(2)}) %collective-permute-start.9) | collective-permute-done | bytes 147488 | tf_op jit(solution)/shard_map/ppermute | solution.py:24
  39.8 5.4 %collective-permute-start.16 = (bf16[4,4,48,384]{3,2,1,0:T(8,128)(2,1)S(1)}, bf16[4,4,48,384]{3,2,1,0:T(8,128)(2,1)}, u32[]{:S(2)}, u32[]{:S(2)}) collective-permute-start(bf16[4,4,48,384]{3,2,1,0:T(8,128)(2,1)S(1)} %pad_maximum_fusion.far0), channel_id=1, source_target_pairs={{0,1},{1,2},{2,3},{3,0},{4,5},{5,6},{6,7},{7,4},{8,9},{9,10},{10,1... | collective-permute-start | bytes 1769480 | tf_op jit(solution)/shard_map/ppermute | solution.py:24
  52.3 4.2 %shard_map.68 = (bf16[2,256,1536]{2,1,0:T(8,128)(2,1)}, bf16[256,1536]{1,0:T(8,128)(2,1)}, f32[256,384]{1,0:T(8,128)S(1)}, f32[256,192]{1,0:T(8,128)S(1)}, bf16[...) custom-call(s32[4]{0:T(128)S(1)} %pad_add_fusion.meta, ...), custom_call_target="tpu_custom_call" | custom-call | flops 1 | bytes 1 | tf_op jit(solution)/shard_map/pallas_call | solution.py:50
  56.5 13.4 %collective-permute-done.11.x2 = bf16[128,1536]{1,0:T(8,128)(2,1)} collective-permute-done((bf16[128,1536]{1,0:T(8,128)(2,1)S(1)}, bf16[128,1536]{1,0:T(8,128)(2,1)}, u32[]{:S(2)}, u32[]{:S(2)}) %collective-permute-start.11) | collective-permute-done | bytes 393248 | tf_op jit(solution)/shard_map/ppermute | solution.py:37
  79.3 5.6 %shard_map.70 = (bf16[256,384]{1,0:T(8,128)(2,1)S(1)}, bf16[384,256]{1,0:T(8,128)(2,1)S(1)}, bf16[3,16,48,384]{3,2,1,0:T(8,128)(2,1)}, bf16[768,256]{1,0:T(8,128...) custom-call(s32[4]{0:T(128)S(1)} %pad_add_fusion.meta, ...), custom_call_target="tpu_custom_call" | custom-call | flops 1 | bytes 1 | tf_op jit(solution)/shard_map/pallas_call | solution.py:50
  85.4 2.2 %collective-permute-start.22 = (bf16[768,256]{1,0:T(8,128)(2,1)S(1)}, bf16[768,256]{1,0:T(8,128)(2,1)S(1)}, u32[]{:S(2)}, u32[]{:S(2)}) collective-permute-start(bf16[768,256]{1,0:T(8,128)(2,1)S(1)} %get-tuple-element.141), channel_id=1, source_target_pairs={{0,32},{1,33},{2,34},{3,35},{4,36},{5,37},{6,38},{7,39},{8,40},{9,... | collective-permute-start | bytes 1179656 | tf_op jit(solution)/shard_map/ppermute | solution.py:24
  92.2 2.0 %collective-permute-start.26 = (bf16[4,96,384]{2,1,0:T(8,128)(2,1)S(1)}, bf16[4,96,384]{2,1,0:T(8,128)(2,1)S(1)}, u32[]{:S(2)}, u32[]{:S(2)}) collective-permute-start(bf16[4,96,384]{2,1,0:T(8,128)(2,1)S(1)} %get-tuple-element.155), channel_id=1, source_target_pairs={{0,32},{1,33},{2,34},{3,35},{4,36},{5,37},{6,38},{7,39},{8,40},{9,... | collective-permute-start | bytes 884744 | tf_op jit(solution)/shard_map/ppermute | solution.py:24
  94.2 3.1 %collective-permute-done.21.m1 = bf16[768,256]{1,0:T(8,128)(2,1)S(1)} collective-permute-done((bf16[768,256]{1,0:T(8,128)(2,1)S(1)}, bf16[768,256]{1,0:T(8,128)(2,1)S(1)}, u32[]{:S(2)}, u32[]{:S(2)}) %collective-permute-start.21) | collective-permute-done | bytes 393248 | tf_op jit(solution)/shard_map/ppermute | solution.py:24
  99.2 1.9 %shard_map.71.conv = f32[1152,384]{1,0:T(8,128)S(1)} custom-call(s32[4]{0:T(128)S(1)} %pad_add_fusion.meta, bf16[768,256]{1,0:T(8,128)(2,1)S(1)} %get-tuple-element.144.x0, bf16[768,256]{1,0:T(8,128)(2,1)S(1)} %collective-permute-done.17.x1, bf16[768,256]{1,0:T(8,128)(2,1)S(1)} %collective-permute-done.18.x2, ...), custom_call_target="tpu_custom_call" | custom-call | flops 1 | bytes 1 | tf_op jit(solution)/shard_map/pallas_call | solution.py:50
  101.2 2.2 %collective-permute-done.26.p2 = bf16[4,96,384]{2,1,0:T(8,128)(2,1)S(1)} collective-permute-done((bf16[4,96,384]{2,1,0:T(8,128)(2,1)S(1)}, bf16[4,96,384]{2,1,0:T(8,128)(2,1)S(1)}, u32[]{:S(2)}, u32[]{:S(2)}) %collective-permute-start.26) | collective-permute-done | bytes 294944 | tf_op jit(solution)/shard_map/ppermute | solution.py:24
  104.0 12.0 %collective-permute-done.24.later = bf16[256,384]{1,0:T(8,128)(2,1)S(1)} collective-permute-done((bf16[256,384]{1,0:T(8,128)(2,1)S(1)}, bf16[256,384]{1,0:T(8,128)(2,1)S(1)}, u32[]{:S(2)}, u32[]{:S(2)}) %collective-permute-start.24) | collective-permute-done | bytes 196640 | tf_op jit(solution)/shard_map/ppermute | solution.py:37
  116.8 2.9 %collective-permute-start.28 = (bf16[384,384]{1,0:T(8,128)(2,1)S(1)}, bf16[384,384]{1,0:T(8,128)(2,1)S(1)}, u32[]{:S(2)}, u32[]{:S(2)}) collective-permute-start(bf16[384,384]{1,0:T(8,128)(2,1)S(1)} %get-tuple-element.163), channel_id=1, source_target_pairs={{0,1},{1,2},{2,3},{3,0},{4,5},{5,6},{6,7},{7,4},{8,9},{9,10},{10,1... | collective-permute-start | bytes 884744 | tf_op jit(solution)/shard_map/ppermute | solution.py:24
  119.9 2.2 %collective-permute-start.30 = (bf16[384,384]{1,0:T(8,128)(2,1)S(1)}, bf16[384,384]{1,0:T(8,128)(2,1)S(1)}, u32[]{:S(2)}, u32[]{:S(2)}) collective-permute-start(bf16[384,384]{1,0:T(8,128)(2,1)S(1)} %get-tuple-element.165), channel_id=1, source_target_pairs={{0,3},{1,0},{2,1},{3,2},{4,7},{5,4},{6,5},{7,6},{8,11},{9,8},{10,9... | collective-permute-start | bytes 884744 | tf_op jit(solution)/shard_map/ppermute | solution.py:24
  123.9 3.6 %collective-permute-done.29.got2 = bf16[384,384]{1,0:T(8,128)(2,1)S(1)} collective-permute-done((bf16[384,384]{1,0:T(8,128)(2,1)S(1)}, bf16[384,384]{1,0:T(8,128)(2,1)S(1)}, u32[]{:S(2)}, u32[]{:S(2)}) %collective-permute-start.29) | collective-permute-done | bytes 294944 | tf_op jit(solution)/shard_map/ppermute | solution.py:24
  128.9 2.8 %collective-permute-start.33 = (bf16[96,384]{1,0:T(8,128)(2,1)S(1)}, bf16[96,384]{1,0:T(8,128)(2,1)S(1)}, u32[]{:S(2)}, u32[]{:S(2)}) collective-permute-start(bf16[96,384]{1,0:T(8,128)(2,1)S(1)} %get-tuple-element.175), channel_id=1, source_target_pairs={{0,8},{1,9},{2,10},{3,11},{4,12},{5,13},{6,14},{7,15},{8,0},{9,1},... | collective-permute-start | bytes 221192 | tf_op jit(solution)/shard_map/ppermute | solution.py:24
  131.8 2.1 %shard_map.75 = (f32[128,1536]{1,0:T(8,128)S(1)}, f32[128,1536]{1,0:T(8,128)S(1)}) custom-call(s32[4]{0:T(128)S(1)} %pad_add_fusion.meta, bf16[256,384]{1,0:T(8,128)(2,1)S(1)} %get-tuple-element.167.hg, bf16[256,384]{1,0:T(8,128)(2,1)S(1)} %collective-permute-done.24.later, bf16[256,384]{1,0:T(8,128)(2,1)S(1)} %collective-permute-done.20.earlier, ...), custom_call_target="tpu_custom_call" | custom-call | flops 1 | bytes 1 | tf_op jit(solution)/shard_map/pallas_call | solution.py:50
  133.9 3.6 %collective-permute-start.31 = (f32[128,1536]{1,0:T(8,128)S(1)}, f32[128,1536]{1,0:T(8,128)S(1)}, u32[]{:S(2)}, u32[]{:S(2)}) collective-permute-start(f32[128,1536]{1,0:T(8,128)S(1)} %get-tuple-element.172), channel_id=1, source_target_pairs={{0,64},{1,65},{2,66},{3,67},{4,68},{5,69},{6,70},{7,71},{8,72},{9,... | collective-permute-start | bytes 2359304 | tf_op jit(solution)/shard_map/ppermute | solution.py:24
  137.6 2.9 %collective-permute-start.35 = (bf16[48,384]{1,0:T(8,128)(2,1)S(1)}, bf16[48,384]{1,0:T(8,128)(2,1)S(1)}, u32[]{:S(2)}, u32[]{:S(2)}) collective-permute-start(bf16[48,384]{1,0:T(8,128)(2,1)S(1)} %slice.49), channel_id=1, source_target_pairs={{0,128},{1,129},{2,130},{3,131},{4,132},{5,133},{6,134},{7,135},{8... | collective-permute-start | bytes 110600 | tf_op jit(solution)/shard_map/ppermute | solution.py:24
  140.5 3.9 %collective-permute-done.35 = bf16[48,384]{1,0:T(8,128)(2,1)S(1)} collective-permute-done((bf16[48,384]{1,0:T(8,128)(2,1)S(1)}, bf16[48,384]{1,0:T(8,128)(2,1)S(1)}, u32[]{:S(2)}, u32[]{:S(2)}) %collective-permute-start.35) | collective-permute-done | bytes 36896 | tf_op jit(solution)/shard_map/ppermute | solution.py:24
  145.2 3.4 %collective-permute-start.36 = (f32[3,6,384]{2,1,0:T(8,128)S(1)}, f32[3,6,384]{2,1,0:T(8,128)S(1)}, u32[]{:S(2)}, u32[]{:S(2)}) collective-permute-start(f32[3,6,384]{2,1,0:T(8,128)S(1)} %get-tuple-element.184), channel_id=1, source_target_pairs={{0,64},{1,65},{2,66},{3,67},{4,68},{5,69},{6,70},{7,71},{8,72},{9,... | collective-permute-start | bytes 82952 | tf_op jit(solution)/shard_map/ppermute | solution.py:24
  (120 shorter events, 45.9 us)
Async XLA Ops:
  1.7 19.5 %collective-permute-start = (bf16[3,48,768]{2,1,0:T(8,128)(2,1)S(1)}, bf16[3,48,768]{2,1,0:T(8,128)(2,1)S(1)}, u32[]{:S(2)}, u32[]{:S(2)}) collective-permute-start(bf16[3,48,768]{2,1,0:T(8,128)(2,1)S(1)} %constant_dynamic-slice_fusion.4), channel_id=1, source_target_pairs={{0,140},{1,141},{2,142},{3,143},{4,136},{5,137},{6,138},{7,139},{8... | collective-permute-start | bytes 663560 | tf_op jit(solution)/shard_map/ppermute | solution.py:24
  2.4 14.6 %collective-permute-start.2 = (bf16[128,1536]{1,0:T(8,128)(2,1)}, bf16[128,1536]{1,0:T(8,128)(2,1)S(1)}, u32[]{:S(2)}, u32[]{:S(2)}) collective-permute-start(bf16[128,1536]{1,0:T(8,128)(2,1)} %bitcast.25), channel_id=1, source_target_pairs={{0,64},{1,65},{2,66},{3,67},{4,68},{5,69},{6,70},{7,71},{8,72},{9,... | collective-permute-start | bytes 1179656 | tf_op jit(solution)/shard_map/ppermute | solution.py:24
  11.1 10.2 %collective-permute-start.3 = (bf16[128,1536]{1,0:T(8,128)(2,1)}, bf16[128,1536]{1,0:T(8,128)(2,1)S(1)}, u32[]{:S(2)}, u32[]{:S(2)}) collective-permute-start(bf16[128,1536]{1,0:T(8,128)(2,1)} %bitcast.23), channel_id=1, source_target_pairs={{0,64},{1,65},{2,66},{3,67},{4,68},{5,69},{6,70},{7,71},{8,72},{9,... | collective-permute-start | bytes 1179656 | tf_op jit(solution)/shard_map/ppermute | solution.py:24
  12.1 9.1 %collective-permute-start.4 = (bf16[48,1536]{1,0:T(8,128)(2,1)S(1)}, bf16[48,1536]{1,0:T(8,128)(2,1)S(1)}, u32[]{:S(2)}, u32[]{:S(2)}) collective-permute-start(bf16[48,1536]{1,0:T(8,128)(2,1)S(1)} %slice_bitcast_fusion), channel_id=1, source_target_pairs={{0,8},{1,9},{2,10},{3,11},{4,12},{5,13},{6,14},{7,15},{8,16},{9,17... | collective-permute-start | bytes 442376 | tf_op jit(solution)/shard_map/ppermute | solution.py:37
  22.0 17.7 %collective-permute-start.7 = (bf16[3,384,384]{2,1,0:T(8,128)(2,1)}, bf16[3,384,384]{2,1,0:T(8,128)(2,1)S(1)}, u32[]{:S(2)}, u32[]{:S(2)}) collective-permute-start(bf16[3,384,384]{2,1,0:T(8,128)(2,1)} %get-tuple-element.98), channel_id=1, source_target_pairs={{0,64},{1,65},{2,66},{3,67},{4,68},{5,69},{6,70},{7,71},{8,72},{9,... | collective-permute-start | bytes 2654216 | tf_op jit(solution)/shard_map/ppermute | solution.py:24
  25.3 11.2 %collective-permute-start.6 = (bf16[80,1536]{1,0:T(8,128)(2,1)S(1)}, bf16[80,1536]{1,0:T(8,128)(2,1)S(1)}, u32[]{:S(2)}, u32[]{:S(2)}) collective-permute-start(bf16[80,1536]{1,0:T(8,128)(2,1)S(1)} %slice.32), channel_id=1, source_target_pairs={{0,8},{1,9},{2,10},{3,11},{4,12},{5,13},{6,14},{7,15},{8,16},{9,17... | collective-permute-start | bytes 737288 | tf_op jit(solution)/shard_map/ppermute | solution.py:37
  39.8 31.5 %collective-permute-start.16 = (bf16[4,4,48,384]{3,2,1,0:T(8,128)(2,1)S(1)}, bf16[4,4,48,384]{3,2,1,0:T(8,128)(2,1)}, u32[]{:S(2)}, u32[]{:S(2)}) collective-permute-start(bf16[4,4,48,384]{3,2,1,0:T(8,128)(2,1)S(1)} %pad_maximum_fusion.far0), channel_id=1, source_target_pairs={{0,1},{1,2},{2,3},{3,0},{4,5},{5,6},{6,7},{7,4},{8,9},{9,10},{10,1... | collective-permute-start | bytes 1769480 | tf_op jit(solution)/shard_map/ppermute | solution.py:24
  45.2 26.1 %collective-permute-start.15 = (bf16[4,4,48,384]{3,2,1,0:T(8,128)(2,1)S(1)}, bf16[4,4,48,384]{3,2,1,0:T(8,128)(2,1)}, u32[]{:S(2)}, u32[]{:S(2)}) collective-permute-start(bf16[4,4,48,384]{3,2,1,0:T(8,128)(2,1)S(1)} %pad_maximum_fusion.far0), channel_id=1, source_target_pairs={{0,2},{1,3},{2,0},{3,1},{4,6},{5,7},{6,4},{7,5},{8,10},{9,11},{10,... | collective-permute-start | bytes 1769480 | tf_op jit(solution)/shard_map/ppermute | solution.py:24
  47.1 24.2 %collective-permute-start.14 = (bf16[4,4,48,384]{3,2,1,0:T(8,128)(2,1)S(1)}, bf16[4,4,48,384]{3,2,1,0:T(8,128)(2,1)}, u32[]{:S(2)}, u32[]{:S(2)}) collective-permute-start(bf16[4,4,48,384]{3,2,1,0:T(8,128)(2,1)S(1)} %pad_maximum_fusion.far0), channel_id=1, source_target_pairs={{0,3},{1,0},{2,1},{3,2},{4,7},{5,4},{6,5},{7,6},{8,11},{9,8},{10,9... | collective-permute-start | bytes 1769480 | tf_op jit(solution)/shard_map/ppermute | solution.py:24
  48.4 21.5 %collective-permute-start.11 = (bf16[128,1536]{1,0:T(8,128)(2,1)S(1)}, bf16[128,1536]{1,0:T(8,128)(2,1)}, u32[]{:S(2)}, u32[]{:S(2)}) collective-permute-start(bf16[128,1536]{1,0:T(8,128)(2,1)S(1)} %bitcast.27), channel_id=1, source_target_pairs={{8,0},{9,1},{10,2},{11,3},{12,4},{13,5},{14,6},{15,7},{16,8},{17,9... | collective-permute-start | bytes 1179656 | tf_op jit(solution)/shard_map/ppermute | solution.py:37
  71.3 13.6 %collective-permute-start.17 = (bf16[768,256]{1,0:T(8,128)(2,1)S(1)}, bf16[768,256]{1,0:T(8,128)(2,1)S(1)}, u32[]{:S(2)}, u32[]{:S(2)}) collective-permute-start(bf16[768,256]{1,0:T(8,128)(2,1)S(1)} %get-tuple-element.131), channel_id=1, source_target_pairs={{0,16},{1,17},{2,18},{3,19},{4,20},{5,21},{6,22},{7,23},{8,24},{9,... | collective-permute-start | bytes 1179656 | tf_op jit(solution)/shard_map/ppermute | solution.py:24
  72.6 12.3 %collective-permute-start.18 = (bf16[768,256]{1,0:T(8,128)(2,1)S(1)}, bf16[768,256]{1,0:T(8,128)(2,1)S(1)}, u32[]{:S(2)}, u32[]{:S(2)}) collective-permute-start(bf16[768,256]{1,0:T(8,128)(2,1)S(1)} %get-tuple-element.132), channel_id=1, source_target_pairs={{0,32},{1,33},{2,34},{3,35},{4,36},{5,37},{6,38},{7,39},{8,40},{9,... | collective-permute-start | bytes 1179656 | tf_op jit(solution)/shard_map/ppermute | solution.py:24
  73.9 11.0 %collective-permute-start.19 = (bf16[768,256]{1,0:T(8,128)(2,1)S(1)}, bf16[768,256]{1,0:T(8,128)(2,1)S(1)}, u32[]{:S(2)}, u32[]{:S(2)}) collective-permute-start(bf16[768,256]{1,0:T(8,128)(2,1)S(1)} %get-tuple-element.133), channel_id=1, source_target_pairs={{0,48},{1,49},{2,50},{3,51},{4,52},{5,53},{6,54},{7,55},{8,56},{9,... | collective-permute-start | bytes 1179656 | tf_op jit(solution)/shard_map/ppermute | solution.py:24
  84.9 12.4 %collective-permute-start.21 = (bf16[768,256]{1,0:T(8,128)(2,1)S(1)}, bf16[768,256]{1,0:T(8,128)(2,1)S(1)}, u32[]{:S(2)}, u32[]{:S(2)}) collective-permute-start(bf16[768,256]{1,0:T(8,128)(2,1)S(1)} %get-tuple-element.140), channel_id=1, source_target_pairs={{0,16},{1,17},{2,18},{3,19},{4,20},{5,21},{6,22},{7,23},{8,24},{9,... | collective-permute-start | bytes 1179656 | tf_op jit(solution)/shard_map/ppermute | solution.py:24
  85.4 12.0 %collective-permute-start.22 = (bf16[768,256]{1,0:T(8,128)(2,1)S(1)}, bf16[768,256]{1,0:T(8,128)(2,1)S(1)}, u32[]{:S(2)}, u32[]{:S(2)}) collective-permute-start(bf16[768,256]{1,0:T(8,128)(2,1)S(1)} %get-tuple-element.141), channel_id=1, source_target_pairs={{0,32},{1,33},{2,34},{3,35},{4,36},{5,37},{6,38},{7,39},{8,40},{9,... | collective-permute-start | bytes 1179656 | tf_op jit(solution)/shard_map/ppermute | solution.py:24
  87.6 10.4 %collective-permute-start.23 = (bf16[768,256]{1,0:T(8,128)(2,1)S(1)}, bf16[768,256]{1,0:T(8,128)(2,1)S(1)}, u32[]{:S(2)}, u32[]{:S(2)}) collective-permute-start(bf16[768,256]{1,0:T(8,128)(2,1)S(1)} %get-tuple-element.142), channel_id=1, source_target_pairs={{0,48},{1,49},{2,50},{3,51},{4,52},{5,53},{6,54},{7,55},{8,56},{9,... | collective-permute-start | bytes 1179656 | tf_op jit(solution)/shard_map/ppermute | solution.py:24
  90.7 10.4 %collective-permute-start.25 = (bf16[4,96,384]{2,1,0:T(8,128)(2,1)S(1)}, bf16[4,96,384]{2,1,0:T(8,128)(2,1)S(1)}, u32[]{:S(2)}, u32[]{:S(2)}) collective-permute-start(bf16[4,96,384]{2,1,0:T(8,128)(2,1)S(1)} %get-tuple-element.154), channel_id=1, source_target_pairs={{0,16},{1,17},{2,18},{3,19},{4,20},{5,21},{6,22},{7,23},{8,24},{9,... | collective-permute-start | bytes 884744 | tf_op jit(solution)/shard_map/ppermute | solution.py:24
  92.2 11.2 %collective-permute-start.26 = (bf16[4,96,384]{2,1,0:T(8,128)(2,1)S(1)}, bf16[4,96,384]{2,1,0:T(8,128)(2,1)S(1)}, u32[]{:S(2)}, u32[]{:S(2)}) collective-permute-start(bf16[4,96,384]{2,1,0:T(8,128)(2,1)S(1)} %get-tuple-element.155), channel_id=1, source_target_pairs={{0,32},{1,33},{2,34},{3,35},{4,36},{5,37},{6,38},{7,39},{8,40},{9,... | collective-permute-start | bytes 884744 | tf_op jit(solution)/shard_map/ppermute | solution.py:24
  98.0 18.0 %collective-permute-start.24 = (bf16[256,384]{1,0:T(8,128)(2,1)S(1)}, bf16[256,384]{1,0:T(8,128)(2,1)S(1)}, u32[]{:S(2)}, u32[]{:S(2)}) collective-permute-start(bf16[256,384]{1,0:T(8,128)(2,1)S(1)} %get-tuple-element.167.hg), channel_id=1, source_target_pairs={{8,0},{9,1},{10,2},{11,3},{12,4},{13,5},{14,6},{15,7},{16,8},{17,9... | collective-permute-start | bytes 589832 | tf_op jit(solution)/shard_map/ppermute | solution.py:37
  119.6 7.8 %collective-permute-start.29 = (bf16[384,384]{1,0:T(8,128)(2,1)S(1)}, bf16[384,384]{1,0:T(8,128)(2,1)S(1)}, u32[]{:S(2)}, u32[]{:S(2)}) collective-permute-start(bf16[384,384]{1,0:T(8,128)(2,1)S(1)} %get-tuple-element.164), channel_id=1, source_target_pairs={{0,2},{1,3},{2,0},{3,1},{4,6},{5,7},{6,4},{7,5},{8,10},{9,11},{10,... | collective-permute-start | bytes 884744 | tf_op jit(solution)/shard_map/ppermute | solution.py:24
  119.9 7.7 %collective-permute-start.30 = (bf16[384,384]{1,0:T(8,128)(2,1)S(1)}, bf16[384,384]{1,0:T(8,128)(2,1)S(1)}, u32[]{:S(2)}, u32[]{:S(2)}) collective-permute-start(bf16[384,384]{1,0:T(8,128)(2,1)S(1)} %get-tuple-element.165), channel_id=1, source_target_pairs={{0,3},{1,0},{2,1},{3,2},{4,7},{5,4},{6,5},{7,6},{8,11},{9,8},{10,9... | collective-permute-start | bytes 884744 | tf_op jit(solution)/shard_map/ppermute | solution.py:24
  128.4 9.2 %collective-permute-start.32 = (bf16[96,384]{1,0:T(8,128)(2,1)S(1)}, bf16[96,384]{1,0:T(8,128)(2,1)S(1)}, u32[]{:S(2)}, u32[]{:S(2)}) collective-permute-start(bf16[96,384]{1,0:T(8,128)(2,1)S(1)} %get-tuple-element.174), channel_id=1, source_target_pairs={{0,4},{1,5},{2,6},{3,7},{4,8},{5,9},{6,10},{7,11},{8,12},{9,13},{1... | collective-permute-start | bytes 221192 | tf_op jit(solution)/shard_map/ppermute | solution.py:24
  128.9 8.7 %collective-permute-start.33 = (bf16[96,384]{1,0:T(8,128)(2,1)S(1)}, bf16[96,384]{1,0:T(8,128)(2,1)S(1)}, u32[]{:S(2)}, u32[]{:S(2)}) collective-permute-start(bf16[96,384]{1,0:T(8,128)(2,1)S(1)} %get-tuple-element.175), channel_id=1, source_target_pairs={{0,8},{1,9},{2,10},{3,11},{4,12},{5,13},{6,14},{7,15},{8,0},{9,1},... | collective-permute-start | bytes 221192 | tf_op jit(solution)/shard_map/ppermute | solution.py:24
  133.9 14.7 %collective-permute-start.31 = (f32[128,1536]{1,0:T(8,128)S(1)}, f32[128,1536]{1,0:T(8,128)S(1)}, u32[]{:S(2)}, u32[]{:S(2)}) collective-permute-start(f32[128,1536]{1,0:T(8,128)S(1)} %get-tuple-element.172), channel_id=1, source_target_pairs={{0,64},{1,65},{2,66},{3,67},{4,68},{5,69},{6,70},{7,71},{8,72},{9,... | collective-permute-start | bytes 2359304 | tf_op jit(solution)/shard_map/ppermute | solution.py:24
  (29 other events, 236.5 us)

commit v4 on v3

--- a/solution.py
+++ b/solution.py
@@ -32,9 +32,14 @@
     return send(value, lambda x, y, z, c: (x + steps * c, y + steps * (1 - c), z, c))
 
 
-def shifted(value, steps):
-    first, last = (max(0, -steps), min(64, 64 - steps))
-    return lax.ppermute(value, "seq", [(source, source + steps) for source in range(first, last)])
+def flip(value):
+    return send(value, lambda x, y, z, c: (x, y, z // 4 * 4 + (z + 2) % 4, c))
+
+
+def hop(value):
+    up = [d for d in range(256) if coords(d)[2] % 4 < 2 and coords(d)[0] < 3]
+    down = [d for d in range(256) if coords(d)[2] % 4 >= 2 and coords(d)[0] > 0]
+    return send(value, lambda x, y, z, c: (x + 1 if z % 4 < 2 else x - 1, y, z, c), up + down)
 
 
 def dot(left, right, dims):
@@ -100,8 +105,9 @@
     for k, (own, other) in enumerate(((x0, x0o), (x1, x1o))):
         taps[k, :rows] = own[...]
         taps[k, rows:] = other[...]
-        total += dot(taps[k, :, lanes(zh * 2 + core, quarter)], mine[k], (1, 0))
-        total += dot(taps[k, :, lanes(zh * 2 + 1 - core, quarter)], got[k], (1, 0))
+        t = meta[4] if k == 0 else 1
+        total += dot(taps[k, :, lanes(zh * 2 + core, quarter)], mine[t], (1, 0))
+        total += dot(taps[k, :, lanes(zh * 2 + 1 - core, quarter)], got[t], (1, 0))
     pre[...] = total
     arriving[...] = dot(ogs[...], pw[...], (1, 1))
     outs = (keep, send1, send2, send3)
@@ -114,8 +120,9 @@
     rows, quarter = x2.shape[0], order.shape[0]
     tap[:rows] = x2[...]
     tap[rows:] = x2o[...]
-    total = near[...] + dot(tap[:, lanes(zh * 2 + core, quarter)], mine[2], (1, 0))
-    pre[...] = total + dot(tap[:, lanes(zh * 2 + 1 - core, quarter)], got[2], (1, 0))
+    t = 2 - meta[4]
+    total = near[...] + dot(tap[:, lanes(zh * 2 + core, quarter)], mine[t], (1, 0))
+    pre[...] = total + dot(tap[:, lanes(zh * 2 + 1 - core, quarter)], got[t], (1, 0))
     spread_block(meta, tap, order, (own, send1, send2, send3), 0)
 
 
@@ -132,9 +139,9 @@
                 wfar[t, x * 4 + y] = far[k, t]
             pws[y, x] = far[k, 3]
     pre = near[...]
-    for t in range(3):
+    for k, t in enumerate((meta[4], 1, 2 - meta[4])):
         columns = lanes(1 - zh, half)
-        block = tap2[:, columns] if t == 2 else taps[t, :, columns]
+        block = tap2[:, columns] if k == 2 else taps[k, :, columns]
         pre += dot(block, wfar[t].reshape(half, width), (1, 0))
     other = jnp.zeros(arriving.shape, F32)
     for y in range(4):
@@ -178,8 +185,9 @@
         turned = m[last:]
         total[0] += dot(x[...], turned, (1, 1))
         total[1] += dot(m[:last], turned, (1, 1))
-    conv[:early] = total[0]
-    conv[early:] = total[1]
+    conv[pl.ds(pl.multiple_of(meta[4] * last, last), last)] = total[0][:last]
+    conv[last:2 * last] = total[0][last:]
+    conv[pl.ds(pl.multiple_of((2 - meta[4]) * last, last), last)] = total[1]
 
 
 def pack_kernel(meta, conv, p0, p1, p2, p3, own, send1, send2, send3):
@@ -210,13 +218,13 @@
         out[...] = jnp.concatenate(parts, 0).astype(out.dtype)
 
 
-def input_kernel(meta, hg, later, earlier, mine, got, wfar, kept, other):
+def input_kernel(meta, hg, flipped, hopped, mine, got, wfar, kept, other):
     core, zh = meta[0], meta[1]
     quarter = mine.shape[1]
     rows = kept.shape[0]
-    grads = (later[...], hg[...], earlier[...])
+    grads = ((flipped[...], 2 - meta[4]), (hg[...], 1), (hopped[...], meta[4]))
     for weights, at, size in ((mine, zh * 2 + core, quarter), (got, zh * 2 + 1 - core, quarter), (wfar, 1 - zh, 2 * quarter)):
-        total = sum(dot(grads[t], weights[t], (1, 1)) for t in range(3))
+        total = sum(dot(grad, weights[t], (1, 1)) for grad, t in grads)
         kept[:, lanes(at, size)] = total[:rows]
         other[:, lanes(at, size)] = total[rows:]
 
@@ -227,12 +235,12 @@
     H = conv_weight.shape[2]
     Cq, Hq, Hh = C // 4, H // 4, H // 2
     piece = C // 32
-    hops = DILATION_STEP // rows
+    assert DILATION_STEP == 8 * rows
     dp, seq = lax.axis_index("dp"), lax.axis_index("seq")
     zh, core = dp // 2, dp % 2
     xi, zl, yi = seq // 16, seq // 4 % 4, seq % 4
     a, b = jnp.where(core == 0, xi, yi), jnp.where(core == 0, yi, xi)
-    meta = jnp.stack([core, zh, a, b]).astype(jnp.int32)
+    meta = jnp.stack([core, zh, a, b, jnp.where(zl < 2, 2, 0)]).astype(jnp.int32)
 
     def columns(value, c):
         return jnp.concatenate(
@@ -270,40 +278,40 @@
     holders = [d for d in range(256) if coords(d)[3] == coords(d)[0] // 2]
     conv_piece = send(conv_piece, mirror, holders)
     point_piece = send(point_piece, mirror)
-    first = rows * 3 // 8
-    prev = shifted(x[:first], hops)
+    first = rows // 2
+    flipped = flip(x[:first])
     x_other = send(x, partner)
     og_other = send(og, partner)
     conv_weight, _ = lax.optimization_barrier((conv_weight, x_other))
     mine, theirs = run(split_kernel, meta, [conv_weight], [shape((3, Cq, Hh), BF16)] * 2)
-    conv_piece, point_piece, x_late, x_other, og_other, theirs, prev, mine = lax.optimization_barrier(
-        (conv_piece, point_piece, x, x_other, og_other, theirs, prev, mine)
+    conv_piece, point_piece, x_late, x_other, og_other, theirs, flipped, mine = lax.optimization_barrier(
+        (conv_piece, point_piece, x, x_other, og_other, theirs, flipped, mine)
     )
     got = send(theirs, partner)
     handed = send(columns(conv_piece, 1 - core), partner, holders)
     conv_piece = jnp.where(core == xi // 2, columns(conv_piece, core), handed)
     far = jnp.concatenate([conv_piece, point_piece[None]])
-    prev = jnp.concatenate([prev, shifted(x_late[first:], hops)])
+    flipped = jnp.concatenate([flipped, flip(x_late[first:])])
     fars = [send_a(far, -k) for k in (1, 2, 3)]
-    far, prev, x_late, got, *fars = lax.optimization_barrier((far, prev, x_late, got, *fars))
-    following = shifted(x_late, -hops)
+    far, flipped, got, *fars = lax.optimization_barrier((far, flipped, got, *fars))
+    hopped = hop(flipped)
     far = jnp.stack([far, *fars])
     fars = [far] + [send_b(far, -k) for k in (1, 2, 3)]
-    prev_other = send(prev, partner)
+    flipped_other = send(flipped, partner)
     spread = order(Cq, Cq // 64, 1)
     taps, ogs, near, arriving, *early = run(
-        near_kernel, meta, [prev, prev_other, x, x_other, og, og_other, mine, got, point_weight, spread],
+        near_kernel, meta, [flipped, flipped_other, x, x_other, og, og_other, mine, got, point_weight, spread],
         [shape((2, 2 * rows, C), BF16), shape((2 * rows, C), BF16), shape((2 * rows, Hh), F32),
          shape((2 * rows, Hq), F32)] + [shape((2 * Cq, 2 * rows), BF16)] * 4,
     )
-    following, taps = lax.optimization_barrier((following, taps))
-    following_other = send(following, partner)
+    hopped, taps = lax.optimization_barrier((hopped, taps))
+    hopped_other = send(hopped, partner)
     tap, near, *late = run(
-        late_kernel, meta, [following, following_other, near, mine, got, spread],
+        late_kernel, meta, [hopped, hopped_other, near, mine, got, spread],
         [shape((2 * rows, C), BF16), shape((2 * rows, Hh), F32)] + [shape((Cq, 2 * rows), BF16)] * 4,
     )
-    rest = lax.optimization_barrier((*fars, *early))
-    fars, early = rest[:4], rest[4:]
+    rest = lax.optimization_barrier((*fars, *early, *late))
+    fars, early, late = rest[:4], rest[4:8], rest[8:]
     early = [early[0]] + [send_a(part, k + 1) for k, part in enumerate(early[1:])]
     hg, hidden_t, wfar, *messages = run(
         forward_kernel, meta, [taps, tap, ogs, near, arriving, *fars, order(Hh, Hq // 64, 2), *late],
@@ -317,11 +325,11 @@
     block = (4, Hh // 4, Hh)
     p_own, *sends = run(point_kernel, meta, [ogs, hidden_t], [shape(block, F32)] + [shape(block, BF16)] * 3)
     p_all = [p_own] + [send_a(part, k + 1) for k, part in enumerate(sends)]
-    earlier = shifted(hg, hops)
-    earlier, hg_late, *messages = lax.optimization_barrier((earlier, hg, *messages))
-    later = shifted(hg_late, -hops)
+    hg_flipped = flip(hg)
+    hg_flipped, *messages = lax.optimization_barrier((hg_flipped, *messages))
+    hg_hopped = hop(hg_flipped)
     conv, = run(gradient_kernel, meta, [*early, *messages], [shape((3 * Cq, Hh), F32)])
-    later, conv, *p_all = lax.optimization_barrier((later, conv, *p_all))
+    hg_hopped, conv, *p_all = lax.optimization_barrier((hg_hopped, conv, *p_all))
     n = 12 * (Cq // 16)
     big = (n + Hh // 4, Hh)
     total, *sends = run(pack_kernel, meta, [conv, *p_all], [shape(big, F32)] + [shape(big, BF16)] * 3)
@@ -333,7 +341,7 @@
     )
     hg_late, last = lax.optimization_barrier((hg, last))
     kept, other = run(
-        input_kernel, meta, [hg_late, later, earlier, mine, got, wfar.reshape(3, 2 * Cq, Hh)],
+        input_kernel, meta, [hg_late, hg_flipped, hg_hopped, mine, got, wfar.reshape(3, 2 * Cq, Hh)],
         [shape((rows, C), F32)] * 2,
     )
     in_grad = (og.astype(F32) + kept + send(other, partner)).astype(BF16)

time: 151 us -> 137 us (0.907)
  starting transfers between devices: 69.9 us -> 59.4 us
  local copies, waits for them, and re-layouts: 11.8 us -> 9.14 us
    ppermute x5 -> x0, waiting for transfers between devices: 26.1 us -> none  [shifted(): lax.ppermute(value, 'seq', [(source, source + steps) for source in range(...]
    ppermute x32 -> x37, waiting for transfers between devices: 19.7 us -> 45.7 us  [send(): return lax.ppermute(value, ('dp', 'seq'), pairs)]
    ppermute x5 -> x0, starting transfers between devices: 13.8 us -> none  [shifted(): lax.ppermute(value, 'seq', [(source, source + steps) for source in range(...]
    ppermute x32 -> x37, starting transfers between devices: 56.1 us -> 59.4 us  [send(): return lax.ppermute(value, ('dp', 'seq'), pairs)]
    unnamed x32 -> x24, local copies, waits for them, and re-layouts: 7.25 us -> 4.52 us
  transfers between devices with their start and end apart: 37 -> 37, of which waited for: 15 -> 13; matrix products, arithmetic and copies ran while one was open for 3% -> 4% of each run, Pallas kernels for 12% -> 13%
where the time goes in v4:
time: 137 us
  starting transfers between devices  59.4 us (43%)
  waiting for transfers between devices  45.7 us (33%)
  Pallas kernels  19.3 us (14%)
  local copies, waits for them, and re-layouts  9.14 us (7%)
  other arithmetic  2.24 us (2%)
    ppermute x37, starting transfers between devices, send(): return lax.ppermute(value, ('dp', 'seq'), pairs)  59.4 us
    ppermute x37, waiting for transfers between devices, send(): return lax.ppermute(value, ('dp', 'seq'), pairs)  45.7 us
    pallas_call x9, Pallas kernels, run(): pl.pallas_call(kernel, out_shape=outs, in_specs=[pl.BlockSpec(memory_spac...  19.3 us
    unnamed x24, local copies, waits for them, and re-layouts  4.52 us
  transfers between devices with their start and end apart: 37, of which 13 were waited for; matrix products, arithmetic and copies ran while one was open for 4% of the time, Pallas kernels for 13%

profile of v4, /device:TPU:1, one launch (start us, length us, event | category | flops | bytes accessed | tf_op | source)
XLA Modules:
  0.0 136.8 jit_solution(11011103372247805563)
XLA Ops:
  2.4 8.7 %collective-permute-start.2 = (bf16[128,1536]{1,0:T(8,128)(2,1)}, bf16[128,1536]{1,0:T(8,128)(2,1)S(1)}, u32[]{:S(2)}, u32[]{:S(2)}) collective-permute-start(bf16[128,1536]{1,0:T(8,128)(2,1)} %bitcast.26), channel_id=1, source_target_pairs={{0,64},{1,65},{2,66},{3,67},{4,68},{5,69},{6,70},{7,71},{8,72},{9,... | collective-permute-start | bytes 1179656 | tf_op jit(solution)/shard_map/ppermute | solution.py:24
  12.1 2.2 %collective-permute-start.4 = (bf16[64,1536]{1,0:T(8,128)(2,1)S(1)}, bf16[64,1536]{1,0:T(8,128)(2,1)S(1)}, u32[]{:S(2)}, u32[]{:S(2)}) collective-permute-start(bf16[64,1536]{1,0:T(8,128)(2,1)S(1)} %slice_bitcast_fusion), channel_id=1, source_target_pairs={{0,8},{1,9},{2,10},{3,11},{4,12},{5,13},{6,14},{7,15},{8,0},{9,1},... | collective-permute-start | bytes 589832 | tf_op jit(solution)/shard_map/ppermute | solution.py:24
  19.4 4.0 %collective-permute-done.4 = bf16[64,1536]{1,0:T(8,128)(2,1)S(1)} collective-permute-done((bf16[64,1536]{1,0:T(8,128)(2,1)S(1)}, bf16[64,1536]{1,0:T(8,128)(2,1)S(1)}, u32[]{:S(2)}, u32[]{:S(2)}) %collective-permute-start.4) | collective-permute-done | bytes 196640 | tf_op jit(solution)/shard_map/ppermute | solution.py:24
  30.5 2.6 %collective-permute-start.9 = (bf16[4,48,384]{2,1,0:T(8,128)(2,1)S(1)}, bf16[4,48,384]{2,1,0:T(8,128)(2,1)S(1)}, u32[]{:S(2)}, u32[]{:S(2)}) collective-permute-start(bf16[4,48,384]{2,1,0:T(8,128)(2,1)S(1)} %pad_maximum_fusion.2), channel_id=1, source_target_pairs={{0,32},{1,33},{2,34},{3,35},{4,36},{5,37},{6,38},{7,39},{8,40},{9,... | collective-permute-start | bytes 442376 | tf_op jit(solution)/shard_map/ppermute | solution.py:24
  34.2 4.0 %collective-permute-done.6 = bf16[64,1536]{1,0:T(8,128)(2,1)S(1)} collective-permute-done((bf16[64,1536]{1,0:T(8,128)(2,1)S(1)}, bf16[64,1536]{1,0:T(8,128)(2,1)S(1)}, u32[]{:S(2)}, u32[]{:S(2)}) %collective-permute-start.6) | collective-permute-done | bytes 196640 | tf_op jit(solution)/shard_map/ppermute | solution.py:24
  38.9 3.1 %collective-permute-start.11 = (bf16[128,1536]{1,0:T(8,128)(2,1)S(1)}, bf16[128,1536]{1,0:T(8,128)(2,1)S(1)}, u32[]{:S(2)}, u32[]{:S(2)}) collective-permute-start(bf16[128,1536]{1,0:T(8,128)(2,1)S(1)} %pad_maximum_fusion.1.x0), channel_id=1, source_target_pairs={{0,16},{1,17},{2,18},{3,19},{4,20},{5,21},{6,22},{7,23},{16,32},{1... | collective-permute-start | bytes 1179656 | tf_op jit(solution)/shard_map/ppermute | solution.py:24
  46.5 4.2 %shard_map.68 = (bf16[2,256,1536]{2,1,0:T(8,128)(2,1)}, bf16[256,1536]{1,0:T(8,128)(2,1)}, f32[256,384]{1,0:T(8,128)S(1)}, f32[256,192]{1,0:T(8,128)S(1)}, bf16[...) custom-call(s32[5]{0:T(128)S(1)} %stack.38.meta, ...), custom_call_target="tpu_custom_call" | custom-call | flops 1 | bytes 1 | tf_op jit(solution)/shard_map/pallas_call | solution.py:55
  50.8 2.0 %collective-permute-start.13 = (bf16[128,1536]{1,0:T(8,128)(2,1)S(1)}, bf16[128,1536]{1,0:T(8,128)(2,1)S(1)}, u32[]{:S(2)}, u32[]{:S(2)}) collective-permute-start(bf16[128,1536]{1,0:T(8,128)(2,1)S(1)} %collective-permute-done.11.x2), channel_id=1, source_target_pairs={{0,64},{1,65},{2,66},{3,67},{4,68},{5,69},{6,70},{7,71},{8,72},{9,... | collective-permute-start | bytes 1179656 | tf_op jit(solution)/shard_map/ppermute | solution.py:24
  57.6 10.0 %collective-permute-done.15.far2 = bf16[4,4,48,384]{3,2,1,0:T(8,128)(2,1)S(1)} collective-permute-done((bf16[4,4,48,384]{3,2,1,0:T(8,128)(2,1)S(1)}, bf16[4,4,48,384]{3,2,1,0:T(8,128)(2,1)S(1)}, u32[]{:S(2)}, u32[]{:S(2)}) %collective-permute-start.15) | collective-permute-done | bytes 589856 | tf_op jit(solution)/shard_map/ppermute | solution.py:24
  68.8 3.4 %collective-permute-start.18 = (bf16[768,256]{1,0:T(8,128)(2,1)S(1)}, bf16[768,256]{1,0:T(8,128)(2,1)S(1)}, u32[]{:S(2)}, u32[]{:S(2)}) collective-permute-start(bf16[768,256]{1,0:T(8,128)(2,1)S(1)} %get-tuple-element.137), channel_id=1, source_target_pairs={{0,32},{1,33},{2,34},{3,35},{4,36},{5,37},{6,38},{7,39},{8,40},{9,... | collective-permute-start | bytes 1179656 | tf_op jit(solution)/shard_map/ppermute | solution.py:24
  73.1 5.2 %shard_map.70 = (bf16[256,384]{1,0:T(8,128)(2,1)S(1)}, bf16[384,256]{1,0:T(8,128)(2,1)S(1)}, bf16[3,16,48,384]{3,2,1,0:T(8,128)(2,1)}, bf16[768,256]{1,0:T(8,128...) custom-call(s32[5]{0:T(128)S(1)} %stack.38.meta, ...), custom_call_target="tpu_custom_call" | custom-call | flops 1 | bytes 1 | tf_op jit(solution)/shard_map/pallas_call | solution.py:55
  78.2 3.4 %collective-permute-done.18.x2 = bf16[768,256]{1,0:T(8,128)(2,1)S(1)} collective-permute-done((bf16[768,256]{1,0:T(8,128)(2,1)S(1)}, bf16[768,256]{1,0:T(8,128)(2,1)S(1)}, u32[]{:S(2)}, u32[]{:S(2)}) %collective-permute-start.18) | collective-permute-done | bytes 393248 | tf_op jit(solution)/shard_map/ppermute | solution.py:24
  82.8 2.1 %collective-permute-start.22 = (bf16[768,256]{1,0:T(8,128)(2,1)S(1)}, bf16[768,256]{1,0:T(8,128)(2,1)S(1)}, u32[]{:S(2)}, u32[]{:S(2)}) collective-permute-start(bf16[768,256]{1,0:T(8,128)(2,1)S(1)} %get-tuple-element.146), channel_id=1, source_target_pairs={{0,32},{1,33},{2,34},{3,35},{4,36},{5,37},{6,38},{7,39},{8,40},{9,... | collective-permute-start | bytes 1179656 | tf_op jit(solution)/shard_map/ppermute | solution.py:24
  87.5 5.9 %collective-permute-done.20.flipped = bf16[256,384]{1,0:T(8,128)(2,1)S(1)} collective-permute-done((bf16[256,384]{1,0:T(8,128)(2,1)S(1)}, bf16[256,384]{1,0:T(8,128)(2,1)S(1)}, u32[]{:S(2)}, u32[]{:S(2)}) %collective-permute-start.20) | collective-permute-done | bytes 196640 | tf_op jit(solution)/shard_map/ppermute | solution.py:24
  93.4 2.1 %collective-permute-start.26 = (bf16[4,96,384]{2,1,0:T(8,128)(2,1)S(1)}, bf16[4,96,384]{2,1,0:T(8,128)(2,1)S(1)}, u32[]{:S(2)}, u32[]{:S(2)}) collective-permute-start(bf16[4,96,384]{2,1,0:T(8,128)(2,1)S(1)} %get-tuple-element.160), channel_id=1, source_target_pairs={{0,32},{1,33},{2,34},{3,35},{4,36},{5,37},{6,38},{7,39},{8,40},{9,... | collective-permute-start | bytes 884744 | tf_op jit(solution)/shard_map/ppermute | solution.py:24
  100.6 2.2 %collective-permute-done.27.p3 = bf16[4,96,384]{2,1,0:T(8,128)(2,1)S(1)} collective-permute-done((bf16[4,96,384]{2,1,0:T(8,128)(2,1)S(1)}, bf16[4,96,384]{2,1,0:T(8,128)(2,1)S(1)}, u32[]{:S(2)}, u32[]{:S(2)}) %collective-permute-start.27) | collective-permute-done | bytes 294944 | tf_op jit(solution)/shard_map/ppermute | solution.py:24
  108.2 2.5 %collective-permute-done.28.got1 = bf16[384,384]{1,0:T(8,128)(2,1)S(1)} collective-permute-done((bf16[384,384]{1,0:T(8,128)(2,1)S(1)}, bf16[384,384]{1,0:T(8,128)(2,1)S(1)}, u32[]{:S(2)}, u32[]{:S(2)}) %collective-permute-start.28) | collective-permute-done | bytes 294944 | tf_op jit(solution)/shard_map/ppermute | solution.py:24
  110.8 3.1 %collective-permute-done.29.got2 = bf16[384,384]{1,0:T(8,128)(2,1)S(1)} collective-permute-done((bf16[384,384]{1,0:T(8,128)(2,1)S(1)}, bf16[384,384]{1,0:T(8,128)(2,1)S(1)}, u32[]{:S(2)}, u32[]{:S(2)}) %collective-permute-start.29) | collective-permute-done | bytes 294944 | tf_op jit(solution)/shard_map/ppermute | solution.py:24
  115.3 2.1 %collective-permute-start.33 = (bf16[96,384]{1,0:T(8,128)(2,1)S(1)}, bf16[96,384]{1,0:T(8,128)(2,1)S(1)}, u32[]{:S(2)}, u32[]{:S(2)}) collective-permute-start(bf16[96,384]{1,0:T(8,128)(2,1)S(1)} %get-tuple-element.179), channel_id=1, source_target_pairs={{0,8},{1,9},{2,10},{3,11},{4,12},{5,13},{6,14},{7,15},{8,0},{9,1},... | collective-permute-start | bytes 221192 | tf_op jit(solution)/shard_map/ppermute | solution.py:24
  117.5 2.3 %collective-permute-start.34 = (bf16[96,384]{1,0:T(8,128)(2,1)S(1)}, bf16[96,384]{1,0:T(8,128)(2,1)S(1)}, u32[]{:S(2)}, u32[]{:S(2)}) collective-permute-start(bf16[96,384]{1,0:T(8,128)(2,1)S(1)} %get-tuple-element.180), channel_id=1, source_target_pairs={{0,12},{1,13},{2,14},{3,15},{4,0},{5,1},{6,2},{7,3},{8,4},{9,5},{1... | collective-permute-start | bytes 221192 | tf_op jit(solution)/shard_map/ppermute | solution.py:24
  119.7 2.1 %shard_map.75 = (f32[128,1536]{1,0:T(8,128)S(1)}, f32[128,1536]{1,0:T(8,128)S(1)}) custom-call(s32[5]{0:T(128)S(1)} %stack.38.meta, bf16[256,384]{1,0:T(8,128)(2,1)S(1)} %get-tuple-element.172.hg, bf16[256,384]{1,0:T(8,128)(2,1)S(1)} %collective-permute-done.20.flipped, bf16[256,384]{1,0:T(8,128)(2,1)S(1)} %collective-permute-done.24.hopped, ...), custom_call_target="tpu_custom_call" | custom-call | flops 1 | bytes 1 | tf_op jit(solution)/shard_map/pallas_call | solution.py:55
  121.9 2.8 %collective-permute-start.31 = (f32[128,1536]{1,0:T(8,128)S(1)}, f32[128,1536]{1,0:T(8,128)S(1)}, u32[]{:S(2)}, u32[]{:S(2)}) collective-permute-start(f32[128,1536]{1,0:T(8,128)S(1)} %get-tuple-element.176), channel_id=1, source_target_pairs={{0,64},{1,65},{2,66},{3,67},{4,68},{5,69},{6,70},{7,71},{8,72},{9,... | collective-permute-start | bytes 2359304 | tf_op jit(solution)/shard_map/ppermute | solution.py:24
  125.9 5.7 %collective-permute-done.35 = bf16[48,384]{1,0:T(8,128)(2,1)S(1)} collective-permute-done((bf16[48,384]{1,0:T(8,128)(2,1)S(1)}, bf16[48,384]{1,0:T(8,128)(2,1)S(1)}, u32[]{:S(2)}, u32[]{:S(2)}) %collective-permute-start.35) | collective-permute-done | bytes 36896 | tf_op jit(solution)/shard_map/ppermute | solution.py:24
  132.4 2.6 %collective-permute-start.36 = (f32[3,6,384]{2,1,0:T(8,128)S(1)}, f32[3,6,384]{2,1,0:T(8,128)S(1)}, u32[]{:S(2)}, u32[]{:S(2)}) collective-permute-start(f32[3,6,384]{2,1,0:T(8,128)S(1)} %get-tuple-element.188), channel_id=1, source_target_pairs={{0,64},{1,65},{2,66},{3,67},{4,68},{5,69},{6,70},{7,71},{8,72},{9,... | collective-permute-start | bytes 82952 | tf_op jit(solution)/shard_map/ppermute | solution.py:24
  (112 shorter events, 47.4 us)
Async XLA Ops:
  1.7 21.7 %collective-permute-start = (bf16[3,48,768]{2,1,0:T(8,128)(2,1)S(1)}, bf16[3,48,768]{2,1,0:T(8,128)(2,1)S(1)}, u32[]{:S(2)}, u32[]{:S(2)}) collective-permute-start(bf16[3,48,768]{2,1,0:T(8,128)(2,1)S(1)} %constant_dynamic-slice_fusion.4), channel_id=1, source_target_pairs={{0,140},{1,141},{2,142},{3,143},{4,136},{5,137},{6,138},{7,139},{8... | collective-permute-start | bytes 663560 | tf_op jit(solution)/shard_map/ppermute | solution.py:24
  2.4 12.7 %collective-permute-start.2 = (bf16[128,1536]{1,0:T(8,128)(2,1)}, bf16[128,1536]{1,0:T(8,128)(2,1)S(1)}, u32[]{:S(2)}, u32[]{:S(2)}) collective-permute-start(bf16[128,1536]{1,0:T(8,128)(2,1)} %bitcast.26), channel_id=1, source_target_pairs={{0,64},{1,65},{2,66},{3,67},{4,68},{5,69},{6,70},{7,71},{8,72},{9,... | collective-permute-start | bytes 1179656 | tf_op jit(solution)/shard_map/ppermute | solution.py:24
  11.1 12.4 %collective-permute-start.3 = (bf16[128,1536]{1,0:T(8,128)(2,1)}, bf16[128,1536]{1,0:T(8,128)(2,1)S(1)}, u32[]{:S(2)}, u32[]{:S(2)}) collective-permute-start(bf16[128,1536]{1,0:T(8,128)(2,1)} %bitcast.24), channel_id=1, source_target_pairs={{0,64},{1,65},{2,66},{3,67},{4,68},{5,69},{6,70},{7,71},{8,72},{9,... | collective-permute-start | bytes 1179656 | tf_op jit(solution)/shard_map/ppermute | solution.py:24
  12.1 11.3 %collective-permute-start.4 = (bf16[64,1536]{1,0:T(8,128)(2,1)S(1)}, bf16[64,1536]{1,0:T(8,128)(2,1)S(1)}, u32[]{:S(2)}, u32[]{:S(2)}) collective-permute-start(bf16[64,1536]{1,0:T(8,128)(2,1)S(1)} %slice_bitcast_fusion), channel_id=1, source_target_pairs={{0,8},{1,9},{2,10},{3,11},{4,12},{5,13},{6,14},{7,15},{8,0},{9,1},... | collective-permute-start | bytes 589832 | tf_op jit(solution)/shard_map/ppermute | solution.py:24
  23.4 14.9 %collective-permute-start.7 = (bf16[3,384,384]{2,1,0:T(8,128)(2,1)}, bf16[3,384,384]{2,1,0:T(8,128)(2,1)S(1)}, u32[]{:S(2)}, u32[]{:S(2)}) collective-permute-start(bf16[3,384,384]{2,1,0:T(8,128)(2,1)} %get-tuple-element.100), channel_id=1, source_target_pairs={{0,64},{1,65},{2,66},{3,67},{4,68},{5,69},{6,70},{7,71},{8,72},{9,... | collective-permute-start | bytes 2654216 | tf_op jit(solution)/shard_map/ppermute | solution.py:24
  27.0 11.3 %collective-permute-start.6 = (bf16[64,1536]{1,0:T(8,128)(2,1)S(1)}, bf16[64,1536]{1,0:T(8,128)(2,1)S(1)}, u32[]{:S(2)}, u32[]{:S(2)}) collective-permute-start(bf16[64,1536]{1,0:T(8,128)(2,1)S(1)} %slice.32), channel_id=1, source_target_pairs={{0,8},{1,9},{2,10},{3,11},{4,12},{5,13},{6,14},{7,15},{8,0},{9,1},... | collective-permute-start | bytes 589832 | tf_op jit(solution)/shard_map/ppermute | solution.py:24
  29.2 9.1 %collective-permute-start.10 = (bf16[4,48,384]{2,1,0:T(8,128)(2,1)S(1)}, bf16[4,48,384]{2,1,0:T(8,128)(2,1)S(1)}, u32[]{:S(2)}, u32[]{:S(2)}) collective-permute-start(bf16[4,48,384]{2,1,0:T(8,128)(2,1)S(1)} %pad_maximum_fusion.2), channel_id=1, source_target_pairs={{0,16},{1,17},{2,18},{3,19},{4,20},{5,21},{6,22},{7,23},{8,24},{9,... | collective-permute-start | bytes 442376 | tf_op jit(solution)/shard_map/ppermute | solution.py:24
  38.3 8.2 %collective-permute-start.12 = (bf16[128,1536]{1,0:T(8,128)(2,1)S(1)}, bf16[128,1536]{1,0:T(8,128)(2,1)S(1)}, u32[]{:S(2)}, u32[]{:S(2)}) collective-permute-start(bf16[128,1536]{1,0:T(8,128)(2,1)S(1)} %pad_maximum_fusion.1.x0), channel_id=1, source_target_pairs={{0,64},{1,65},{2,66},{3,67},{4,68},{5,69},{6,70},{7,71},{8,72},{9,... | collective-permute-start | bytes 1179656 | tf_op jit(solution)/shard_map/ppermute | solution.py:24
  38.9 11.9 %collective-permute-start.11 = (bf16[128,1536]{1,0:T(8,128)(2,1)S(1)}, bf16[128,1536]{1,0:T(8,128)(2,1)S(1)}, u32[]{:S(2)}, u32[]{:S(2)}) collective-permute-start(bf16[128,1536]{1,0:T(8,128)(2,1)S(1)} %pad_maximum_fusion.1.x0), channel_id=1, source_target_pairs={{0,16},{1,17},{2,18},{3,19},{4,20},{5,21},{6,22},{7,23},{16,32},{1... | collective-permute-start | bytes 1179656 | tf_op jit(solution)/shard_map/ppermute | solution.py:24
  42.2 15.4 %collective-permute-start.16 = (bf16[4,4,48,384]{3,2,1,0:T(8,128)(2,1)S(1)}, bf16[4,4,48,384]{3,2,1,0:T(8,128)(2,1)S(1)}, u32[]{:S(2)}, u32[]{:S(2)}) collective-permute-start(bf16[4,4,48,384]{3,2,1,0:T(8,128)(2,1)S(1)} %pad_maximum_fusion.far0), channel_id=1, source_target_pairs={{0,1},{1,2},{2,3},{3,0},{4,5},{5,6},{6,7},{7,4},{8,9},{9,10},{10,1... | collective-permute-start | bytes 1769480 | tf_op jit(solution)/shard_map/ppermute | solution.py:24
  43.1 24.5 %collective-permute-start.15 = (bf16[4,4,48,384]{3,2,1,0:T(8,128)(2,1)S(1)}, bf16[4,4,48,384]{3,2,1,0:T(8,128)(2,1)S(1)}, u32[]{:S(2)}, u32[]{:S(2)}) collective-permute-start(bf16[4,4,48,384]{3,2,1,0:T(8,128)(2,1)S(1)} %pad_maximum_fusion.far0), channel_id=1, source_target_pairs={{0,2},{1,3},{2,0},{3,1},{4,6},{5,7},{6,4},{7,5},{8,10},{9,11},{10,... | collective-permute-start | bytes 1769480 | tf_op jit(solution)/shard_map/ppermute | solution.py:24
  44.4 23.2 %collective-permute-start.14 = (bf16[4,4,48,384]{3,2,1,0:T(8,128)(2,1)S(1)}, bf16[4,4,48,384]{3,2,1,0:T(8,128)(2,1)S(1)}, u32[]{:S(2)}, u32[]{:S(2)}) collective-permute-start(bf16[4,4,48,384]{3,2,1,0:T(8,128)(2,1)S(1)} %pad_maximum_fusion.far0), channel_id=1, source_target_pairs={{0,3},{1,0},{2,1},{3,2},{4,7},{5,4},{6,5},{7,6},{8,11},{9,8},{10,9... | collective-permute-start | bytes 1769480 | tf_op jit(solution)/shard_map/ppermute | solution.py:24
  67.6 10.7 %collective-permute-start.17 = (bf16[768,256]{1,0:T(8,128)(2,1)S(1)}, bf16[768,256]{1,0:T(8,128)(2,1)S(1)}, u32[]{:S(2)}, u32[]{:S(2)}) collective-permute-start(bf16[768,256]{1,0:T(8,128)(2,1)S(1)} %get-tuple-element.136), channel_id=1, source_target_pairs={{0,16},{1,17},{2,18},{3,19},{4,20},{5,21},{6,22},{7,23},{8,24},{9,... | collective-permute-start | bytes 1179656 | tf_op jit(solution)/shard_map/ppermute | solution.py:24
  68.8 12.8 %collective-permute-start.18 = (bf16[768,256]{1,0:T(8,128)(2,1)S(1)}, bf16[768,256]{1,0:T(8,128)(2,1)S(1)}, u32[]{:S(2)}, u32[]{:S(2)}) collective-permute-start(bf16[768,256]{1,0:T(8,128)(2,1)S(1)} %get-tuple-element.137), channel_id=1, source_target_pairs={{0,32},{1,33},{2,34},{3,35},{4,36},{5,37},{6,38},{7,39},{8,40},{9,... | collective-permute-start | bytes 1179656 | tf_op jit(solution)/shard_map/ppermute | solution.py:24
  72.2 9.4 %collective-permute-start.19 = (bf16[768,256]{1,0:T(8,128)(2,1)S(1)}, bf16[768,256]{1,0:T(8,128)(2,1)S(1)}, u32[]{:S(2)}, u32[]{:S(2)}) collective-permute-start(bf16[768,256]{1,0:T(8,128)(2,1)S(1)} %get-tuple-element.138), channel_id=1, source_target_pairs={{0,48},{1,49},{2,50},{3,51},{4,52},{5,53},{6,54},{7,55},{8,56},{9,... | collective-permute-start | bytes 1179656 | tf_op jit(solution)/shard_map/ppermute | solution.py:24
  81.6 13.9 %collective-permute-start.21 = (bf16[768,256]{1,0:T(8,128)(2,1)S(1)}, bf16[768,256]{1,0:T(8,128)(2,1)S(1)}, u32[]{:S(2)}, u32[]{:S(2)}) collective-permute-start(bf16[768,256]{1,0:T(8,128)(2,1)S(1)} %get-tuple-element.145), channel_id=1, source_target_pairs={{0,16},{1,17},{2,18},{3,19},{4,20},{5,21},{6,22},{7,23},{8,24},{9,... | collective-permute-start | bytes 1179656 | tf_op jit(solution)/shard_map/ppermute | solution.py:24
  82.8 13.7 %collective-permute-start.22 = (bf16[768,256]{1,0:T(8,128)(2,1)S(1)}, bf16[768,256]{1,0:T(8,128)(2,1)S(1)}, u32[]{:S(2)}, u32[]{:S(2)}) collective-permute-start(bf16[768,256]{1,0:T(8,128)(2,1)S(1)} %get-tuple-element.146), channel_id=1, source_target_pairs={{0,32},{1,33},{2,34},{3,35},{4,36},{5,37},{6,38},{7,39},{8,40},{9,... | collective-permute-start | bytes 1179656 | tf_op jit(solution)/shard_map/ppermute | solution.py:24
  84.9 11.6 %collective-permute-start.23 = (bf16[768,256]{1,0:T(8,128)(2,1)S(1)}, bf16[768,256]{1,0:T(8,128)(2,1)S(1)}, u32[]{:S(2)}, u32[]{:S(2)}) collective-permute-start(bf16[768,256]{1,0:T(8,128)(2,1)S(1)} %get-tuple-element.147), channel_id=1, source_target_pairs={{0,48},{1,49},{2,50},{3,51},{4,52},{5,53},{6,54},{7,55},{8,56},{9,... | collective-permute-start | bytes 1179656 | tf_op jit(solution)/shard_map/ppermute | solution.py:24
  87.0 12.7 %collective-permute-start.25 = (bf16[4,96,384]{2,1,0:T(8,128)(2,1)S(1)}, bf16[4,96,384]{2,1,0:T(8,128)(2,1)S(1)}, u32[]{:S(2)}, u32[]{:S(2)}) collective-permute-start(bf16[4,96,384]{2,1,0:T(8,128)(2,1)S(1)} %get-tuple-element.159), channel_id=1, source_target_pairs={{0,16},{1,17},{2,18},{3,19},{4,20},{5,21},{6,22},{7,23},{8,24},{9,... | collective-permute-start | bytes 884744 | tf_op jit(solution)/shard_map/ppermute | solution.py:24
  105.1 8.8 %collective-permute-start.29 = (bf16[384,384]{1,0:T(8,128)(2,1)S(1)}, bf16[384,384]{1,0:T(8,128)(2,1)S(1)}, u32[]{:S(2)}, u32[]{:S(2)}) collective-permute-start(bf16[384,384]{1,0:T(8,128)(2,1)S(1)} %get-tuple-element.169), channel_id=1, source_target_pairs={{0,2},{1,3},{2,0},{3,1},{4,6},{5,7},{6,4},{7,5},{8,10},{9,11},{10,... | collective-permute-start | bytes 884744 | tf_op jit(solution)/shard_map/ppermute | solution.py:24
  106.5 8.0 %collective-permute-start.30 = (bf16[384,384]{1,0:T(8,128)(2,1)S(1)}, bf16[384,384]{1,0:T(8,128)(2,1)S(1)}, u32[]{:S(2)}, u32[]{:S(2)}) collective-permute-start(bf16[384,384]{1,0:T(8,128)(2,1)S(1)} %get-tuple-element.170), channel_id=1, source_target_pairs={{0,3},{1,0},{2,1},{3,2},{4,7},{5,4},{6,5},{7,6},{8,11},{9,8},{10,9... | collective-permute-start | bytes 884744 | tf_op jit(solution)/shard_map/ppermute | solution.py:24
  115.3 9.4 %collective-permute-start.32 = (bf16[96,384]{1,0:T(8,128)(2,1)S(1)}, bf16[96,384]{1,0:T(8,128)(2,1)S(1)}, u32[]{:S(2)}, u32[]{:S(2)}) collective-permute-start(bf16[96,384]{1,0:T(8,128)(2,1)S(1)} %get-tuple-element.178), channel_id=1, source_target_pairs={{0,4},{1,5},{2,6},{3,7},{4,8},{5,9},{6,10},{7,11},{8,12},{9,13},{1... | collective-permute-start | bytes 221192 | tf_op jit(solution)/shard_map/ppermute | solution.py:24
  115.3 9.3 %collective-permute-start.33 = (bf16[96,384]{1,0:T(8,128)(2,1)S(1)}, bf16[96,384]{1,0:T(8,128)(2,1)S(1)}, u32[]{:S(2)}, u32[]{:S(2)}) collective-permute-start(bf16[96,384]{1,0:T(8,128)(2,1)S(1)} %get-tuple-element.179), channel_id=1, source_target_pairs={{0,8},{1,9},{2,10},{3,11},{4,12},{5,13},{6,14},{7,15},{8,0},{9,1},... | collective-permute-start | bytes 221192 | tf_op jit(solution)/shard_map/ppermute | solution.py:24
  121.9 13.2 %collective-permute-start.31 = (f32[128,1536]{1,0:T(8,128)S(1)}, f32[128,1536]{1,0:T(8,128)S(1)}, u32[]{:S(2)}, u32[]{:S(2)}) collective-permute-start(f32[128,1536]{1,0:T(8,128)S(1)} %get-tuple-element.176), channel_id=1, source_target_pairs={{0,64},{1,65},{2,66},{3,67},{4,68},{5,69},{6,70},{7,71},{8,72},{9,... | collective-permute-start | bytes 2359304 | tf_op jit(solution)/shard_map/ppermute | solution.py:24
  (25 other events, 213.8 us)

commit v5 on v4

--- a/solution.py
+++ b/solution.py
@@ -209,13 +209,38 @@
     for t, out in enumerate((kept, send1, send2, send3)):
         parts = []
         for u in range(2):
-            for g in range(3):
-                at = (2 * g + u) * 2 * piece + t * row
-                parts += [total[at:at + row], total[at + piece:at + piece + row]]
+            first = [(2 * g + u) * 2 * piece + t * row for g in range(3)]
+            parts += [total[at:at + row] for at in first]
             for p in range(4):
                 at = (12 + p) * piece + u * piece // 2 + t * thin
                 parts.append(total[at:at + thin])
+            parts += [total[at + piece:at + piece + row] for at in first]
         out[...] = jnp.concatenate(parts, 0).astype(out.dtype)
+
+
+def split_sum_kernel(meta, own, got1, got2, got3, kept, to_z, to_core, to_both):
+    total = own[...] + got1[...].astype(F32) + got2[...].astype(F32) + got3[...].astype(F32)
+    half, size = total.shape[0] // 2, kept.shape[0]
+    kept[...] = total[:size]
+    to_core[...] = total[size:half]
+    to_z[...] = total[half:half + size]
+    to_both[...] = total[half + size:]
+
+
+def output_kernel(meta, kept, from_z, from_core, from_both, conv, point):
+    here, there = kept[...] + from_z[...], from_core[...] + from_both[...]
+    taps, row = conv.shape[:2]
+    width = here.shape[1]
+    half = width // 2
+    first = meta[0] == 0
+    for t in range(taps):
+        a, b = here[t * row:(t + 1) * row], there[t * row:(t + 1) * row]
+        even, odd = jnp.where(first, a, b), jnp.where(first, b, a)
+        conv[t] = jnp.concatenate([even[:, :half], odd[:, :half], even[:, half:], odd[:, half:]], 1)
+    thin = point.shape[0]
+    for p in range(point.shape[1] // width):
+        at = taps * row + p * thin
+        point[:, p * width:(p + 1) * width] = here[at:at + thin]
 
 
 def input_kernel(meta, hg, flipped, hopped, mine, got, wfar, kept, other):
@@ -270,30 +295,26 @@
     def partner(x, y, z, c):
         return x, y, z, 1 - c
 
-    def beside(first, second, axis):
-        return jnp.where(core == 0, jnp.concatenate([first, second], axis), jnp.concatenate([second, first], axis))
-
     conv_piece = lax.dynamic_slice_in_dim(conv_weight, (xi * 4 + yi) % 8 * piece, piece, 1)
     point_piece = lax.dynamic_slice(point_weight, (xi * (Hq // 4), yi * Hh), (Hq // 4, Hh))
     holders = [d for d in range(256) if coords(d)[3] == coords(d)[0] // 2]
     conv_piece = send(conv_piece, mirror, holders)
     point_piece = send(point_piece, mirror)
-    first = rows // 2
+    first = rows * 3 // 8
     flipped = flip(x[:first])
     x_other = send(x, partner)
     og_other = send(og, partner)
-    conv_weight, _ = lax.optimization_barrier((conv_weight, x_other))
+    conv_piece, point_piece, x_late, x_other, og_other, flipped, conv_weight = lax.optimization_barrier(
+        (conv_piece, point_piece, x, x_other, og_other, flipped, conv_weight)
+    )
     mine, theirs = run(split_kernel, meta, [conv_weight], [shape((3, Cq, Hh), BF16)] * 2)
-    conv_piece, point_piece, x_late, x_other, og_other, theirs, flipped, mine = lax.optimization_barrier(
-        (conv_piece, point_piece, x, x_other, og_other, theirs, flipped, mine)
-    )
-    got = send(theirs, partner)
     handed = send(columns(conv_piece, 1 - core), partner, holders)
     conv_piece = jnp.where(core == xi // 2, columns(conv_piece, core), handed)
     far = jnp.concatenate([conv_piece, point_piece[None]])
     flipped = jnp.concatenate([flipped, flip(x_late[first:])])
     fars = [send_a(far, -k) for k in (1, 2, 3)]
-    far, flipped, got, *fars = lax.optimization_barrier((far, flipped, got, *fars))
+    far, flipped, mine, theirs, *fars = lax.optimization_barrier((far, flipped, mine, theirs, *fars))
+    got = send(theirs, partner)
     hopped = hop(flipped)
     far = jnp.stack([far, *fars])
     fars = [far] + [send_b(far, -k) for k in (1, 2, 3)]
@@ -319,50 +340,48 @@
         + [shape((Cq + Hh, 2 * rows), BF16)] * 4,
         [pltpu.VMEM((4, 4, Hq // 4, Hh), BF16)],
     )
-    hg, *rest = lax.optimization_barrier((hg, *early, *messages))
-    early, messages = rest[:4], rest[4:]
+    for k in (1, 2, 3):
+        early[k], messages[k] = lax.optimization_barrier((early[k], messages[k]))
     messages = [messages[0]] + [send_a(part, k + 1) for k, part in enumerate(messages[1:])]
     block = (4, Hh // 4, Hh)
     p_own, *sends = run(point_kernel, meta, [ogs, hidden_t], [shape(block, F32)] + [shape(block, BF16)] * 3)
     p_all = [p_own] + [send_a(part, k + 1) for k, part in enumerate(sends)]
     hg_flipped = flip(hg)
-    hg_flipped, *messages = lax.optimization_barrier((hg_flipped, *messages))
+    conv, = run(gradient_kernel, meta, [*early, *messages], [shape((3 * Cq, Hh), F32)])
+    hg_flipped, conv, *p_all = lax.optimization_barrier((hg_flipped, conv, *p_all))
     hg_hopped = hop(hg_flipped)
-    conv, = run(gradient_kernel, meta, [*early, *messages], [shape((3 * Cq, Hh), F32)])
-    hg_hopped, conv, *p_all = lax.optimization_barrier((hg_hopped, conv, *p_all))
     n = 12 * (Cq // 16)
     big = (n + Hh // 4, Hh)
     total, *sends = run(pack_kernel, meta, [conv, *p_all], [shape(big, F32)] + [shape(big, BF16)] * 3)
     got_b = [send_b(part, k + 1) for k, part in enumerate(sends)]
+    *got_b, hg_hopped = lax.optimization_barrier((*got_b, hg_hopped))
     small = (big[0] // 4, Hh)
     last, *sends = run(
         slice_kernel, meta, [total, *got_b],
         [shape(small, F32)] + [shape(small, BF16)] * 3,
     )
     hg_late, last = lax.optimization_barrier((hg, last))
-    kept, other = run(
+    mine_rows, other_rows = run(
         input_kernel, meta, [hg_late, hg_flipped, hg_hopped, mine, got, wfar.reshape(3, 2 * Cq, Hh)],
         [shape((rows, C), F32)] * 2,
     )
-    in_grad = (og.astype(F32) + kept + send(other, partner)).astype(BF16)
-
+    in_grad = (og.astype(F32) + mine_rows + send(other_rows, partner)).astype(BF16)
     got_z = [
         send(part, lambda x, y, z, c: (x, y, z // 4 * 4 + (z + t + 1) % 4, c)) for t, part in enumerate(sends)
     ]
-    for part in got_z:
-        last = last + part.astype(F32)
-    last = last.reshape(2, small[0] // 2, Hh)
-    got_z = send(last[1].astype(BF16), lambda x, y, z, c: (x, y, z + 4, c))
-    last = last[0] + got_z.astype(F32)
-    n = 6 * (Cq // 64)
-    conv = last[:n].reshape(3, 2, Cq // 64, Hh)
-    point_mine = last[n:].reshape(C // Hh, Hq // 64, Hh).transpose(1, 0, 2).reshape(Hq // 64, C)
-    kept, swapped = conv[:, 0], send(conv[:, 1], partner)
-    in_grad, swapped = lax.optimization_barrier((in_grad, swapped))
-    kept, swapped = (part.reshape(3, Cq // 64, 2, 1, Hq) for part in (kept, swapped))
-    conv_mine = jnp.where(
-        core == 0, jnp.concatenate([kept, swapped], 3), jnp.concatenate([swapped, kept], 3)
-    ).reshape(3, Cq // 64, H)
+    conv_rows = 3 * (Cq // 64)
+    point_rows = small[0] // 2 - 2 * conv_rows
+    halves = (conv_rows + point_rows, Hh), (conv_rows, Hh)
+    kept, to_z, to_core, to_both = run(
+        split_sum_kernel, meta, [last, *got_z], [shape(halves[k], F32) for k in (0, 0, 1, 1)]
+    )
+    from_z = send(to_z, lambda x, y, z, c: (x, y, z + 4, c))
+    from_both = send(to_both, lambda x, y, z, c: (x, y, z + 4, 1 - c))
+    in_grad, from_core = lax.optimization_barrier((in_grad, send(to_core, partner)))
+    conv_mine, point_mine = run(
+        output_kernel, meta, [kept, from_z, from_core, from_both],
+        [shape((3, Cq // 64, H), F32), shape((Hq // 64, C), F32)],
+    )
     return in_grad[None], conv_mine, point_mine
 
 

time: 137 us -> 139 us (1.015)
  waiting for transfers between devices: 45.7 us -> 48.5 us
    ppermute x37 -> x38, waiting for transfers between devices: 45.7 us -> 48.5 us  [send(): return lax.ppermute(value, ('dp', 'seq'), pairs)]
    pallas_call x9 -> x11, Pallas kernels: 19.3 us -> 20.1 us  [run(): pl.pallas_call(kernel, out_shape=outs, in_specs=[pl.BlockSpec(memory_spac...]
    ppermute x37 -> x38, starting transfers between devices: 59.4 us -> 58.8 us  [send(): return lax.ppermute(value, ('dp', 'seq'), pairs)]
  transfers between devices with their start and end apart: 37 -> 38, of which waited for: 13 -> 13; matrix products, arithmetic and copies ran while one was open for 4% -> 3% of each run, Pallas kernels for 13% -> 11%
where the time goes in v5:
time: 139 us; the launch traced here: 138 us
  starting transfers between devices  58.8 us (42%)
  waiting for transfers between devices  48.5 us (35%)
  Pallas kernels  20.1 us (14%)
  local copies, waits for them, and re-layouts  7.93 us (6%)
  other arithmetic  1.53 us (1%)
    ppermute x38, starting transfers between devices, send(): return lax.ppermute(value, ('dp', 'seq'), pairs)  58.8 us
    ppermute x38, waiting for transfers between devices, send(): return lax.ppermute(value, ('dp', 'seq'), pairs)  48.5 us
    pallas_call x11, Pallas kernels, run(): pl.pallas_call(kernel, out_shape=outs, in_specs=[pl.BlockSpec(memory_spac...  20.1 us
    unnamed x24, local copies, waits for them, and re-layouts  3.95 us
  transfers between devices with their start and end apart: 38, of which 13 were waited for; matrix products, arithmetic and copies ran while one was open for 3% of the time, Pallas kernels for 11%

profile of v5, /device:TPU:1, one launch (start us, length us, event | category | flops | bytes accessed | tf_op | source)
XLA Modules:
  0.0 138.0 jit_solution(9037957894047042361)
XLA Ops:
  2.5 8.7 %collective-permute-start.2 = (bf16[128,1536]{1,0:T(8,128)(2,1)}, bf16[128,1536]{1,0:T(8,128)(2,1)S(1)}, u32[]{:S(2)}, u32[]{:S(2)}) collective-permute-start(bf16[128,1536]{1,0:T(8,128)(2,1)} %bitcast.20), channel_id=1, source_target_pairs={{0,64},{1,65},{2,66},{3,67},{4,68},{5,69},{6,70},{7,71},{8,72},{9,... | collective-permute-start | bytes 1179656 | tf_op jit(solution)/shard_map/ppermute | solution.py:24
  12.2 2.2 %collective-permute-start.4 = (bf16[48,1536]{1,0:T(8,128)(2,1)S(1)}, bf16[48,1536]{1,0:T(8,128)(2,1)S(1)}, u32[]{:S(2)}, u32[]{:S(2)}) collective-permute-start(bf16[48,1536]{1,0:T(8,128)(2,1)S(1)} %slice_bitcast_fusion), channel_id=1, source_target_pairs={{0,8},{1,9},{2,10},{3,11},{4,12},{5,13},{6,14},{7,15},{8,0},{9,1},... | collective-permute-start | bytes 442376 | tf_op jit(solution)/shard_map/ppermute | solution.py:24
  15.1 4.2 %collective-permute-done.1 = bf16[48,384]{1,0:T(8,128)(2,1)S(1)} collective-permute-done((bf16[48,384]{1,0:T(8,128)(2,1)S(1)}, bf16[48,384]{1,0:T(8,128)(2,1)S(1)}, u32[]{:S(2)}, u32[]{:S(2)}) %collective-permute-start.1) | collective-permute-done | bytes 36896 | tf_op jit(solution)/shard_map/ppermute | solution.py:24
  27.6 2.6 %collective-permute-start.8 = (bf16[4,48,384]{2,1,0:T(8,128)(2,1)S(1)}, bf16[4,48,384]{2,1,0:T(8,128)(2,1)S(1)}, u32[]{:S(2)}, u32[]{:S(2)}) collective-permute-start(bf16[4,48,384]{2,1,0:T(8,128)(2,1)S(1)} %pad_maximum_fusion.2), channel_id=1, source_target_pairs={{0,32},{1,33},{2,34},{3,35},{4,36},{5,37},{6,38},{7,39},{8,40},{9,... | collective-permute-start | bytes 442376 | tf_op jit(solution)/shard_map/ppermute | solution.py:24
  31.3 6.2 %collective-permute-done.6 = bf16[80,1536]{1,0:T(8,128)(2,1)S(1)} collective-permute-done((bf16[80,1536]{1,0:T(8,128)(2,1)S(1)}, bf16[80,1536]{1,0:T(8,128)(2,1)S(1)}, u32[]{:S(2)}, u32[]{:S(2)}) %collective-permute-start.6) | collective-permute-done | bytes 245792 | tf_op jit(solution)/shard_map/ppermute | solution.py:24
  38.2 3.1 %collective-permute-start.10 = (bf16[128,1536]{1,0:T(8,128)(2,1)S(1)}, bf16[128,1536]{1,0:T(8,128)(2,1)S(1)}, u32[]{:S(2)}, u32[]{:S(2)}) collective-permute-start(bf16[128,1536]{1,0:T(8,128)(2,1)S(1)} %pad_maximum_fusion.1.x0), channel_id=1, source_target_pairs={{0,16},{1,17},{2,18},{3,19},{4,20},{5,21},{6,22},{7,23},{16,32},{1... | collective-permute-start | bytes 1179656 | tf_op jit(solution)/shard_map/ppermute | solution.py:24
  41.5 2.6 %collective-permute-start.16 = (bf16[4,4,48,384]{3,2,1,0:T(8,128)(2,1)S(1)}, bf16[4,4,48,384]{3,2,1,0:T(8,128)(2,1)S(1)}, u32[]{:S(2)}, u32[]{:S(2)}) collective-permute-start(bf16[4,4,48,384]{3,2,1,0:T(8,128)(2,1)S(1)} %pad_maximum_fusion.far0), channel_id=1, source_target_pairs={{0,1},{1,2},{2,3},{3,0},{4,5},{5,6},{6,7},{7,4},{8,9},{9,10},{10,1... | collective-permute-start | bytes 1769480 | tf_op jit(solution)/shard_map/ppermute | solution.py:24
  48.5 4.1 %shard_map.68 = (bf16[2,256,1536]{2,1,0:T(8,128)(2,1)}, bf16[256,1536]{1,0:T(8,128)(2,1)}, f32[256,384]{1,0:T(8,128)S(1)}, f32[256,192]{1,0:T(8,128)S(1)}, bf16[...) custom-call(s32[5]{0:T(128)S(1)} %stack.38.meta, ...), custom_call_target="tpu_custom_call" | custom-call | flops 1 | bytes 1 | tf_op jit(solution)/shard_map/pallas_call | solution.py:55
  58.1 10.2 %collective-permute-done.15.far2 = bf16[4,4,48,384]{3,2,1,0:T(8,128)(2,1)S(1)} collective-permute-done((bf16[4,4,48,384]{3,2,1,0:T(8,128)(2,1)S(1)}, bf16[4,4,48,384]{3,2,1,0:T(8,128)(2,1)S(1)}, u32[]{:S(2)}, u32[]{:S(2)}) %collective-permute-start.15) | collective-permute-done | bytes 589856 | tf_op jit(solution)/shard_map/ppermute | solution.py:24
  69.6 3.4 %collective-permute-start.19 = (bf16[768,256]{1,0:T(8,128)(2,1)S(1)}, bf16[768,256]{1,0:T(8,128)(2,1)S(1)}, u32[]{:S(2)}, u32[]{:S(2)}) collective-permute-start(bf16[768,256]{1,0:T(8,128)(2,1)S(1)} %get-tuple-element.139), channel_id=1, source_target_pairs={{0,32},{1,33},{2,34},{3,35},{4,36},{5,37},{6,38},{7,39},{8,40},{9,... | collective-permute-start | bytes 1179656 | tf_op jit(solution)/shard_map/ppermute | solution.py:24
  73.9 5.1 %shard_map.70 = (bf16[256,384]{1,0:T(8,128)(2,1)S(1)}, bf16[384,256]{1,0:T(8,128)(2,1)S(1)}, bf16[3,16,48,384]{3,2,1,0:T(8,128)(2,1)}, bf16[768,256]{1,0:T(8,128...) custom-call(s32[5]{0:T(128)S(1)} %stack.38.meta, ...), custom_call_target="tpu_custom_call" | custom-call | flops 1 | bytes 1 | tf_op jit(solution)/shard_map/pallas_call | solution.py:55
  80.2 2.4 %collective-permute-done.19.x2 = bf16[768,256]{1,0:T(8,128)(2,1)S(1)} collective-permute-done((bf16[768,256]{1,0:T(8,128)(2,1)S(1)}, bf16[768,256]{1,0:T(8,128)(2,1)S(1)}, u32[]{:S(2)}, u32[]{:S(2)}) %collective-permute-start.19) | collective-permute-done | bytes 393248 | tf_op jit(solution)/shard_map/ppermute | solution.py:24
  86.0 2.3 %collective-permute-start.25 = (bf16[4,96,384]{2,1,0:T(8,128)(2,1)S(1)}, bf16[4,96,384]{2,1,0:T(8,128)(2,1)S(1)}, u32[]{:S(2)}, u32[]{:S(2)}) collective-permute-start(bf16[4,96,384]{2,1,0:T(8,128)(2,1)S(1)} %get-tuple-element.152), channel_id=1, source_target_pairs={{0,32},{1,33},{2,34},{3,35},{4,36},{5,37},{6,38},{7,39},{8,40},{9,... | collective-permute-start | bytes 884744 | tf_op jit(solution)/shard_map/ppermute | solution.py:24
  88.9 3.3 %collective-permute-done.22.m2 = bf16[768,256]{1,0:T(8,128)(2,1)S(1)} collective-permute-done((bf16[768,256]{1,0:T(8,128)(2,1)S(1)}, bf16[768,256]{1,0:T(8,128)(2,1)S(1)}, u32[]{:S(2)}, u32[]{:S(2)}) %collective-permute-start.22) | collective-permute-done | bytes 393248 | tf_op jit(solution)/shard_map/ppermute | solution.py:24
  94.2 4.4 %collective-permute-done.17.flipped = bf16[256,384]{1,0:T(8,128)(2,1)S(1)} collective-permute-done((bf16[256,384]{1,0:T(8,128)(2,1)S(1)}, bf16[256,384]{1,0:T(8,128)(2,1)S(1)}, u32[]{:S(2)}, u32[]{:S(2)}) %collective-permute-start.17) | collective-permute-done | bytes 196640 | tf_op jit(solution)/shard_map/ppermute | solution.py:24
  101.0 2.7 %collective-permute-start.29 = (bf16[384,384]{1,0:T(8,128)(2,1)S(1)}, bf16[384,384]{1,0:T(8,128)(2,1)S(1)}, u32[]{:S(2)}, u32[]{:S(2)}) collective-permute-start(bf16[384,384]{1,0:T(8,128)(2,1)S(1)} %get-tuple-element.162), channel_id=1, source_target_pairs={{0,3},{1,0},{2,1},{3,2},{4,7},{5,4},{6,5},{7,6},{8,11},{9,8},{10,9... | collective-permute-start | bytes 884744 | tf_op jit(solution)/shard_map/ppermute | solution.py:24
  105.0 5.3 %collective-permute-done.30.hopped = bf16[256,384]{1,0:T(8,128)(2,1)S(1)} collective-permute-done((bf16[256,384]{1,0:T(8,128)(2,1)S(1)}, bf16[256,384]{1,0:T(8,128)(2,1)S(1)}, u32[]{:S(2)}, u32[]{:S(2)}) %collective-permute-start.30) | collective-permute-done | bytes 196640 | tf_op jit(solution)/shard_map/ppermute | solution.py:24
  113.2 2.3 %collective-permute-start.31 = (f32[128,1536]{1,0:T(8,128)S(1)}, f32[128,1536]{1,0:T(8,128)S(1)}, u32[]{:S(2)}, u32[]{:S(2)}) collective-permute-start(f32[128,1536]{1,0:T(8,128)S(1)} %get-tuple-element.172), channel_id=1, source_target_pairs={{0,64},{1,65},{2,66},{3,67},{4,68},{5,69},{6,70},{7,71},{8,72},{9,... | collective-permute-start | bytes 2359304 | tf_op jit(solution)/shard_map/ppermute | solution.py:24
  115.5 4.5 %collective-permute-start.33 = (bf16[96,384]{1,0:T(8,128)(2,1)S(1)}, bf16[96,384]{1,0:T(8,128)(2,1)S(1)}, u32[]{:S(2)}, u32[]{:S(2)}) collective-permute-start(bf16[96,384]{1,0:T(8,128)(2,1)S(1)} %get-tuple-element.175), channel_id=1, source_target_pairs={{0,8},{1,9},{2,10},{3,11},{4,12},{5,13},{6,14},{7,15},{8,0},{9,1},... | collective-permute-start | bytes 221192 | tf_op jit(solution)/shard_map/ppermute | solution.py:24
  120.0 2.2 %collective-permute-done.32.got1 = bf16[96,384]{1,0:T(8,128)(2,1)S(1)} collective-permute-done((bf16[96,384]{1,0:T(8,128)(2,1)S(1)}, bf16[96,384]{1,0:T(8,128)(2,1)S(1)}, u32[]{:S(2)}, u32[]{:S(2)}) %collective-permute-start.32) | collective-permute-done | bytes 73760 | tf_op jit(solution)/shard_map/ppermute | solution.py:24
  122.2 3.4 %collective-permute-done.33.got2 = bf16[96,384]{1,0:T(8,128)(2,1)S(1)} collective-permute-done((bf16[96,384]{1,0:T(8,128)(2,1)S(1)}, bf16[96,384]{1,0:T(8,128)(2,1)S(1)}, u32[]{:S(2)}, u32[]{:S(2)}) %collective-permute-start.33) | collective-permute-done | bytes 73760 | tf_op jit(solution)/shard_map/ppermute | solution.py:24
  127.1 2.8 %collective-permute-start.37 = (f32[18,384]{1,0:T(8,128)S(1)}, f32[18,384]{1,0:T(8,128)S(1)}, u32[]{:S(2)}, u32[]{:S(2)}) collective-permute-start(f32[18,384]{1,0:T(8,128)S(1)} %get-tuple-element.182), channel_id=1, source_target_pairs={{0,192},{1,193},{2,194},{3,195},{4,196},{5,197},{6,198},{7,199},{8... | collective-permute-start | bytes 82952 | tf_op jit(solution)/shard_map/ppermute | solution.py:24
  129.9 2.6 %collective-permute-start.36 = (f32[30,384]{1,0:T(8,128)S(1)}, f32[30,384]{1,0:T(8,128)S(1)}, u32[]{:S(2)}, u32[]{:S(2)}) collective-permute-start(f32[30,384]{1,0:T(8,128)S(1)} %get-tuple-element.180), channel_id=1, source_target_pairs={{0,128},{1,129},{2,130},{3,131},{4,132},{5,133},{6,134},{7,135},{8... | collective-permute-start | bytes 138248 | tf_op jit(solution)/shard_map/ppermute | solution.py:24
  134.4 2.3 %collective-permute-done.36.from_z = f32[30,384]{1,0:T(8,128)S(1)} collective-permute-done((f32[30,384]{1,0:T(8,128)S(1)}, f32[30,384]{1,0:T(8,128)S(1)}, u32[]{:S(2)}, u32[]{:S(2)}) %collective-permute-start.36) | collective-permute-done | bytes 46112 | tf_op jit(solution)/shard_map/ppermute | solution.py:24
  (103 shorter events, 44.0 us)
Async XLA Ops:
  1.8 19.6 %collective-permute-start = (bf16[3,48,768]{2,1,0:T(8,128)(2,1)S(1)}, bf16[3,48,768]{2,1,0:T(8,128)(2,1)S(1)}, u32[]{:S(2)}, u32[]{:S(2)}) collective-permute-start(bf16[3,48,768]{2,1,0:T(8,128)(2,1)S(1)} %constant_dynamic-slice_fusion.4), channel_id=1, source_target_pairs={{0,140},{1,141},{2,142},{3,143},{4,136},{5,137},{6,138},{7,139},{8... | collective-permute-start | bytes 663560 | tf_op jit(solution)/shard_map/ppermute | solution.py:24
  2.5 18.9 %collective-permute-start.2 = (bf16[128,1536]{1,0:T(8,128)(2,1)}, bf16[128,1536]{1,0:T(8,128)(2,1)S(1)}, u32[]{:S(2)}, u32[]{:S(2)}) collective-permute-start(bf16[128,1536]{1,0:T(8,128)(2,1)} %bitcast.20), channel_id=1, source_target_pairs={{0,64},{1,65},{2,66},{3,67},{4,68},{5,69},{6,70},{7,71},{8,72},{9,... | collective-permute-start | bytes 1179656 | tf_op jit(solution)/shard_map/ppermute | solution.py:24
  11.1 10.2 %collective-permute-start.3 = (bf16[128,1536]{1,0:T(8,128)(2,1)}, bf16[128,1536]{1,0:T(8,128)(2,1)S(1)}, u32[]{:S(2)}, u32[]{:S(2)}) collective-permute-start(bf16[128,1536]{1,0:T(8,128)(2,1)} %bitcast.18), channel_id=1, source_target_pairs={{0,64},{1,65},{2,66},{3,67},{4,68},{5,69},{6,70},{7,71},{8,72},{9,... | collective-permute-start | bytes 1179656 | tf_op jit(solution)/shard_map/ppermute | solution.py:24
  24.1 13.4 %collective-permute-start.6 = (bf16[80,1536]{1,0:T(8,128)(2,1)S(1)}, bf16[80,1536]{1,0:T(8,128)(2,1)S(1)}, u32[]{:S(2)}, u32[]{:S(2)}) collective-permute-start(bf16[80,1536]{1,0:T(8,128)(2,1)S(1)} %slice.11), channel_id=1, source_target_pairs={{0,8},{1,9},{2,10},{3,11},{4,12},{5,13},{6,14},{7,15},{8,0},{9,1},... | collective-permute-start | bytes 737288 | tf_op jit(solution)/shard_map/ppermute | solution.py:24
  26.2 11.3 %collective-permute-start.9 = (bf16[4,48,384]{2,1,0:T(8,128)(2,1)S(1)}, bf16[4,48,384]{2,1,0:T(8,128)(2,1)S(1)}, u32[]{:S(2)}, u32[]{:S(2)}) collective-permute-start(bf16[4,48,384]{2,1,0:T(8,128)(2,1)S(1)} %pad_maximum_fusion.2), channel_id=1, source_target_pairs={{0,16},{1,17},{2,18},{3,19},{4,20},{5,21},{6,22},{7,23},{8,24},{9,... | collective-permute-start | bytes 442376 | tf_op jit(solution)/shard_map/ppermute | solution.py:24
  27.6 9.9 %collective-permute-start.8 = (bf16[4,48,384]{2,1,0:T(8,128)(2,1)S(1)}, bf16[4,48,384]{2,1,0:T(8,128)(2,1)S(1)}, u32[]{:S(2)}, u32[]{:S(2)}) collective-permute-start(bf16[4,48,384]{2,1,0:T(8,128)(2,1)S(1)} %pad_maximum_fusion.2), channel_id=1, source_target_pairs={{0,32},{1,33},{2,34},{3,35},{4,36},{5,37},{6,38},{7,39},{8,40},{9,... | collective-permute-start | bytes 442376 | tf_op jit(solution)/shard_map/ppermute | solution.py:24
  37.5 10.0 %collective-permute-start.12 = (bf16[3,384,384]{2,1,0:T(8,128)(2,1)S(1)}, bf16[3,384,384]{2,1,0:T(8,128)(2,1)S(1)}, u32[]{:S(2)}, u32[]{:S(2)}) collective-permute-start(bf16[3,384,384]{2,1,0:T(8,128)(2,1)S(1)} %get-tuple-element.105), channel_id=1, source_target_pairs={{0,64},{1,65},{2,66},{3,67},{4,68},{5,69},{6,70},{7,71},{8,72},{9,... | collective-permute-start | bytes 2654216 | tf_op jit(solution)/shard_map/ppermute | solution.py:24
  38.2 14.4 %collective-permute-start.10 = (bf16[128,1536]{1,0:T(8,128)(2,1)S(1)}, bf16[128,1536]{1,0:T(8,128)(2,1)S(1)}, u32[]{:S(2)}, u32[]{:S(2)}) collective-permute-start(bf16[128,1536]{1,0:T(8,128)(2,1)S(1)} %pad_maximum_fusion.1.x0), channel_id=1, source_target_pairs={{0,16},{1,17},{2,18},{3,19},{4,20},{5,21},{6,22},{7,23},{16,32},{1... | collective-permute-start | bytes 1179656 | tf_op jit(solution)/shard_map/ppermute | solution.py:24
  41.5 16.7 %collective-permute-start.16 = (bf16[4,4,48,384]{3,2,1,0:T(8,128)(2,1)S(1)}, bf16[4,4,48,384]{3,2,1,0:T(8,128)(2,1)S(1)}, u32[]{:S(2)}, u32[]{:S(2)}) collective-permute-start(bf16[4,4,48,384]{3,2,1,0:T(8,128)(2,1)S(1)} %pad_maximum_fusion.far0), channel_id=1, source_target_pairs={{0,1},{1,2},{2,3},{3,0},{4,5},{5,6},{6,7},{7,4},{8,9},{9,10},{10,1... | collective-permute-start | bytes 1769480 | tf_op jit(solution)/shard_map/ppermute | solution.py:24
  44.1 24.2 %collective-permute-start.15 = (bf16[4,4,48,384]{3,2,1,0:T(8,128)(2,1)S(1)}, bf16[4,4,48,384]{3,2,1,0:T(8,128)(2,1)S(1)}, u32[]{:S(2)}, u32[]{:S(2)}) collective-permute-start(bf16[4,4,48,384]{3,2,1,0:T(8,128)(2,1)S(1)} %pad_maximum_fusion.far0), channel_id=1, source_target_pairs={{0,2},{1,3},{2,0},{3,1},{4,6},{5,7},{6,4},{7,5},{8,10},{9,11},{10,... | collective-permute-start | bytes 1769480 | tf_op jit(solution)/shard_map/ppermute | solution.py:24
  45.4 22.9 %collective-permute-start.14 = (bf16[4,4,48,384]{3,2,1,0:T(8,128)(2,1)S(1)}, bf16[4,4,48,384]{3,2,1,0:T(8,128)(2,1)S(1)}, u32[]{:S(2)}, u32[]{:S(2)}) collective-permute-start(bf16[4,4,48,384]{3,2,1,0:T(8,128)(2,1)S(1)} %pad_maximum_fusion.far0), channel_id=1, source_target_pairs={{0,3},{1,0},{2,1},{3,2},{4,7},{5,4},{6,5},{7,6},{8,11},{9,8},{10,9... | collective-permute-start | bytes 1769480 | tf_op jit(solution)/shard_map/ppermute | solution.py:24
  68.3 10.7 %collective-permute-start.18 = (bf16[768,256]{1,0:T(8,128)(2,1)S(1)}, bf16[768,256]{1,0:T(8,128)(2,1)S(1)}, u32[]{:S(2)}, u32[]{:S(2)}) collective-permute-start(bf16[768,256]{1,0:T(8,128)(2,1)S(1)} %get-tuple-element.136), channel_id=1, source_target_pairs={{0,16},{1,17},{2,18},{3,19},{4,20},{5,21},{6,22},{7,23},{8,24},{9,... | collective-permute-start | bytes 1179656 | tf_op jit(solution)/shard_map/ppermute | solution.py:24
  69.6 13.1 %collective-permute-start.19 = (bf16[768,256]{1,0:T(8,128)(2,1)S(1)}, bf16[768,256]{1,0:T(8,128)(2,1)S(1)}, u32[]{:S(2)}, u32[]{:S(2)}) collective-permute-start(bf16[768,256]{1,0:T(8,128)(2,1)S(1)} %get-tuple-element.139), channel_id=1, source_target_pairs={{0,32},{1,33},{2,34},{3,35},{4,36},{5,37},{6,38},{7,39},{8,40},{9,... | collective-permute-start | bytes 1179656 | tf_op jit(solution)/shard_map/ppermute | solution.py:24
  73.0 9.7 %collective-permute-start.20 = (bf16[768,256]{1,0:T(8,128)(2,1)S(1)}, bf16[768,256]{1,0:T(8,128)(2,1)S(1)}, u32[]{:S(2)}, u32[]{:S(2)}) collective-permute-start(bf16[768,256]{1,0:T(8,128)(2,1)S(1)} %get-tuple-element.142), channel_id=1, source_target_pairs={{0,48},{1,49},{2,50},{3,51},{4,52},{5,53},{6,54},{7,55},{8,56},{9,... | collective-permute-start | bytes 1179656 | tf_op jit(solution)/shard_map/ppermute | solution.py:24
  82.7 9.6 %collective-permute-start.22 = (bf16[768,256]{1,0:T(8,128)(2,1)S(1)}, bf16[768,256]{1,0:T(8,128)(2,1)S(1)}, u32[]{:S(2)}, u32[]{:S(2)}) collective-permute-start(bf16[768,256]{1,0:T(8,128)(2,1)S(1)} %get-tuple-element.147), channel_id=1, source_target_pairs={{0,32},{1,33},{2,34},{3,35},{4,36},{5,37},{6,38},{7,39},{8,40},{9,... | collective-permute-start | bytes 1179656 | tf_op jit(solution)/shard_map/ppermute | solution.py:24
  82.7 9.5 %collective-permute-start.23 = (bf16[768,256]{1,0:T(8,128)(2,1)S(1)}, bf16[768,256]{1,0:T(8,128)(2,1)S(1)}, u32[]{:S(2)}, u32[]{:S(2)}) collective-permute-start(bf16[768,256]{1,0:T(8,128)(2,1)S(1)} %get-tuple-element.148), channel_id=1, source_target_pairs={{0,48},{1,49},{2,50},{3,51},{4,52},{5,53},{6,54},{7,55},{8,56},{9,... | collective-permute-start | bytes 1179656 | tf_op jit(solution)/shard_map/ppermute | solution.py:24
  85.9 12.6 %collective-permute-start.24 = (bf16[4,96,384]{2,1,0:T(8,128)(2,1)S(1)}, bf16[4,96,384]{2,1,0:T(8,128)(2,1)S(1)}, u32[]{:S(2)}, u32[]{:S(2)}) collective-permute-start(bf16[4,96,384]{2,1,0:T(8,128)(2,1)S(1)} %get-tuple-element.151), channel_id=1, source_target_pairs={{0,16},{1,17},{2,18},{3,19},{4,20},{5,21},{6,22},{7,23},{8,24},{9,... | collective-permute-start | bytes 884744 | tf_op jit(solution)/shard_map/ppermute | solution.py:24
  86.0 12.5 %collective-permute-start.25 = (bf16[4,96,384]{2,1,0:T(8,128)(2,1)S(1)}, bf16[4,96,384]{2,1,0:T(8,128)(2,1)S(1)}, u32[]{:S(2)}, u32[]{:S(2)}) collective-permute-start(bf16[4,96,384]{2,1,0:T(8,128)(2,1)S(1)} %get-tuple-element.152), channel_id=1, source_target_pairs={{0,32},{1,33},{2,34},{3,35},{4,36},{5,37},{6,38},{7,39},{8,40},{9,... | collective-permute-start | bytes 884744 | tf_op jit(solution)/shard_map/ppermute | solution.py:24
  88.3 10.2 %collective-permute-start.26 = (bf16[4,96,384]{2,1,0:T(8,128)(2,1)S(1)}, bf16[4,96,384]{2,1,0:T(8,128)(2,1)S(1)}, u32[]{:S(2)}, u32[]{:S(2)}) collective-permute-start(bf16[4,96,384]{2,1,0:T(8,128)(2,1)S(1)} %get-tuple-element.153), channel_id=1, source_target_pairs={{0,48},{1,49},{2,50},{3,51},{4,52},{5,53},{6,54},{7,55},{8,56},{9,... | collective-permute-start | bytes 884744 | tf_op jit(solution)/shard_map/ppermute | solution.py:24
  99.3 11.0 %collective-permute-start.27 = (bf16[384,384]{1,0:T(8,128)(2,1)S(1)}, bf16[384,384]{1,0:T(8,128)(2,1)S(1)}, u32[]{:S(2)}, u32[]{:S(2)}) collective-permute-start(bf16[384,384]{1,0:T(8,128)(2,1)S(1)} %get-tuple-element.160), channel_id=1, source_target_pairs={{0,1},{1,2},{2,3},{3,0},{4,5},{5,6},{6,7},{7,4},{8,9},{9,10},{10,1... | collective-permute-start | bytes 884744 | tf_op jit(solution)/shard_map/ppermute | solution.py:24
  101.0 9.3 %collective-permute-start.28 = (bf16[384,384]{1,0:T(8,128)(2,1)S(1)}, bf16[384,384]{1,0:T(8,128)(2,1)S(1)}, u32[]{:S(2)}, u32[]{:S(2)}) collective-permute-start(bf16[384,384]{1,0:T(8,128)(2,1)S(1)} %get-tuple-element.161), channel_id=1, source_target_pairs={{0,2},{1,3},{2,0},{3,1},{4,6},{5,7},{6,4},{7,5},{8,10},{9,11},{10,... | collective-permute-start | bytes 884744 | tf_op jit(solution)/shard_map/ppermute | solution.py:24
  101.0 9.3 %collective-permute-start.29 = (bf16[384,384]{1,0:T(8,128)(2,1)S(1)}, bf16[384,384]{1,0:T(8,128)(2,1)S(1)}, u32[]{:S(2)}, u32[]{:S(2)}) collective-permute-start(bf16[384,384]{1,0:T(8,128)(2,1)S(1)} %get-tuple-element.162), channel_id=1, source_target_pairs={{0,3},{1,0},{2,1},{3,2},{4,7},{5,4},{6,5},{7,6},{8,11},{9,8},{10,9... | collective-permute-start | bytes 884744 | tf_op jit(solution)/shard_map/ppermute | solution.py:24
  113.2 19.3 %collective-permute-start.31 = (f32[128,1536]{1,0:T(8,128)S(1)}, f32[128,1536]{1,0:T(8,128)S(1)}, u32[]{:S(2)}, u32[]{:S(2)}) collective-permute-start(f32[128,1536]{1,0:T(8,128)S(1)} %get-tuple-element.172), channel_id=1, source_target_pairs={{0,64},{1,65},{2,66},{3,67},{4,68},{5,69},{6,70},{7,71},{8,72},{9,... | collective-permute-start | bytes 2359304 | tf_op jit(solution)/shard_map/ppermute | solution.py:24
  115.5 10.2 %collective-permute-start.33 = (bf16[96,384]{1,0:T(8,128)(2,1)S(1)}, bf16[96,384]{1,0:T(8,128)(2,1)S(1)}, u32[]{:S(2)}, u32[]{:S(2)}) collective-permute-start(bf16[96,384]{1,0:T(8,128)(2,1)S(1)} %get-tuple-element.175), channel_id=1, source_target_pairs={{0,8},{1,9},{2,10},{3,11},{4,12},{5,13},{6,14},{7,15},{8,0},{9,1},... | collective-permute-start | bytes 221192 | tf_op jit(solution)/shard_map/ppermute | solution.py:24
  (26 other events, 228.2 us)

commit v6 on v5

--- a/solution.py
+++ b/solution.py
@@ -202,33 +202,31 @@
         out[12 * piece:] = point.astype(out.dtype)
 
 
-def slice_kernel(meta, own, got1, got2, got3, kept, send1, send2, send3):
+def slice_kernel(meta, own, got1, got2, got3, out):
     total = own[...] + got1[...].astype(F32) + got2[...].astype(F32) + got3[...].astype(F32)
     piece = total.shape[0] // 16
     row, thin = piece // 4, piece // 8
-    for t, out in enumerate((kept, send1, send2, send3)):
-        parts = []
+    for t in range(4):
         for u in range(2):
             first = [(2 * g + u) * 2 * piece + t * row for g in range(3)]
-            parts += [total[at:at + row] for at in first]
+            parts = [total[at:at + row] for at in first]
             for p in range(4):
                 at = (12 + p) * piece + u * piece // 2 + t * thin
                 parts.append(total[at:at + thin])
             parts += [total[at + piece:at + piece + row] for at in first]
-        out[...] = jnp.concatenate(parts, 0).astype(out.dtype)
-
-
-def split_sum_kernel(meta, own, got1, got2, got3, kept, to_z, to_core, to_both):
-    total = own[...] + got1[...].astype(F32) + got2[...].astype(F32) + got3[...].astype(F32)
-    half, size = total.shape[0] // 2, kept.shape[0]
+            z = lax.rem(meta[1] + u, 2) * 4 + lax.rem(meta[5] + t, 4)
+            out[z] = jnp.concatenate(parts, 0).astype(out.dtype)
+
+
+def split_sum_kernel(meta, parts, kept, to_core):
+    total = sum(parts[z].astype(F32) for z in range(parts.shape[0]))
+    size = kept.shape[0]
     kept[...] = total[:size]
-    to_core[...] = total[size:half]
-    to_z[...] = total[half:half + size]
-    to_both[...] = total[half + size:]
-
-
-def output_kernel(meta, kept, from_z, from_core, from_both, conv, point):
-    here, there = kept[...] + from_z[...], from_core[...] + from_both[...]
+    to_core[...] = total[size:]
+
+
+def output_kernel(meta, kept, from_core, conv, point):
+    here, there = kept[...], from_core[...]
     taps, row = conv.shape[:2]
     width = here.shape[1]
     half = width // 2
@@ -265,7 +263,7 @@
     zh, core = dp // 2, dp % 2
     xi, zl, yi = seq // 16, seq // 4 % 4, seq % 4
     a, b = jnp.where(core == 0, xi, yi), jnp.where(core == 0, yi, xi)
-    meta = jnp.stack([core, zh, a, b, jnp.where(zl < 2, 2, 0)]).astype(jnp.int32)
+    meta = jnp.stack([core, zh, a, b, jnp.where(zl < 2, 2, 0), zl]).astype(jnp.int32)
 
     def columns(value, c):
         return jnp.concatenate(
@@ -300,24 +298,27 @@
     holders = [d for d in range(256) if coords(d)[3] == coords(d)[0] // 2]
     conv_piece = send(conv_piece, mirror, holders)
     point_piece = send(point_piece, mirror)
-    first = rows * 3 // 8
-    flipped = flip(x[:first])
+    first, tail = flip(x[:rows // 2]), x[rows // 2:]
     x_other = send(x, partner)
     og_other = send(og, partner)
-    conv_piece, point_piece, x_late, x_other, og_other, flipped, conv_weight = lax.optimization_barrier(
-        (conv_piece, point_piece, x, x_other, og_other, flipped, conv_weight)
+    conv_piece, point_piece, tail, x_other, og_other, first, conv_weight = lax.optimization_barrier(
+        (conv_piece, point_piece, tail, x_other, og_other, first, conv_weight)
     )
     mine, theirs = run(split_kernel, meta, [conv_weight], [shape((3, Cq, Hh), BF16)] * 2)
     handed = send(columns(conv_piece, 1 - core), partner, holders)
     conv_piece = jnp.where(core == xi // 2, columns(conv_piece, core), handed)
     far = jnp.concatenate([conv_piece, point_piece[None]])
-    flipped = jnp.concatenate([flipped, flip(x_late[first:])])
+    tail, hopped = flip(tail), hop(first)
     fars = [send_a(far, -k) for k in (1, 2, 3)]
-    far, flipped, mine, theirs, *fars = lax.optimization_barrier((far, flipped, mine, theirs, *fars))
+    far, first, tail, hopped, mine, theirs, *fars = lax.optimization_barrier(
+        (far, first, tail, hopped, mine, theirs, *fars)
+    )
+    flipped = jnp.concatenate([first, tail])
     got = send(theirs, partner)
-    hopped = hop(flipped)
+    hopped = jnp.concatenate([hopped, hop(tail)])
     far = jnp.stack([far, *fars])
     fars = [far] + [send_b(far, -k) for k in (1, 2, 3)]
+    flipped, got = lax.optimization_barrier((flipped, got))
     flipped_other = send(flipped, partner)
     spread = order(Cq, Cq // 64, 1)
     taps, ogs, near, arriving, *early = run(
@@ -345,42 +346,32 @@
     messages = [messages[0]] + [send_a(part, k + 1) for k, part in enumerate(messages[1:])]
     block = (4, Hh // 4, Hh)
     p_own, *sends = run(point_kernel, meta, [ogs, hidden_t], [shape(block, F32)] + [shape(block, BF16)] * 3)
+    hg_flipped, *sends = lax.optimization_barrier((flip(hg), *sends))
     p_all = [p_own] + [send_a(part, k + 1) for k, part in enumerate(sends)]
-    hg_flipped = flip(hg)
     conv, = run(gradient_kernel, meta, [*early, *messages], [shape((3 * Cq, Hh), F32)])
-    hg_flipped, conv, *p_all = lax.optimization_barrier((hg_flipped, conv, *p_all))
-    hg_hopped = hop(hg_flipped)
+    hg_late, conv = lax.optimization_barrier((hg_flipped, conv))
+    hg_hopped = hop(hg_late)
     n = 12 * (Cq // 16)
     big = (n + Hh // 4, Hh)
     total, *sends = run(pack_kernel, meta, [conv, *p_all], [shape(big, F32)] + [shape(big, BF16)] * 3)
     got_b = [send_b(part, k + 1) for k, part in enumerate(sends)]
-    *got_b, hg_hopped = lax.optimization_barrier((*got_b, hg_hopped))
-    small = (big[0] // 4, Hh)
-    last, *sends = run(
-        slice_kernel, meta, [total, *got_b],
-        [shape(small, F32)] + [shape(small, BF16)] * 3,
-    )
-    hg_late, last = lax.optimization_barrier((hg, last))
+    half = big[0] // 8
+    by_z, = run(slice_kernel, meta, [total, *got_b], [shape((8, half, Hh), BF16)])
+    hg_late, by_z = lax.optimization_barrier((hg, by_z))
     mine_rows, other_rows = run(
         input_kernel, meta, [hg_late, hg_flipped, hg_hopped, mine, got, wfar.reshape(3, 2 * Cq, Hh)],
         [shape((rows, C), F32)] * 2,
     )
     in_grad = (og.astype(F32) + mine_rows + send(other_rows, partner)).astype(BF16)
-    got_z = [
-        send(part, lambda x, y, z, c: (x, y, z // 4 * 4 + (z + t + 1) % 4, c)) for t, part in enumerate(sends)
-    ]
+    rings = [[index_of(x, y, z, c) for z in range(8)] for x in range(4) for y in range(4) for c in range(2)]
+    by_z = lax.all_to_all(by_z, ("dp", "seq"), 0, 0, axis_index_groups=rings)
     conv_rows = 3 * (Cq // 64)
-    point_rows = small[0] // 2 - 2 * conv_rows
-    halves = (conv_rows + point_rows, Hh), (conv_rows, Hh)
-    kept, to_z, to_core, to_both = run(
-        split_sum_kernel, meta, [last, *got_z], [shape(halves[k], F32) for k in (0, 0, 1, 1)]
-    )
-    from_z = send(to_z, lambda x, y, z, c: (x, y, z + 4, c))
-    from_both = send(to_both, lambda x, y, z, c: (x, y, z + 4, 1 - c))
+    kept, to_core = run(
+        split_sum_kernel, meta, [by_z], [shape((half - conv_rows, Hh), F32), shape((conv_rows, Hh), F32)]
+    )
     in_grad, from_core = lax.optimization_barrier((in_grad, send(to_core, partner)))
     conv_mine, point_mine = run(
-        output_kernel, meta, [kept, from_z, from_core, from_both],
-        [shape((3, Cq // 64, H), F32), shape((Hq // 64, C), F32)],
+        output_kernel, meta, [kept, from_core], [shape((3, Cq // 64, H), F32), shape((Hq // 64, C), F32)]
     )
     return in_grad[None], conv_mine, point_mine
 

time: 139 us -> 135 us (0.971)
  waiting for transfers between devices: 48.5 us -> 28.6 us
  blocking collectives: 0 us -> 15.7 us
  other arithmetic: 1.53 us -> 3.38 us
    ppermute x38 -> x34, waiting for transfers between devices: 48.5 us -> 28.6 us  [send(): return lax.ppermute(value, ('dp', 'seq'), pairs)]
    all_to_all x0 -> x1, blocking collectives: none -> 15.7 us  [local(): by_z = lax.all_to_all(by_z, ('dp', 'seq'), 0, 0, axis_index_groups=rings)]
    concatenate x1 -> x2, other arithmetic: 0.03 us -> 1.91 us  [the longest x1 0.96 us: local(): flipped = jnp.concatenate([first, tail])]
    ppermute x38 -> x34, starting transfers between devices: 58.8 us -> 58.5 us  [send(): return lax.ppermute(value, ('dp', 'seq'), pairs)]
  transfers between devices with their start and end apart: 38 -> 34, of which waited for: 13 -> 12; matrix products, arithmetic and copies ran while one was open for 3% -> 4% of each run, Pallas kernels for 11% -> 12%
where the time goes in v6:
time: 135 us; the launch traced here: 134 us
  starting transfers between devices  58.5 us (43%)
  waiting for transfers between devices  28.6 us (21%)
  Pallas kernels  20.1 us (15%)
  blocking collectives  15.7 us (12%)
  local copies, waits for them, and re-layouts  6.89 us (5%)
  other arithmetic  3.38 us (3%)
    ppermute x34, starting transfers between devices, send(): return lax.ppermute(value, ('dp', 'seq'), pairs)  58.5 us
    ppermute x34, waiting for transfers between devices, send(): return lax.ppermute(value, ('dp', 'seq'), pairs)  28.6 us
    pallas_call x11, Pallas kernels, run(): pl.pallas_call(kernel, out_shape=outs, in_specs=[pl.BlockSpec(memory_spac...  20.1 us
    all_to_all x1, blocking collectives, local(): by_z = lax.all_to_all(by_z, ('dp', 'seq'), 0, 0, axis_index_groups=rings)  15.7 us
    unnamed x24, local copies, waits for them, and re-layouts  3.06 us
  transfers between devices with their start and end apart: 34, of which 12 were waited for; matrix products, arithmetic and copies ran while one was open for 4% of the time, Pallas kernels for 12%

profile of v6, /device:TPU:1, one launch (start us, length us, event | category | flops | bytes accessed | tf_op | source)
XLA Modules:
  0.0 134.2 jit_solution(15785004222571480213)
XLA Ops:
  2.5 8.7 %collective-permute-start.2 = (bf16[128,1536]{1,0:T(8,128)(2,1)}, bf16[128,1536]{1,0:T(8,128)(2,1)S(1)}, u32[]{:S(2)}, u32[]{:S(2)}) collective-permute-start(bf16[128,1536]{1,0:T(8,128)(2,1)} %bitcast.23), channel_id=1, source_target_pairs={{0,64},{1,65},{2,66},{3,67},{4,68},{5,69},{6,70},{7,71},{8,72},{9,... | collective-permute-start | bytes 1179656 | tf_op jit(solution)/shard_map/ppermute | solution.py:24
  13.0 2.1 %collective-permute-start.4 = (bf16[64,1536]{1,0:T(8,128)(2,1)}, bf16[64,1536]{1,0:T(8,128)(2,1)S(1)}, u32[]{:S(2)}, u32[]{:S(2)}) collective-permute-start(bf16[64,1536]{1,0:T(8,128)(2,1)} %get-tuple-element.173), channel_id=1, source_target_pairs={{0,8},{1,9},{2,10},{3,11},{4,12},{5,13},{6,14},{7,15},{8,0},{9,1},... | collective-permute-start | bytes 589832 | tf_op jit(solution)/shard_map/ppermute | solution.py:24
  15.8 4.2 %collective-permute-done.1 = bf16[48,384]{1,0:T(8,128)(2,1)S(1)} collective-permute-done((bf16[48,384]{1,0:T(8,128)(2,1)S(1)}, bf16[48,384]{1,0:T(8,128)(2,1)S(1)}, u32[]{:S(2)}, u32[]{:S(2)}) %collective-permute-start.1) | collective-permute-done | bytes 36896 | tf_op jit(solution)/shard_map/ppermute | solution.py:24
  20.0 4.4 %collective-permute-done.4 = bf16[64,1536]{1,0:T(8,128)(2,1)S(1)} collective-permute-done((bf16[64,1536]{1,0:T(8,128)(2,1)}, bf16[64,1536]{1,0:T(8,128)(2,1)S(1)}, u32[]{:S(2)}, u32[]{:S(2)}) %collective-permute-start.4) | collective-permute-done | bytes 196640 | tf_op jit(solution)/shard_map/ppermute | solution.py:24
  26.1 3.8 %collective-permute-start.7 = (bf16[64,1536]{1,0:T(8,128)(2,1)S(1)}, bf16[64,1536]{1,0:T(8,128)(2,1)}, u32[]{:S(2)}, u32[]{:S(2)}) collective-permute-start(bf16[64,1536]{1,0:T(8,128)(2,1)S(1)} %collective-permute-done.4), channel_id=1, source_target_pairs={{0,16},{1,17},{2,18},{3,19},{4,20},{5,21},{6,22},{7,23},{16,32},{1... | collective-permute-start | bytes 589832 | tf_op jit(solution)/shard_map/ppermute | solution.py:24
  31.4 2.6 %collective-permute-start.9 = (bf16[4,48,384]{2,1,0:T(8,128)(2,1)S(1)}, bf16[4,48,384]{2,1,0:T(8,128)(2,1)S(1)}, u32[]{:S(2)}, u32[]{:S(2)}) collective-permute-start(bf16[4,48,384]{2,1,0:T(8,128)(2,1)S(1)} %pad_maximum_fusion.3), channel_id=1, source_target_pairs={{0,32},{1,33},{2,34},{3,35},{4,36},{5,37},{6,38},{7,39},{8,40},{9,... | collective-permute-start | bytes 442376 | tf_op jit(solution)/shard_map/ppermute | solution.py:24
  38.1 3.7 %collective-permute-start.12 = (bf16[3,384,384]{2,1,0:T(8,128)(2,1)S(1)}, bf16[3,384,384]{2,1,0:T(8,128)(2,1)S(1)}, u32[]{:S(2)}, u32[]{:S(2)}) collective-permute-start(bf16[3,384,384]{2,1,0:T(8,128)(2,1)S(1)} %get-tuple-element.98), channel_id=1, source_target_pairs={{0,64},{1,65},{2,66},{3,67},{4,68},{5,69},{6,70},{7,71},{8,72},{9,... | collective-permute-start | bytes 2654216 | tf_op jit(solution)/shard_map/ppermute | solution.py:24
  45.7 2.0 %collective-permute-start.16 = (bf16[4,4,48,384]{3,2,1,0:T(8,128)(2,1)S(1)}, bf16[4,4,48,384]{3,2,1,0:T(8,128)(2,1)S(1)}, u32[]{:S(2)}, u32[]{:S(2)}) collective-permute-start(bf16[4,4,48,384]{3,2,1,0:T(8,128)(2,1)S(1)} %pad_maximum_fusion.far0), channel_id=1, source_target_pairs={{0,2},{1,3},{2,0},{3,1},{4,6},{5,7},{6,4},{7,5},{8,10},{9,11},{10,... | collective-permute-start | bytes 1769480 | tf_op jit(solution)/shard_map/ppermute | solution.py:24
  47.7 2.0 %collective-permute-start.15 = (bf16[4,4,48,384]{3,2,1,0:T(8,128)(2,1)S(1)}, bf16[4,4,48,384]{3,2,1,0:T(8,128)(2,1)S(1)}, u32[]{:S(2)}, u32[]{:S(2)}) collective-permute-start(bf16[4,4,48,384]{3,2,1,0:T(8,128)(2,1)S(1)} %pad_maximum_fusion.far0), channel_id=1, source_target_pairs={{0,3},{1,0},{2,1},{3,2},{4,7},{5,4},{6,5},{7,6},{8,11},{9,8},{10,9... | collective-permute-start | bytes 1769480 | tf_op jit(solution)/shard_map/ppermute | solution.py:24
  50.7 4.2 %shard_map.68 = (bf16[2,256,1536]{2,1,0:T(8,128)(2,1)}, bf16[256,1536]{1,0:T(8,128)(2,1)}, f32[256,384]{1,0:T(8,128)S(1)}, f32[256,192]{1,0:T(8,128)S(1)}, bf16[...) custom-call(s32[6]{0:T(128)S(1)} %stack.42.meta, ...), custom_call_target="tpu_custom_call" | custom-call | flops 1 | bytes 1 | tf_op jit(solution)/shard_map/pallas_call | solution.py:55
  60.9 3.0 %collective-permute-done.16.far2 = bf16[4,4,48,384]{3,2,1,0:T(8,128)(2,1)S(1)} collective-permute-done((bf16[4,4,48,384]{3,2,1,0:T(8,128)(2,1)S(1)}, bf16[4,4,48,384]{3,2,1,0:T(8,128)(2,1)S(1)}, u32[]{:S(2)}, u32[]{:S(2)}) %collective-permute-start.16) | collective-permute-done | bytes 589856 | tf_op jit(solution)/shard_map/ppermute | solution.py:24
  65.3 2.7 %collective-permute-start.20 = (bf16[768,256]{1,0:T(8,128)(2,1)S(1)}, bf16[768,256]{1,0:T(8,128)(2,1)S(1)}, u32[]{:S(2)}, u32[]{:S(2)}) collective-permute-start(bf16[768,256]{1,0:T(8,128)(2,1)S(1)} %get-tuple-element.142), channel_id=1, source_target_pairs={{0,32},{1,33},{2,34},{3,35},{4,36},{5,37},{6,38},{7,39},{8,40},{9,... | collective-permute-start | bytes 1179656 | tf_op jit(solution)/shard_map/ppermute | solution.py:24
  69.2 5.1 %shard_map.70 = (bf16[256,384]{1,0:T(8,128)(2,1)S(1)}, bf16[384,256]{1,0:T(8,128)(2,1)S(1)}, bf16[3,16,48,384]{3,2,1,0:T(8,128)(2,1)}, bf16[768,256]{1,0:T(8,128...) custom-call(s32[6]{0:T(128)S(1)} %stack.42.meta, ...), custom_call_target="tpu_custom_call" | custom-call | flops 1 | bytes 1 | tf_op jit(solution)/shard_map/pallas_call | solution.py:55
  74.7 2.5 %collective-permute-done.20.x2 = bf16[768,256]{1,0:T(8,128)(2,1)S(1)} collective-permute-done((bf16[768,256]{1,0:T(8,128)(2,1)S(1)}, bf16[768,256]{1,0:T(8,128)(2,1)S(1)}, u32[]{:S(2)}, u32[]{:S(2)}) %collective-permute-start.20) | collective-permute-done | bytes 393248 | tf_op jit(solution)/shard_map/ppermute | solution.py:24
  78.1 2.0 %collective-permute-start.24 = (bf16[768,256]{1,0:T(8,128)(2,1)S(1)}, bf16[768,256]{1,0:T(8,128)(2,1)S(1)}, u32[]{:S(2)}, u32[]{:S(2)}) collective-permute-start(bf16[768,256]{1,0:T(8,128)(2,1)S(1)} %get-tuple-element.151), channel_id=1, source_target_pairs={{0,48},{1,49},{2,50},{3,51},{4,52},{5,53},{6,54},{7,55},{8,56},{9,... | collective-permute-start | bytes 1179656 | tf_op jit(solution)/shard_map/ppermute | solution.py:24
  81.2 3.5 %collective-permute-done.18.flipped = bf16[256,384]{1,0:T(8,128)(2,1)S(1)} collective-permute-done((bf16[256,384]{1,0:T(8,128)(2,1)S(1)}, bf16[256,384]{1,0:T(8,128)(2,1)S(1)}, u32[]{:S(2)}, u32[]{:S(2)}) %collective-permute-start.18) | collective-permute-done | bytes 196640 | tf_op jit(solution)/shard_map/ppermute | solution.py:24
  84.7 3.9 %collective-permute-start.25 = (bf16[4,96,384]{2,1,0:T(8,128)(2,1)S(1)}, bf16[4,96,384]{2,1,0:T(8,128)(2,1)S(1)}, u32[]{:S(2)}, u32[]{:S(2)}) collective-permute-start(bf16[4,96,384]{2,1,0:T(8,128)(2,1)S(1)} %get-tuple-element.154), channel_id=1, source_target_pairs={{0,16},{1,17},{2,18},{3,19},{4,20},{5,21},{6,22},{7,23},{8,24},{9,... | collective-permute-start | bytes 884744 | tf_op jit(solution)/shard_map/ppermute | solution.py:24
  88.6 2.4 %collective-permute-start.27 = (bf16[4,96,384]{2,1,0:T(8,128)(2,1)S(1)}, bf16[4,96,384]{2,1,0:T(8,128)(2,1)S(1)}, u32[]{:S(2)}, u32[]{:S(2)}) collective-permute-start(bf16[4,96,384]{2,1,0:T(8,128)(2,1)S(1)} %get-tuple-element.156), channel_id=1, source_target_pairs={{0,48},{1,49},{2,50},{3,51},{4,52},{5,53},{6,54},{7,55},{8,56},{9,... | collective-permute-start | bytes 884744 | tf_op jit(solution)/shard_map/ppermute | solution.py:24
  93.0 3.0 %collective-permute-done.26.p2 = bf16[4,96,384]{2,1,0:T(8,128)(2,1)S(1)} collective-permute-done((bf16[4,96,384]{2,1,0:T(8,128)(2,1)S(1)}, bf16[4,96,384]{2,1,0:T(8,128)(2,1)S(1)}, u32[]{:S(2)}, u32[]{:S(2)}) %collective-permute-start.26) | collective-permute-done | bytes 294944 | tf_op jit(solution)/shard_map/ppermute | solution.py:24
  99.7 2.5 %collective-permute-start.31 = (bf16[256,384]{1,0:T(8,128)(2,1)S(1)}, bf16[256,384]{1,0:T(8,128)(2,1)S(1)}, u32[]{:S(2)}, u32[]{:S(2)}) collective-permute-start(bf16[256,384]{1,0:T(8,128)(2,1)S(1)} %collective-permute-done.18.flipped), channel_id=1, source_target_pairs={{0,16},{1,17},{2,18},{3,19},{4,20},{5,21},{6,22},{7,23},{16,32},{1... | collective-permute-start | bytes 589832 | tf_op jit(solution)/shard_map/ppermute | solution.py:24
  102.2 5.1 %collective-permute-done.28.got1 = bf16[384,384]{1,0:T(8,128)(2,1)S(1)} collective-permute-done((bf16[384,384]{1,0:T(8,128)(2,1)S(1)}, bf16[384,384]{1,0:T(8,128)(2,1)S(1)}, u32[]{:S(2)}, u32[]{:S(2)}) %collective-permute-start.28) | collective-permute-done | bytes 294944 | tf_op jit(solution)/shard_map/ppermute | solution.py:24
  108.4 2.1 %shard_map.75 = (f32[128,1536]{1,0:T(8,128)S(1)}, f32[128,1536]{1,0:T(8,128)S(1)}) custom-call(s32[6]{0:T(128)S(1)} %stack.42.meta, bf16[256,384]{1,0:T(8,128)(2,1)S(1)} %get-tuple-element.161.hg, bf16[256,384]{1,0:T(8,128)(2,1)S(1)} %collective-permute-done.18.flipped, bf16[256,384]{1,0:T(8,128)(2,1)S(1)} %collective-permute-done.31.hopped, ...), custom_call_target="tpu_custom_call" | custom-call | flops 1 | bytes 1 | tf_op jit(solution)/shard_map/pallas_call | solution.py:55
  110.5 4.4 %collective-permute-start.32 = (f32[128,1536]{1,0:T(8,128)S(1)}, f32[128,1536]{1,0:T(8,128)S(1)}, u32[]{:S(2)}, u32[]{:S(2)}) collective-permute-start(f32[128,1536]{1,0:T(8,128)S(1)} %get-tuple-element.165), channel_id=1, source_target_pairs={{0,64},{1,65},{2,66},{3,67},{4,68},{5,69},{6,70},{7,71},{8,72},{9,... | collective-permute-start | bytes 2359304 | tf_op jit(solution)/shard_map/ppermute | solution.py:24
  114.9 15.7 %all_to_all.5.parts = bf16[8,48,384]{2,1,0:T(8,128)(2,1)S(1)} all-to-all(bf16[8,48,384]{2,1,0:T(8,128)(2,1)S(1)} %shard_map.74), channel_id=1, replica_groups={{0,4,8,12,128,132,136,140},{64,68,72,76,192,196,200,204},{1,5,9,13,129,..., dimensions={0} | all-to-all | bytes 589824 | tf_op jit(solution)/shard_map/all_to_all | solution.py:367
  (96 shorter events, 37.7 us)
Async XLA Ops:
  1.8 22.6 %collective-permute-start = (bf16[3,48,768]{2,1,0:T(8,128)(2,1)S(1)}, bf16[3,48,768]{2,1,0:T(8,128)(2,1)S(1)}, u32[]{:S(2)}, u32[]{:S(2)}) collective-permute-start(bf16[3,48,768]{2,1,0:T(8,128)(2,1)S(1)} %constant_dynamic-slice_fusion.4), channel_id=1, source_target_pairs={{0,140},{1,141},{2,142},{3,143},{4,136},{5,137},{6,138},{7,139},{8... | collective-permute-start | bytes 663560 | tf_op jit(solution)/shard_map/ppermute | solution.py:24
  2.5 21.9 %collective-permute-start.2 = (bf16[128,1536]{1,0:T(8,128)(2,1)}, bf16[128,1536]{1,0:T(8,128)(2,1)S(1)}, u32[]{:S(2)}, u32[]{:S(2)}) collective-permute-start(bf16[128,1536]{1,0:T(8,128)(2,1)} %bitcast.23), channel_id=1, source_target_pairs={{0,64},{1,65},{2,66},{3,67},{4,68},{5,69},{6,70},{7,71},{8,72},{9,... | collective-permute-start | bytes 1179656 | tf_op jit(solution)/shard_map/ppermute | solution.py:24
  11.1 13.2 %collective-permute-start.3 = (bf16[128,1536]{1,0:T(8,128)(2,1)}, bf16[128,1536]{1,0:T(8,128)(2,1)S(1)}, u32[]{:S(2)}, u32[]{:S(2)}) collective-permute-start(bf16[128,1536]{1,0:T(8,128)(2,1)} %bitcast.21), channel_id=1, source_target_pairs={{0,64},{1,65},{2,66},{3,67},{4,68},{5,69},{6,70},{7,71},{8,72},{9,... | collective-permute-start | bytes 1179656 | tf_op jit(solution)/shard_map/ppermute | solution.py:24
  13.0 11.4 %collective-permute-start.4 = (bf16[64,1536]{1,0:T(8,128)(2,1)}, bf16[64,1536]{1,0:T(8,128)(2,1)S(1)}, u32[]{:S(2)}, u32[]{:S(2)}) collective-permute-start(bf16[64,1536]{1,0:T(8,128)(2,1)} %get-tuple-element.173), channel_id=1, source_target_pairs={{0,8},{1,9},{2,10},{3,11},{4,12},{5,13},{6,14},{7,15},{8,0},{9,1},... | collective-permute-start | bytes 589832 | tf_op jit(solution)/shard_map/ppermute | solution.py:24
  26.0 11.4 %collective-permute-start.6 = (bf16[64,1536]{1,0:T(8,128)(2,1)S(1)}, bf16[64,1536]{1,0:T(8,128)(2,1)}, u32[]{:S(2)}, u32[]{:S(2)}) collective-permute-start(bf16[64,1536]{1,0:T(8,128)(2,1)S(1)} %get-tuple-element.91), channel_id=1, source_target_pairs={{0,8},{1,9},{2,10},{3,11},{4,12},{5,13},{6,14},{7,15},{8,0},{9,1},... | collective-permute-start | bytes 589832 | tf_op jit(solution)/shard_map/ppermute | solution.py:24
  26.1 11.3 %collective-permute-start.7 = (bf16[64,1536]{1,0:T(8,128)(2,1)S(1)}, bf16[64,1536]{1,0:T(8,128)(2,1)}, u32[]{:S(2)}, u32[]{:S(2)}) collective-permute-start(bf16[64,1536]{1,0:T(8,128)(2,1)S(1)} %collective-permute-done.4), channel_id=1, source_target_pairs={{0,16},{1,17},{2,18},{3,19},{4,20},{5,21},{6,22},{7,23},{16,32},{1... | collective-permute-start | bytes 589832 | tf_op jit(solution)/shard_map/ppermute | solution.py:24
  41.9 7.8 %collective-permute-start.11 = (bf16[64,1536]{1,0:T(8,128)(2,1)}, bf16[64,1536]{1,0:T(8,128)(2,1)S(1)}, u32[]{:S(2)}, u32[]{:S(2)}) collective-permute-start(bf16[64,1536]{1,0:T(8,128)(2,1)} %collective-permute-done.6), channel_id=1, source_target_pairs={{0,16},{1,17},{2,18},{3,19},{4,20},{5,21},{6,22},{7,23},{16,32},{1... | collective-permute-start | bytes 589832 | tf_op jit(solution)/shard_map/ppermute | solution.py:24
  44.6 16.3 %collective-permute-start.17 = (bf16[4,4,48,384]{3,2,1,0:T(8,128)(2,1)S(1)}, bf16[4,4,48,384]{3,2,1,0:T(8,128)(2,1)S(1)}, u32[]{:S(2)}, u32[]{:S(2)}) collective-permute-start(bf16[4,4,48,384]{3,2,1,0:T(8,128)(2,1)S(1)} %pad_maximum_fusion.far0), channel_id=1, source_target_pairs={{0,1},{1,2},{2,3},{3,0},{4,5},{5,6},{6,7},{7,4},{8,9},{9,10},{10,1... | collective-permute-start | bytes 1769480 | tf_op jit(solution)/shard_map/ppermute | solution.py:24
  45.7 18.3 %collective-permute-start.16 = (bf16[4,4,48,384]{3,2,1,0:T(8,128)(2,1)S(1)}, bf16[4,4,48,384]{3,2,1,0:T(8,128)(2,1)S(1)}, u32[]{:S(2)}, u32[]{:S(2)}) collective-permute-start(bf16[4,4,48,384]{3,2,1,0:T(8,128)(2,1)S(1)} %pad_maximum_fusion.far0), channel_id=1, source_target_pairs={{0,2},{1,3},{2,0},{3,1},{4,6},{5,7},{6,4},{7,5},{8,10},{9,11},{10,... | collective-permute-start | bytes 1769480 | tf_op jit(solution)/shard_map/ppermute | solution.py:24
  47.7 16.2 %collective-permute-start.15 = (bf16[4,4,48,384]{3,2,1,0:T(8,128)(2,1)S(1)}, bf16[4,4,48,384]{3,2,1,0:T(8,128)(2,1)S(1)}, u32[]{:S(2)}, u32[]{:S(2)}) collective-permute-start(bf16[4,4,48,384]{3,2,1,0:T(8,128)(2,1)S(1)} %pad_maximum_fusion.far0), channel_id=1, source_target_pairs={{0,3},{1,0},{2,1},{3,2},{4,7},{5,4},{6,5},{7,6},{8,11},{9,8},{10,9... | collective-permute-start | bytes 1769480 | tf_op jit(solution)/shard_map/ppermute | solution.py:24
  63.9 10.4 %collective-permute-start.19 = (bf16[768,256]{1,0:T(8,128)(2,1)S(1)}, bf16[768,256]{1,0:T(8,128)(2,1)S(1)}, u32[]{:S(2)}, u32[]{:S(2)}) collective-permute-start(bf16[768,256]{1,0:T(8,128)(2,1)S(1)} %get-tuple-element.139), channel_id=1, source_target_pairs={{0,16},{1,17},{2,18},{3,19},{4,20},{5,21},{6,22},{7,23},{8,24},{9,... | collective-permute-start | bytes 1179656 | tf_op jit(solution)/shard_map/ppermute | solution.py:24
  65.3 12.0 %collective-permute-start.20 = (bf16[768,256]{1,0:T(8,128)(2,1)S(1)}, bf16[768,256]{1,0:T(8,128)(2,1)S(1)}, u32[]{:S(2)}, u32[]{:S(2)}) collective-permute-start(bf16[768,256]{1,0:T(8,128)(2,1)S(1)} %get-tuple-element.142), channel_id=1, source_target_pairs={{0,32},{1,33},{2,34},{3,35},{4,36},{5,37},{6,38},{7,39},{8,40},{9,... | collective-permute-start | bytes 1179656 | tf_op jit(solution)/shard_map/ppermute | solution.py:24
  68.0 10.1 %collective-permute-start.21 = (bf16[768,256]{1,0:T(8,128)(2,1)S(1)}, bf16[768,256]{1,0:T(8,128)(2,1)S(1)}, u32[]{:S(2)}, u32[]{:S(2)}) collective-permute-start(bf16[768,256]{1,0:T(8,128)(2,1)S(1)} %get-tuple-element.145), channel_id=1, source_target_pairs={{0,48},{1,49},{2,50},{3,51},{4,52},{5,53},{6,54},{7,55},{8,56},{9,... | collective-permute-start | bytes 1179656 | tf_op jit(solution)/shard_map/ppermute | solution.py:24
  74.3 14.3 %collective-permute-start.22 = (bf16[768,256]{1,0:T(8,128)(2,1)S(1)}, bf16[768,256]{1,0:T(8,128)(2,1)S(1)}, u32[]{:S(2)}, u32[]{:S(2)}) collective-permute-start(bf16[768,256]{1,0:T(8,128)(2,1)S(1)} %get-tuple-element.149), channel_id=1, source_target_pairs={{0,16},{1,17},{2,18},{3,19},{4,20},{5,21},{6,22},{7,23},{8,24},{9,... | collective-permute-start | bytes 1179656 | tf_op jit(solution)/shard_map/ppermute | solution.py:24
  74.7 10.0 %collective-permute-start.18 = (bf16[256,384]{1,0:T(8,128)(2,1)S(1)}, bf16[256,384]{1,0:T(8,128)(2,1)S(1)}, u32[]{:S(2)}, u32[]{:S(2)}) collective-permute-start(bf16[256,384]{1,0:T(8,128)(2,1)S(1)} %get-tuple-element.161.hg), channel_id=1, source_target_pairs={{0,8},{1,9},{2,10},{3,11},{4,12},{5,13},{6,14},{7,15},{8,0},{9,1},... | collective-permute-start | bytes 589832 | tf_op jit(solution)/shard_map/ppermute | solution.py:24
  77.2 13.8 %collective-permute-start.23 = (bf16[768,256]{1,0:T(8,128)(2,1)S(1)}, bf16[768,256]{1,0:T(8,128)(2,1)S(1)}, u32[]{:S(2)}, u32[]{:S(2)}) collective-permute-start(bf16[768,256]{1,0:T(8,128)(2,1)S(1)} %get-tuple-element.150), channel_id=1, source_target_pairs={{0,32},{1,33},{2,34},{3,35},{4,36},{5,37},{6,38},{7,39},{8,40},{9,... | collective-permute-start | bytes 1179656 | tf_op jit(solution)/shard_map/ppermute | solution.py:24
  78.1 12.9 %collective-permute-start.24 = (bf16[768,256]{1,0:T(8,128)(2,1)S(1)}, bf16[768,256]{1,0:T(8,128)(2,1)S(1)}, u32[]{:S(2)}, u32[]{:S(2)}) collective-permute-start(bf16[768,256]{1,0:T(8,128)(2,1)S(1)} %get-tuple-element.151), channel_id=1, source_target_pairs={{0,48},{1,49},{2,50},{3,51},{4,52},{5,53},{6,54},{7,55},{8,56},{9,... | collective-permute-start | bytes 1179656 | tf_op jit(solution)/shard_map/ppermute | solution.py:24
  84.7 8.3 %collective-permute-start.25 = (bf16[4,96,384]{2,1,0:T(8,128)(2,1)S(1)}, bf16[4,96,384]{2,1,0:T(8,128)(2,1)S(1)}, u32[]{:S(2)}, u32[]{:S(2)}) collective-permute-start(bf16[4,96,384]{2,1,0:T(8,128)(2,1)S(1)} %get-tuple-element.154), channel_id=1, source_target_pairs={{0,16},{1,17},{2,18},{3,19},{4,20},{5,21},{6,22},{7,23},{8,24},{9,... | collective-permute-start | bytes 884744 | tf_op jit(solution)/shard_map/ppermute | solution.py:24
  88.6 7.6 %collective-permute-start.27 = (bf16[4,96,384]{2,1,0:T(8,128)(2,1)S(1)}, bf16[4,96,384]{2,1,0:T(8,128)(2,1)S(1)}, u32[]{:S(2)}, u32[]{:S(2)}) collective-permute-start(bf16[4,96,384]{2,1,0:T(8,128)(2,1)S(1)} %get-tuple-element.156), channel_id=1, source_target_pairs={{0,48},{1,49},{2,50},{3,51},{4,52},{5,53},{6,54},{7,55},{8,56},{9,... | collective-permute-start | bytes 884744 | tf_op jit(solution)/shard_map/ppermute | solution.py:24
  96.9 10.3 %collective-permute-start.28 = (bf16[384,384]{1,0:T(8,128)(2,1)S(1)}, bf16[384,384]{1,0:T(8,128)(2,1)S(1)}, u32[]{:S(2)}, u32[]{:S(2)}) collective-permute-start(bf16[384,384]{1,0:T(8,128)(2,1)S(1)} %get-tuple-element.158), channel_id=1, source_target_pairs={{0,1},{1,2},{2,3},{3,0},{4,5},{5,6},{6,7},{7,4},{8,9},{9,10},{10,1... | collective-permute-start | bytes 884744 | tf_op jit(solution)/shard_map/ppermute | solution.py:24
  97.0 10.2 %collective-permute-start.29 = (bf16[384,384]{1,0:T(8,128)(2,1)S(1)}, bf16[384,384]{1,0:T(8,128)(2,1)S(1)}, u32[]{:S(2)}, u32[]{:S(2)}) collective-permute-start(bf16[384,384]{1,0:T(8,128)(2,1)S(1)} %get-tuple-element.159), channel_id=1, source_target_pairs={{0,2},{1,3},{2,0},{3,1},{4,6},{5,7},{6,4},{7,5},{8,10},{9,11},{10,... | collective-permute-start | bytes 884744 | tf_op jit(solution)/shard_map/ppermute | solution.py:24
  98.0 9.6 %collective-permute-start.30 = (bf16[384,384]{1,0:T(8,128)(2,1)S(1)}, bf16[384,384]{1,0:T(8,128)(2,1)S(1)}, u32[]{:S(2)}, u32[]{:S(2)}) collective-permute-start(bf16[384,384]{1,0:T(8,128)(2,1)S(1)} %get-tuple-element.160), channel_id=1, source_target_pairs={{0,3},{1,0},{2,1},{3,2},{4,7},{5,4},{6,5},{7,6},{8,11},{9,8},{10,9... | collective-permute-start | bytes 884744 | tf_op jit(solution)/shard_map/ppermute | solution.py:24
  99.7 8.7 %collective-permute-start.31 = (bf16[256,384]{1,0:T(8,128)(2,1)S(1)}, bf16[256,384]{1,0:T(8,128)(2,1)S(1)}, u32[]{:S(2)}, u32[]{:S(2)}) collective-permute-start(bf16[256,384]{1,0:T(8,128)(2,1)S(1)} %collective-permute-done.18.flipped), channel_id=1, source_target_pairs={{0,16},{1,17},{2,18},{3,19},{4,20},{5,21},{6,22},{7,23},{16,32},{1... | collective-permute-start | bytes 589832 | tf_op jit(solution)/shard_map/ppermute | solution.py:24
  110.5 21.6 %collective-permute-start.32 = (f32[128,1536]{1,0:T(8,128)S(1)}, f32[128,1536]{1,0:T(8,128)S(1)}, u32[]{:S(2)}, u32[]{:S(2)}) collective-permute-start(f32[128,1536]{1,0:T(8,128)S(1)} %get-tuple-element.165), channel_id=1, source_target_pairs={{0,64},{1,65},{2,66},{3,67},{4,68},{5,69},{6,70},{7,71},{8,72},{9,... | collective-permute-start | bytes 2359304 | tf_op jit(solution)/shard_map/ppermute | solution.py:24
  (22 other events, 178.9 us)

commit v7 on v6

--- a/solution.py
+++ b/solution.py
@@ -298,27 +298,26 @@
     holders = [d for d in range(256) if coords(d)[3] == coords(d)[0] // 2]
     conv_piece = send(conv_piece, mirror, holders)
     point_piece = send(point_piece, mirror)
-    first, tail = flip(x[:rows // 2]), x[rows // 2:]
+    first, tail = flip(x[:rows * 3 // 8]), x[rows * 3 // 8:]
     x_other = send(x, partner)
     og_other = send(og, partner)
-    conv_piece, point_piece, tail, x_other, og_other, first, conv_weight = lax.optimization_barrier(
-        (conv_piece, point_piece, tail, x_other, og_other, first, conv_weight)
-    )
+    conv_weight, _ = lax.optimization_barrier((conv_weight, x_other))
     mine, theirs = run(split_kernel, meta, [conv_weight], [shape((3, Cq, Hh), BF16)] * 2)
+    conv_piece, point_piece, tail, x_other, og_other, first, mine, theirs = lax.optimization_barrier(
+        (conv_piece, point_piece, tail, x_other, og_other, first, mine, theirs)
+    )
+    got = send(theirs, partner)
     handed = send(columns(conv_piece, 1 - core), partner, holders)
+    handed, got = lax.optimization_barrier((handed, got))
     conv_piece = jnp.where(core == xi // 2, columns(conv_piece, core), handed)
     far = jnp.concatenate([conv_piece, point_piece[None]])
     tail, hopped = flip(tail), hop(first)
     fars = [send_a(far, -k) for k in (1, 2, 3)]
-    far, first, tail, hopped, mine, theirs, *fars = lax.optimization_barrier(
-        (far, first, tail, hopped, mine, theirs, *fars)
-    )
+    far, first, tail, hopped, *fars = lax.optimization_barrier((far, first, tail, hopped, *fars))
     flipped = jnp.concatenate([first, tail])
-    got = send(theirs, partner)
     hopped = jnp.concatenate([hopped, hop(tail)])
     far = jnp.stack([far, *fars])
     fars = [far] + [send_b(far, -k) for k in (1, 2, 3)]
-    flipped, got = lax.optimization_barrier((flipped, got))
     flipped_other = send(flipped, partner)
     spread = order(Cq, Cq // 64, 1)
     taps, ogs, near, arriving, *early = run(
@@ -346,30 +345,29 @@
     messages = [messages[0]] + [send_a(part, k + 1) for k, part in enumerate(messages[1:])]
     block = (4, Hh // 4, Hh)
     p_own, *sends = run(point_kernel, meta, [ogs, hidden_t], [shape(block, F32)] + [shape(block, BF16)] * 3)
-    hg_flipped, *sends = lax.optimization_barrier((flip(hg), *sends))
+    hg_flipped, sends[2] = lax.optimization_barrier((flip(hg), sends[2]))
+    hg_hopped = hop(hg_flipped)
     p_all = [p_own] + [send_a(part, k + 1) for k, part in enumerate(sends)]
     conv, = run(gradient_kernel, meta, [*early, *messages], [shape((3 * Cq, Hh), F32)])
-    hg_late, conv = lax.optimization_barrier((hg_flipped, conv))
-    hg_hopped = hop(hg_late)
     n = 12 * (Cq // 16)
     big = (n + Hh // 4, Hh)
     total, *sends = run(pack_kernel, meta, [conv, *p_all], [shape(big, F32)] + [shape(big, BF16)] * 3)
     got_b = [send_b(part, k + 1) for k, part in enumerate(sends)]
     half = big[0] // 8
     by_z, = run(slice_kernel, meta, [total, *got_b], [shape((8, half, Hh), BF16)])
+    rings = [[index_of(x, y, z, c) for z in range(8)] for x in range(4) for y in range(4) for c in range(2)]
+    by_z = lax.all_to_all(by_z, ("dp", "seq"), 0, 0, axis_index_groups=rings)
     hg_late, by_z = lax.optimization_barrier((hg, by_z))
     mine_rows, other_rows = run(
         input_kernel, meta, [hg_late, hg_flipped, hg_hopped, mine, got, wfar.reshape(3, 2 * Cq, Hh)],
         [shape((rows, C), F32)] * 2,
     )
     in_grad = (og.astype(F32) + mine_rows + send(other_rows, partner)).astype(BF16)
-    rings = [[index_of(x, y, z, c) for z in range(8)] for x in range(4) for y in range(4) for c in range(2)]
-    by_z = lax.all_to_all(by_z, ("dp", "seq"), 0, 0, axis_index_groups=rings)
     conv_rows = 3 * (Cq // 64)
     kept, to_core = run(
         split_sum_kernel, meta, [by_z], [shape((half - conv_rows, Hh), F32), shape((conv_rows, Hh), F32)]
     )
-    in_grad, from_core = lax.optimization_barrier((in_grad, send(to_core, partner)))
+    from_core = send(to_core, partner)
     conv_mine, point_mine = run(
         output_kernel, meta, [kept, from_core], [shape((3, Cq // 64, H), F32), shape((Hq // 64, C), F32)]
     )

time: 135 us -> 138 us (1.022)
  blocking collectives: 15.7 us -> 0 us
  waiting for transfers between devices: 28.6 us -> 38 us
  starting transfers between devices: 58.5 us -> 64.4 us
  local copies, waits for them, and re-layouts: 6.89 us -> 9.78 us
    all_to_all x1 -> x0, blocking collectives: 15.7 us -> none  [local(): by_z = lax.all_to_all(by_z, ('dp', 'seq'), 0, 0, axis_index_groups=rings)]
    all_to_all x0 -> x1, waiting for transfers between devices: none -> 5.97 us  [local(): by_z = lax.all_to_all(by_z, ('dp', 'seq'), 0, 0, axis_index_groups=rings)]
    all_to_all x0 -> x1, starting transfers between devices: none -> 4.06 us  [local(): by_z = lax.all_to_all(by_z, ('dp', 'seq'), 0, 0, axis_index_groups=rings)]
    ppermute x34, waiting for transfers between devices: 28.6 us -> 32.1 us  [send(): return lax.ppermute(value, ('dp', 'seq'), pairs)]
    unnamed x24 -> x31, local copies, waits for them, and re-layouts: 3.06 us -> 5.91 us
    ppermute x34, starting transfers between devices: 58.5 us -> 60.3 us  [send(): return lax.ppermute(value, ('dp', 'seq'), pairs)]
  transfers between devices with their start and end apart: 34 -> 35, of which waited for: 12 -> 12; matrix products, arithmetic and copies ran while one was open for 4% -> 4% of each run, Pallas kernels for 12% -> 12%
where the time goes in v7:
time: 138 us; the launch traced here: 137 us
  starting transfers between devices  64.4 us (47%)
  waiting for transfers between devices  38 us (28%)
  Pallas kernels  21.1 us (15%)
  local copies, waits for them, and re-layouts  9.78 us (7%)
  other arithmetic  2.48 us (2%)
    ppermute x34, starting transfers between devices, send(): return lax.ppermute(value, ('dp', 'seq'), pairs)  60.3 us
    ppermute x34, waiting for transfers between devices, send(): return lax.ppermute(value, ('dp', 'seq'), pairs)  32.1 us
    pallas_call x11, Pallas kernels, run(): pl.pallas_call(kernel, out_shape=outs, in_specs=[pl.BlockSpec(memory_spac...  21.1 us
    all_to_all x1, waiting for transfers between devices, local(): by_z = lax.all_to_all(by_z, ('dp', 'seq'), 0, 0, axis_index_groups=rings)  5.97 us
    unnamed x31, local copies, waits for them, and re-layouts  5.91 us
    all_to_all x1, starting transfers between devices, local(): by_z = lax.all_to_all(by_z, ('dp', 'seq'), 0, 0, axis_index_groups=rings)  4.06 us
  transfers between devices with their start and end apart: 35, of which 12 were waited for; matrix products, arithmetic and copies ran while one was open for 4% of the time, Pallas kernels for 12%

profile of v7, /device:TPU:1, one launch (start us, length us, event | category | flops | bytes accessed | tf_op | source)
XLA Modules:
  0.0 136.9 jit_solution(10261824741732324033)
XLA Ops:
  1.4 6.4 %collective-permute-start.1 = (bf16[48,384]{1,0:T(8,128)(2,1)S(1)}, bf16[48,384]{1,0:T(8,128)(2,1)}, u32[]{:S(2)}, u32[]{:S(2)}) collective-permute-start(bf16[48,384]{1,0:T(8,128)(2,1)S(1)} %dynamic_slice.19), channel_id=1, source_target_pairs={{0,140},{1,141},{2,142},{3,143},{4,136},{5,137},{6,138},{7,139},{8... | collective-permute-start | bytes 110600 | tf_op jit(solution)/shard_map/ppermute | solution.py:24
  8.8 2.2 %collective-permute-start.4 = (bf16[48,1536]{1,0:T(8,128)(2,1)S(1)}, bf16[48,1536]{1,0:T(8,128)(2,1)}, u32[]{:S(2)}, u32[]{:S(2)}) collective-permute-start(bf16[48,1536]{1,0:T(8,128)(2,1)S(1)} %slice_bitcast_fusion.1), channel_id=1, source_target_pairs={{0,8},{1,9},{2,10},{3,11},{4,12},{5,13},{6,14},{7,15},{8,0},{9,1},... | collective-permute-start | bytes 442376 | tf_op jit(solution)/shard_map/ppermute | solution.py:24
  12.6 2.6 %collective-permute-start.3 = (bf16[128,1536]{1,0:T(8,128)(2,1)}, bf16[128,1536]{1,0:T(8,128)(2,1)S(1)}, u32[]{:S(2)}, u32[]{:S(2)}) collective-permute-start(bf16[128,1536]{1,0:T(8,128)(2,1)} %bitcast.22), channel_id=1, source_target_pairs={{0,64},{1,65},{2,66},{3,67},{4,68},{5,69},{6,70},{7,71},{8,72},{9,... | collective-permute-start | bytes 1179656 | tf_op jit(solution)/shard_map/ppermute | solution.py:24
  20.6 3.9 %collective-permute-start.6 = (bf16[3,384,384]{2,1,0:T(8,128)(2,1)S(1)}, bf16[3,384,384]{2,1,0:T(8,128)(2,1)S(1)}, u32[]{:S(2)}, u32[]{:S(2)}) collective-permute-start(bf16[3,384,384]{2,1,0:T(8,128)(2,1)S(1)} %get-tuple-element.86), channel_id=1, source_target_pairs={{0,64},{1,65},{2,66},{3,67},{4,68},{5,69},{6,70},{7,71},{8,72},{9,... | collective-permute-start | bytes 2654216 | tf_op jit(solution)/shard_map/ppermute | solution.py:24
  26.1 3.1 %collective-permute-start.8 = (bf16[48,1536]{1,0:T(8,128)(2,1)}, bf16[48,1536]{1,0:T(8,128)(2,1)S(1)}, u32[]{:S(2)}, u32[]{:S(2)}) collective-permute-start(bf16[48,1536]{1,0:T(8,128)(2,1)} %collective-permute-done.4), channel_id=1, source_target_pairs={{0,16},{1,17},{2,18},{3,19},{4,20},{5,21},{6,22},{7,23},{16,32},{1... | collective-permute-start | bytes 442376 | tf_op jit(solution)/shard_map/ppermute | solution.py:24
  31.9 2.6 %collective-permute-start.10 = (bf16[4,48,384]{2,1,0:T(8,128)(2,1)S(1)}, bf16[4,48,384]{2,1,0:T(8,128)(2,1)S(1)}, u32[]{:S(2)}, u32[]{:S(2)}) collective-permute-start(bf16[4,48,384]{2,1,0:T(8,128)(2,1)S(1)} %pad_maximum_fusion.2), channel_id=1, source_target_pairs={{0,32},{1,33},{2,34},{3,35},{4,36},{5,37},{6,38},{7,39},{8,40},{9,... | collective-permute-start | bytes 442376 | tf_op jit(solution)/shard_map/ppermute | solution.py:24
  35.6 6.8 %collective-permute-done.7 = bf16[80,1536]{1,0:T(8,128)(2,1)S(1)} collective-permute-done((bf16[80,1536]{1,0:T(8,128)(2,1)S(1)}, bf16[80,1536]{1,0:T(8,128)(2,1)S(1)}, u32[]{:S(2)}, u32[]{:S(2)}) %collective-permute-start.7) | collective-permute-done | bytes 245792 | tf_op jit(solution)/shard_map/ppermute | solution.py:24
  42.5 2.4 %collective-permute-start.12 = (bf16[80,1536]{1,0:T(8,128)(2,1)S(1)}, bf16[80,1536]{1,0:T(8,128)(2,1)S(1)}, u32[]{:S(2)}, u32[]{:S(2)}) collective-permute-start(bf16[80,1536]{1,0:T(8,128)(2,1)S(1)} %collective-permute-done.7), channel_id=1, source_target_pairs={{0,16},{1,17},{2,18},{3,19},{4,20},{5,21},{6,22},{7,23},{16,32},{1... | collective-permute-start | bytes 737288 | tf_op jit(solution)/shard_map/ppermute | solution.py:24
  48.3 2.3 %collective-permute-start.15 = (bf16[4,4,48,384]{3,2,1,0:T(8,128)(2,1)S(1)}, bf16[4,4,48,384]{3,2,1,0:T(8,128)(2,1)S(1)}, u32[]{:S(2)}, u32[]{:S(2)}) collective-permute-start(bf16[4,4,48,384]{3,2,1,0:T(8,128)(2,1)S(1)} %pad_maximum_fusion.far0), channel_id=1, source_target_pairs={{0,3},{1,0},{2,1},{3,2},{4,7},{5,4},{6,5},{7,6},{8,11},{9,8},{10,9... | collective-permute-start | bytes 1769480 | tf_op jit(solution)/shard_map/ppermute | solution.py:24
  50.8 4.2 %shard_map.68 = (bf16[2,256,1536]{2,1,0:T(8,128)(2,1)}, bf16[256,1536]{1,0:T(8,128)(2,1)}, f32[256,384]{1,0:T(8,128)S(1)}, f32[256,192]{1,0:T(8,128)S(1)}, bf16[...) custom-call(s32[6]{0:T(128)S(1)} %stack.42.meta, ...), custom_call_target="tpu_custom_call" | custom-call | flops 1 | bytes 1 | tf_op jit(solution)/shard_map/pallas_call | solution.py:55
  55.0 2.2 %collective-permute-start.14 = (bf16[128,1536]{1,0:T(8,128)(2,1)S(1)}, bf16[128,1536]{1,0:T(8,128)(2,1)S(1)}, u32[]{:S(2)}, u32[]{:S(2)}) collective-permute-start(bf16[128,1536]{1,0:T(8,128)(2,1)S(1)} %pad_maximum_fusion.1.x2), channel_id=1, source_target_pairs={{0,64},{1,65},{2,66},{3,67},{4,68},{5,69},{6,70},{7,71},{8,72},{9,... | collective-permute-start | bytes 1179656 | tf_op jit(solution)/shard_map/ppermute | solution.py:24
  60.8 4.5 %collective-permute-done.16.far2 = bf16[4,4,48,384]{3,2,1,0:T(8,128)(2,1)S(1)} collective-permute-done((bf16[4,4,48,384]{3,2,1,0:T(8,128)(2,1)S(1)}, bf16[4,4,48,384]{3,2,1,0:T(8,128)(2,1)S(1)}, u32[]{:S(2)}, u32[]{:S(2)}) %collective-permute-start.16) | collective-permute-done | bytes 589856 | tf_op jit(solution)/shard_map/ppermute | solution.py:24
  66.6 2.7 %collective-permute-start.19 = (bf16[768,256]{1,0:T(8,128)(2,1)S(1)}, bf16[768,256]{1,0:T(8,128)(2,1)S(1)}, u32[]{:S(2)}, u32[]{:S(2)}) collective-permute-start(bf16[768,256]{1,0:T(8,128)(2,1)S(1)} %get-tuple-element.131), channel_id=1, source_target_pairs={{0,32},{1,33},{2,34},{3,35},{4,36},{5,37},{6,38},{7,39},{8,40},{9,... | collective-permute-start | bytes 1179656 | tf_op jit(solution)/shard_map/ppermute | solution.py:24
  70.6 5.1 %shard_map.70 = (bf16[256,384]{1,0:T(8,128)(2,1)S(1)}, bf16[384,256]{1,0:T(8,128)(2,1)S(1)}, bf16[3,16,48,384]{3,2,1,0:T(8,128)(2,1)}, bf16[768,256]{1,0:T(8,128...) custom-call(s32[6]{0:T(128)S(1)} %stack.42.meta, ...), custom_call_target="tpu_custom_call" | custom-call | flops 1 | bytes 1 | tf_op jit(solution)/shard_map/pallas_call | solution.py:55
  76.1 2.5 %collective-permute-done.19.x2 = bf16[768,256]{1,0:T(8,128)(2,1)S(1)} collective-permute-done((bf16[768,256]{1,0:T(8,128)(2,1)S(1)}, bf16[768,256]{1,0:T(8,128)(2,1)S(1)}, u32[]{:S(2)}, u32[]{:S(2)}) %collective-permute-start.19) | collective-permute-done | bytes 393248 | tf_op jit(solution)/shard_map/ppermute | solution.py:24
  82.7 4.6 %collective-permute-done.26.flipped = bf16[256,384]{1,0:T(8,128)(2,1)} collective-permute-done((bf16[256,384]{1,0:T(8,128)(2,1)S(1)}, bf16[256,384]{1,0:T(8,128)(2,1)}, u32[]{:S(2)}, u32[]{:S(2)}) %collective-permute-start.26) | collective-permute-done | bytes 196640 | tf_op jit(solution)/shard_map/ppermute | solution.py:24
  87.2 3.3 %collective-permute-start.25 = (bf16[4,96,384]{2,1,0:T(8,128)(2,1)S(1)}, bf16[4,96,384]{2,1,0:T(8,128)(2,1)S(1)}, u32[]{:S(2)}, u32[]{:S(2)}) collective-permute-start(bf16[4,96,384]{2,1,0:T(8,128)(2,1)S(1)} %get-tuple-element.144), channel_id=1, source_target_pairs={{0,32},{1,33},{2,34},{3,35},{4,36},{5,37},{6,38},{7,39},{8,40},{9,... | collective-permute-start | bytes 884744 | tf_op jit(solution)/shard_map/ppermute | solution.py:24
  95.4 2.3 %collective-permute-done.27.p3 = bf16[4,96,384]{2,1,0:T(8,128)(2,1)S(1)} collective-permute-done((bf16[4,96,384]{2,1,0:T(8,128)(2,1)S(1)}, bf16[4,96,384]{2,1,0:T(8,128)(2,1)S(1)}, u32[]{:S(2)}, u32[]{:S(2)}) %collective-permute-start.27) | collective-permute-done | bytes 294944 | tf_op jit(solution)/shard_map/ppermute | solution.py:24
  102.5 6.3 %collective-permute-done.28.got1 = bf16[384,384]{1,0:T(8,128)(2,1)S(1)} collective-permute-done((bf16[384,384]{1,0:T(8,128)(2,1)S(1)}, bf16[384,384]{1,0:T(8,128)(2,1)S(1)}, u32[]{:S(2)}, u32[]{:S(2)}) %collective-permute-start.28) | collective-permute-done | bytes 294944 | tf_op jit(solution)/shard_map/ppermute | solution.py:24
  110.9 4.1 %all-to-all-start = ((bf16[8,48,384]{2,1,0:T(8,128)(2,1)}), bf16[8,48,384]{2,1,0:T(8,128)(2,1)}, u32[]{:S(2)}, u32[]{:S(2)}) async-start(bf16[8,48,384]{2,1,0:T(8,128)(2,1)} %copy-done.10), calls=%async_computation | async-start | bytes 589824 | tf_op jit(solution)/shard_map/all_to_all | solution.py:359
  115.0 3.8 %collective-permute-start.31 = (bf16[256,384]{1,0:T(8,128)(2,1)}, bf16[256,384]{1,0:T(8,128)(2,1)}, u32[]{:S(2)}, u32[]{:S(2)}) collective-permute-start(bf16[256,384]{1,0:T(8,128)(2,1)} %collective-permute-done.26.flipped), channel_id=1, source_target_pairs={{0,16},{1,17},{2,18},{3,19},{4,20},{5,21},{6,22},{7,23},{16,32},{1... | collective-permute-start | bytes 589832 | tf_op jit(solution)/shard_map/ppermute | solution.py:24
  118.8 6.0 %all-to-all-done.parts = bf16[8,48,384]{2,1,0:T(8,128)(2,1)} async-done(((bf16[8,48,384]{2,1,0:T(8,128)(2,1)}), bf16[8,48,384]{2,1,0:T(8,128)(2,1)}, u32[]{:S(2)}, u32[]{:S(2)}) %all-to-all-start) | async-done | bytes 294944 | tf_op jit(solution)/shard_map/all_to_all | solution.py:359
  125.7 2.6 %shard_map.75 = (f32[128,1536]{1,0:T(8,128)S(1)}, f32[128,1536]{1,0:T(8,128)S(1)}) custom-call(s32[6]{0:T(128)S(1)} %stack.42.meta, bf16[256,384]{1,0:T(8,128)(2,1)S(1)} %copy-done.14, bf16[256,384]{1,0:T(8,128)(2,1)} %collective-permute-done.26.flipped, bf16[256,384]{1,0:T(8,128)(2,1)} %collective-permute-done.31.hopped, ...), custom_call_target="tpu_custom_call" | custom-call | flops 1 | bytes 1 | tf_op jit(solution)/shard_map/pallas_call | solution.py:55
  128.3 4.1 %collective-permute-start.32 = (f32[128,1536]{1,0:T(8,128)S(1)}, f32[128,1536]{1,0:T(8,128)S(1)}, u32[]{:S(2)}, u32[]{:S(2)}) collective-permute-start(f32[128,1536]{1,0:T(8,128)S(1)} %get-tuple-element.155), channel_id=1, source_target_pairs={{0,64},{1,65},{2,66},{3,67},{4,68},{5,69},{6,70},{7,71},{8,72},{9,... | collective-permute-start | bytes 2359304 | tf_op jit(solution)/shard_map/ppermute | solution.py:24
  (105 shorter events, 45.2 us)
Async XLA Ops:
  1.4 19.2 %collective-permute-start.1 = (bf16[48,384]{1,0:T(8,128)(2,1)S(1)}, bf16[48,384]{1,0:T(8,128)(2,1)}, u32[]{:S(2)}, u32[]{:S(2)}) collective-permute-start(bf16[48,384]{1,0:T(8,128)(2,1)S(1)} %dynamic_slice.19), channel_id=1, source_target_pairs={{0,140},{1,141},{2,142},{3,143},{4,136},{5,137},{6,138},{7,139},{8... | collective-permute-start | bytes 110600 | tf_op jit(solution)/shard_map/ppermute | solution.py:24
  8.8 11.8 %collective-permute-start.4 = (bf16[48,1536]{1,0:T(8,128)(2,1)S(1)}, bf16[48,1536]{1,0:T(8,128)(2,1)}, u32[]{:S(2)}, u32[]{:S(2)}) collective-permute-start(bf16[48,1536]{1,0:T(8,128)(2,1)S(1)} %slice_bitcast_fusion.1), channel_id=1, source_target_pairs={{0,8},{1,9},{2,10},{3,11},{4,12},{5,13},{6,14},{7,15},{8,0},{9,1},... | collective-permute-start | bytes 442376 | tf_op jit(solution)/shard_map/ppermute | solution.py:24
  11.9 8.7 %collective-permute-start = (bf16[3,48,768]{2,1,0:T(8,128)(2,1)S(1)}, bf16[3,48,768]{2,1,0:T(8,128)(2,1)S(1)}, u32[]{:S(2)}, u32[]{:S(2)}) collective-permute-start(bf16[3,48,768]{2,1,0:T(8,128)(2,1)S(1)} %constant_dynamic-slice_fusion.4), channel_id=1, source_target_pairs={{0,140},{1,141},{2,142},{3,143},{4,136},{5,137},{6,138},{7,139},{8... | collective-permute-start | bytes 663560 | tf_op jit(solution)/shard_map/ppermute | solution.py:24
  20.6 8.8 %collective-permute-start.6 = (bf16[3,384,384]{2,1,0:T(8,128)(2,1)S(1)}, bf16[3,384,384]{2,1,0:T(8,128)(2,1)S(1)}, u32[]{:S(2)}, u32[]{:S(2)}) collective-permute-start(bf16[3,384,384]{2,1,0:T(8,128)(2,1)S(1)} %get-tuple-element.86), channel_id=1, source_target_pairs={{0,64},{1,65},{2,66},{3,67},{4,68},{5,69},{6,70},{7,71},{8,72},{9,... | collective-permute-start | bytes 2654216 | tf_op jit(solution)/shard_map/ppermute | solution.py:24
  26.1 9.5 %collective-permute-start.8 = (bf16[48,1536]{1,0:T(8,128)(2,1)}, bf16[48,1536]{1,0:T(8,128)(2,1)S(1)}, u32[]{:S(2)}, u32[]{:S(2)}) collective-permute-start(bf16[48,1536]{1,0:T(8,128)(2,1)} %collective-permute-done.4), channel_id=1, source_target_pairs={{0,16},{1,17},{2,18},{3,19},{4,20},{5,21},{6,22},{7,23},{16,32},{1... | collective-permute-start | bytes 442376 | tf_op jit(solution)/shard_map/ppermute | solution.py:24
  29.3 13.2 %collective-permute-start.7 = (bf16[80,1536]{1,0:T(8,128)(2,1)S(1)}, bf16[80,1536]{1,0:T(8,128)(2,1)S(1)}, u32[]{:S(2)}, u32[]{:S(2)}) collective-permute-start(bf16[80,1536]{1,0:T(8,128)(2,1)S(1)} %slice_bitcast_fusion), channel_id=1, source_target_pairs={{0,8},{1,9},{2,10},{3,11},{4,12},{5,13},{6,14},{7,15},{8,0},{9,1},... | collective-permute-start | bytes 737288 | tf_op jit(solution)/shard_map/ppermute | solution.py:24
  30.5 11.9 %collective-permute-start.11 = (bf16[4,48,384]{2,1,0:T(8,128)(2,1)S(1)}, bf16[4,48,384]{2,1,0:T(8,128)(2,1)S(1)}, u32[]{:S(2)}, u32[]{:S(2)}) collective-permute-start(bf16[4,48,384]{2,1,0:T(8,128)(2,1)S(1)} %pad_maximum_fusion.2), channel_id=1, source_target_pairs={{0,16},{1,17},{2,18},{3,19},{4,20},{5,21},{6,22},{7,23},{8,24},{9,... | collective-permute-start | bytes 442376 | tf_op jit(solution)/shard_map/ppermute | solution.py:24
  31.9 10.6 %collective-permute-start.10 = (bf16[4,48,384]{2,1,0:T(8,128)(2,1)S(1)}, bf16[4,48,384]{2,1,0:T(8,128)(2,1)S(1)}, u32[]{:S(2)}, u32[]{:S(2)}) collective-permute-start(bf16[4,48,384]{2,1,0:T(8,128)(2,1)S(1)} %pad_maximum_fusion.2), channel_id=1, source_target_pairs={{0,32},{1,33},{2,34},{3,35},{4,36},{5,37},{6,38},{7,39},{8,40},{9,... | collective-permute-start | bytes 442376 | tf_op jit(solution)/shard_map/ppermute | solution.py:24
  46.9 13.9 %collective-permute-start.17 = (bf16[4,4,48,384]{3,2,1,0:T(8,128)(2,1)S(1)}, bf16[4,4,48,384]{3,2,1,0:T(8,128)(2,1)S(1)}, u32[]{:S(2)}, u32[]{:S(2)}) collective-permute-start(bf16[4,4,48,384]{3,2,1,0:T(8,128)(2,1)S(1)} %pad_maximum_fusion.far0), channel_id=1, source_target_pairs={{0,1},{1,2},{2,3},{3,0},{4,5},{5,6},{6,7},{7,4},{8,9},{9,10},{10,1... | collective-permute-start | bytes 1769480 | tf_op jit(solution)/shard_map/ppermute | solution.py:24
  48.2 17.1 %collective-permute-start.16 = (bf16[4,4,48,384]{3,2,1,0:T(8,128)(2,1)S(1)}, bf16[4,4,48,384]{3,2,1,0:T(8,128)(2,1)S(1)}, u32[]{:S(2)}, u32[]{:S(2)}) collective-permute-start(bf16[4,4,48,384]{3,2,1,0:T(8,128)(2,1)S(1)} %pad_maximum_fusion.far0), channel_id=1, source_target_pairs={{0,2},{1,3},{2,0},{3,1},{4,6},{5,7},{6,4},{7,5},{8,10},{9,11},{10,... | collective-permute-start | bytes 1769480 | tf_op jit(solution)/shard_map/ppermute | solution.py:24
  48.3 17.0 %collective-permute-start.15 = (bf16[4,4,48,384]{3,2,1,0:T(8,128)(2,1)S(1)}, bf16[4,4,48,384]{3,2,1,0:T(8,128)(2,1)S(1)}, u32[]{:S(2)}, u32[]{:S(2)}) collective-permute-start(bf16[4,4,48,384]{3,2,1,0:T(8,128)(2,1)S(1)} %pad_maximum_fusion.far0), channel_id=1, source_target_pairs={{0,3},{1,0},{2,1},{3,2},{4,7},{5,4},{6,5},{7,6},{8,11},{9,8},{10,9... | collective-permute-start | bytes 1769480 | tf_op jit(solution)/shard_map/ppermute | solution.py:24
  65.3 10.4 %collective-permute-start.18 = (bf16[768,256]{1,0:T(8,128)(2,1)S(1)}, bf16[768,256]{1,0:T(8,128)(2,1)S(1)}, u32[]{:S(2)}, u32[]{:S(2)}) collective-permute-start(bf16[768,256]{1,0:T(8,128)(2,1)S(1)} %get-tuple-element.128), channel_id=1, source_target_pairs={{0,16},{1,17},{2,18},{3,19},{4,20},{5,21},{6,22},{7,23},{8,24},{9,... | collective-permute-start | bytes 1179656 | tf_op jit(solution)/shard_map/ppermute | solution.py:24
  66.6 12.0 %collective-permute-start.19 = (bf16[768,256]{1,0:T(8,128)(2,1)S(1)}, bf16[768,256]{1,0:T(8,128)(2,1)S(1)}, u32[]{:S(2)}, u32[]{:S(2)}) collective-permute-start(bf16[768,256]{1,0:T(8,128)(2,1)S(1)} %get-tuple-element.131), channel_id=1, source_target_pairs={{0,32},{1,33},{2,34},{3,35},{4,36},{5,37},{6,38},{7,39},{8,40},{9,... | collective-permute-start | bytes 1179656 | tf_op jit(solution)/shard_map/ppermute | solution.py:24
  69.4 10.1 %collective-permute-start.20 = (bf16[768,256]{1,0:T(8,128)(2,1)S(1)}, bf16[768,256]{1,0:T(8,128)(2,1)S(1)}, u32[]{:S(2)}, u32[]{:S(2)}) collective-permute-start(bf16[768,256]{1,0:T(8,128)(2,1)S(1)} %get-tuple-element.134), channel_id=1, source_target_pairs={{0,48},{1,49},{2,50},{3,51},{4,52},{5,53},{6,54},{7,55},{8,56},{9,... | collective-permute-start | bytes 1179656 | tf_op jit(solution)/shard_map/ppermute | solution.py:24
  75.7 14.8 %collective-permute-start.21 = (bf16[768,256]{1,0:T(8,128)(2,1)S(1)}, bf16[768,256]{1,0:T(8,128)(2,1)S(1)}, u32[]{:S(2)}, u32[]{:S(2)}) collective-permute-start(bf16[768,256]{1,0:T(8,128)(2,1)S(1)} %get-tuple-element.138), channel_id=1, source_target_pairs={{0,16},{1,17},{2,18},{3,19},{4,20},{5,21},{6,22},{7,23},{8,24},{9,... | collective-permute-start | bytes 1179656 | tf_op jit(solution)/shard_map/ppermute | solution.py:24
  76.1 11.1 %collective-permute-start.26 = (bf16[256,384]{1,0:T(8,128)(2,1)S(1)}, bf16[256,384]{1,0:T(8,128)(2,1)}, u32[]{:S(2)}, u32[]{:S(2)}) collective-permute-start(bf16[256,384]{1,0:T(8,128)(2,1)S(1)} %get-tuple-element.151.hg), channel_id=1, source_target_pairs={{0,8},{1,9},{2,10},{3,11},{4,12},{5,13},{6,14},{7,15},{8,0},{9,1},... | collective-permute-start | bytes 589832 | tf_op jit(solution)/shard_map/ppermute | solution.py:24
  78.6 14.0 %collective-permute-start.22 = (bf16[768,256]{1,0:T(8,128)(2,1)S(1)}, bf16[768,256]{1,0:T(8,128)(2,1)S(1)}, u32[]{:S(2)}, u32[]{:S(2)}) collective-permute-start(bf16[768,256]{1,0:T(8,128)(2,1)S(1)} %get-tuple-element.139), channel_id=1, source_target_pairs={{0,32},{1,33},{2,34},{3,35},{4,36},{5,37},{6,38},{7,39},{8,40},{9,... | collective-permute-start | bytes 1179656 | tf_op jit(solution)/shard_map/ppermute | solution.py:24
  79.5 13.1 %collective-permute-start.23 = (bf16[768,256]{1,0:T(8,128)(2,1)S(1)}, bf16[768,256]{1,0:T(8,128)(2,1)S(1)}, u32[]{:S(2)}, u32[]{:S(2)}) collective-permute-start(bf16[768,256]{1,0:T(8,128)(2,1)S(1)} %get-tuple-element.140), channel_id=1, source_target_pairs={{0,48},{1,49},{2,50},{3,51},{4,52},{5,53},{6,54},{7,55},{8,56},{9,... | collective-permute-start | bytes 1179656 | tf_op jit(solution)/shard_map/ppermute | solution.py:24
  82.6 11.9 %collective-permute-start.24 = (bf16[4,96,384]{2,1,0:T(8,128)(2,1)S(1)}, bf16[4,96,384]{2,1,0:T(8,128)(2,1)S(1)}, u32[]{:S(2)}, u32[]{:S(2)}) collective-permute-start(bf16[4,96,384]{2,1,0:T(8,128)(2,1)S(1)} %get-tuple-element.143), channel_id=1, source_target_pairs={{0,16},{1,17},{2,18},{3,19},{4,20},{5,21},{6,22},{7,23},{8,24},{9,... | collective-permute-start | bytes 884744 | tf_op jit(solution)/shard_map/ppermute | solution.py:24
  98.5 10.3 %collective-permute-start.28 = (bf16[384,384]{1,0:T(8,128)(2,1)S(1)}, bf16[384,384]{1,0:T(8,128)(2,1)S(1)}, u32[]{:S(2)}, u32[]{:S(2)}) collective-permute-start(bf16[384,384]{1,0:T(8,128)(2,1)S(1)} %get-tuple-element.148), channel_id=1, source_target_pairs={{0,1},{1,2},{2,3},{3,0},{4,5},{5,6},{6,7},{7,4},{8,9},{9,10},{10,1... | collective-permute-start | bytes 884744 | tf_op jit(solution)/shard_map/ppermute | solution.py:24
  98.8 10.1 %collective-permute-start.29 = (bf16[384,384]{1,0:T(8,128)(2,1)S(1)}, bf16[384,384]{1,0:T(8,128)(2,1)S(1)}, u32[]{:S(2)}, u32[]{:S(2)}) collective-permute-start(bf16[384,384]{1,0:T(8,128)(2,1)S(1)} %get-tuple-element.149), channel_id=1, source_target_pairs={{0,2},{1,3},{2,0},{3,1},{4,6},{5,7},{6,4},{7,5},{8,10},{9,11},{10,... | collective-permute-start | bytes 884744 | tf_op jit(solution)/shard_map/ppermute | solution.py:24
  100.8 8.7 %collective-permute-start.30 = (bf16[384,384]{1,0:T(8,128)(2,1)S(1)}, bf16[384,384]{1,0:T(8,128)(2,1)S(1)}, u32[]{:S(2)}, u32[]{:S(2)}) collective-permute-start(bf16[384,384]{1,0:T(8,128)(2,1)S(1)} %get-tuple-element.150), channel_id=1, source_target_pairs={{0,3},{1,0},{2,1},{3,2},{4,7},{5,4},{6,5},{7,6},{8,11},{9,8},{10,9... | collective-permute-start | bytes 884744 | tf_op jit(solution)/shard_map/ppermute | solution.py:24
  110.9 13.8 %all-to-all-start = ((bf16[8,48,384]{2,1,0:T(8,128)(2,1)}), bf16[8,48,384]{2,1,0:T(8,128)(2,1)}, u32[]{:S(2)}, u32[]{:S(2)}) async-start(bf16[8,48,384]{2,1,0:T(8,128)(2,1)} %copy-done.10), calls=%async_computation | async-start | bytes 589824 | tf_op jit(solution)/shard_map/all_to_all | solution.py:359
  115.0 9.8 %collective-permute-start.31 = (bf16[256,384]{1,0:T(8,128)(2,1)}, bf16[256,384]{1,0:T(8,128)(2,1)}, u32[]{:S(2)}, u32[]{:S(2)}) collective-permute-start(bf16[256,384]{1,0:T(8,128)(2,1)} %collective-permute-done.26.flipped), channel_id=1, source_target_pairs={{0,16},{1,17},{2,18},{3,19},{4,20},{5,21},{6,22},{7,23},{16,32},{1... | collective-permute-start | bytes 589832 | tf_op jit(solution)/shard_map/ppermute | solution.py:24
  (26 other events, 235.5 us)

commit v8 on v7

--- a/solution.py
+++ b/solution.py
@@ -298,24 +298,23 @@
     holders = [d for d in range(256) if coords(d)[3] == coords(d)[0] // 2]
     conv_piece = send(conv_piece, mirror, holders)
     point_piece = send(point_piece, mirror)
-    first, tail = flip(x[:rows * 3 // 8]), x[rows * 3 // 8:]
+    first = rows // 2
+    flipped = flip(x[:first])
     x_other = send(x, partner)
     og_other = send(og, partner)
     conv_weight, _ = lax.optimization_barrier((conv_weight, x_other))
     mine, theirs = run(split_kernel, meta, [conv_weight], [shape((3, Cq, Hh), BF16)] * 2)
-    conv_piece, point_piece, tail, x_other, og_other, first, mine, theirs = lax.optimization_barrier(
-        (conv_piece, point_piece, tail, x_other, og_other, first, mine, theirs)
+    conv_piece, point_piece, x_late, x_other, og_other, theirs, flipped, mine = lax.optimization_barrier(
+        (conv_piece, point_piece, x, x_other, og_other, theirs, flipped, mine)
     )
     got = send(theirs, partner)
     handed = send(columns(conv_piece, 1 - core), partner, holders)
-    handed, got = lax.optimization_barrier((handed, got))
     conv_piece = jnp.where(core == xi // 2, columns(conv_piece, core), handed)
     far = jnp.concatenate([conv_piece, point_piece[None]])
-    tail, hopped = flip(tail), hop(first)
+    flipped = jnp.concatenate([flipped, flip(x_late[first:])])
     fars = [send_a(far, -k) for k in (1, 2, 3)]
-    far, first, tail, hopped, *fars = lax.optimization_barrier((far, first, tail, hopped, *fars))
-    flipped = jnp.concatenate([first, tail])
-    hopped = jnp.concatenate([hopped, hop(tail)])
+    far, flipped, got, *fars = lax.optimization_barrier((far, flipped, got, *fars))
+    hopped = hop(flipped)
     far = jnp.stack([far, *fars])
     fars = [far] + [send_b(far, -k) for k in (1, 2, 3)]
     flipped_other = send(flipped, partner)
@@ -355,13 +354,14 @@
     got_b = [send_b(part, k + 1) for k, part in enumerate(sends)]
     half = big[0] // 8
     by_z, = run(slice_kernel, meta, [total, *got_b], [shape((8, half, Hh), BF16)])
-    rings = [[index_of(x, y, z, c) for z in range(8)] for x in range(4) for y in range(4) for c in range(2)]
-    by_z = lax.all_to_all(by_z, ("dp", "seq"), 0, 0, axis_index_groups=rings)
-    hg_late, by_z = lax.optimization_barrier((hg, by_z))
+    hg_late, hg_hopped, by_z = lax.optimization_barrier((hg, hg_hopped, by_z))
     mine_rows, other_rows = run(
         input_kernel, meta, [hg_late, hg_flipped, hg_hopped, mine, got, wfar.reshape(3, 2 * Cq, Hh)],
         [shape((rows, C), F32)] * 2,
     )
+    rings = [[index_of(x, y, z, c) for z in range(8)] for x in range(4) for y in range(4) for c in range(2)]
+    by_z = lax.all_to_all(by_z, ("dp", "seq"), 0, 0, axis_index_groups=rings)
+    by_z, mine_rows, other_rows = lax.optimization_barrier((by_z, mine_rows, other_rows))
     in_grad = (og.astype(F32) + mine_rows + send(other_rows, partner)).astype(BF16)
     conv_rows = 3 * (Cq // 64)
     kept, to_core = run(

time: 138 us -> 140 us (1.014)
  starting transfers between devices: 64.4 us -> 55.4 us
  local copies, waits for them, and re-layouts: 9.78 us -> 14.8 us
  waiting for transfers between devices: 38 us -> 41.6 us
  other arithmetic: 2.48 us -> 6.08 us
    ppermute x34 -> x33, starting transfers between devices: 60.3 us -> 48.2 us  [send(): return lax.ppermute(value, ('dp', 'seq'), pairs)]
    unnamed x31 -> x50, local copies, waits for them, and re-layouts: 5.91 us -> 11.1 us
    ppermute x34 -> x33, waiting for transfers between devices: 32.1 us -> 36.3 us  [send(): return lax.ppermute(value, ('dp', 'seq'), pairs)]
    all_to_all x1, starting transfers between devices: 4.06 us -> 7.15 us  [local(): by_z = lax.all_to_all(by_z, ('dp', 'seq'), 0, 0, axis_index_groups=rings)]
  transfers between devices with their start and end apart: 35 -> 34, of which waited for: 12 -> 16; matrix products, arithmetic and copies ran while one was open for 4% -> 5% of each run, Pallas kernels for 12% -> 14%
where the time goes in v8:
time: 140 us; the launch traced here: 139 us
  starting transfers between devices  55.4 us (40%)
  waiting for transfers between devices  41.6 us (30%)
  Pallas kernels  20.5 us (15%)
  local copies, waits for them, and re-layouts  14.8 us (11%)
  other arithmetic  6.08 us (4%)
    ppermute x33, starting transfers between devices, send(): return lax.ppermute(value, ('dp', 'seq'), pairs)  48.2 us
    ppermute x33, waiting for transfers between devices, send(): return lax.ppermute(value, ('dp', 'seq'), pairs)  36.3 us
    pallas_call x11, Pallas kernels, run(): pl.pallas_call(kernel, out_shape=outs, in_specs=[pl.BlockSpec(memory_spac...  20.5 us
    unnamed x50, local copies, waits for them, and re-layouts  11.1 us
    all_to_all x1, starting transfers between devices, local(): by_z = lax.all_to_all(by_z, ('dp', 'seq'), 0, 0, axis_index_groups=rings)  7.15 us
    all_to_all x1, waiting for transfers between devices, local(): by_z = lax.all_to_all(by_z, ('dp', 'seq'), 0, 0, axis_index_groups=rings)  5.34 us
  transfers between devices with their start and end apart: 34, of which 16 were waited for; matrix products, arithmetic and copies ran while one was open for 5% of the time, Pallas kernels for 14%

profile of v8, /device:TPU:1, one launch (start us, length us, event | category | flops | bytes accessed | tf_op | source)
XLA Modules:
  0.0 139.4 jit_solution(12971533725843481684)
XLA Ops:
  2.4 8.7 %collective-permute-start.2 = (bf16[128,1536]{1,0:T(8,128)(2,1)}, bf16[128,1536]{1,0:T(8,128)(2,1)S(1)}, u32[]{:S(2)}, u32[]{:S(2)}) collective-permute-start(bf16[128,1536]{1,0:T(8,128)(2,1)} %bitcast.22), channel_id=1, source_target_pairs={{0,64},{1,65},{2,66},{3,67},{4,68},{5,69},{6,70},{7,71},{8,72},{9,... | collective-permute-start | bytes 1179656 | tf_op jit(solution)/shard_map/ppermute | solution.py:24
  12.1 2.2 %collective-permute-start.4 = (bf16[64,1536]{1,0:T(8,128)(2,1)S(1)}, bf16[64,1536]{1,0:T(8,128)(2,1)S(1)}, u32[]{:S(2)}, u32[]{:S(2)}) collective-permute-start(bf16[64,1536]{1,0:T(8,128)(2,1)S(1)} %slice_bitcast_fusion), channel_id=1, source_target_pairs={{0,8},{1,9},{2,10},{3,11},{4,12},{5,13},{6,14},{7,15},{8,0},{9,1},... | collective-permute-start | bytes 589832 | tf_op jit(solution)/shard_map/ppermute | solution.py:24
  19.2 4.2 %collective-permute-done.4 = bf16[64,1536]{1,0:T(8,128)(2,1)S(1)} collective-permute-done((bf16[64,1536]{1,0:T(8,128)(2,1)S(1)}, bf16[64,1536]{1,0:T(8,128)(2,1)S(1)}, u32[]{:S(2)}, u32[]{:S(2)}) %collective-permute-start.4) | collective-permute-done | bytes 196640 | tf_op jit(solution)/shard_map/ppermute | solution.py:24
  28.4 2.1 %collective-permute-done.5 = bf16[3,48,384]{2,1,0:T(8,128)(2,1)} collective-permute-done((bf16[3,48,384]{2,1,0:T(8,128)(2,1)}, bf16[3,48,384]{2,1,0:T(8,128)(2,1)}, u32[]{:S(2)}, u32[]{:S(2)}) %collective-permute-start.5) | collective-permute-done | bytes 110624 | tf_op jit(solution)/shard_map/ppermute | solution.py:24
  33.7 2.6 %collective-permute-start.9 = (bf16[4,48,384]{2,1,0:T(8,128)(2,1)S(1)}, bf16[4,48,384]{2,1,0:T(8,128)(2,1)S(1)}, u32[]{:S(2)}, u32[]{:S(2)}) collective-permute-start(bf16[4,48,384]{2,1,0:T(8,128)(2,1)S(1)} %pad_maximum_fusion.2), channel_id=1, source_target_pairs={{0,32},{1,33},{2,34},{3,35},{4,36},{5,37},{6,38},{7,39},{8,40},{9,... | collective-permute-start | bytes 442376 | tf_op jit(solution)/shard_map/ppermute | solution.py:24
  37.4 2.2 %collective-permute-done.6 = bf16[64,1536]{1,0:T(8,128)(2,1)S(1)} collective-permute-done((bf16[64,1536]{1,0:T(8,128)(2,1)S(1)}, bf16[64,1536]{1,0:T(8,128)(2,1)S(1)}, u32[]{:S(2)}, u32[]{:S(2)}) %collective-permute-start.6) | collective-permute-done | bytes 196640 | tf_op jit(solution)/shard_map/ppermute | solution.py:24
  41.3 3.4 %collective-permute-start.11 = (bf16[128,1536]{1,0:T(8,128)(2,1)S(1)}, bf16[128,1536]{1,0:T(8,128)(2,1)S(1)}, u32[]{:S(2)}, u32[]{:S(2)}) collective-permute-start(bf16[128,1536]{1,0:T(8,128)(2,1)S(1)} %pad_maximum_fusion.1.x0), channel_id=1, source_target_pairs={{0,16},{1,17},{2,18},{3,19},{4,20},{5,21},{6,22},{7,23},{16,32},{1... | collective-permute-start | bytes 1179656 | tf_op jit(solution)/shard_map/ppermute | solution.py:24
  47.1 2.0 %collective-permute-start.14 = (bf16[4,4,48,384]{3,2,1,0:T(8,128)(2,1)S(1)}, bf16[4,4,48,384]{3,2,1,0:T(8,128)(2,1)S(1)}, u32[]{:S(2)}, u32[]{:S(2)}) collective-permute-start(bf16[4,4,48,384]{3,2,1,0:T(8,128)(2,1)S(1)} %pad_maximum_fusion.far0), channel_id=1, source_target_pairs={{0,3},{1,0},{2,1},{3,2},{4,7},{5,4},{6,5},{7,6},{8,11},{9,8},{10,9... | collective-permute-start | bytes 1769480 | tf_op jit(solution)/shard_map/ppermute | solution.py:24
  49.3 4.2 %shard_map.68 = (bf16[2,256,1536]{2,1,0:T(8,128)(2,1)}, bf16[256,1536]{1,0:T(8,128)(2,1)}, f32[256,384]{1,0:T(8,128)S(1)}, f32[256,192]{1,0:T(8,128)S(1)}, bf16[...) custom-call(s32[6]{0:T(128)S(1)} %stack.42.meta, ...), custom_call_target="tpu_custom_call" | custom-call | flops 1 | bytes 1 | tf_op jit(solution)/shard_map/pallas_call | solution.py:55
  53.5 2.0 %collective-permute-start.13 = (bf16[128,1536]{1,0:T(8,128)(2,1)S(1)}, bf16[128,1536]{1,0:T(8,128)(2,1)S(1)}, u32[]{:S(2)}, u32[]{:S(2)}) collective-permute-start(bf16[128,1536]{1,0:T(8,128)(2,1)S(1)} %collective-permute-done.11.x2), channel_id=1, source_target_pairs={{0,64},{1,65},{2,66},{3,67},{4,68},{5,69},{6,70},{7,71},{8,72},{9,... | collective-permute-start | bytes 1179656 | tf_op jit(solution)/shard_map/ppermute | solution.py:24
  60.2 10.2 %collective-permute-done.15.far2 = bf16[4,4,48,384]{3,2,1,0:T(8,128)(2,1)S(1)} collective-permute-done((bf16[4,4,48,384]{3,2,1,0:T(8,128)(2,1)S(1)}, bf16[4,4,48,384]{3,2,1,0:T(8,128)(2,1)S(1)}, u32[]{:S(2)}, u32[]{:S(2)}) %collective-permute-start.15) | collective-permute-done | bytes 589856 | tf_op jit(solution)/shard_map/ppermute | solution.py:24
  71.7 3.5 %collective-permute-start.20 = (bf16[768,256]{1,0:T(8,128)(2,1)S(1)}, bf16[768,256]{1,0:T(8,128)(2,1)S(1)}, u32[]{:S(2)}, u32[]{:S(2)}) collective-permute-start(bf16[768,256]{1,0:T(8,128)(2,1)S(1)} %get-tuple-element.132), channel_id=1, source_target_pairs={{0,32},{1,33},{2,34},{3,35},{4,36},{5,37},{6,38},{7,39},{8,40},{9,... | collective-permute-start | bytes 1179656 | tf_op jit(solution)/shard_map/ppermute | solution.py:24
  76.0 5.1 %shard_map.70 = (bf16[256,384]{1,0:T(8,128)(2,1)S(1)}, bf16[384,256]{1,0:T(8,128)(2,1)S(1)}, bf16[3,16,48,384]{3,2,1,0:T(8,128)(2,1)}, bf16[768,256]{1,0:T(8,128...) custom-call(s32[6]{0:T(128)S(1)} %stack.42.meta, ...), custom_call_target="tpu_custom_call" | custom-call | flops 1 | bytes 1 | tf_op jit(solution)/shard_map/pallas_call | solution.py:55
  82.3 2.4 %collective-permute-done.20.x2 = bf16[768,256]{1,0:T(8,128)(2,1)S(1)} collective-permute-done((bf16[768,256]{1,0:T(8,128)(2,1)S(1)}, bf16[768,256]{1,0:T(8,128)(2,1)S(1)}, u32[]{:S(2)}, u32[]{:S(2)}) %collective-permute-start.20) | collective-permute-done | bytes 393248 | tf_op jit(solution)/shard_map/ppermute | solution.py:24
  87.8 2.3 %collective-permute-done.17.flipped = bf16[256,384]{1,0:T(8,128)(2,1)S(1)} collective-permute-done((bf16[256,384]{1,0:T(8,128)(2,1)S(1)}, bf16[256,384]{1,0:T(8,128)(2,1)S(1)}, u32[]{:S(2)}, u32[]{:S(2)}) %collective-permute-start.17) | collective-permute-done | bytes 196640 | tf_op jit(solution)/shard_map/ppermute | solution.py:24
  90.2 2.9 %collective-permute-start.26 = (bf16[4,96,384]{2,1,0:T(8,128)(2,1)S(1)}, bf16[4,96,384]{2,1,0:T(8,128)(2,1)S(1)}, u32[]{:S(2)}, u32[]{:S(2)}) collective-permute-start(bf16[4,96,384]{2,1,0:T(8,128)(2,1)S(1)} %get-tuple-element.144), channel_id=1, source_target_pairs={{0,32},{1,33},{2,34},{3,35},{4,36},{5,37},{6,38},{7,39},{8,40},{9,... | collective-permute-start | bytes 884744 | tf_op jit(solution)/shard_map/ppermute | solution.py:24
  94.4 1.9 %shard_map.72.conv = f32[1152,384]{1,0:T(8,128)S(1)} custom-call(s32[6]{0:T(128)S(1)} %stack.42.meta, bf16[768,256]{1,0:T(8,128)(2,1)S(1)} %get-tuple-element.128.x0, bf16[768,256]{1,0:T(8,128)(2,1)S(1)} %collective-permute-done.19.x1, bf16[768,256]{1,0:T(8,128)(2,1)S(1)} %collective-permute-done.20.x2, bf16[768,256]{1,0:T(8,128)(2,1)S(1)} %collective-permute-done.21.x3, ...), custom_call_target="tpu_custom_call" | custom-call | flops 1 | bytes 1 | tf_op jit(solution)/shard_map/pallas_call | solution.py:55
  97.3 2.9 %collective-permute-done.26.p2 = bf16[4,96,384]{2,1,0:T(8,128)(2,1)S(1)} collective-permute-done((bf16[4,96,384]{2,1,0:T(8,128)(2,1)S(1)}, bf16[4,96,384]{2,1,0:T(8,128)(2,1)S(1)}, u32[]{:S(2)}, u32[]{:S(2)}) %collective-permute-start.26) | collective-permute-done | bytes 294944 | tf_op jit(solution)/shard_map/ppermute | solution.py:24
  104.8 2.0 %collective-permute-start.18 = (bf16[256,384]{1,0:T(8,128)(2,1)S(1)}, bf16[256,384]{1,0:T(8,128)(2,1)S(1)}, u32[]{:S(2)}, u32[]{:S(2)}) collective-permute-start(bf16[256,384]{1,0:T(8,128)(2,1)S(1)} %collective-permute-done.17.flipped), channel_id=1, source_target_pairs={{0,16},{1,17},{2,18},{3,19},{4,20},{5,21},{6,22},{7,23},{16,32},{1... | collective-permute-start | bytes 589832 | tf_op jit(solution)/shard_map/ppermute | solution.py:24
  106.8 4.8 %collective-permute-done.28.got1 = bf16[384,384]{1,0:T(8,128)(2,1)S(1)} collective-permute-done((bf16[384,384]{1,0:T(8,128)(2,1)S(1)}, bf16[384,384]{1,0:T(8,128)(2,1)S(1)}, u32[]{:S(2)}, u32[]{:S(2)}) %collective-permute-start.28) | collective-permute-done | bytes 294944 | tf_op jit(solution)/shard_map/ppermute | solution.py:24
  114.4 7.1 %all-to-all-start = ((bf16[8,48,384]{2,1,0:T(8,128)(2,1)}), bf16[8,48,384]{2,1,0:T(8,128)(2,1)}, u32[]{:S(2)}, u32[]{:S(2)}) async-start(bf16[8,48,384]{2,1,0:T(8,128)(2,1)} %copy-done.10), calls=%async_computation | async-start | bytes 589824 | tf_op jit(solution)/shard_map/all_to_all | solution.py:363
  124.3 2.1 %shard_map.75 = (f32[128,1536]{1,0:T(8,128)S(1)}, f32[128,1536]{1,0:T(8,128)S(1)}) custom-call(s32[6]{0:T(128)S(1)} %stack.42.meta, bf16[256,384]{1,0:T(8,128)(2,1)S(1)} %copy-done.17, bf16[256,384]{1,0:T(8,128)(2,1)S(1)} %copy-done.19, bf16[256,384]{1,0:T(8,128)(2,1)S(1)} %copy-done.21, bf16[3,384,384]{2,1,0:T(8,128)(2,1)S(1)} %copy-done.1, ...), custom_call_target="tpu_custom_call" | custom-call | flops 1 | bytes 1 | tf_op jit(solution)/shard_map/pallas_call | solution.py:55
  128.2 5.3 %all-to-all-done.parts = bf16[8,48,384]{2,1,0:T(8,128)(2,1)} async-done(((bf16[8,48,384]{2,1,0:T(8,128)(2,1)}), bf16[8,48,384]{2,1,0:T(8,128)(2,1)}, u32[]{:S(2)}, u32[]{:S(2)}) %all-to-all-start) | async-done | bytes 294944 | tf_op jit(solution)/shard_map/all_to_all | solution.py:363
  137.3 2.1 %fusion.2 = bf16[1,128,1536]{2,1,0:T(8,128)(2,1)} fusion(f32[128,1536]{1,0:T(8,128)S(1)} %collective-permute-done.31, f32[128,1536]{1,0:T(8,128)} %copy-done.12, bf16[1,128,1536]{2,1,0:T(8,128)(2,1)} %param.5), kind=kLoop, calls=%fused_computation.6 | loop fusion | flops 786432 | bytes 2359296 | tf_op jit(solution)/shard_map/broadcast_in_dim | solution.py:374
  (121 shorter events, 50.1 us)
Async XLA Ops:
  1.7 21.7 %collective-permute-start = (bf16[3,48,768]{2,1,0:T(8,128)(2,1)S(1)}, bf16[3,48,768]{2,1,0:T(8,128)(2,1)S(1)}, u32[]{:S(2)}, u32[]{:S(2)}) collective-permute-start(bf16[3,48,768]{2,1,0:T(8,128)(2,1)S(1)} %constant_dynamic-slice_fusion.4), channel_id=1, source_target_pairs={{0,140},{1,141},{2,142},{3,143},{4,136},{5,137},{6,138},{7,139},{8... | collective-permute-start | bytes 663560 | tf_op jit(solution)/shard_map/ppermute | solution.py:24
  2.4 12.7 %collective-permute-start.2 = (bf16[128,1536]{1,0:T(8,128)(2,1)}, bf16[128,1536]{1,0:T(8,128)(2,1)S(1)}, u32[]{:S(2)}, u32[]{:S(2)}) collective-permute-start(bf16[128,1536]{1,0:T(8,128)(2,1)} %bitcast.22), channel_id=1, source_target_pairs={{0,64},{1,65},{2,66},{3,67},{4,68},{5,69},{6,70},{7,71},{8,72},{9,... | collective-permute-start | bytes 1179656 | tf_op jit(solution)/shard_map/ppermute | solution.py:24
  11.1 12.4 %collective-permute-start.3 = (bf16[128,1536]{1,0:T(8,128)(2,1)}, bf16[128,1536]{1,0:T(8,128)(2,1)S(1)}, u32[]{:S(2)}, u32[]{:S(2)}) collective-permute-start(bf16[128,1536]{1,0:T(8,128)(2,1)} %bitcast.20), channel_id=1, source_target_pairs={{0,64},{1,65},{2,66},{3,67},{4,68},{5,69},{6,70},{7,71},{8,72},{9,... | collective-permute-start | bytes 1179656 | tf_op jit(solution)/shard_map/ppermute | solution.py:24
  12.1 11.3 %collective-permute-start.4 = (bf16[64,1536]{1,0:T(8,128)(2,1)S(1)}, bf16[64,1536]{1,0:T(8,128)(2,1)S(1)}, u32[]{:S(2)}, u32[]{:S(2)}) collective-permute-start(bf16[64,1536]{1,0:T(8,128)(2,1)S(1)} %slice_bitcast_fusion), channel_id=1, source_target_pairs={{0,8},{1,9},{2,10},{3,11},{4,12},{5,13},{6,14},{7,15},{8,0},{9,1},... | collective-permute-start | bytes 589832 | tf_op jit(solution)/shard_map/ppermute | solution.py:24
  24.1 16.5 %collective-permute-start.7 = (bf16[3,384,384]{2,1,0:T(8,128)(2,1)S(1)}, bf16[3,384,384]{2,1,0:T(8,128)(2,1)S(1)}, u32[]{:S(2)}, u32[]{:S(2)}) collective-permute-start(bf16[3,384,384]{2,1,0:T(8,128)(2,1)S(1)} %get-tuple-element.90), channel_id=1, source_target_pairs={{0,64},{1,65},{2,66},{3,67},{4,68},{5,69},{6,70},{7,71},{8,72},{9,... | collective-permute-start | bytes 2654216 | tf_op jit(solution)/shard_map/ppermute | solution.py:24
  28.3 11.3 %collective-permute-start.6 = (bf16[64,1536]{1,0:T(8,128)(2,1)S(1)}, bf16[64,1536]{1,0:T(8,128)(2,1)S(1)}, u32[]{:S(2)}, u32[]{:S(2)}) collective-permute-start(bf16[64,1536]{1,0:T(8,128)(2,1)S(1)} %slice.11), channel_id=1, source_target_pairs={{0,8},{1,9},{2,10},{3,11},{4,12},{5,13},{6,14},{7,15},{8,0},{9,1},... | collective-permute-start | bytes 589832 | tf_op jit(solution)/shard_map/ppermute | solution.py:24
  40.6 8.6 %collective-permute-start.12 = (bf16[128,1536]{1,0:T(8,128)(2,1)S(1)}, bf16[128,1536]{1,0:T(8,128)(2,1)S(1)}, u32[]{:S(2)}, u32[]{:S(2)}) collective-permute-start(bf16[128,1536]{1,0:T(8,128)(2,1)S(1)} %pad_maximum_fusion.1.x0), channel_id=1, source_target_pairs={{0,64},{1,65},{2,66},{3,67},{4,68},{5,69},{6,70},{7,71},{8,72},{9,... | collective-permute-start | bytes 1179656 | tf_op jit(solution)/shard_map/ppermute | solution.py:24
  41.3 12.1 %collective-permute-start.11 = (bf16[128,1536]{1,0:T(8,128)(2,1)S(1)}, bf16[128,1536]{1,0:T(8,128)(2,1)S(1)}, u32[]{:S(2)}, u32[]{:S(2)}) collective-permute-start(bf16[128,1536]{1,0:T(8,128)(2,1)S(1)} %pad_maximum_fusion.1.x0), channel_id=1, source_target_pairs={{0,16},{1,17},{2,18},{3,19},{4,20},{5,21},{6,22},{7,23},{16,32},{1... | collective-permute-start | bytes 1179656 | tf_op jit(solution)/shard_map/ppermute | solution.py:24
  44.8 15.4 %collective-permute-start.16 = (bf16[4,4,48,384]{3,2,1,0:T(8,128)(2,1)S(1)}, bf16[4,4,48,384]{3,2,1,0:T(8,128)(2,1)S(1)}, u32[]{:S(2)}, u32[]{:S(2)}) collective-permute-start(bf16[4,4,48,384]{3,2,1,0:T(8,128)(2,1)S(1)} %pad_maximum_fusion.far0), channel_id=1, source_target_pairs={{0,1},{1,2},{2,3},{3,0},{4,5},{5,6},{6,7},{7,4},{8,9},{9,10},{10,1... | collective-permute-start | bytes 1769480 | tf_op jit(solution)/shard_map/ppermute | solution.py:24
  45.2 25.2 %collective-permute-start.15 = (bf16[4,4,48,384]{3,2,1,0:T(8,128)(2,1)S(1)}, bf16[4,4,48,384]{3,2,1,0:T(8,128)(2,1)S(1)}, u32[]{:S(2)}, u32[]{:S(2)}) collective-permute-start(bf16[4,4,48,384]{3,2,1,0:T(8,128)(2,1)S(1)} %pad_maximum_fusion.far0), channel_id=1, source_target_pairs={{0,2},{1,3},{2,0},{3,1},{4,6},{5,7},{6,4},{7,5},{8,10},{9,11},{10,... | collective-permute-start | bytes 1769480 | tf_op jit(solution)/shard_map/ppermute | solution.py:24
  47.1 23.3 %collective-permute-start.14 = (bf16[4,4,48,384]{3,2,1,0:T(8,128)(2,1)S(1)}, bf16[4,4,48,384]{3,2,1,0:T(8,128)(2,1)S(1)}, u32[]{:S(2)}, u32[]{:S(2)}) collective-permute-start(bf16[4,4,48,384]{3,2,1,0:T(8,128)(2,1)S(1)} %pad_maximum_fusion.far0), channel_id=1, source_target_pairs={{0,3},{1,0},{2,1},{3,2},{4,7},{5,4},{6,5},{7,6},{8,11},{9,8},{10,9... | collective-permute-start | bytes 1769480 | tf_op jit(solution)/shard_map/ppermute | solution.py:24
  70.4 10.7 %collective-permute-start.19 = (bf16[768,256]{1,0:T(8,128)(2,1)S(1)}, bf16[768,256]{1,0:T(8,128)(2,1)S(1)}, u32[]{:S(2)}, u32[]{:S(2)}) collective-permute-start(bf16[768,256]{1,0:T(8,128)(2,1)S(1)} %get-tuple-element.129), channel_id=1, source_target_pairs={{0,16},{1,17},{2,18},{3,19},{4,20},{5,21},{6,22},{7,23},{8,24},{9,... | collective-permute-start | bytes 1179656 | tf_op jit(solution)/shard_map/ppermute | solution.py:24
  71.7 13.1 %collective-permute-start.20 = (bf16[768,256]{1,0:T(8,128)(2,1)S(1)}, bf16[768,256]{1,0:T(8,128)(2,1)S(1)}, u32[]{:S(2)}, u32[]{:S(2)}) collective-permute-start(bf16[768,256]{1,0:T(8,128)(2,1)S(1)} %get-tuple-element.132), channel_id=1, source_target_pairs={{0,32},{1,33},{2,34},{3,35},{4,36},{5,37},{6,38},{7,39},{8,40},{9,... | collective-permute-start | bytes 1179656 | tf_op jit(solution)/shard_map/ppermute | solution.py:24
  75.2 9.6 %collective-permute-start.21 = (bf16[768,256]{1,0:T(8,128)(2,1)S(1)}, bf16[768,256]{1,0:T(8,128)(2,1)S(1)}, u32[]{:S(2)}, u32[]{:S(2)}) collective-permute-start(bf16[768,256]{1,0:T(8,128)(2,1)S(1)} %get-tuple-element.135), channel_id=1, source_target_pairs={{0,48},{1,49},{2,50},{3,51},{4,52},{5,53},{6,54},{7,55},{8,56},{9,... | collective-permute-start | bytes 1179656 | tf_op jit(solution)/shard_map/ppermute | solution.py:24
  81.1 12.0 %collective-permute-start.22 = (bf16[768,256]{1,0:T(8,128)(2,1)S(1)}, bf16[768,256]{1,0:T(8,128)(2,1)S(1)}, u32[]{:S(2)}, u32[]{:S(2)}) collective-permute-start(bf16[768,256]{1,0:T(8,128)(2,1)S(1)} %get-tuple-element.139), channel_id=1, source_target_pairs={{0,16},{1,17},{2,18},{3,19},{4,20},{5,21},{6,22},{7,23},{8,24},{9,... | collective-permute-start | bytes 1179656 | tf_op jit(solution)/shard_map/ppermute | solution.py:24
  84.7 9.7 %collective-permute-start.23 = (bf16[768,256]{1,0:T(8,128)(2,1)S(1)}, bf16[768,256]{1,0:T(8,128)(2,1)S(1)}, u32[]{:S(2)}, u32[]{:S(2)}) collective-permute-start(bf16[768,256]{1,0:T(8,128)(2,1)S(1)} %get-tuple-element.140), channel_id=1, source_target_pairs={{0,32},{1,33},{2,34},{3,35},{4,36},{5,37},{6,38},{7,39},{8,40},{9,... | collective-permute-start | bytes 1179656 | tf_op jit(solution)/shard_map/ppermute | solution.py:24
  84.7 9.7 %collective-permute-start.24 = (bf16[768,256]{1,0:T(8,128)(2,1)S(1)}, bf16[768,256]{1,0:T(8,128)(2,1)S(1)}, u32[]{:S(2)}, u32[]{:S(2)}) collective-permute-start(bf16[768,256]{1,0:T(8,128)(2,1)S(1)} %get-tuple-element.141), channel_id=1, source_target_pairs={{0,48},{1,49},{2,50},{3,51},{4,52},{5,53},{6,54},{7,55},{8,56},{9,... | collective-permute-start | bytes 1179656 | tf_op jit(solution)/shard_map/ppermute | solution.py:24
  87.8 9.6 %collective-permute-start.25 = (bf16[4,96,384]{2,1,0:T(8,128)(2,1)S(1)}, bf16[4,96,384]{2,1,0:T(8,128)(2,1)S(1)}, u32[]{:S(2)}, u32[]{:S(2)}) collective-permute-start(bf16[4,96,384]{2,1,0:T(8,128)(2,1)S(1)} %get-tuple-element.143), channel_id=1, source_target_pairs={{0,16},{1,17},{2,18},{3,19},{4,20},{5,21},{6,22},{7,23},{8,24},{9,... | collective-permute-start | bytes 884744 | tf_op jit(solution)/shard_map/ppermute | solution.py:24
  90.2 10.1 %collective-permute-start.26 = (bf16[4,96,384]{2,1,0:T(8,128)(2,1)S(1)}, bf16[4,96,384]{2,1,0:T(8,128)(2,1)S(1)}, u32[]{:S(2)}, u32[]{:S(2)}) collective-permute-start(bf16[4,96,384]{2,1,0:T(8,128)(2,1)S(1)} %get-tuple-element.144), channel_id=1, source_target_pairs={{0,32},{1,33},{2,34},{3,35},{4,36},{5,37},{6,38},{7,39},{8,40},{9,... | collective-permute-start | bytes 884744 | tf_op jit(solution)/shard_map/ppermute | solution.py:24
  101.6 10.0 %collective-permute-start.28 = (bf16[384,384]{1,0:T(8,128)(2,1)S(1)}, bf16[384,384]{1,0:T(8,128)(2,1)S(1)}, u32[]{:S(2)}, u32[]{:S(2)}) collective-permute-start(bf16[384,384]{1,0:T(8,128)(2,1)S(1)} %get-tuple-element.147), channel_id=1, source_target_pairs={{0,1},{1,2},{2,3},{3,0},{4,5},{5,6},{6,7},{7,4},{8,9},{9,10},{10,1... | collective-permute-start | bytes 884744 | tf_op jit(solution)/shard_map/ppermute | solution.py:24
  101.6 9.9 %collective-permute-start.29 = (bf16[384,384]{1,0:T(8,128)(2,1)S(1)}, bf16[384,384]{1,0:T(8,128)(2,1)S(1)}, u32[]{:S(2)}, u32[]{:S(2)}) collective-permute-start(bf16[384,384]{1,0:T(8,128)(2,1)S(1)} %get-tuple-element.148), channel_id=1, source_target_pairs={{0,2},{1,3},{2,0},{3,1},{4,6},{5,7},{6,4},{7,5},{8,10},{9,11},{10,... | collective-permute-start | bytes 884744 | tf_op jit(solution)/shard_map/ppermute | solution.py:24
  103.0 9.2 %collective-permute-start.30 = (bf16[384,384]{1,0:T(8,128)(2,1)S(1)}, bf16[384,384]{1,0:T(8,128)(2,1)S(1)}, u32[]{:S(2)}, u32[]{:S(2)}) collective-permute-start(bf16[384,384]{1,0:T(8,128)(2,1)S(1)} %get-tuple-element.149), channel_id=1, source_target_pairs={{0,3},{1,0},{2,1},{3,2},{4,7},{5,4},{6,5},{7,6},{8,11},{9,8},{10,9... | collective-permute-start | bytes 884744 | tf_op jit(solution)/shard_map/ppermute | solution.py:24
  104.8 8.9 %collective-permute-start.18 = (bf16[256,384]{1,0:T(8,128)(2,1)S(1)}, bf16[256,384]{1,0:T(8,128)(2,1)S(1)}, u32[]{:S(2)}, u32[]{:S(2)}) collective-permute-start(bf16[256,384]{1,0:T(8,128)(2,1)S(1)} %collective-permute-done.17.flipped), channel_id=1, source_target_pairs={{0,16},{1,17},{2,18},{3,19},{4,20},{5,21},{6,22},{7,23},{16,32},{1... | collective-permute-start | bytes 589832 | tf_op jit(solution)/shard_map/ppermute | solution.py:24
  114.4 19.2 %all-to-all-start = ((bf16[8,48,384]{2,1,0:T(8,128)(2,1)}), bf16[8,48,384]{2,1,0:T(8,128)(2,1)}, u32[]{:S(2)}, u32[]{:S(2)}) async-start(bf16[8,48,384]{2,1,0:T(8,128)(2,1)} %copy-done.10), calls=%async_computation | async-start | bytes 589824 | tf_op jit(solution)/shard_map/all_to_all | solution.py:363
  (35 other events, 264.1 us)

commit v9 on v8

--- a/solution.py
+++ b/solution.py
@@ -58,7 +58,7 @@
         in_specs=[pl.BlockSpec(memory_space=pltpu.SMEM)] + [vmem] * len(arrays),
         out_specs=[vmem] * len(outs),
         scratch_shapes=scratch,
-        compiler_params=pltpu.CompilerParams(vmem_limit_bytes=48 * 1024 * 1024),
+        compiler_params=pltpu.CompilerParams(vmem_limit_bytes=16 * 1024 * 1024),
         cost_estimate=pl.CostEstimate(flops=1, bytes_accessed=1, transcendentals=0),
     )(scalars, *arrays)
 

time: 140 us -> 140 us (level)
  waiting for transfers between devices: 41.6 us -> 46.7 us
  Pallas kernels: 20.5 us -> 17.1 us
  local copies, waits for them, and re-layouts: 14.8 us -> 11.8 us
    ppermute x33, waiting for transfers between devices: 36.3 us -> 41.5 us  [send(): return lax.ppermute(value, ('dp', 'seq'), pairs)]
    pallas_call x11, Pallas kernels: 20.5 us -> 17.1 us  [run(): pl.pallas_call(kernel, out_shape=outs, in_specs=[pl.BlockSpec(memory_spac...]
    unnamed x50 -> x34, local copies, waits for them, and re-layouts: 11.1 us -> 8.14 us
  transfers between devices with their start and end apart: 34 -> 34, of which waited for: 16 -> 19; matrix products, arithmetic and copies ran while one was open for 5% -> 5% of each run, Pallas kernels for 14% -> 12%
where the time goes in v9:
time: 140 us; the launch traced here: 139 us
  starting transfers between devices  56.6 us (40%)
  waiting for transfers between devices  46.7 us (33%)
  Pallas kernels  17.1 us (12%)
  local copies, waits for them, and re-layouts  11.8 us (8%)
  other arithmetic  6.08 us (4%)
    ppermute x33, starting transfers between devices, send(): return lax.ppermute(value, ('dp', 'seq'), pairs)  49.5 us
    ppermute x33, waiting for transfers between devices, send(): return lax.ppermute(value, ('dp', 'seq'), pairs)  41.5 us
    pallas_call x11, Pallas kernels, run(): pl.pallas_call(kernel, out_shape=outs, in_specs=[pl.BlockSpec(memory_spac...  17.1 us
    unnamed x34, local copies, waits for them, and re-layouts  8.14 us
    all_to_all x1, starting transfers between devices, local(): by_z = lax.all_to_all(by_z, ('dp', 'seq'), 0, 0, axis_index_groups=rings)  7.16 us
    all_to_all x1, waiting for transfers between devices, local(): by_z = lax.all_to_all(by_z, ('dp', 'seq'), 0, 0, axis_index_groups=rings)  5.25 us
  transfers between devices with their start and end apart: 34, of which 19 were waited for; matrix products, arithmetic and copies ran while one was open for 5% of the time, Pallas kernels for 12%

profile of v9, /device:TPU:1, one launch (start us, length us, event | category | flops | bytes accessed | tf_op | source)
XLA Modules:
  0.0 139.3 jit_solution(14692638938586497870)
XLA Ops:
  2.4 8.7 %collective-permute-start.2 = (bf16[128,1536]{1,0:T(8,128)(2,1)}, bf16[128,1536]{1,0:T(8,128)(2,1)S(1)}, u32[]{:S(2)}, u32[]{:S(2)}) collective-permute-start(bf16[128,1536]{1,0:T(8,128)(2,1)} %bitcast.22), channel_id=1, source_target_pairs={{0,64},{1,65},{2,66},{3,67},{4,68},{5,69},{6,70},{7,71},{8,72},{9,... | collective-permute-start | bytes 1179656 | tf_op jit(solution)/shard_map/ppermute | solution.py:24
  12.1 2.2 %collective-permute-start.4 = (bf16[64,1536]{1,0:T(8,128)(2,1)S(1)}, bf16[64,1536]{1,0:T(8,128)(2,1)S(1)}, u32[]{:S(2)}, u32[]{:S(2)}) collective-permute-start(bf16[64,1536]{1,0:T(8,128)(2,1)S(1)} %slice_bitcast_fusion), channel_id=1, source_target_pairs={{0,8},{1,9},{2,10},{3,11},{4,12},{5,13},{6,14},{7,15},{8,0},{9,1},... | collective-permute-start | bytes 589832 | tf_op jit(solution)/shard_map/ppermute | solution.py:24
  19.2 4.2 %collective-permute-done.4 = bf16[64,1536]{1,0:T(8,128)(2,1)S(1)} collective-permute-done((bf16[64,1536]{1,0:T(8,128)(2,1)S(1)}, bf16[64,1536]{1,0:T(8,128)(2,1)S(1)}, u32[]{:S(2)}, u32[]{:S(2)}) %collective-permute-start.4) | collective-permute-done | bytes 196640 | tf_op jit(solution)/shard_map/ppermute | solution.py:24
  28.4 2.1 %collective-permute-done.5 = bf16[3,48,384]{2,1,0:T(8,128)(2,1)} collective-permute-done((bf16[3,48,384]{2,1,0:T(8,128)(2,1)}, bf16[3,48,384]{2,1,0:T(8,128)(2,1)}, u32[]{:S(2)}, u32[]{:S(2)}) %collective-permute-start.5) | collective-permute-done | bytes 110624 | tf_op jit(solution)/shard_map/ppermute | solution.py:24
  33.7 2.6 %collective-permute-start.9 = (bf16[4,48,384]{2,1,0:T(8,128)(2,1)S(1)}, bf16[4,48,384]{2,1,0:T(8,128)(2,1)S(1)}, u32[]{:S(2)}, u32[]{:S(2)}) collective-permute-start(bf16[4,48,384]{2,1,0:T(8,128)(2,1)S(1)} %pad_maximum_fusion.2), channel_id=1, source_target_pairs={{0,32},{1,33},{2,34},{3,35},{4,36},{5,37},{6,38},{7,39},{8,40},{9,... | collective-permute-start | bytes 442376 | tf_op jit(solution)/shard_map/ppermute | solution.py:24
  37.4 2.2 %collective-permute-done.6 = bf16[64,1536]{1,0:T(8,128)(2,1)S(1)} collective-permute-done((bf16[64,1536]{1,0:T(8,128)(2,1)S(1)}, bf16[64,1536]{1,0:T(8,128)(2,1)S(1)}, u32[]{:S(2)}, u32[]{:S(2)}) %collective-permute-start.6) | collective-permute-done | bytes 196640 | tf_op jit(solution)/shard_map/ppermute | solution.py:24
  41.3 3.4 %collective-permute-start.11 = (bf16[128,1536]{1,0:T(8,128)(2,1)S(1)}, bf16[128,1536]{1,0:T(8,128)(2,1)S(1)}, u32[]{:S(2)}, u32[]{:S(2)}) collective-permute-start(bf16[128,1536]{1,0:T(8,128)(2,1)S(1)} %pad_maximum_fusion.1.x0), channel_id=1, source_target_pairs={{0,16},{1,17},{2,18},{3,19},{4,20},{5,21},{6,22},{7,23},{16,32},{1... | collective-permute-start | bytes 1179656 | tf_op jit(solution)/shard_map/ppermute | solution.py:24
  47.1 2.0 %collective-permute-start.14 = (bf16[4,4,48,384]{3,2,1,0:T(8,128)(2,1)S(1)}, bf16[4,4,48,384]{3,2,1,0:T(8,128)(2,1)S(1)}, u32[]{:S(2)}, u32[]{:S(2)}) collective-permute-start(bf16[4,4,48,384]{3,2,1,0:T(8,128)(2,1)S(1)} %pad_maximum_fusion.far0), channel_id=1, source_target_pairs={{0,3},{1,0},{2,1},{3,2},{4,7},{5,4},{6,5},{7,6},{8,11},{9,8},{10,9... | collective-permute-start | bytes 1769480 | tf_op jit(solution)/shard_map/ppermute | solution.py:24
  49.2 2.3 %shard_map.68 = (bf16[2,256,1536]{2,1,0:T(8,128)(2,1)S(1)}, bf16[256,1536]{1,0:T(8,128)(2,1)S(1)}, f32[256,384]{1,0:T(8,128)S(1)}, f32[256,192]{1,0:T(8,128)S(1)...) custom-call(s32[6]{0:T(128)S(1)} %stack.42.meta, ...), custom_call_target="tpu_custom_call" | custom-call | flops 1 | bytes 1 | tf_op jit(solution)/shard_map/pallas_call | solution.py:55
  57.1 2.8 %collective-permute-done.16.far3 = bf16[4,4,48,384]{3,2,1,0:T(8,128)(2,1)S(1)} collective-permute-done((bf16[4,4,48,384]{3,2,1,0:T(8,128)(2,1)S(1)}, bf16[4,4,48,384]{3,2,1,0:T(8,128)(2,1)S(1)}, u32[]{:S(2)}, u32[]{:S(2)}) %collective-permute-start.16) | collective-permute-done | bytes 589856 | tf_op jit(solution)/shard_map/ppermute | solution.py:24
  59.9 10.5 %collective-permute-done.15.far2 = bf16[4,4,48,384]{3,2,1,0:T(8,128)(2,1)S(1)} collective-permute-done((bf16[4,4,48,384]{3,2,1,0:T(8,128)(2,1)S(1)}, bf16[4,4,48,384]{3,2,1,0:T(8,128)(2,1)S(1)}, u32[]{:S(2)}, u32[]{:S(2)}) %collective-permute-start.15) | collective-permute-done | bytes 589856 | tf_op jit(solution)/shard_map/ppermute | solution.py:24
  71.7 3.5 %collective-permute-start.20 = (bf16[768,256]{1,0:T(8,128)(2,1)S(1)}, bf16[768,256]{1,0:T(8,128)(2,1)S(1)}, u32[]{:S(2)}, u32[]{:S(2)}) collective-permute-start(bf16[768,256]{1,0:T(8,128)(2,1)S(1)} %get-tuple-element.132), channel_id=1, source_target_pairs={{0,32},{1,33},{2,34},{3,35},{4,36},{5,37},{6,38},{7,39},{8,40},{9,... | collective-permute-start | bytes 1179656 | tf_op jit(solution)/shard_map/ppermute | solution.py:24
  76.0 2.6 %shard_map.70 = (bf16[256,384]{1,0:T(8,128)(2,1)S(1)}, bf16[384,256]{1,0:T(8,128)(2,1)S(1)}, bf16[3,16,48,384]{3,2,1,0:T(8,128)(2,1)S(1)}, bf16[768,256]{1,0:T(8...) custom-call(s32[6]{0:T(128)S(1)} %stack.42.meta, ...), custom_call_target="tpu_custom_call" | custom-call | flops 1 | bytes 1 | tf_op jit(solution)/shard_map/pallas_call | solution.py:55
  79.1 3.2 %collective-permute-start.22 = (bf16[768,256]{1,0:T(8,128)(2,1)S(1)}, bf16[768,256]{1,0:T(8,128)(2,1)S(1)}, u32[]{:S(2)}, u32[]{:S(2)}) collective-permute-start(bf16[768,256]{1,0:T(8,128)(2,1)S(1)} %get-tuple-element.139), channel_id=1, source_target_pairs={{0,16},{1,17},{2,18},{3,19},{4,20},{5,21},{6,22},{7,23},{8,24},{9,... | collective-permute-start | bytes 1179656 | tf_op jit(solution)/shard_map/ppermute | solution.py:24
  82.3 2.5 %collective-permute-done.20.x2 = bf16[768,256]{1,0:T(8,128)(2,1)S(1)} collective-permute-done((bf16[768,256]{1,0:T(8,128)(2,1)S(1)}, bf16[768,256]{1,0:T(8,128)(2,1)S(1)}, u32[]{:S(2)}, u32[]{:S(2)}) %collective-permute-start.20) | collective-permute-done | bytes 393248 | tf_op jit(solution)/shard_map/ppermute | solution.py:24
  87.9 2.3 %collective-permute-done.17.flipped = bf16[256,384]{1,0:T(8,128)(2,1)S(1)} collective-permute-done((bf16[256,384]{1,0:T(8,128)(2,1)S(1)}, bf16[256,384]{1,0:T(8,128)(2,1)S(1)}, u32[]{:S(2)}, u32[]{:S(2)}) %collective-permute-start.17) | collective-permute-done | bytes 196640 | tf_op jit(solution)/shard_map/ppermute | solution.py:24
  90.2 2.9 %collective-permute-start.26 = (bf16[4,96,384]{2,1,0:T(8,128)(2,1)S(1)}, bf16[4,96,384]{2,1,0:T(8,128)(2,1)S(1)}, u32[]{:S(2)}, u32[]{:S(2)}) collective-permute-start(bf16[4,96,384]{2,1,0:T(8,128)(2,1)S(1)} %get-tuple-element.144), channel_id=1, source_target_pairs={{0,32},{1,33},{2,34},{3,35},{4,36},{5,37},{6,38},{7,39},{8,40},{9,... | collective-permute-start | bytes 884744 | tf_op jit(solution)/shard_map/ppermute | solution.py:24
  97.4 2.9 %collective-permute-done.26.p2 = bf16[4,96,384]{2,1,0:T(8,128)(2,1)S(1)} collective-permute-done((bf16[4,96,384]{2,1,0:T(8,128)(2,1)S(1)}, bf16[4,96,384]{2,1,0:T(8,128)(2,1)S(1)}, u32[]{:S(2)}, u32[]{:S(2)}) %collective-permute-start.26) | collective-permute-done | bytes 294944 | tf_op jit(solution)/shard_map/ppermute | solution.py:24
  104.3 2.5 %collective-permute-start.18 = (bf16[256,384]{1,0:T(8,128)(2,1)S(1)}, bf16[256,384]{1,0:T(8,128)(2,1)S(1)}, u32[]{:S(2)}, u32[]{:S(2)}) collective-permute-start(bf16[256,384]{1,0:T(8,128)(2,1)S(1)} %collective-permute-done.17.flipped), channel_id=1, source_target_pairs={{0,16},{1,17},{2,18},{3,19},{4,20},{5,21},{6,22},{7,23},{16,32},{1... | collective-permute-start | bytes 589832 | tf_op jit(solution)/shard_map/ppermute | solution.py:24
  106.8 4.8 %collective-permute-done.28.got1 = bf16[384,384]{1,0:T(8,128)(2,1)S(1)} collective-permute-done((bf16[384,384]{1,0:T(8,128)(2,1)S(1)}, bf16[384,384]{1,0:T(8,128)(2,1)S(1)}, u32[]{:S(2)}, u32[]{:S(2)}) %collective-permute-start.28) | collective-permute-done | bytes 294944 | tf_op jit(solution)/shard_map/ppermute | solution.py:24
  114.4 7.2 %all-to-all-start = ((bf16[8,48,384]{2,1,0:T(8,128)(2,1)}), bf16[8,48,384]{2,1,0:T(8,128)(2,1)}, u32[]{:S(2)}, u32[]{:S(2)}) async-start(bf16[8,48,384]{2,1,0:T(8,128)(2,1)} %copy-done.3), calls=%async_computation | async-start | bytes 589824 | tf_op jit(solution)/shard_map/all_to_all | solution.py:363
  124.3 2.1 %shard_map.75 = (f32[128,1536]{1,0:T(8,128)S(1)}, f32[128,1536]{1,0:T(8,128)S(1)}) custom-call(s32[6]{0:T(128)S(1)} %stack.42.meta, bf16[256,384]{1,0:T(8,128)(2,1)S(1)} %copy-done.9, bf16[256,384]{1,0:T(8,128)(2,1)S(1)} %copy-done.11, bf16[256,384]{1,0:T(8,128)(2,1)S(1)} %copy-done.13, bf16[3,384,384]{2,1,0:T(8,128)(2,1)S(1)} %get-tuple-element.94.mine, ...), custom_call_target="tpu_custom_call" | custom-call | flops 1 | bytes 1 | tf_op jit(solution)/shard_map/pallas_call | solution.py:55
  128.2 5.2 %all-to-all-done.parts = bf16[8,48,384]{2,1,0:T(8,128)(2,1)} async-done(((bf16[8,48,384]{2,1,0:T(8,128)(2,1)}), bf16[8,48,384]{2,1,0:T(8,128)(2,1)}, u32[]{:S(2)}, u32[]{:S(2)}) %all-to-all-start) | async-done | bytes 294944 | tf_op jit(solution)/shard_map/all_to_all | solution.py:363
  137.2 2.1 %fusion.2 = bf16[1,128,1536]{2,1,0:T(8,128)(2,1)} fusion(f32[128,1536]{1,0:T(8,128)S(1)} %collective-permute-done.31, f32[128,1536]{1,0:T(8,128)} %copy-done.4, bf16[1,128,1536]{2,1,0:T(8,128)(2,1)} %param.5), kind=kLoop, calls=%fused_computation.6 | loop fusion | flops 786432 | bytes 2359296 | tf_op jit(solution)/shard_map/broadcast_in_dim | solution.py:374
  (105 shorter events, 51.6 us)
Async XLA Ops:
  1.7 21.7 %collective-permute-start = (bf16[3,48,768]{2,1,0:T(8,128)(2,1)S(1)}, bf16[3,48,768]{2,1,0:T(8,128)(2,1)S(1)}, u32[]{:S(2)}, u32[]{:S(2)}) collective-permute-start(bf16[3,48,768]{2,1,0:T(8,128)(2,1)S(1)} %constant_dynamic-slice_fusion.4), channel_id=1, source_target_pairs={{0,140},{1,141},{2,142},{3,143},{4,136},{5,137},{6,138},{7,139},{8... | collective-permute-start | bytes 663560 | tf_op jit(solution)/shard_map/ppermute | solution.py:24
  2.4 12.7 %collective-permute-start.2 = (bf16[128,1536]{1,0:T(8,128)(2,1)}, bf16[128,1536]{1,0:T(8,128)(2,1)S(1)}, u32[]{:S(2)}, u32[]{:S(2)}) collective-permute-start(bf16[128,1536]{1,0:T(8,128)(2,1)} %bitcast.22), channel_id=1, source_target_pairs={{0,64},{1,65},{2,66},{3,67},{4,68},{5,69},{6,70},{7,71},{8,72},{9,... | collective-permute-start | bytes 1179656 | tf_op jit(solution)/shard_map/ppermute | solution.py:24
  11.1 12.4 %collective-permute-start.3 = (bf16[128,1536]{1,0:T(8,128)(2,1)}, bf16[128,1536]{1,0:T(8,128)(2,1)S(1)}, u32[]{:S(2)}, u32[]{:S(2)}) collective-permute-start(bf16[128,1536]{1,0:T(8,128)(2,1)} %bitcast.20), channel_id=1, source_target_pairs={{0,64},{1,65},{2,66},{3,67},{4,68},{5,69},{6,70},{7,71},{8,72},{9,... | collective-permute-start | bytes 1179656 | tf_op jit(solution)/shard_map/ppermute | solution.py:24
  12.1 11.3 %collective-permute-start.4 = (bf16[64,1536]{1,0:T(8,128)(2,1)S(1)}, bf16[64,1536]{1,0:T(8,128)(2,1)S(1)}, u32[]{:S(2)}, u32[]{:S(2)}) collective-permute-start(bf16[64,1536]{1,0:T(8,128)(2,1)S(1)} %slice_bitcast_fusion), channel_id=1, source_target_pairs={{0,8},{1,9},{2,10},{3,11},{4,12},{5,13},{6,14},{7,15},{8,0},{9,1},... | collective-permute-start | bytes 589832 | tf_op jit(solution)/shard_map/ppermute | solution.py:24
  24.1 16.5 %collective-permute-start.7 = (bf16[3,384,384]{2,1,0:T(8,128)(2,1)}, bf16[3,384,384]{2,1,0:T(8,128)(2,1)S(1)}, u32[]{:S(2)}, u32[]{:S(2)}) collective-permute-start(bf16[3,384,384]{2,1,0:T(8,128)(2,1)} %get-tuple-element.90), channel_id=1, source_target_pairs={{0,64},{1,65},{2,66},{3,67},{4,68},{5,69},{6,70},{7,71},{8,72},{9,... | collective-permute-start | bytes 2654216 | tf_op jit(solution)/shard_map/ppermute | solution.py:24
  28.3 11.3 %collective-permute-start.6 = (bf16[64,1536]{1,0:T(8,128)(2,1)S(1)}, bf16[64,1536]{1,0:T(8,128)(2,1)S(1)}, u32[]{:S(2)}, u32[]{:S(2)}) collective-permute-start(bf16[64,1536]{1,0:T(8,128)(2,1)S(1)} %slice.11), channel_id=1, source_target_pairs={{0,8},{1,9},{2,10},{3,11},{4,12},{5,13},{6,14},{7,15},{8,0},{9,1},... | collective-permute-start | bytes 589832 | tf_op jit(solution)/shard_map/ppermute | solution.py:24
  40.6 8.6 %collective-permute-start.12 = (bf16[128,1536]{1,0:T(8,128)(2,1)S(1)}, bf16[128,1536]{1,0:T(8,128)(2,1)S(1)}, u32[]{:S(2)}, u32[]{:S(2)}) collective-permute-start(bf16[128,1536]{1,0:T(8,128)(2,1)S(1)} %pad_maximum_fusion.1.x0), channel_id=1, source_target_pairs={{0,64},{1,65},{2,66},{3,67},{4,68},{5,69},{6,70},{7,71},{8,72},{9,... | collective-permute-start | bytes 1179656 | tf_op jit(solution)/shard_map/ppermute | solution.py:24
  41.3 11.9 %collective-permute-start.11 = (bf16[128,1536]{1,0:T(8,128)(2,1)S(1)}, bf16[128,1536]{1,0:T(8,128)(2,1)S(1)}, u32[]{:S(2)}, u32[]{:S(2)}) collective-permute-start(bf16[128,1536]{1,0:T(8,128)(2,1)S(1)} %pad_maximum_fusion.1.x0), channel_id=1, source_target_pairs={{0,16},{1,17},{2,18},{3,19},{4,20},{5,21},{6,22},{7,23},{16,32},{1... | collective-permute-start | bytes 1179656 | tf_op jit(solution)/shard_map/ppermute | solution.py:24
  44.8 15.1 %collective-permute-start.16 = (bf16[4,4,48,384]{3,2,1,0:T(8,128)(2,1)S(1)}, bf16[4,4,48,384]{3,2,1,0:T(8,128)(2,1)S(1)}, u32[]{:S(2)}, u32[]{:S(2)}) collective-permute-start(bf16[4,4,48,384]{3,2,1,0:T(8,128)(2,1)S(1)} %pad_maximum_fusion.far0), channel_id=1, source_target_pairs={{0,1},{1,2},{2,3},{3,0},{4,5},{5,6},{6,7},{7,4},{8,9},{9,10},{10,1... | collective-permute-start | bytes 1769480 | tf_op jit(solution)/shard_map/ppermute | solution.py:24
  45.2 25.2 %collective-permute-start.15 = (bf16[4,4,48,384]{3,2,1,0:T(8,128)(2,1)S(1)}, bf16[4,4,48,384]{3,2,1,0:T(8,128)(2,1)S(1)}, u32[]{:S(2)}, u32[]{:S(2)}) collective-permute-start(bf16[4,4,48,384]{3,2,1,0:T(8,128)(2,1)S(1)} %pad_maximum_fusion.far0), channel_id=1, source_target_pairs={{0,2},{1,3},{2,0},{3,1},{4,6},{5,7},{6,4},{7,5},{8,10},{9,11},{10,... | collective-permute-start | bytes 1769480 | tf_op jit(solution)/shard_map/ppermute | solution.py:24
  47.1 23.3 %collective-permute-start.14 = (bf16[4,4,48,384]{3,2,1,0:T(8,128)(2,1)S(1)}, bf16[4,4,48,384]{3,2,1,0:T(8,128)(2,1)S(1)}, u32[]{:S(2)}, u32[]{:S(2)}) collective-permute-start(bf16[4,4,48,384]{3,2,1,0:T(8,128)(2,1)S(1)} %pad_maximum_fusion.far0), channel_id=1, source_target_pairs={{0,3},{1,0},{2,1},{3,2},{4,7},{5,4},{6,5},{7,6},{8,11},{9,8},{10,9... | collective-permute-start | bytes 1769480 | tf_op jit(solution)/shard_map/ppermute | solution.py:24
  70.4 8.6 %collective-permute-start.19 = (bf16[768,256]{1,0:T(8,128)(2,1)S(1)}, bf16[768,256]{1,0:T(8,128)(2,1)S(1)}, u32[]{:S(2)}, u32[]{:S(2)}) collective-permute-start(bf16[768,256]{1,0:T(8,128)(2,1)S(1)} %get-tuple-element.129), channel_id=1, source_target_pairs={{0,16},{1,17},{2,18},{3,19},{4,20},{5,21},{6,22},{7,23},{8,24},{9,... | collective-permute-start | bytes 1179656 | tf_op jit(solution)/shard_map/ppermute | solution.py:24
  71.7 13.1 %collective-permute-start.20 = (bf16[768,256]{1,0:T(8,128)(2,1)S(1)}, bf16[768,256]{1,0:T(8,128)(2,1)S(1)}, u32[]{:S(2)}, u32[]{:S(2)}) collective-permute-start(bf16[768,256]{1,0:T(8,128)(2,1)S(1)} %get-tuple-element.132), channel_id=1, source_target_pairs={{0,32},{1,33},{2,34},{3,35},{4,36},{5,37},{6,38},{7,39},{8,40},{9,... | collective-permute-start | bytes 1179656 | tf_op jit(solution)/shard_map/ppermute | solution.py:24
  75.2 9.6 %collective-permute-start.21 = (bf16[768,256]{1,0:T(8,128)(2,1)S(1)}, bf16[768,256]{1,0:T(8,128)(2,1)S(1)}, u32[]{:S(2)}, u32[]{:S(2)}) collective-permute-start(bf16[768,256]{1,0:T(8,128)(2,1)S(1)} %get-tuple-element.135), channel_id=1, source_target_pairs={{0,48},{1,49},{2,50},{3,51},{4,52},{5,53},{6,54},{7,55},{8,56},{9,... | collective-permute-start | bytes 1179656 | tf_op jit(solution)/shard_map/ppermute | solution.py:24
  79.1 14.0 %collective-permute-start.22 = (bf16[768,256]{1,0:T(8,128)(2,1)S(1)}, bf16[768,256]{1,0:T(8,128)(2,1)S(1)}, u32[]{:S(2)}, u32[]{:S(2)}) collective-permute-start(bf16[768,256]{1,0:T(8,128)(2,1)S(1)} %get-tuple-element.139), channel_id=1, source_target_pairs={{0,16},{1,17},{2,18},{3,19},{4,20},{5,21},{6,22},{7,23},{8,24},{9,... | collective-permute-start | bytes 1179656 | tf_op jit(solution)/shard_map/ppermute | solution.py:24
  84.8 9.6 %collective-permute-start.23 = (bf16[768,256]{1,0:T(8,128)(2,1)S(1)}, bf16[768,256]{1,0:T(8,128)(2,1)S(1)}, u32[]{:S(2)}, u32[]{:S(2)}) collective-permute-start(bf16[768,256]{1,0:T(8,128)(2,1)S(1)} %get-tuple-element.140), channel_id=1, source_target_pairs={{0,32},{1,33},{2,34},{3,35},{4,36},{5,37},{6,38},{7,39},{8,40},{9,... | collective-permute-start | bytes 1179656 | tf_op jit(solution)/shard_map/ppermute | solution.py:24
  84.8 9.6 %collective-permute-start.24 = (bf16[768,256]{1,0:T(8,128)(2,1)S(1)}, bf16[768,256]{1,0:T(8,128)(2,1)S(1)}, u32[]{:S(2)}, u32[]{:S(2)}) collective-permute-start(bf16[768,256]{1,0:T(8,128)(2,1)S(1)} %get-tuple-element.141), channel_id=1, source_target_pairs={{0,48},{1,49},{2,50},{3,51},{4,52},{5,53},{6,54},{7,55},{8,56},{9,... | collective-permute-start | bytes 1179656 | tf_op jit(solution)/shard_map/ppermute | solution.py:24
  87.8 9.6 %collective-permute-start.25 = (bf16[4,96,384]{2,1,0:T(8,128)(2,1)S(1)}, bf16[4,96,384]{2,1,0:T(8,128)(2,1)S(1)}, u32[]{:S(2)}, u32[]{:S(2)}) collective-permute-start(bf16[4,96,384]{2,1,0:T(8,128)(2,1)S(1)} %get-tuple-element.143), channel_id=1, source_target_pairs={{0,16},{1,17},{2,18},{3,19},{4,20},{5,21},{6,22},{7,23},{8,24},{9,... | collective-permute-start | bytes 884744 | tf_op jit(solution)/shard_map/ppermute | solution.py:24
  90.2 10.1 %collective-permute-start.26 = (bf16[4,96,384]{2,1,0:T(8,128)(2,1)S(1)}, bf16[4,96,384]{2,1,0:T(8,128)(2,1)S(1)}, u32[]{:S(2)}, u32[]{:S(2)}) collective-permute-start(bf16[4,96,384]{2,1,0:T(8,128)(2,1)S(1)} %get-tuple-element.144), channel_id=1, source_target_pairs={{0,32},{1,33},{2,34},{3,35},{4,36},{5,37},{6,38},{7,39},{8,40},{9,... | collective-permute-start | bytes 884744 | tf_op jit(solution)/shard_map/ppermute | solution.py:24
  101.5 10.0 %collective-permute-start.28 = (bf16[384,384]{1,0:T(8,128)(2,1)S(1)}, bf16[384,384]{1,0:T(8,128)(2,1)S(1)}, u32[]{:S(2)}, u32[]{:S(2)}) collective-permute-start(bf16[384,384]{1,0:T(8,128)(2,1)S(1)} %get-tuple-element.147), channel_id=1, source_target_pairs={{0,1},{1,2},{2,3},{3,0},{4,5},{5,6},{6,7},{7,4},{8,9},{9,10},{10,1... | collective-permute-start | bytes 884744 | tf_op jit(solution)/shard_map/ppermute | solution.py:24
  101.6 9.9 %collective-permute-start.29 = (bf16[384,384]{1,0:T(8,128)(2,1)S(1)}, bf16[384,384]{1,0:T(8,128)(2,1)S(1)}, u32[]{:S(2)}, u32[]{:S(2)}) collective-permute-start(bf16[384,384]{1,0:T(8,128)(2,1)S(1)} %get-tuple-element.148), channel_id=1, source_target_pairs={{0,2},{1,3},{2,0},{3,1},{4,6},{5,7},{6,4},{7,5},{8,10},{9,11},{10,... | collective-permute-start | bytes 884744 | tf_op jit(solution)/shard_map/ppermute | solution.py:24
  102.5 9.7 %collective-permute-start.30 = (bf16[384,384]{1,0:T(8,128)(2,1)S(1)}, bf16[384,384]{1,0:T(8,128)(2,1)S(1)}, u32[]{:S(2)}, u32[]{:S(2)}) collective-permute-start(bf16[384,384]{1,0:T(8,128)(2,1)S(1)} %get-tuple-element.149), channel_id=1, source_target_pairs={{0,3},{1,0},{2,1},{3,2},{4,7},{5,4},{6,5},{7,6},{8,11},{9,8},{10,9... | collective-permute-start | bytes 884744 | tf_op jit(solution)/shard_map/ppermute | solution.py:24
  104.3 9.4 %collective-permute-start.18 = (bf16[256,384]{1,0:T(8,128)(2,1)S(1)}, bf16[256,384]{1,0:T(8,128)(2,1)S(1)}, u32[]{:S(2)}, u32[]{:S(2)}) collective-permute-start(bf16[256,384]{1,0:T(8,128)(2,1)S(1)} %collective-permute-done.17.flipped), channel_id=1, source_target_pairs={{0,16},{1,17},{2,18},{3,19},{4,20},{5,21},{6,22},{7,23},{16,32},{1... | collective-permute-start | bytes 589832 | tf_op jit(solution)/shard_map/ppermute | solution.py:24
  114.4 19.1 %all-to-all-start = ((bf16[8,48,384]{2,1,0:T(8,128)(2,1)}), bf16[8,48,384]{2,1,0:T(8,128)(2,1)}, u32[]{:S(2)}, u32[]{:S(2)}) async-start(bf16[8,48,384]{2,1,0:T(8,128)(2,1)} %copy-done.3), calls=%async_computation | async-start | bytes 589824 | tf_op jit(solution)/shard_map/all_to_all | solution.py:363
  (27 other events, 194.6 us)

commit v10 on v6

--- a/solution.py
+++ b/solution.py
@@ -58,7 +58,7 @@
         in_specs=[pl.BlockSpec(memory_space=pltpu.SMEM)] + [vmem] * len(arrays),
         out_specs=[vmem] * len(outs),
         scratch_shapes=scratch,
-        compiler_params=pltpu.CompilerParams(vmem_limit_bytes=48 * 1024 * 1024),
+        compiler_params=pltpu.CompilerParams(vmem_limit_bytes=16 * 1024 * 1024),
         cost_estimate=pl.CostEstimate(flops=1, bytes_accessed=1, transcendentals=0),
     )(scalars, *arrays)
 
@@ -346,7 +346,7 @@
     messages = [messages[0]] + [send_a(part, k + 1) for k, part in enumerate(messages[1:])]
     block = (4, Hh // 4, Hh)
     p_own, *sends = run(point_kernel, meta, [ogs, hidden_t], [shape(block, F32)] + [shape(block, BF16)] * 3)
-    hg_flipped, *sends = lax.optimization_barrier((flip(hg), *sends))
+    hg_flipped, sends[2] = lax.optimization_barrier((flip(hg), sends[2]))
     p_all = [p_own] + [send_a(part, k + 1) for k, part in enumerate(sends)]
     conv, = run(gradient_kernel, meta, [*early, *messages], [shape((3 * Cq, Hh), F32)])
     hg_late, conv = lax.optimization_barrier((hg_flipped, conv))

time: 135 us -> 135 us (level)
  Pallas kernels: 20.1 us -> 15.8 us
  starting transfers between devices: 58.5 us -> 62 us
  local copies, waits for them, and re-layouts: 6.89 us -> 3.85 us
  blocking collectives: 15.7 us -> 17.5 us
  waiting for transfers between devices: 28.6 us -> 30.1 us
    pallas_call x11, Pallas kernels: 20.1 us -> 15.8 us  [run(): pl.pallas_call(kernel, out_shape=outs, in_specs=[pl.BlockSpec(memory_spac...]
    ppermute x34, starting transfers between devices: 58.5 us -> 62 us  [send(): return lax.ppermute(value, ('dp', 'seq'), pairs)]
    unnamed x24 -> x8, local copies, waits for them, and re-layouts: 3.06 us -> 0.02 us
    all_to_all x1, blocking collectives: 15.7 us -> 17.5 us  [local(): by_z = lax.all_to_all(by_z, ('dp', 'seq'), 0, 0, axis_index_groups=rings)]
    ppermute x34, waiting for transfers between devices: 28.6 us -> 30.1 us  [send(): return lax.ppermute(value, ('dp', 'seq'), pairs)]
  transfers between devices with their start and end apart: 34 -> 34, of which waited for: 12 -> 12; matrix products, arithmetic and copies ran while one was open for 4% -> 5% of each run, Pallas kernels for 12% -> 9%
where the time goes in v10:
time: 135 us
  starting transfers between devices  62 us (46%)
  waiting for transfers between devices  30.1 us (22%)
  blocking collectives  17.5 us (13%)
  Pallas kernels  15.8 us (12%)
  other arithmetic  4.29 us (3%)
  local copies, waits for them, and re-layouts  3.85 us (3%)
    ppermute x34, starting transfers between devices, send(): return lax.ppermute(value, ('dp', 'seq'), pairs)  62 us
    ppermute x34, waiting for transfers between devices, send(): return lax.ppermute(value, ('dp', 'seq'), pairs)  30.1 us
    all_to_all x1, blocking collectives, local(): by_z = lax.all_to_all(by_z, ('dp', 'seq'), 0, 0, axis_index_groups=rings)  17.5 us
    pallas_call x11, Pallas kernels, run(): pl.pallas_call(kernel, out_shape=outs, in_specs=[pl.BlockSpec(memory_spac...  15.8 us
  transfers between devices with their start and end apart: 34, of which 12 were waited for; matrix products, arithmetic and copies ran while one was open for 5% of the time, Pallas kernels for 9%

profile of v10, /device:TPU:1, one launch (start us, length us, event | category | flops | bytes accessed | tf_op | source)
XLA Modules:
  0.0 134.6 jit_solution(325251099409779716)
XLA Ops:
  2.5 8.7 %collective-permute-start.2 = (bf16[128,1536]{1,0:T(8,128)(2,1)}, bf16[128,1536]{1,0:T(8,128)(2,1)S(1)}, u32[]{:S(2)}, u32[]{:S(2)}) collective-permute-start(bf16[128,1536]{1,0:T(8,128)(2,1)} %bitcast.23), channel_id=1, source_target_pairs={{0,64},{1,65},{2,66},{3,67},{4,68},{5,69},{6,70},{7,71},{8,72},{9,... | collective-permute-start | bytes 1179656 | tf_op jit(solution)/shard_map/ppermute | solution.py:24
  13.0 2.1 %collective-permute-start.4 = (bf16[64,1536]{1,0:T(8,128)(2,1)}, bf16[64,1536]{1,0:T(8,128)(2,1)S(1)}, u32[]{:S(2)}, u32[]{:S(2)}) collective-permute-start(bf16[64,1536]{1,0:T(8,128)(2,1)} %get-tuple-element.169), channel_id=1, source_target_pairs={{0,8},{1,9},{2,10},{3,11},{4,12},{5,13},{6,14},{7,15},{8,0},{9,1},... | collective-permute-start | bytes 589832 | tf_op jit(solution)/shard_map/ppermute | solution.py:24
  15.8 4.2 %collective-permute-done.1 = bf16[48,384]{1,0:T(8,128)(2,1)S(1)} collective-permute-done((bf16[48,384]{1,0:T(8,128)(2,1)S(1)}, bf16[48,384]{1,0:T(8,128)(2,1)S(1)}, u32[]{:S(2)}, u32[]{:S(2)}) %collective-permute-start.1) | collective-permute-done | bytes 36896 | tf_op jit(solution)/shard_map/ppermute | solution.py:24
  20.0 4.4 %collective-permute-done.4 = bf16[64,1536]{1,0:T(8,128)(2,1)S(1)} collective-permute-done((bf16[64,1536]{1,0:T(8,128)(2,1)}, bf16[64,1536]{1,0:T(8,128)(2,1)S(1)}, u32[]{:S(2)}, u32[]{:S(2)}) %collective-permute-start.4) | collective-permute-done | bytes 196640 | tf_op jit(solution)/shard_map/ppermute | solution.py:24
  26.1 3.8 %collective-permute-start.7 = (bf16[64,1536]{1,0:T(8,128)(2,1)S(1)}, bf16[64,1536]{1,0:T(8,128)(2,1)}, u32[]{:S(2)}, u32[]{:S(2)}) collective-permute-start(bf16[64,1536]{1,0:T(8,128)(2,1)S(1)} %collective-permute-done.4), channel_id=1, source_target_pairs={{0,16},{1,17},{2,18},{3,19},{4,20},{5,21},{6,22},{7,23},{16,32},{1... | collective-permute-start | bytes 589832 | tf_op jit(solution)/shard_map/ppermute | solution.py:24
  31.4 2.6 %collective-permute-start.9 = (bf16[4,48,384]{2,1,0:T(8,128)(2,1)S(1)}, bf16[4,48,384]{2,1,0:T(8,128)(2,1)S(1)}, u32[]{:S(2)}, u32[]{:S(2)}) collective-permute-start(bf16[4,48,384]{2,1,0:T(8,128)(2,1)S(1)} %pad_maximum_fusion.3), channel_id=1, source_target_pairs={{0,32},{1,33},{2,34},{3,35},{4,36},{5,37},{6,38},{7,39},{8,40},{9,... | collective-permute-start | bytes 442376 | tf_op jit(solution)/shard_map/ppermute | solution.py:24
  38.1 3.7 %collective-permute-start.12 = (bf16[3,384,384]{2,1,0:T(8,128)(2,1)S(1)}, bf16[3,384,384]{2,1,0:T(8,128)(2,1)S(1)}, u32[]{:S(2)}, u32[]{:S(2)}) collective-permute-start(bf16[3,384,384]{2,1,0:T(8,128)(2,1)S(1)} %get-tuple-element.96), channel_id=1, source_target_pairs={{0,64},{1,65},{2,66},{3,67},{4,68},{5,69},{6,70},{7,71},{8,72},{9,... | collective-permute-start | bytes 2654216 | tf_op jit(solution)/shard_map/ppermute | solution.py:24
  46.6 2.1 %collective-permute-start.16 = (bf16[4,4,48,384]{3,2,1,0:T(8,128)(2,1)S(1)}, bf16[4,4,48,384]{3,2,1,0:T(8,128)(2,1)S(1)}, u32[]{:S(2)}, u32[]{:S(2)}) collective-permute-start(bf16[4,4,48,384]{3,2,1,0:T(8,128)(2,1)S(1)} %pad_maximum_fusion.far0), channel_id=1, source_target_pairs={{0,2},{1,3},{2,0},{3,1},{4,6},{5,7},{6,4},{7,5},{8,10},{9,11},{10,... | collective-permute-start | bytes 1769480 | tf_op jit(solution)/shard_map/ppermute | solution.py:24
  48.7 2.0 %collective-permute-start.15 = (bf16[4,4,48,384]{3,2,1,0:T(8,128)(2,1)S(1)}, bf16[4,4,48,384]{3,2,1,0:T(8,128)(2,1)S(1)}, u32[]{:S(2)}, u32[]{:S(2)}) collective-permute-start(bf16[4,4,48,384]{3,2,1,0:T(8,128)(2,1)S(1)} %pad_maximum_fusion.far0), channel_id=1, source_target_pairs={{0,3},{1,0},{2,1},{3,2},{4,7},{5,4},{6,5},{7,6},{8,11},{9,8},{10,9... | collective-permute-start | bytes 1769480 | tf_op jit(solution)/shard_map/ppermute | solution.py:24
  51.7 2.3 %shard_map.68 = (bf16[2,256,1536]{2,1,0:T(8,128)(2,1)S(1)}, bf16[256,1536]{1,0:T(8,128)(2,1)S(1)}, f32[256,384]{1,0:T(8,128)S(1)}, f32[256,192]{1,0:T(8,128)S(1)...) custom-call(s32[6]{0:T(128)S(1)} %stack.42.meta, ...), custom_call_target="tpu_custom_call" | custom-call | flops 1 | bytes 1 | tf_op jit(solution)/shard_map/pallas_call | solution.py:55
  58.1 6.1 %collective-permute-done.16.far2 = bf16[4,4,48,384]{3,2,1,0:T(8,128)(2,1)S(1)} collective-permute-done((bf16[4,4,48,384]{3,2,1,0:T(8,128)(2,1)S(1)}, bf16[4,4,48,384]{3,2,1,0:T(8,128)(2,1)S(1)}, u32[]{:S(2)}, u32[]{:S(2)}) %collective-permute-start.16) | collective-permute-done | bytes 589856 | tf_op jit(solution)/shard_map/ppermute | solution.py:24
  65.4 2.7 %collective-permute-start.20 = (bf16[768,256]{1,0:T(8,128)(2,1)S(1)}, bf16[768,256]{1,0:T(8,128)(2,1)S(1)}, u32[]{:S(2)}, u32[]{:S(2)}) collective-permute-start(bf16[768,256]{1,0:T(8,128)(2,1)S(1)} %get-tuple-element.138), channel_id=1, source_target_pairs={{0,32},{1,33},{2,34},{3,35},{4,36},{5,37},{6,38},{7,39},{8,40},{9,... | collective-permute-start | bytes 1179656 | tf_op jit(solution)/shard_map/ppermute | solution.py:24
  69.3 2.7 %shard_map.70 = (bf16[256,384]{1,0:T(8,128)(2,1)S(1)}, bf16[384,256]{1,0:T(8,128)(2,1)S(1)}, bf16[3,16,48,384]{3,2,1,0:T(8,128)(2,1)S(1)}, bf16[768,256]{1,0:T(8...) custom-call(s32[6]{0:T(128)S(1)} %stack.42.meta, ...), custom_call_target="tpu_custom_call" | custom-call | flops 1 | bytes 1 | tf_op jit(solution)/shard_map/pallas_call | solution.py:55
  73.0 4.4 %collective-permute-done.20.x2 = bf16[768,256]{1,0:T(8,128)(2,1)S(1)} collective-permute-done((bf16[768,256]{1,0:T(8,128)(2,1)S(1)}, bf16[768,256]{1,0:T(8,128)(2,1)S(1)}, u32[]{:S(2)}, u32[]{:S(2)}) %collective-permute-start.20) | collective-permute-done | bytes 393248 | tf_op jit(solution)/shard_map/ppermute | solution.py:24
  78.6 2.1 %collective-permute-start.24 = (bf16[768,256]{1,0:T(8,128)(2,1)S(1)}, bf16[768,256]{1,0:T(8,128)(2,1)S(1)}, u32[]{:S(2)}, u32[]{:S(2)}) collective-permute-start(bf16[768,256]{1,0:T(8,128)(2,1)S(1)} %get-tuple-element.147), channel_id=1, source_target_pairs={{0,48},{1,49},{2,50},{3,51},{4,52},{5,53},{6,54},{7,55},{8,56},{9,... | collective-permute-start | bytes 1179656 | tf_op jit(solution)/shard_map/ppermute | solution.py:24
  81.9 6.2 %collective-permute-start.26 = (bf16[4,96,384]{2,1,0:T(8,128)(2,1)S(1)}, bf16[4,96,384]{2,1,0:T(8,128)(2,1)S(1)}, u32[]{:S(2)}, u32[]{:S(2)}) collective-permute-start(bf16[4,96,384]{2,1,0:T(8,128)(2,1)S(1)} %get-tuple-element.151), channel_id=1, source_target_pairs={{0,32},{1,33},{2,34},{3,35},{4,36},{5,37},{6,38},{7,39},{8,40},{9,... | collective-permute-start | bytes 884744 | tf_op jit(solution)/shard_map/ppermute | solution.py:24
  88.1 2.7 %collective-permute-start.27 = (bf16[4,96,384]{2,1,0:T(8,128)(2,1)S(1)}, bf16[4,96,384]{2,1,0:T(8,128)(2,1)S(1)}, u32[]{:S(2)}, u32[]{:S(2)}) collective-permute-start(bf16[4,96,384]{2,1,0:T(8,128)(2,1)S(1)} %get-tuple-element.152), channel_id=1, source_target_pairs={{0,48},{1,49},{2,50},{3,51},{4,52},{5,53},{6,54},{7,55},{8,56},{9,... | collective-permute-start | bytes 884744 | tf_op jit(solution)/shard_map/ppermute | solution.py:24
  90.8 1.9 %shard_map.72.conv = f32[1152,384]{1,0:T(8,128)S(1)} custom-call(s32[6]{0:T(128)S(1)} %stack.42.meta, bf16[768,256]{1,0:T(8,128)(2,1)S(1)} %get-tuple-element.134.x0, bf16[768,256]{1,0:T(8,128)(2,1)S(1)} %collective-permute-done.19.x1, bf16[768,256]{1,0:T(8,128)(2,1)S(1)} %collective-permute-done.20.x2, bf16[768,256]{1,0:T(8,128)(2,1)S(1)} %collective-permute-done.21.x3, ...), custom_call_target="tpu_custom_call" | custom-call | flops 1 | bytes 1 | tf_op jit(solution)/shard_map/pallas_call | solution.py:55
  96.7 3.3 %collective-permute-start.29 = (bf16[384,384]{1,0:T(8,128)(2,1)S(1)}, bf16[384,384]{1,0:T(8,128)(2,1)S(1)}, u32[]{:S(2)}, u32[]{:S(2)}) collective-permute-start(bf16[384,384]{1,0:T(8,128)(2,1)S(1)} %get-tuple-element.155), channel_id=1, source_target_pairs={{0,2},{1,3},{2,0},{3,1},{4,6},{5,7},{6,4},{7,5},{8,10},{9,11},{10,... | collective-permute-start | bytes 884744 | tf_op jit(solution)/shard_map/ppermute | solution.py:24
  100.2 3.2 %collective-permute-start.31 = (bf16[256,384]{1,0:T(8,128)(2,1)S(1)}, bf16[256,384]{1,0:T(8,128)(2,1)S(1)}, u32[]{:S(2)}, u32[]{:S(2)}) collective-permute-start(bf16[256,384]{1,0:T(8,128)(2,1)S(1)} %collective-permute-done.18.flipped), channel_id=1, source_target_pairs={{0,16},{1,17},{2,18},{3,19},{4,20},{5,21},{6,22},{7,23},{16,32},{1... | collective-permute-start | bytes 589832 | tf_op jit(solution)/shard_map/ppermute | solution.py:24
  103.8 3.8 %collective-permute-done.29.got2 = bf16[384,384]{1,0:T(8,128)(2,1)S(1)} collective-permute-done((bf16[384,384]{1,0:T(8,128)(2,1)S(1)}, bf16[384,384]{1,0:T(8,128)(2,1)S(1)}, u32[]{:S(2)}, u32[]{:S(2)}) %collective-permute-start.29) | collective-permute-done | bytes 294944 | tf_op jit(solution)/shard_map/ppermute | solution.py:24
  108.3 2.1 %shard_map.75 = (f32[128,1536]{1,0:T(8,128)S(1)}, f32[128,1536]{1,0:T(8,128)S(1)}) custom-call(s32[6]{0:T(128)S(1)} %stack.42.meta, bf16[256,384]{1,0:T(8,128)(2,1)S(1)} %get-tuple-element.157.hg, bf16[256,384]{1,0:T(8,128)(2,1)S(1)} %collective-permute-done.18.flipped, bf16[256,384]{1,0:T(8,128)(2,1)S(1)} %collective-permute-done.31.hopped, ...), custom_call_target="tpu_custom_call" | custom-call | flops 1 | bytes 1 | tf_op jit(solution)/shard_map/pallas_call | solution.py:55
  110.4 3.0 %collective-permute-start.32 = (f32[128,1536]{1,0:T(8,128)S(1)}, f32[128,1536]{1,0:T(8,128)S(1)}, u32[]{:S(2)}, u32[]{:S(2)}) collective-permute-start(f32[128,1536]{1,0:T(8,128)S(1)} %get-tuple-element.161), channel_id=1, source_target_pairs={{0,64},{1,65},{2,66},{3,67},{4,68},{5,69},{6,70},{7,71},{8,72},{9,... | collective-permute-start | bytes 2359304 | tf_op jit(solution)/shard_map/ppermute | solution.py:24
  113.4 17.5 %all_to_all.5.parts = bf16[8,48,384]{2,1,0:T(8,128)(2,1)S(1)} all-to-all(bf16[8,48,384]{2,1,0:T(8,128)(2,1)S(1)} %shard_map.74), channel_id=1, replica_groups={{0,4,8,12,128,132,136,140},{64,68,72,76,192,196,200,204},{1,5,9,13,129,..., dimensions={0} | all-to-all | bytes 589824 | tf_op jit(solution)/shard_map/all_to_all | solution.py:367
  (80 shorter events, 36.1 us)
Async XLA Ops:
  1.8 22.6 %collective-permute-start = (bf16[3,48,768]{2,1,0:T(8,128)(2,1)S(1)}, bf16[3,48,768]{2,1,0:T(8,128)(2,1)S(1)}, u32[]{:S(2)}, u32[]{:S(2)}) collective-permute-start(bf16[3,48,768]{2,1,0:T(8,128)(2,1)S(1)} %constant_dynamic-slice_fusion.4), channel_id=1, source_target_pairs={{0,140},{1,141},{2,142},{3,143},{4,136},{5,137},{6,138},{7,139},{8... | collective-permute-start | bytes 663560 | tf_op jit(solution)/shard_map/ppermute | solution.py:24
  2.5 21.9 %collective-permute-start.2 = (bf16[128,1536]{1,0:T(8,128)(2,1)}, bf16[128,1536]{1,0:T(8,128)(2,1)S(1)}, u32[]{:S(2)}, u32[]{:S(2)}) collective-permute-start(bf16[128,1536]{1,0:T(8,128)(2,1)} %bitcast.23), channel_id=1, source_target_pairs={{0,64},{1,65},{2,66},{3,67},{4,68},{5,69},{6,70},{7,71},{8,72},{9,... | collective-permute-start | bytes 1179656 | tf_op jit(solution)/shard_map/ppermute | solution.py:24
  11.1 13.2 %collective-permute-start.3 = (bf16[128,1536]{1,0:T(8,128)(2,1)}, bf16[128,1536]{1,0:T(8,128)(2,1)S(1)}, u32[]{:S(2)}, u32[]{:S(2)}) collective-permute-start(bf16[128,1536]{1,0:T(8,128)(2,1)} %bitcast.21), channel_id=1, source_target_pairs={{0,64},{1,65},{2,66},{3,67},{4,68},{5,69},{6,70},{7,71},{8,72},{9,... | collective-permute-start | bytes 1179656 | tf_op jit(solution)/shard_map/ppermute | solution.py:24
  13.0 11.4 %collective-permute-start.4 = (bf16[64,1536]{1,0:T(8,128)(2,1)}, bf16[64,1536]{1,0:T(8,128)(2,1)S(1)}, u32[]{:S(2)}, u32[]{:S(2)}) collective-permute-start(bf16[64,1536]{1,0:T(8,128)(2,1)} %get-tuple-element.169), channel_id=1, source_target_pairs={{0,8},{1,9},{2,10},{3,11},{4,12},{5,13},{6,14},{7,15},{8,0},{9,1},... | collective-permute-start | bytes 589832 | tf_op jit(solution)/shard_map/ppermute | solution.py:24
  26.0 11.4 %collective-permute-start.6 = (bf16[64,1536]{1,0:T(8,128)(2,1)S(1)}, bf16[64,1536]{1,0:T(8,128)(2,1)}, u32[]{:S(2)}, u32[]{:S(2)}) collective-permute-start(bf16[64,1536]{1,0:T(8,128)(2,1)S(1)} %get-tuple-element.89), channel_id=1, source_target_pairs={{0,8},{1,9},{2,10},{3,11},{4,12},{5,13},{6,14},{7,15},{8,0},{9,1},... | collective-permute-start | bytes 589832 | tf_op jit(solution)/shard_map/ppermute | solution.py:24
  26.1 11.3 %collective-permute-start.7 = (bf16[64,1536]{1,0:T(8,128)(2,1)S(1)}, bf16[64,1536]{1,0:T(8,128)(2,1)}, u32[]{:S(2)}, u32[]{:S(2)}) collective-permute-start(bf16[64,1536]{1,0:T(8,128)(2,1)S(1)} %collective-permute-done.4), channel_id=1, source_target_pairs={{0,16},{1,17},{2,18},{3,19},{4,20},{5,21},{6,22},{7,23},{16,32},{1... | collective-permute-start | bytes 589832 | tf_op jit(solution)/shard_map/ppermute | solution.py:24
  41.9 8.8 %collective-permute-start.11 = (bf16[64,1536]{1,0:T(8,128)(2,1)}, bf16[64,1536]{1,0:T(8,128)(2,1)S(1)}, u32[]{:S(2)}, u32[]{:S(2)}) collective-permute-start(bf16[64,1536]{1,0:T(8,128)(2,1)} %collective-permute-done.6), channel_id=1, source_target_pairs={{0,16},{1,17},{2,18},{3,19},{4,20},{5,21},{6,22},{7,23},{16,32},{1... | collective-permute-start | bytes 589832 | tf_op jit(solution)/shard_map/ppermute | solution.py:24
  45.6 12.5 %collective-permute-start.17 = (bf16[4,4,48,384]{3,2,1,0:T(8,128)(2,1)S(1)}, bf16[4,4,48,384]{3,2,1,0:T(8,128)(2,1)S(1)}, u32[]{:S(2)}, u32[]{:S(2)}) collective-permute-start(bf16[4,4,48,384]{3,2,1,0:T(8,128)(2,1)S(1)} %pad_maximum_fusion.far0), channel_id=1, source_target_pairs={{0,1},{1,2},{2,3},{3,0},{4,5},{5,6},{6,7},{7,4},{8,9},{9,10},{10,1... | collective-permute-start | bytes 1769480 | tf_op jit(solution)/shard_map/ppermute | solution.py:24
  46.6 17.6 %collective-permute-start.16 = (bf16[4,4,48,384]{3,2,1,0:T(8,128)(2,1)S(1)}, bf16[4,4,48,384]{3,2,1,0:T(8,128)(2,1)S(1)}, u32[]{:S(2)}, u32[]{:S(2)}) collective-permute-start(bf16[4,4,48,384]{3,2,1,0:T(8,128)(2,1)S(1)} %pad_maximum_fusion.far0), channel_id=1, source_target_pairs={{0,2},{1,3},{2,0},{3,1},{4,6},{5,7},{6,4},{7,5},{8,10},{9,11},{10,... | collective-permute-start | bytes 1769480 | tf_op jit(solution)/shard_map/ppermute | solution.py:24
  48.7 15.5 %collective-permute-start.15 = (bf16[4,4,48,384]{3,2,1,0:T(8,128)(2,1)S(1)}, bf16[4,4,48,384]{3,2,1,0:T(8,128)(2,1)S(1)}, u32[]{:S(2)}, u32[]{:S(2)}) collective-permute-start(bf16[4,4,48,384]{3,2,1,0:T(8,128)(2,1)S(1)} %pad_maximum_fusion.far0), channel_id=1, source_target_pairs={{0,3},{1,0},{2,1},{3,2},{4,7},{5,4},{6,5},{7,6},{8,11},{9,8},{10,9... | collective-permute-start | bytes 1769480 | tf_op jit(solution)/shard_map/ppermute | solution.py:24
  64.2 8.1 %collective-permute-start.19 = (bf16[768,256]{1,0:T(8,128)(2,1)S(1)}, bf16[768,256]{1,0:T(8,128)(2,1)S(1)}, u32[]{:S(2)}, u32[]{:S(2)}) collective-permute-start(bf16[768,256]{1,0:T(8,128)(2,1)S(1)} %get-tuple-element.135), channel_id=1, source_target_pairs={{0,16},{1,17},{2,18},{3,19},{4,20},{5,21},{6,22},{7,23},{8,24},{9,... | collective-permute-start | bytes 1179656 | tf_op jit(solution)/shard_map/ppermute | solution.py:24
  65.4 12.1 %collective-permute-start.20 = (bf16[768,256]{1,0:T(8,128)(2,1)S(1)}, bf16[768,256]{1,0:T(8,128)(2,1)S(1)}, u32[]{:S(2)}, u32[]{:S(2)}) collective-permute-start(bf16[768,256]{1,0:T(8,128)(2,1)S(1)} %get-tuple-element.138), channel_id=1, source_target_pairs={{0,32},{1,33},{2,34},{3,35},{4,36},{5,37},{6,38},{7,39},{8,40},{9,... | collective-permute-start | bytes 1179656 | tf_op jit(solution)/shard_map/ppermute | solution.py:24
  68.1 10.6 %collective-permute-start.21 = (bf16[768,256]{1,0:T(8,128)(2,1)S(1)}, bf16[768,256]{1,0:T(8,128)(2,1)S(1)}, u32[]{:S(2)}, u32[]{:S(2)}) collective-permute-start(bf16[768,256]{1,0:T(8,128)(2,1)S(1)} %get-tuple-element.141), channel_id=1, source_target_pairs={{0,48},{1,49},{2,50},{3,51},{4,52},{5,53},{6,54},{7,55},{8,56},{9,... | collective-permute-start | bytes 1179656 | tf_op jit(solution)/shard_map/ppermute | solution.py:24
  72.3 15.7 %collective-permute-start.22 = (bf16[768,256]{1,0:T(8,128)(2,1)S(1)}, bf16[768,256]{1,0:T(8,128)(2,1)S(1)}, u32[]{:S(2)}, u32[]{:S(2)}) collective-permute-start(bf16[768,256]{1,0:T(8,128)(2,1)S(1)} %get-tuple-element.145), channel_id=1, source_target_pairs={{0,16},{1,17},{2,18},{3,19},{4,20},{5,21},{6,22},{7,23},{8,24},{9,... | collective-permute-start | bytes 1179656 | tf_op jit(solution)/shard_map/ppermute | solution.py:24
  72.4 9.5 %collective-permute-start.18 = (bf16[256,384]{1,0:T(8,128)(2,1)S(1)}, bf16[256,384]{1,0:T(8,128)(2,1)S(1)}, u32[]{:S(2)}, u32[]{:S(2)}) collective-permute-start(bf16[256,384]{1,0:T(8,128)(2,1)S(1)} %get-tuple-element.157.hg), channel_id=1, source_target_pairs={{0,8},{1,9},{2,10},{3,11},{4,12},{5,13},{6,14},{7,15},{8,0},{9,1},... | collective-permute-start | bytes 589832 | tf_op jit(solution)/shard_map/ppermute | solution.py:24
  77.4 13.4 %collective-permute-start.23 = (bf16[768,256]{1,0:T(8,128)(2,1)S(1)}, bf16[768,256]{1,0:T(8,128)(2,1)S(1)}, u32[]{:S(2)}, u32[]{:S(2)}) collective-permute-start(bf16[768,256]{1,0:T(8,128)(2,1)S(1)} %get-tuple-element.146), channel_id=1, source_target_pairs={{0,32},{1,33},{2,34},{3,35},{4,36},{5,37},{6,38},{7,39},{8,40},{9,... | collective-permute-start | bytes 1179656 | tf_op jit(solution)/shard_map/ppermute | solution.py:24
  78.6 12.2 %collective-permute-start.24 = (bf16[768,256]{1,0:T(8,128)(2,1)S(1)}, bf16[768,256]{1,0:T(8,128)(2,1)S(1)}, u32[]{:S(2)}, u32[]{:S(2)}) collective-permute-start(bf16[768,256]{1,0:T(8,128)(2,1)S(1)} %get-tuple-element.147), channel_id=1, source_target_pairs={{0,48},{1,49},{2,50},{3,51},{4,52},{5,53},{6,54},{7,55},{8,56},{9,... | collective-permute-start | bytes 1179656 | tf_op jit(solution)/shard_map/ppermute | solution.py:24
  81.8 10.9 %collective-permute-start.25 = (bf16[4,96,384]{2,1,0:T(8,128)(2,1)S(1)}, bf16[4,96,384]{2,1,0:T(8,128)(2,1)S(1)}, u32[]{:S(2)}, u32[]{:S(2)}) collective-permute-start(bf16[4,96,384]{2,1,0:T(8,128)(2,1)S(1)} %get-tuple-element.150), channel_id=1, source_target_pairs={{0,16},{1,17},{2,18},{3,19},{4,20},{5,21},{6,22},{7,23},{8,24},{9,... | collective-permute-start | bytes 884744 | tf_op jit(solution)/shard_map/ppermute | solution.py:24
  81.9 12.2 %collective-permute-start.26 = (bf16[4,96,384]{2,1,0:T(8,128)(2,1)S(1)}, bf16[4,96,384]{2,1,0:T(8,128)(2,1)S(1)}, u32[]{:S(2)}, u32[]{:S(2)}) collective-permute-start(bf16[4,96,384]{2,1,0:T(8,128)(2,1)S(1)} %get-tuple-element.151), channel_id=1, source_target_pairs={{0,32},{1,33},{2,34},{3,35},{4,36},{5,37},{6,38},{7,39},{8,40},{9,... | collective-permute-start | bytes 884744 | tf_op jit(solution)/shard_map/ppermute | solution.py:24
  88.1 7.8 %collective-permute-start.27 = (bf16[4,96,384]{2,1,0:T(8,128)(2,1)S(1)}, bf16[4,96,384]{2,1,0:T(8,128)(2,1)S(1)}, u32[]{:S(2)}, u32[]{:S(2)}) collective-permute-start(bf16[4,96,384]{2,1,0:T(8,128)(2,1)S(1)} %get-tuple-element.152), channel_id=1, source_target_pairs={{0,48},{1,49},{2,50},{3,51},{4,52},{5,53},{6,54},{7,55},{8,56},{9,... | collective-permute-start | bytes 884744 | tf_op jit(solution)/shard_map/ppermute | solution.py:24
  96.7 10.9 %collective-permute-start.29 = (bf16[384,384]{1,0:T(8,128)(2,1)S(1)}, bf16[384,384]{1,0:T(8,128)(2,1)S(1)}, u32[]{:S(2)}, u32[]{:S(2)}) collective-permute-start(bf16[384,384]{1,0:T(8,128)(2,1)S(1)} %get-tuple-element.155), channel_id=1, source_target_pairs={{0,2},{1,3},{2,0},{3,1},{4,6},{5,7},{6,4},{7,5},{8,10},{9,11},{10,... | collective-permute-start | bytes 884744 | tf_op jit(solution)/shard_map/ppermute | solution.py:24
  100.0 7.6 %collective-permute-start.30 = (bf16[384,384]{1,0:T(8,128)(2,1)S(1)}, bf16[384,384]{1,0:T(8,128)(2,1)S(1)}, u32[]{:S(2)}, u32[]{:S(2)}) collective-permute-start(bf16[384,384]{1,0:T(8,128)(2,1)S(1)} %get-tuple-element.156), channel_id=1, source_target_pairs={{0,3},{1,0},{2,1},{3,2},{4,7},{5,4},{6,5},{7,6},{8,11},{9,8},{10,9... | collective-permute-start | bytes 884744 | tf_op jit(solution)/shard_map/ppermute | solution.py:24
  100.2 8.2 %collective-permute-start.31 = (bf16[256,384]{1,0:T(8,128)(2,1)S(1)}, bf16[256,384]{1,0:T(8,128)(2,1)S(1)}, u32[]{:S(2)}, u32[]{:S(2)}) collective-permute-start(bf16[256,384]{1,0:T(8,128)(2,1)S(1)} %collective-permute-done.18.flipped), channel_id=1, source_target_pairs={{0,16},{1,17},{2,18},{3,19},{4,20},{5,21},{6,22},{7,23},{16,32},{1... | collective-permute-start | bytes 589832 | tf_op jit(solution)/shard_map/ppermute | solution.py:24
  110.4 22.0 %collective-permute-start.32 = (f32[128,1536]{1,0:T(8,128)S(1)}, f32[128,1536]{1,0:T(8,128)S(1)}, u32[]{:S(2)}, u32[]{:S(2)}) collective-permute-start(f32[128,1536]{1,0:T(8,128)S(1)} %get-tuple-element.161), channel_id=1, source_target_pairs={{0,64},{1,65},{2,66},{3,67},{4,68},{5,69},{6,70},{7,71},{8,72},{9,... | collective-permute-start | bytes 2359304 | tf_op jit(solution)/shard_map/ppermute | solution.py:24
  (14 other events, 134.0 us)
